TPU v7x, 512 devices: a whole 4x4x16 slice. The times are simulated.
512 devices in a mesh: dp: 64 (over z, y), context: 8 (over x, core).
Axes of the slice: x: 4, y: 4, z: 16, core: 2. Of those that a mesh axis runs over, the one named last changes fastest.
Arguments:
- hidden_in: bfloat16 [64, 1024, 2048], P('dp', 'context'), may hold values from -6 to 6
- cotangent: bfloat16 [64, 1024, 2048], P('dp', 'context'), may hold values from -6 to 6
- tile_depth: int32 [64, 8], P('dp'), may hold values from 1 to 4, as said below
- w_qkv: bfloat16 [3, 2048, 1024], P(None, 'dp', 'context'), may hold values from -0.125 to 0.125
- w_out: bfloat16 [1024, 2048], P('context', 'dp'), may hold values from -0.1875 to 0.1875
- gain: float32 [2048], replicated, may hold values from 0.1 to 1.9
Outputs:
- hidden_out: bfloat16 [64, 1024, 2048], P('dp', 'context')
- grad_in: bfloat16 [64, 1024, 2048], P('dp', 'context')
- grad_qkv: float32 [3, 2048, 1024], P(None, 'dp', 'context')
- grad_out: float32 [1024, 2048], P('context', 'dp')
Inputs may be any that keep to these rules, and one draw needn't show every extreme that they name: `tile_depth`: in every document at most 1 tiles have depth 2 or more and at most 1 have depth 3 or more; some document has exactly 1 and 1 such tiles.
All inputs are finite; a program needn't handle non-finite values.
Results may differ from a plain program's by a relative error of at most 0.028.
Values may be sent and summed in bfloat16 or wider, within the bound.
No kernel may reach another device: no remote copies, remote signals or barrier semaphores. Data moves between devices by JAX's collectives and lax.ppermute only.
A program may use at most 64 MiB of HBM per device.

v0:
```python
import jax
import jax.numpy as jnp
from jax import lax
from jax.sharding import PartitionSpec as P

HD = 128


def from_root(value, axis, source):
    kept = jnp.where(lax.axis_index(axis) == source, value, 0).astype(value.dtype)
    return lax.psum(kept, axis)


def slot_plan(depth, level, cap, me):
    alive = depth >= level
    alive_int = alive.astype(jnp.int32)
    rank = jnp.cumsum(alive_int) - alive_int
    places = jnp.arange(depth.shape[0], dtype=jnp.int32)
    owners = [jnp.sum(jnp.where(alive & (rank == 0), places, 0))]
    valid = [jnp.any(alive & (rank == 0))]
    own_alive = jnp.any(alive & (places == me))
    own_slot = jnp.sum(jnp.where(places == me, jnp.minimum(rank, cap - 1), 0))
    return (owners, valid, own_alive, own_slot)


def gather_slots(tile_rows, owners, valid):
    pieces = []
    for owner, usable in zip(owners, valid):
        got = from_root(tile_rows, "context", owner)
        pieces.append(jnp.where(usable, got, jnp.zeros_like(got)))
    return pieces[0]


def head_sum(terms):
    return lax.psum(terms.astype(jnp.bfloat16), "context").astype(jnp.float32)


def forward_level(state, plan, full_qkv, full_out, gain):
    owners, valid, own_alive, own_slot = plan
    tile = state.shape[0]
    x32 = state.astype(jnp.float32)
    inv = lax.rsqrt(jnp.mean(x32 * x32, -1, keepdims=True) + 1e-06)
    normed = (x32 * inv * gain).astype(jnp.bfloat16)
    rows = gather_slots(normed, owners, valid)
    count = rows.shape[0]
    local_heads = full_qkv.shape[2] // HD
    qkv = jnp.einsum("rd,tdc->trc", rows, full_qkv, preferred_element_type=jnp.float32).astype(
        jnp.bfloat16
    )
    heads = qkv.reshape(3, count, local_heads, HD)
    query, key, value = (heads[0], heads[1], heads[2])
    valid_rows = jnp.repeat(jnp.stack(valid), tile)
    pos = jnp.arange(count)
    allowed = valid_rows[None, :] & (pos[None, :] <= pos[:, None])
    scores = jnp.einsum("qhd,khd->hqk", query, key, preferred_element_type=jnp.float32) * HD ** (
        -0.5
    )
    scores = jnp.where(allowed[None], scores, -1e30)
    top = jnp.max(scores, -1, keepdims=True)
    expo = jnp.exp(scores - top)
    prob = expo / jnp.sum(expo, -1, keepdims=True)
    probb = prob.astype(jnp.bfloat16)
    attn = jnp.einsum("hqk,khd->qhd", probb, value, preferred_element_type=jnp.float32).astype(
        jnp.bfloat16
    )
    attn_flat = attn.reshape(count, local_heads * HD)
    mixed = head_sum(jnp.dot(attn_flat, full_out, preferred_element_type=jnp.float32))
    new_state = (x32 + jnp.where(own_alive, mixed, jnp.zeros_like(mixed))).astype(jnp.bfloat16)
    return (new_state, (x32, inv, rows, query, key, value, prob, probb, attn, attn_flat))


def backward_level(grad_tile, keep, plan, full_qkv, full_out, gain):
    owners, valid, own_alive, own_slot = plan
    x32, inv, rows, query, key, value, prob, probb, attn, attn_flat = keep
    count = rows.shape[0]
    local_heads = query.shape[1]
    masked = jnp.where(own_alive, grad_tile, jnp.zeros_like(grad_tile))
    grad_rows = gather_slots(masked, owners, valid)
    dattn = jnp.einsum("rd,cd->rc", grad_rows, full_out, preferred_element_type=jnp.float32).astype(
        jnp.bfloat16
    )
    grad_wo = jnp.einsum("rc,rd->cd", attn_flat, grad_rows, preferred_element_type=jnp.float32)
    dheads = dattn.reshape(count, local_heads, HD)
    delta = jnp.sum(dheads.astype(jnp.float32) * attn.astype(jnp.float32), -1)
    dprob = jnp.einsum("qhd,khd->hqk", dheads, value, preferred_element_type=jnp.float32)
    dscore = (prob * (dprob - delta.T[:, :, None]) * HD ** (-0.5)).astype(jnp.bfloat16)
    d_query = jnp.einsum("hqk,khd->qhd", dscore, key, preferred_element_type=jnp.float32).astype(
        jnp.bfloat16
    )
    d_key = jnp.einsum("hqk,qhd->khd", dscore, query, preferred_element_type=jnp.float32).astype(
        jnp.bfloat16
    )
    d_value = jnp.einsum("hqk,qhd->khd", probb, dheads, preferred_element_type=jnp.float32).astype(
        jnp.bfloat16
    )
    dqkv = jnp.stack([d_query, d_key, d_value]).reshape(3, count, local_heads * HD)
    grad_wqkv = jnp.einsum("rd,trc->tdc", rows, dqkv, preferred_element_type=jnp.float32)
    dnorm = head_sum(jnp.einsum("trc,tdc->rd", dqkv, full_qkv, preferred_element_type=jnp.float32))
    scaled = dnorm * gain
    dx = inv * scaled - x32 * inv**3 * jnp.mean(x32 * scaled, -1, keepdims=True)
    dx = jnp.where(own_alive, dx, jnp.zeros_like(dx))
    new_grad = (grad_tile.astype(jnp.float32) + dx).astype(jnp.bfloat16)
    return (new_grad, grad_wqkv, grad_wo)


def on_device(hidden_in, cotangent, tile_depth, w_qkv, w_out, gain):
    count = lax.axis_size("context")
    me = lax.axis_index("context")
    depth = tile_depth[0]
    plans = [
        slot_plan(depth, 2, max(1, count // 8), me),
        slot_plan(depth, 3, max(1, count // 16), me),
    ]
    full_qkv, full_out = (
        lax.all_gather(w_qkv, "dp", axis=1, tiled=True),
        lax.all_gather(w_out, "dp", axis=1, tiled=True),
    )
    state = hidden_in[0]
    saved = []
    for plan in plans:
        state, keep = forward_level(state, plan, full_qkv, full_out, gain)
        saved.append(keep)
    back_qkv, back_out = (
        lax.all_gather(w_qkv, "dp", axis=1, tiled=True),
        lax.all_gather(w_out, "dp", axis=1, tiled=True),
    )
    grad_state = cotangent[0]
    total_qkv = jnp.zeros(full_qkv.shape, jnp.float32)
    total_out = jnp.zeros(full_out.shape, jnp.float32)
    for index in (1, 0):
        grad_state, part_qkv, part_out = backward_level(
            grad_state, saved[index], plans[index], back_qkv, back_out, gain
        )
        total_qkv = total_qkv + part_qkv
        total_out = total_out + part_out
    shard_qkv, shard_out = (
        lax.psum_scatter(total_qkv, "dp", scatter_dimension=1, tiled=True),
        lax.psum_scatter(total_out, "dp", scatter_dimension=1, tiled=True),
    )
    return (state[None], grad_state[None], shard_qkv, shard_out)


def solution(mesh):
    in_specs = (
        P("dp", "context", None),
        P("dp", "context", None),
        P("dp", None),
        P(None, "dp", "context"),
        P("context", "dp"),
        P(),
    )
    out_specs = (
        P("dp", "context", None),
        P("dp", "context", None),
        P(None, "dp", "context"),
        P("context", "dp"),
    )
    return jax.shard_map(
        on_device, mesh=mesh, in_specs=in_specs, out_specs=out_specs, check_vma=False
    )
```

profile of v0, /device:TPU:6, one launch (start us, length us, event | category | flops | bytes accessed | tf_op | source)
XLA Modules:
  0.0 1202.1 jit_solution(11256619872625842961)
XLA Ops:
  8.1 1.2 fusion.28
  9.3 0.7 convert_bitcast_fusion
  10.3 1.3 fusion.91
  11.7 0.6 select_reduce_fusion.1
  13.0 2.1 fusion.39
  15.1 0.5 all-gather.2.cloned.1.call-update
  15.7 0.6 select_reduce_fusion
  17.0 106.7 %all_gather.9 = bf16[128,2048]{0,1:T(8,128)(2,1)S(1)} all-gather(bf16[128,32]{0,1:T(8,128)(2,1)S(1)} %copy-done.10), channel_id=1, replica_groups=mesh['dp'=64,'context'=8] {'dp'}, dimensions={1}, use_global_device_ids=true | all-gather | bytes 532480 | tf_op jit(solution)/shard_map/all_gather | solution.py:116
  123.6 34.1 %all-gather.2.cloned.1.call-done = bf16[3,2048,128]{2,1,0:T(8,128)(2,1)} async-done(((bf16[3,32,128]{2,1,0:T(8,128)(2,1)}), bf16[3,2048,128]{2,1,0:T(8,128)(2,1)}) %all-gather.2.cloned.1.call-update) | async-done | bytes 1572880 | tf_op jit(solution)/shard_map/all_gather | solution.py:115
  157.8 2.5 fusion.2
  160.3 0.9 fusion.94
  161.2 0.2 convolution_convert_fusion.13
  161.4 1.1 convolution_convert_fusion.1
  162.7 1.5 select_bitcast_fusion
  164.1 68.6 %all-reduce.13.cloned.1.call-done = bf16[128,2048]{1,0:T(8,128)(2,1)} async-done(((bf16[128,2048]{1,0:T(8,128)(2,1)}), bf16[128,2048]{1,0:T(8,128)(2,1)}) %all-reduce.13.cloned.1.call-update) | async-done | bytes 524304 | tf_op jit(solution)/shard_map/psum | solution.py:35
  232.7 2.0 fusion.18
  234.8 1.0 fusion.41
  235.9 77.3 %all-reduce.23.cloned.1.call-done = (bf16[128,2048]{1,0:T(8,128)(2,1)}, bf16[128,2048]{1,0:T(8,128)(2,1)}) async-done(((bf16[128,2048]{1,0:T(8,128)(2,1)}, bf16[128,2048]{1,0:T(8,128)(2,1)}), (bf16[128,2048]{1,0:T(8,128)(2,1)}, bf16[128,2048]{1,0:T(8,128)(2,1)})) %all-reduce.23.cloned.1.call-update) | async-done | bytes 1048592 | tf_op jit(solution)/shard_map/psum | solution.py:11
  313.1 1.1 fusion.3
  314.3 0.8 fusion.95
  315.2 0.2 convolution_convert_fusion.12
  315.4 1.0 fusion.57
  316.7 0.2 fusion.13
  316.9 0.2 fusion.12
  317.1 1.4 fusion
  318.6 76.7 %all-reduce.15.cloned.1.call-done = bf16[128,2048]{1,0:T(8,128)(2,1)} async-done(((bf16[128,2048]{1,0:T(8,128)(2,1)}), bf16[128,2048]{1,0:T(8,128)(2,1)}) %all-reduce.15.cloned.1.call-update) | async-done | bytes 524304 | tf_op jit(solution)/shard_map/psum | solution.py:35
  395.3 1.3 fusion.27
  396.6 3.9 select_select_fusion
  400.6 1.1 convolution_convert_fusion
  401.8 74.3 %all-reduce.17.cloned.1.call-done = bf16[128,2048]{1,0:T(8,128)(2,1)} async-done(((bf16[128,2048]{1,0:T(8,128)(2,1)}), bf16[128,2048]{1,0:T(8,128)(2,1)}) %all-reduce.17.cloned.1.call-update) | async-done | bytes 524304 | tf_op jit(solution)/shard_map/psum | solution.py:11
  476.1 1.0 fusion.56
  477.4 0.2 fusion.16
  477.6 0.2 fusion.15
  477.8 1.5 fusion.1
  479.3 1.2 fusion.42
  480.6 2.9 add_bitcast_fusion
  483.5 5.0 copy.19
  488.5 1.0 copy-done.5
  489.5 1.0 fusion.47
  490.5 2.1 convolution_add_fusion
  492.6 1.3 dynamic-slice
  494.6 63.3 %all-reduce.21.cloned.1.call-done = (bf16[128,2048]{1,0:T(8,128)(2,1)}, bf16[128,2048]{1,0:T(8,128)(2,1)}) async-done(((bf16[128,2048]{1,0:T(8,128)(2,1)}, bf16[128,2048]{1,0:T(8,128)(2,1)}), (bf16[128,2048]{1,0:T(8,128)(2,1)}, bf16[128,2048]{1,0:T(8,128)(2,1)})) %all-reduce.21.cloned.1.call-update) | async-done | bytes 1048592 | tf_op jit(solution)/shard_map/psum | solution.py:35
  557.9 1.3 fusion.37
  559.2 4.0 fusion.38
  563.2 289.6 %all-reduce.19.cloned.1.call-done = f32[3,2048,128]{2,0,1:T(4,128)} async-done(((f32[3,2048,128]{2,0,1:T(4,128)}), f32[3,2048,128]{2,0,1:T(4,128)}) %all-reduce.19.cloned.1.call-update) | async-done | bytes 3145744
  852.9 0.9 constant_dynamic-slice_fusion
  853.7 0.6 copy.20
  854.3 340.3 %reduce-scatter.2.cloned.1.call-done = f32[128,32]{0,1:T(8,128)} async-done(((f32[128,2048]{0,1:T(8,128)}), f32[128,32]{0,1:T(8,128)}) %reduce-scatter.2.cloned.1.call-update) | async-done | bytes 16400 | tf_op jit(solution)/shard_map/reduce_scatter | solution.py:138
  (51 shorter events, 1.7 us)
Async XLA Ops:
  8.0 9.0 copy-start.10
  8.0 115.6 %all-reduce.11.cloned.1.call-start = ((), (), s32[]{:S(2)}) async-start(), calls=%async_computation.1 | async-start | bytes 1048576 | tf_op jit(solution)/shard_map/psum | solution.py:11
  15.0 142.7 %all-gather.2.cloned.1.call-start = ((), (), s32[]{:S(2)}) async-start(), calls=%async_computation.2 | async-start | bytes 1597440 | tf_op jit(solution)/shard_map/all_gather | solution.py:115
  15.6 217.1 %all-reduce.13.cloned.1.call-start = ((), (), s32[]{:S(2)}) async-start(), calls=%async_computation.3 | async-start | bytes 1048576 | tf_op jit(solution)/shard_map/psum | solution.py:35
  160.3 2.4 copy-start.2
  160.3 72.4 %copy-start = (bf16[1,128,2048]{2,1,0:T(8,128)(2,1)S(1)}, bf16[1,128,2048]{2,1,0:T(8,128)(2,1)}, u32[]{:S(2)}) copy-start(bf16[1,128,2048]{2,1,0:T(8,128)(2,1)} %param.6) | copy-start | bytes 1572868
  162.6 72.2 %copy-start.9 = (f32[2048]{0:T(1024)S(1)}, f32[2048]{0:T(1024)}, u32[]{:S(2)}) copy-start(f32[2048]{0:T(1024)} %param.11) | copy-start | bytes 24580
  162.6 150.5 %all-reduce.23.cloned.1.call-start = ((), (), s32[]{:S(2)}) async-start(), calls=%async_computation.9 | async-start | bytes 2097152 | tf_op jit(solution)/shard_map/psum | solution.py:11
  232.7 80.4 %copy-start.1 = (bf16[3,2048,128]{2,1,0:T(8,128)(2,1)S(1)}, bf16[3,2048,128]{2,1,0:T(8,128)(2,1)}, u32[]{:S(2)}) copy-start(bf16[3,2048,128]{2,1,0:T(8,128)(2,1)} %all-gather.2.cloned.1.call-done) | copy-start | bytes 4718596
  235.8 159.5 %all-reduce.15.cloned.1.call-start = ((), (), s32[]{:S(2)}) async-start(), calls=%async_computation.4 | async-start | bytes 1048576 | tf_op jit(solution)/shard_map/psum | solution.py:35
  313.1 2.2 copy-start.4
  318.5 157.5 %all-reduce.17.cloned.1.call-start = ((), (), s32[]{:S(2)}) async-start(), calls=%async_computation.5 | async-start | bytes 1048576 | tf_op jit(solution)/shard_map/psum | solution.py:11
  400.6 157.3 %all-reduce.21.cloned.1.call-start = ((), (), s32[]{:S(2)}) async-start(), calls=%async_computation.8 | async-start | bytes 2097152 | tf_op jit(solution)/shard_map/psum | solution.py:35
  477.8 1.6 copy-start.6
  479.3 1.3 copy-start.8
  479.3 373.6 %all-reduce.19.cloned.1.call-start = ((), (), s32[]{:S(2)}) async-start(), calls=%async_computation.7 | async-start | bytes 8388608
  488.5 1.0 copy-start.5
  488.5 2.0 copy-start.7
  488.5 706.2 %reduce-scatter.2.cloned.1.call-start = ((), (), s32[]{:S(2)}) async-start(), calls=%async_computation.6 | async-start | bytes 1064960 | tf_op jit(solution)/shard_map/reduce_scatter | solution.py:138
  492.6 66.6 %copy-start.3 = (bf16[128,2048]{1,0:T(8,128)(2,1)S(1)}, bf16[128,2048]{1,0:T(8,128)(2,1)}, u32[]{:S(2)}) copy-start(bf16[128,2048]{1,0:T(8,128)(2,1)} %get-tuple-element.19) | copy-start | bytes 1572868
Sparse Core Ops, SparseCore 0:
  15.2 78.6 all-reduce.10
  162.7 69.9 all-reduce.12
  235.9 77.1 all-reduce.22
  318.7 76.6 all-reduce.14
  400.7 75.2 all-reduce.16
  479.4 78.4 all-reduce.20
  561.4 291.4 all-reduce.18
Sparse Core Ops, SparseCore 1:
  18.9 138.9 all-gather.1
  493.9 700.7 reduce-scatter.1
where the time goes:
time: 1200 us
  waiting for transfers between devices  1020 us (85%)
  blocking collectives  107 us (9%)
  other arithmetic  22.1 us (2%)
  matrix products  21.5 us (2%)
  between operations  17.8 us (1%)
    reduce_scatter x1, waiting for transfers between devices, on_device(): lax.psum_scatter(total_out, 'dp', scatter_dimension=1, tiled=True)  340 us
    unnamed x10, waiting for transfers between devices  290 us
    psum x3, waiting for transfers between devices, head_sum(): return lax.psum(terms.astype(jnp.bfloat16), 'context').astype(jnp.float32)  209 us
    psum x3, waiting for transfers between devices, from_root(): return lax.psum(kept, axis)  152 us
    all_gather x1, blocking collectives, on_device(): lax.all_gather(w_out, 'dp', axis=1, tiled=True)  107 us
    all_gather x1, waiting for transfers between devices, on_device(): lax.all_gather(w_qkv, 'dp', axis=1, tiled=True)  34.1 us
  transfers between devices with their start and end apart: 9, of which 8 were waited for; matrix products, arithmetic and copies ran while one was open for 2% of the time, Pallas kernels for 0%

commit v1 on v0

v1 whole, which is shorter than its diff:
```python
import jax
import jax.numpy as jnp
from jax import lax
from jax.sharding import Mesh, PartitionSpec as P

HD = 128
TILE = 128
D = 2048
CTX = 8
NZ = 16
NY = 4
CHUNK = TILE // CTX
SCALE = HD**-0.5
CONTEXT = ("x", "core")
BF = jnp.bfloat16
F32 = jnp.float32


def swap(x, axis):
    return lax.all_to_all(x, axis, 0, 0)


def spread(x, axis, size):
    return swap(jnp.broadcast_to(x[None], (size,) + x.shape), axis)


def dot(a, b, dims):
    return lax.dot_general(a, b, (dims, ((), ())), preferred_element_type=F32)


def gather_weights(w_qkv, w_out):
    shard = jnp.concatenate([w_qkv, w_out.T[None]], 0)
    part = spread(shard, "z", NZ)
    full = spread(part, "y", NY)
    return full.transpose(2, 1, 0, 3, 4).reshape(4, D, HD)


def norm_chunk(x32, gain):
    inv = lax.rsqrt(jnp.mean(x32 * x32, -1, keepdims=True) + 1e-06)
    return inv, (x32 * inv * gain).astype(BF)


def all_rows(chunk):
    return spread(chunk, CONTEXT, CTX).reshape(TILE, D)


def sum_chunk(terms):
    return jnp.sum(swap(terms.astype(BF).reshape(CTX, CHUNK, D), CONTEXT).astype(F32), 0)


def forward(rows, w):
    q = dot(rows, w[0], ((1,), (0,))).astype(BF)
    k = dot(rows, w[1], ((1,), (0,))).astype(BF)
    v = dot(rows, w[2], ((1,), (0,))).astype(BF)
    pos = jnp.arange(TILE)
    scores = dot(q, k, ((1,), (1,))) * SCALE
    scores = jnp.where(pos[None, :] <= pos[:, None], scores, -1e30)
    expo = jnp.exp(scores - jnp.max(scores, -1, keepdims=True))
    prob = expo / jnp.sum(expo, -1, keepdims=True)
    probb = prob.astype(BF)
    attn = dot(probb, v, ((1,), (0,))).astype(BF)
    mixed = dot(attn, w[3], ((1,), (1,)))
    return mixed, (rows, q, k, v, prob, probb, attn)


def backward(dy, keep, w):
    rows, q, k, v, prob, probb, attn = keep
    dattn = dot(dy, w[3], ((1,), (0,))).astype(BF)
    delta = jnp.sum(dattn.astype(F32) * attn.astype(F32), -1, keepdims=True)
    dprob = dot(dattn, v, ((1,), (1,)))
    dscore = (prob * (dprob - delta) * SCALE).astype(BF)
    dq = dot(dscore, k, ((1,), (0,))).astype(BF)
    dk = dot(dscore, q, ((0,), (0,))).astype(BF)
    dv = dot(probb, dattn, ((0,), (0,))).astype(BF)
    dnorm = dot(dq, w[0], ((1,), (1,))) + dot(dk, w[1], ((1,), (1,))) + dot(dv, w[2], ((1,), (1,)))
    return dnorm, (dq, dk, dv)


def norm_grad(e, x32, inv, gain):
    u = e * gain
    return inv * u - x32 * inv**3 * jnp.mean(x32 * u, -1, keepdims=True)


def on_device(hidden_in, cotangent, tile_depth, w_qkv, w_out, gain):
    me = lax.axis_index("x") * 2 + lax.axis_index("core")
    depth = tile_depth[0]
    places = jnp.arange(CTX, dtype=jnp.int32)
    alive = depth >= 2
    owner = jnp.sum(jnp.where(alive, places, 0))
    live2 = jnp.any(alive)
    live3 = jnp.any(depth >= 3)
    mine = jnp.any(alive & (places == me))

    w = gather_weights(w_qkv, w_out)

    def owner_chunk(tile):
        got = swap(tile.reshape(CTX, CHUNK, D), CONTEXT)
        got = lax.dynamic_index_in_dim(got, owner, 0, keepdims=False)
        return jnp.where(live2, got, jnp.zeros_like(got))

    h1 = owner_chunk(hidden_in[0])
    g3 = owner_chunk(cotangent[0])

    x1 = h1.astype(F32)
    inv2, normed2 = norm_chunk(x1, gain)
    rows2 = all_rows(normed2)
    dy3 = all_rows(jnp.where(live3, g3, jnp.zeros_like(g3)))
    mixed2, keep2 = forward(rows2, w)
    h2 = (x1 + sum_chunk(mixed2)).astype(BF)

    x2 = h2.astype(F32)
    inv3, normed3 = norm_chunk(x2, gain)
    rows3 = all_rows(jnp.where(live3, normed3, jnp.zeros_like(normed3)))
    mixed3, keep3 = forward(rows3, w)
    dnorm3, (dq3, dk3, dv3) = backward(dy3, keep3, w)
    g2 = (g3.astype(F32) + norm_grad(sum_chunk(dnorm3), x2, inv3, gain)).astype(BF)
    h3 = (x2 + sum_chunk(mixed3)).astype(BF)

    dy2 = all_rows(g2)
    dnorm2, (dq2, dk2, dv2) = backward(dy2, keep2, w)
    g1 = (g2.astype(F32) + norm_grad(sum_chunk(dnorm2), x1, inv2, gain)).astype(BF)

    def weight_grad(left3, right3, left2, right2):
        left = jnp.concatenate([left3, left2], 0)
        right = jnp.concatenate([right3, right2], 0)
        return dot(left, right, ((0,), (0,))).astype(BF)

    grads = jnp.stack(
        [
            weight_grad(rows3, dq3, rows2, dq2),
            weight_grad(rows3, dk3, rows2, dk2),
            weight_grad(rows3, dv3, rows2, dv2),
            weight_grad(dy3, keep3[-1], dy2, keep2[-1]),
        ]
    )
    grads = grads.reshape(4, NZ, NY, 32, HD).transpose(2, 1, 0, 3, 4)
    part = jnp.sum(swap(grads, "y").astype(F32), 0).astype(BF)
    shard = jnp.sum(swap(part, "z").astype(F32), 0)

    back_h = all_rows(h3)
    back_g = all_rows(g1)
    hidden_out = jnp.where(mine, back_h, hidden_in[0])
    grad_in = jnp.where(mine, back_g, cotangent[0])
    return (hidden_out[None], grad_in[None], shard[:3], shard[3].T)


def solution(mesh):
    grid = Mesh(mesh.devices.reshape(NZ, NY, CTX // 2, 2), ("z", "y") + CONTEXT)
    dp = ("z", "y")
    in_specs = (
        P(dp, CONTEXT, None),
        P(dp, CONTEXT, None),
        P(dp, None),
        P(None, dp, CONTEXT),
        P(CONTEXT, dp),
        P(),
    )
    out_specs = (
        P(dp, CONTEXT, None),
        P(dp, CONTEXT, None),
        P(None, dp, CONTEXT),
        P(CONTEXT, dp),
    )
    return jax.shard_map(
        on_device, mesh=grid, in_specs=in_specs, out_specs=out_specs, check_vma=False
    )
```

time: 1200 us -> 328 us (0.27)
  waiting for transfers between devices: 1020 us -> 130 us
  starting transfers between devices: 0.38 us -> 77.5 us
  blocking collectives: 107 us -> 57.6 us
  between operations: 17.8 us -> 2.99 us
    psum x6 -> x0, waiting for transfers between devices: 360 us -> none  [the longest x3 209 us: head_sum(): return lax.psum(terms.astype(jnp.bfloat16), 'context').astype(jnp.float32)]
    reduce_scatter x1 -> x0, waiting for transfers between devices: 340 us -> none  [on_device(): lax.psum_scatter(total_out, 'dp', scatter_dimension=1, tiled=True)]
    unnamed x10 -> x0, waiting for transfers between devices: 290 us -> none
    all_to_all x0 -> x14, waiting for transfers between devices: none -> 130 us  [swap(): return lax.all_to_all(x, axis, 0, 0)]
    all_gather x1 -> x0, blocking collectives: 107 us -> none  [on_device(): lax.all_gather(w_out, 'dp', axis=1, tiled=True)]
    all_to_all x0 -> x14, starting transfers between devices: none -> 77.5 us  [swap(): return lax.all_to_all(x, axis, 0, 0)]
    all_to_all x0 -> x2, blocking collectives: none -> 57.6 us  [swap(): return lax.all_to_all(x, axis, 0, 0)]
    all_gather x1 -> x0, waiting for transfers between devices: 34.1 us -> none  [on_device(): lax.all_gather(w_qkv, 'dp', axis=1, tiled=True)]
  transfers between devices with their start and end apart: 9 -> 14, of which waited for: 8 -> 14; matrix products, arithmetic and copies ran while one was open for 2% -> 12% of each run, Pallas kernels for 0% -> 0%
where the time goes in v1:
time: 328 us; the launch traced here: 325 us
  waiting for transfers between devices  130 us (40%)
  starting transfers between devices  77.5 us (24%)
  blocking collectives  57.6 us (18%)
  other arithmetic  28.9 us (9%)
  matrix products  16.2 us (5%)
  local copies, waits for them, and re-layouts  12 us (4%)
    all_to_all x14, waiting for transfers between devices, swap(): return lax.all_to_all(x, axis, 0, 0)  130 us
    all_to_all x14, starting transfers between devices, swap(): return lax.all_to_all(x, axis, 0, 0)  77.5 us
    all_to_all x2, blocking collectives, swap(): return lax.all_to_all(x, axis, 0, 0)  57.6 us
    dot_general x32, matrix products, dot(): return lax.dot_general(a, b, (dims, ((), ())), preferred_element_type=F32)  16.2 us
    broadcast_in_dim x4, other arithmetic, spread(): return swap(jnp.broadcast_to(x[None], (size,) + x.shape), axis)  6.94 us
  transfers between devices with their start and end apart: 14, of which 14 were waited for; matrix products, arithmetic and copies ran while one was open for 12% of the time, Pallas kernels for 0%

profile of v1, /device:TPU:6, one launch (start us, length us, event | category | flops | bytes accessed | tf_op | source)
XLA Modules:
  0.0 324.8 jit_solution(1513134962277662180)
XLA Ops:
  1.5 44.1 %all_to_all.80 = bf16[16,4,32,128]{3,2,1,0:T(8,128)(2,1)S(1)} all-to-all(bf16[16,4,32,128]{3,2,1,0:T(8,128)(2,1)S(1)} %broadcast_in_dim.43), channel_id=1, replica_groups=mesh['z'=16,'y'=4,'x'=4,'core'=2] {'z'}, dimensions={0} | all-to-all | bytes 1048576 | tf_op jit(solution)/shard_map/all_to_all | solution.py:20
  45.6 4.8 %all-to-all-start = ((bf16[8,16,2048]{2,1,0:T(8,128)(2,1)}), bf16[8,16,2048]{2,1,0:T(8,128)(2,1)S(1)}, u32[]{:S(2)}, u32[]{:S(2)}) async-start(bf16[8,16,2048]{2,1,0:T(8,128)(2,1)} %bitcast.174), calls=%async_computation | async-start | bytes 1048576 | tf_op jit(solution)/shard_map/all_to_all | solution.py:20
  50.4 8.2 %all-to-all-done = bf16[8,16,2048]{2,1,0:T(8,128)(2,1)S(1)} async-done(((bf16[8,16,2048]{2,1,0:T(8,128)(2,1)}), bf16[8,16,2048]{2,1,0:T(8,128)(2,1)S(1)}, u32[]{:S(2)}, u32[]{:S(2)}) %all-to-all-start) | async-done | bytes 524320 | tf_op jit(solution)/shard_map/all_to_all | solution.py:20
  58.6 1.7 broadcast_in_dim.44
  60.4 4.6 %all-to-all-start.3 = ((bf16[4,16,4,32,128]{4,3,1,2,0:T(8,128)(2,1)}), bf16[4,16,4,32,128]{4,3,1,2,0:T(8,128)(2,1)S(1)}, u32[]{:S(2)}, u32[]{:S(2)}) async-start(bf16[4,16,4,32,128]{4,3,1,2,0:T(8,128)(2,1)} %broadcast_in_dim.44), calls=%async_computation.3 | async-start | bytes 4194304 | tf_op jit(solution)/shard_map/all_to_all | solution.py:20
  70.2 21.0 %all-to-all-done.3 = bf16[4,16,4,32,128]{4,3,1,2,0:T(8,128)(2,1)S(1)} async-done(((bf16[4,16,4,32,128]{4,3,1,2,0:T(8,128)(2,1)}), bf16[4,16,4,32,128]{4,3,1,2,0:T(8,128)(2,1)S(1)}, u32[]{:S(2)}, u32[]{:S(2)}) %all-to-all-start.3) | async-done | bytes 2097184 | tf_op jit(solution)/shard_map/all_to_all | solution.py:20
  92.0 5.5 %all-to-all-start.1 = ((bf16[8,16,2048]{2,1,0:T(8,128)(2,1)}), bf16[8,16,2048]{2,1,0:T(8,128)(2,1)S(1)}, u32[]{:S(2)}, u32[]{:S(2)}) async-start(bf16[8,16,2048]{2,1,0:T(8,128)(2,1)} %broadcast_in_dim.41), calls=%async_computation.1 | async-start | bytes 1048576 | tf_op jit(solution)/shard_map/all_to_all | solution.py:20
  98.6 7.1 %all-to-all-done.1 = bf16[8,16,2048]{2,1,0:T(8,128)(2,1)S(1)} async-done(((bf16[8,16,2048]{2,1,0:T(8,128)(2,1)}), bf16[8,16,2048]{2,1,0:T(8,128)(2,1)S(1)}, u32[]{:S(2)}, u32[]{:S(2)}) %all-to-all-start.1) | async-done | bytes 524320 | tf_op jit(solution)/shard_map/all_to_all | solution.py:20
  105.7 5.5 %all-to-all-start.8 = ((bf16[8,16,2048]{2,1,0:T(8,128)(2,1)}), bf16[8,16,2048]{2,1,0:T(8,128)(2,1)S(1)}, u32[]{:S(2)}, u32[]{:S(2)}) async-start(bf16[8,16,2048]{2,1,0:T(8,128)(2,1)} %bitcast.20), calls=%async_computation.8 | async-start | bytes 1048576 | tf_op jit(solution)/shard_map/all_to_all | solution.py:20
  113.7 5.8 %all-to-all-done.8 = bf16[8,16,2048]{2,1,0:T(8,128)(2,1)S(1)} async-done(((bf16[8,16,2048]{2,1,0:T(8,128)(2,1)}), bf16[8,16,2048]{2,1,0:T(8,128)(2,1)S(1)}, u32[]{:S(2)}, u32[]{:S(2)}) %all-to-all-start.8) | async-done | bytes 524320 | tf_op jit(solution)/shard_map/all_to_all | solution.py:20
  120.3 5.5 %all-to-all-start.4 = ((bf16[8,16,2048]{2,1,0:T(8,128)(2,1)}), bf16[8,16,2048]{2,1,0:T(8,128)(2,1)S(1)}, u32[]{:S(2)}, u32[]{:S(2)}) async-start(bf16[8,16,2048]{2,1,0:T(8,128)(2,1)} %bitcast.179), calls=%async_computation.4 | async-start | bytes 1048576 | tf_op jit(solution)/shard_map/all_to_all | solution.py:20
  125.8 2.1 select_bitcast_fusion
  127.9 6.2 %all-to-all-done.4 = bf16[8,16,2048]{2,1,0:T(8,128)(2,1)S(1)} async-done(((bf16[8,16,2048]{2,1,0:T(8,128)(2,1)}), bf16[8,16,2048]{2,1,0:T(8,128)(2,1)S(1)}, u32[]{:S(2)}, u32[]{:S(2)}) %all-to-all-start.4) | async-done | bytes 524320 | tf_op jit(solution)/shard_map/all_to_all | solution.py:20
  134.9 6.1 %all-to-all-start.9 = ((bf16[8,16,2048]{2,1,0:T(8,128)(2,1)}), bf16[8,16,2048]{2,1,0:T(8,128)(2,1)}, u32[]{:S(2)}, u32[]{:S(2)}) async-start(bf16[8,16,2048]{2,1,0:T(8,128)(2,1)} %broadcast_in_dim.51), calls=%async_computation.9 | async-start | bytes 1048576 | tf_op jit(solution)/shard_map/all_to_all | solution.py:20
  141.1 1.5 fusion.16
  143.2 2.7 fusion.41
  145.9 3.5 %all-to-all-done.9 = bf16[8,16,2048]{2,1,0:T(8,128)(2,1)} async-done(((bf16[8,16,2048]{2,1,0:T(8,128)(2,1)}), bf16[8,16,2048]{2,1,0:T(8,128)(2,1)}, u32[]{:S(2)}, u32[]{:S(2)}) %all-to-all-start.9) | async-done | bytes 524320 | tf_op jit(solution)/shard_map/all_to_all | solution.py:20
  150.2 5.5 %all-to-all-start.5 = ((bf16[8,16,2048]{2,1,0:T(8,128)(2,1)}), bf16[8,16,2048]{2,1,0:T(8,128)(2,1)S(1)}, u32[]{:S(2)}, u32[]{:S(2)}) async-start(bf16[8,16,2048]{2,1,0:T(8,128)(2,1)} %broadcast_in_dim.47), calls=%async_computation.5 | async-start | bytes 1048576 | tf_op jit(solution)/shard_map/all_to_all | solution.py:20
  155.8 1.9 convolution_convert_fusion.13
  157.7 6.3 %all-to-all-done.5 = bf16[8,16,2048]{2,1,0:T(8,128)(2,1)S(1)} async-done(((bf16[8,16,2048]{2,1,0:T(8,128)(2,1)}), bf16[8,16,2048]{2,1,0:T(8,128)(2,1)S(1)}, u32[]{:S(2)}, u32[]{:S(2)}) %all-to-all-start.5) | async-done | bytes 524320 | tf_op jit(solution)/shard_map/all_to_all | solution.py:20
  168.7 6.1 %all-to-all-start.10 = ((bf16[8,16,2048]{2,1,0:T(8,128)(2,1)}), bf16[8,16,2048]{2,1,0:T(8,128)(2,1)}, u32[]{:S(2)}, u32[]{:S(2)}) async-start(bf16[8,16,2048]{2,1,0:T(8,128)(2,1)} %bitcast.180), calls=%async_computation.10 | async-start | bytes 1048576 | tf_op jit(solution)/shard_map/all_to_all | solution.py:20
  175.9 7.3 %all-to-all-done.10 = bf16[8,16,2048]{2,1,0:T(8,128)(2,1)} async-done(((bf16[8,16,2048]{2,1,0:T(8,128)(2,1)}), bf16[8,16,2048]{2,1,0:T(8,128)(2,1)}, u32[]{:S(2)}, u32[]{:S(2)}) %all-to-all-start.10) | async-done | bytes 524320 | tf_op jit(solution)/shard_map/all_to_all | solution.py:20
  183.2 6.1 %all-to-all-start.6 = ((bf16[8,16,2048]{2,1,0:T(8,128)(2,1)}), bf16[8,16,2048]{2,1,0:T(8,128)(2,1)}, u32[]{:S(2)}, u32[]{:S(2)}) async-start(bf16[8,16,2048]{2,1,0:T(8,128)(2,1)} %bitcast.178), calls=%async_computation.6 | async-start | bytes 1048576 | tf_op jit(solution)/shard_map/all_to_all | solution.py:20
  190.4 1.6 fusion.17
  192.5 5.2 %all-to-all-done.6 = bf16[8,16,2048]{2,1,0:T(8,128)(2,1)} async-done(((bf16[8,16,2048]{2,1,0:T(8,128)(2,1)}), bf16[8,16,2048]{2,1,0:T(8,128)(2,1)}, u32[]{:S(2)}, u32[]{:S(2)}) %all-to-all-start.6) | async-done | bytes 524320 | tf_op jit(solution)/shard_map/all_to_all | solution.py:20
  197.7 1.1 convert_reduce_fusion.3
  198.8 1.6 fusion.24
  200.4 13.5 %all_to_all.81 = bf16[8,16,2048]{2,1,0:T(8,128)(2,1)} all-to-all(bf16[8,16,2048]{2,1,0:T(8,128)(2,1)S(1)} %broadcast_in_dim.53), channel_id=1, replica_groups=mesh['z'=16,'y'=4,'x'=4,'core'=2] {'x','core'}, dimensions={0} | all-to-all | bytes 1048576 | tf_op jit(solution)/shard_map/all_to_all | solution.py:20
  214.8 6.1 %all-to-all-start.7 = ((bf16[8,16,2048]{2,1,0:T(8,128)(2,1)}), bf16[8,16,2048]{2,1,0:T(8,128)(2,1)}, u32[]{:S(2)}, u32[]{:S(2)}) async-start(bf16[8,16,2048]{2,1,0:T(8,128)(2,1)} %broadcast_in_dim.49), calls=%async_computation.7 | async-start | bytes 1048576 | tf_op jit(solution)/shard_map/all_to_all | solution.py:20
  220.9 1.4 multiply_reduce_fusion
  224.0 1.5 convolution_convert_fusion
  227.2 2.1 all-to-all-done.7
  229.3 6.1 %all-to-all-start.12 = ((bf16[8,16,2048]{2,1,0:T(8,128)(2,1)}), bf16[8,16,2048]{2,1,0:T(8,128)(2,1)}, u32[]{:S(2)}, u32[]{:S(2)}) async-start(bf16[8,16,2048]{2,1,0:T(8,128)(2,1)} %bitcast.27), calls=%async_computation.12 | async-start | bytes 1048576 | tf_op jit(solution)/shard_map/all_to_all | solution.py:20
  236.4 1.9 copy_bitcast_fusion
  238.3 5.5 %all-to-all-done.12 = bf16[8,16,2048]{2,1,0:T(8,128)(2,1)} async-done(((bf16[8,16,2048]{2,1,0:T(8,128)(2,1)}), bf16[8,16,2048]{2,1,0:T(8,128)(2,1)}, u32[]{:S(2)}, u32[]{:S(2)}) %all-to-all-start.12) | async-done | bytes 524320 | tf_op jit(solution)/shard_map/all_to_all | solution.py:20
  243.8 3.6 %all-to-all-start.14 = ((bf16[4,16,4,32,128]{4,3,1,2,0:T(8,128)(2,1)}), bf16[4,16,4,32,128]{4,3,1,2,0:T(8,128)(2,1)S(1)}, u32[]{:S(2)}, u32[]{:S(2)}) async-start(bf16[4,16,4,32,128]{4,3,1,2,0:T(8,128)(2,1)} %copy_bitcast_fusion), calls=%async_computation.14 | async-start | bytes 4194304 | tf_op jit(solution)/shard_map/all_to_all | solution.py:20
  247.4 1.1 convert_reduce_fusion.1
  248.5 1.6 fusion.27
  250.1 1.5 fusion.37
  251.6 22.2 %all-to-all-done.14 = bf16[4,16,4,32,128]{4,3,1,2,0:T(8,128)(2,1)S(1)} async-done(((bf16[4,16,4,32,128]{4,3,1,2,0:T(8,128)(2,1)}), bf16[4,16,4,32,128]{4,3,1,2,0:T(8,128)(2,1)S(1)}, u32[]{:S(2)}, u32[]{:S(2)}) %all-to-all-start.14) | async-done | bytes 2097184 | tf_op jit(solution)/shard_map/all_to_all | solution.py:20
  274.6 5.5 %all-to-all-start.13 = ((bf16[8,16,2048]{2,1,0:T(8,128)(2,1)}), bf16[8,16,2048]{2,1,0:T(8,128)(2,1)S(1)}, u32[]{:S(2)}, u32[]{:S(2)}) async-start(bf16[8,16,2048]{2,1,0:T(8,128)(2,1)} %broadcast_in_dim.55), calls=%async_computation.13 | async-start | bytes 1048576 | tf_op jit(solution)/shard_map/all_to_all | solution.py:20
  280.1 1.3 reduce_sum.163
  281.4 1.9 copy.40
  283.3 5.1 %all-to-all-done.13 = bf16[8,16,2048]{2,1,0:T(8,128)(2,1)S(1)} async-done(((bf16[8,16,2048]{2,1,0:T(8,128)(2,1)}), bf16[8,16,2048]{2,1,0:T(8,128)(2,1)S(1)}, u32[]{:S(2)}, u32[]{:S(2)}) %all-to-all-start.13) | async-done | bytes 524320 | tf_op jit(solution)/shard_map/all_to_all | solution.py:20
  288.4 6.3 %all-to-all-start.15 = ((bf16[16,4,32,128]{3,2,1,0:T(8,128)(2,1)}), bf16[16,4,32,128]{3,2,1,0:T(8,128)(2,1)S(1)}, u32[]{:S(2)}, u32[]{:S(2)}) async-start(bf16[16,4,32,128]{3,2,1,0:T(8,128)(2,1)} %copy.40), calls=%async_computation.15 | async-start | bytes 1048576 | tf_op jit(solution)/shard_map/all_to_all | solution.py:20
  295.3 1.5 bitcast_select_fusion.1
  296.8 2.5 bitcast_select_fusion
  299.4 24.1 %all-to-all-done.15 = bf16[16,4,32,128]{3,2,1,0:T(8,128)(2,1)S(1)} async-done(((bf16[16,4,32,128]{3,2,1,0:T(8,128)(2,1)}), bf16[16,4,32,128]{3,2,1,0:T(8,128)(2,1)S(1)}, u32[]{:S(2)}, u32[]{:S(2)}) %all-to-all-start.15) | async-done | bytes 524320 | tf_op jit(solution)/shard_map/all_to_all | solution.py:20
  (104 shorter events, 26.7 us)
Async XLA Ops:
  45.6 13.1 %all-to-all-start = ((bf16[8,16,2048]{2,1,0:T(8,128)(2,1)}), bf16[8,16,2048]{2,1,0:T(8,128)(2,1)S(1)}, u32[]{:S(2)}, u32[]{:S(2)}) async-start(bf16[8,16,2048]{2,1,0:T(8,128)(2,1)} %bitcast.174), calls=%async_computation | async-start | bytes 1048576 | tf_op jit(solution)/shard_map/all_to_all | solution.py:20
  58.6 10.9 %copy-start.2 = (bf16[8,16,2048]{2,1,0:T(8,128)(2,1)}, bf16[8,16,2048]{2,1,0:T(8,128)(2,1)S(1)}, u32[]{:S(2)}) copy-start(bf16[8,16,2048]{2,1,0:T(8,128)(2,1)S(1)} %all-to-all-done) | copy-start | bytes 1572868
  60.4 4.6 %copy-start.22 = (s32[1,8]{1,0:T(1,128)S(1)}, s32[1,8]{1,0:T(1,128)}, u32[]{:S(2)}) copy-start(s32[1,8]{1,0:T(1,128)} %param.8) | copy-start | bytes 100
  60.4 9.1 %copy-start.4 = (f32[2048]{0:T(1024)S(1)}, f32[2048]{0:T(1024)}, u32[]{:S(2)}) copy-start(f32[2048]{0:T(1024)} %param.11) | copy-start | bytes 24580
  60.4 30.7 %all-to-all-start.3 = ((bf16[4,16,4,32,128]{4,3,1,2,0:T(8,128)(2,1)}), bf16[4,16,4,32,128]{4,3,1,2,0:T(8,128)(2,1)S(1)}, u32[]{:S(2)}, u32[]{:S(2)}) async-start(bf16[4,16,4,32,128]{4,3,1,2,0:T(8,128)(2,1)} %broadcast_in_dim.44), calls=%async_computation.3 | async-start | bytes 4194304 | tf_op jit(solution)/shard_map/all_to_all | solution.py:20
  92.0 13.8 %all-to-all-start.1 = ((bf16[8,16,2048]{2,1,0:T(8,128)(2,1)}), bf16[8,16,2048]{2,1,0:T(8,128)(2,1)S(1)}, u32[]{:S(2)}, u32[]{:S(2)}) async-start(bf16[8,16,2048]{2,1,0:T(8,128)(2,1)} %broadcast_in_dim.41), calls=%async_computation.1 | async-start | bytes 1048576 | tf_op jit(solution)/shard_map/all_to_all | solution.py:20
  105.7 13.8 %all-to-all-start.8 = ((bf16[8,16,2048]{2,1,0:T(8,128)(2,1)}), bf16[8,16,2048]{2,1,0:T(8,128)(2,1)S(1)}, u32[]{:S(2)}, u32[]{:S(2)}) async-start(bf16[8,16,2048]{2,1,0:T(8,128)(2,1)} %bitcast.20), calls=%async_computation.8 | async-start | bytes 1048576 | tf_op jit(solution)/shard_map/all_to_all | solution.py:20
  111.5 8.8 %copy-start.13 = (bf16[128,128]{1,0:T(8,128)(2,1)}, bf16[128,128]{1,0:T(8,128)(2,1)S(1)}, u32[]{:S(2)}) copy-start(bf16[128,128]{1,0:T(8,128)(2,1)S(1)} %convolution_convert_fusion.19) | copy-start | bytes 98308
  112.3 22.6 %copy-start.20 = (f32[128]{0:T(128)}, f32[128]{0:T(128)S(1)}, u32[]{:S(2)}) copy-start(f32[128]{0:T(128)S(1)} %fusion.55) | copy-start | bytes 1540
  112.6 13.3 %copy-start.5 = (bf16[128,128]{1,0:T(8,128)(2,1)}, bf16[128,128]{1,0:T(8,128)(2,1)S(1)}, u32[]{:S(2)}) copy-start(bf16[128,128]{1,0:T(8,128)(2,1)S(1)} %convolution_convert_fusion.18) | copy-start | bytes 98308
  119.5 0.8 copy-start.3
  120.3 13.8 %all-to-all-start.4 = ((bf16[8,16,2048]{2,1,0:T(8,128)(2,1)}), bf16[8,16,2048]{2,1,0:T(8,128)(2,1)S(1)}, u32[]{:S(2)}, u32[]{:S(2)}) async-start(bf16[8,16,2048]{2,1,0:T(8,128)(2,1)} %bitcast.179), calls=%async_computation.4 | async-start | bytes 1048576 | tf_op jit(solution)/shard_map/all_to_all | solution.py:20
  134.9 14.5 %all-to-all-start.9 = ((bf16[8,16,2048]{2,1,0:T(8,128)(2,1)}), bf16[8,16,2048]{2,1,0:T(8,128)(2,1)}, u32[]{:S(2)}, u32[]{:S(2)}) async-start(bf16[8,16,2048]{2,1,0:T(8,128)(2,1)} %broadcast_in_dim.51), calls=%async_computation.9 | async-start | bytes 1048576 | tf_op jit(solution)/shard_map/all_to_all | solution.py:20
  143.2 21.4 %copy-start.18 = (f32[16]{0:T(128)}, f32[16]{0:T(128)S(1)}, u32[]{:S(2)}) copy-start(f32[16]{0:T(128)S(1)} %get-tuple-element.17) | copy-start | bytes 196
  150.2 13.8 %all-to-all-start.5 = ((bf16[8,16,2048]{2,1,0:T(8,128)(2,1)}), bf16[8,16,2048]{2,1,0:T(8,128)(2,1)S(1)}, u32[]{:S(2)}, u32[]{:S(2)}) async-start(bf16[8,16,2048]{2,1,0:T(8,128)(2,1)} %broadcast_in_dim.47), calls=%async_computation.5 | async-start | bytes 1048576 | tf_op jit(solution)/shard_map/all_to_all | solution.py:20
  164.0 1.1 copy-start.17
  166.3 0.6 copy-start.7
  166.4 1.1 copy-start.9
  166.9 0.6 copy-start.11
  167.6 7.3 %copy-start.15 = (bf16[128,128]{1,0:T(8,128)(2,1)S(1)}, bf16[128,128]{1,0:T(8,128)(2,1)}, u32[]{:S(2)}) copy-start(bf16[128,128]{1,0:T(8,128)(2,1)} %get-tuple-element.23) | copy-start | bytes 98308
  168.7 14.5 %all-to-all-start.10 = ((bf16[8,16,2048]{2,1,0:T(8,128)(2,1)}), bf16[8,16,2048]{2,1,0:T(8,128)(2,1)}, u32[]{:S(2)}, u32[]{:S(2)}) async-start(bf16[8,16,2048]{2,1,0:T(8,128)(2,1)} %bitcast.180), calls=%async_computation.10 | async-start | bytes 1048576 | tf_op jit(solution)/shard_map/all_to_all | solution.py:20
  183.2 14.5 %all-to-all-start.6 = ((bf16[8,16,2048]{2,1,0:T(8,128)(2,1)}), bf16[8,16,2048]{2,1,0:T(8,128)(2,1)}, u32[]{:S(2)}, u32[]{:S(2)}) async-start(bf16[8,16,2048]{2,1,0:T(8,128)(2,1)} %bitcast.178), calls=%async_computation.6 | async-start | bytes 1048576 | tf_op jit(solution)/shard_map/all_to_all | solution.py:20
  200.4 22.0 %copy-start.14 = (bf16[128,128]{1,0:T(8,128)(2,1)S(1)}, bf16[128,128]{1,0:T(8,128)(2,1)}, u32[]{:S(2)}) copy-start(bf16[128,128]{1,0:T(8,128)(2,1)} %copy-done.13) | copy-start | bytes 98308
  200.4 22.0 %copy-start.21 = (f32[128]{0:T(128)S(1)}, f32[128]{0:T(128)}, u32[]{:S(2)}) copy-start(f32[128]{0:T(128)} %copy-done.20) | copy-start | bytes 1540
  214.8 14.5 %all-to-all-start.7 = ((bf16[8,16,2048]{2,1,0:T(8,128)(2,1)}), bf16[8,16,2048]{2,1,0:T(8,128)(2,1)}, u32[]{:S(2)}, u32[]{:S(2)}) async-start(bf16[8,16,2048]{2,1,0:T(8,128)(2,1)} %broadcast_in_dim.49), calls=%async_computation.7 | async-start | bytes 1048576 | tf_op jit(solution)/shard_map/all_to_all | solution.py:20
  223.0 1.1 copy-start.1
  223.0 1.0 copy-start.6
  223.0 1.0 copy-start.16
  223.3 2.3 copy-start.12
  226.1 9.3 %copy-start.10 = (bf16[128,128]{1,0:T(8,128)(2,1)S(1)}, bf16[128,128]{1,0:T(8,128)(2,1)}, u32[]{:S(2)}) copy-start(bf16[128,128]{1,0:T(8,128)(2,1)} %copy-done.9) | copy-start | bytes 98308
  227.2 8.7 %copy-start.8 = (bf16[128,128]{1,0:T(8,128)(2,1)S(1)}, bf16[128,128]{1,0:T(8,128)(2,1)}, u32[]{:S(2)}) copy-start(bf16[128,128]{1,0:T(8,128)(2,1)} %copy-done.7) | copy-start | bytes 98308
  229.3 14.5 %all-to-all-start.12 = ((bf16[8,16,2048]{2,1,0:T(8,128)(2,1)}), bf16[8,16,2048]{2,1,0:T(8,128)(2,1)}, u32[]{:S(2)}, u32[]{:S(2)}) async-start(bf16[8,16,2048]{2,1,0:T(8,128)(2,1)} %bitcast.27), calls=%async_computation.12 | async-start | bytes 1048576 | tf_op jit(solution)/shard_map/all_to_all | solution.py:20
  238.3 11.8 %copy-start.19 = (f32[16]{0:T(128)S(1)}, f32[16]{0:T(128)}, u32[]{:S(2)}) copy-start(f32[16]{0:T(128)} %get-tuple-element.14) | copy-start | bytes 196
  243.8 30.0 %all-to-all-start.14 = ((bf16[4,16,4,32,128]{4,3,1,2,0:T(8,128)(2,1)}), bf16[4,16,4,32,128]{4,3,1,2,0:T(8,128)(2,1)S(1)}, u32[]{:S(2)}, u32[]{:S(2)}) async-start(bf16[4,16,4,32,128]{4,3,1,2,0:T(8,128)(2,1)} %copy_bitcast_fusion), calls=%async_computation.14 | async-start | bytes 4194304 | tf_op jit(solution)/shard_map/all_to_all | solution.py:20
  274.6 13.8 %all-to-all-start.13 = ((bf16[8,16,2048]{2,1,0:T(8,128)(2,1)}), bf16[8,16,2048]{2,1,0:T(8,128)(2,1)S(1)}, u32[]{:S(2)}, u32[]{:S(2)}) async-start(bf16[8,16,2048]{2,1,0:T(8,128)(2,1)} %broadcast_in_dim.55), calls=%async_computation.13 | async-start | bytes 1048576 | tf_op jit(solution)/shard_map/all_to_all | solution.py:20
  280.1 14.6 %copy-start.23 = (s32[1,8]{1,0:T(1,128)S(1)}, s32[1,8]{1,0:T(1,128)}, u32[]{:S(2)}) copy-start(s32[1,8]{1,0:T(1,128)} %param.8) | copy-start | bytes 100
  280.1 15.2 %copy-start = (bf16[1,128,2048]{2,1,0:T(8,128)(2,1)S(1)}, bf16[1,128,2048]{2,1,0:T(8,128)(2,1)}, u32[]{:S(2)}) copy-start(bf16[1,128,2048]{2,1,0:T(8,128)(2,1)} %param.6) | copy-start | bytes 1572868
  288.4 35.1 %all-to-all-start.15 = ((bf16[16,4,32,128]{3,2,1,0:T(8,128)(2,1)}), bf16[16,4,32,128]{3,2,1,0:T(8,128)(2,1)S(1)}, u32[]{:S(2)}, u32[]{:S(2)}) async-start(bf16[16,4,32,128]{3,2,1,0:T(8,128)(2,1)} %copy.40), calls=%async_computation.15 | async-start | bytes 1048576 | tf_op jit(solution)/shard_map/all_to_all | solution.py:20

commit v2 on v1

--- a/solution.py
+++ b/solution.py
@@ -28,11 +28,53 @@
     return lax.dot_general(a, b, (dims, ((), ())), preferred_element_type=F32)
 
 
+def add(a, b):
+    return (a.astype(F32) + b.astype(F32)).astype(BF)
+
+
+def from_core(x):
+    return lax.ppermute(x, "core", [(0, 1), (1, 0)])
+
+
+def from_pair(x, bit):
+    return lax.ppermute(x, "x", [(i, i ^ bit) for i in range(CTX // 2)])
+
+
+def y_pieces(part):
+    y = lax.axis_index("y")
+    part = part.transpose(1, 0, 2, 3)[:, :, None]
+    full = jnp.zeros((part.shape[0], NZ, NY, 32, HD), BF)
+    full = lax.dynamic_update_index_in_dim(full, part, y, 2)
+    for k in range(1, NY):
+        got = lax.ppermute(part, "y", [(i, (i + k) % NY) for i in range(NY)])
+        full = lax.dynamic_update_index_in_dim(full, got, (y - k) % NY, 2)
+    return full.reshape(-1, D, HD)
+
+
 def gather_weights(w_qkv, w_out):
-    shard = jnp.concatenate([w_qkv, w_out.T[None]], 0)
-    part = spread(shard, "z", NZ)
-    full = spread(part, "y", NY)
-    return full.transpose(2, 1, 0, 3, 4).reshape(4, D, HD)
+    first = spread(w_qkv[:2], "z", NZ)
+    second = spread(jnp.stack([w_qkv[2], w_out.T]), "z", NZ)
+    wa, wb = y_pieces(first), y_pieces(second)
+    return wa[0], wa[1], wb[0], wb[1]
+
+
+def from_owner(tile, mine):
+    kept = jnp.where(mine, tile, jnp.zeros_like(tile))
+    kept = kept + from_core(kept)
+    kept = kept + from_pair(kept, 1)
+    return kept + from_pair(kept, 3)
+
+
+def sum_tile(terms):
+    core = lax.axis_index("core")
+    halves = terms.astype(BF).reshape(2, TILE // 2, D)
+    part = lax.dynamic_index_in_dim(halves, core, 0, keepdims=False)
+    part = add(part, from_core(lax.dynamic_index_in_dim(halves, 1 - core, 0, keepdims=False)))
+    part = add(part, from_pair(part, 1))
+    part = add(part, from_pair(part, 3))
+    other = from_core(part)
+    low, high = jnp.where(core == 0, part, other), jnp.where(core == 0, other, part)
+    return jnp.concatenate([low, high], 0).astype(F32)
 
 
 def norm_chunk(x32, gain):
@@ -41,7 +83,7 @@
 
 
 def all_rows(chunk):
-    return spread(chunk, CONTEXT, CTX).reshape(TILE, D)
+    return lax.all_gather(chunk, CONTEXT, tiled=True)
 
 
 def sum_chunk(terms):
@@ -86,39 +128,35 @@
     depth = tile_depth[0]
     places = jnp.arange(CTX, dtype=jnp.int32)
     alive = depth >= 2
-    owner = jnp.sum(jnp.where(alive, places, 0))
-    live2 = jnp.any(alive)
     live3 = jnp.any(depth >= 3)
     mine = jnp.any(alive & (places == me))
 
     w = gather_weights(w_qkv, w_out)
 
-    def owner_chunk(tile):
-        got = swap(tile.reshape(CTX, CHUNK, D), CONTEXT)
-        got = lax.dynamic_index_in_dim(got, owner, 0, keepdims=False)
-        return jnp.where(live2, got, jnp.zeros_like(got))
-
-    h1 = owner_chunk(hidden_in[0])
-    g3 = owner_chunk(cotangent[0])
+    def chunk(tile):
+        return lax.dynamic_index_in_dim(tile.reshape(CTX, CHUNK, D), me, 0, keepdims=False)
+
+    h1 = from_owner(hidden_in[0], mine)
+    g3 = from_owner(cotangent[0], mine)
+    dy3 = jnp.where(live3, g3, jnp.zeros_like(g3))
 
     x1 = h1.astype(F32)
-    inv2, normed2 = norm_chunk(x1, gain)
-    rows2 = all_rows(normed2)
-    dy3 = all_rows(jnp.where(live3, g3, jnp.zeros_like(g3)))
+    inv2, rows2 = norm_chunk(x1, gain)
     mixed2, keep2 = forward(rows2, w)
-    h2 = (x1 + sum_chunk(mixed2)).astype(BF)
+    h2 = all_rows((chunk(h1).astype(F32) + sum_chunk(mixed2)).astype(BF))
 
     x2 = h2.astype(F32)
     inv3, normed3 = norm_chunk(x2, gain)
-    rows3 = all_rows(jnp.where(live3, normed3, jnp.zeros_like(normed3)))
+    rows3 = jnp.where(live3, normed3, jnp.zeros_like(normed3))
     mixed3, keep3 = forward(rows3, w)
     dnorm3, (dq3, dk3, dv3) = backward(dy3, keep3, w)
-    g2 = (g3.astype(F32) + norm_grad(sum_chunk(dnorm3), x2, inv3, gain)).astype(BF)
-    h3 = (x2 + sum_chunk(mixed3)).astype(BF)
-
-    dy2 = all_rows(g2)
+    x2c = chunk(h2).astype(F32)
+    inv3c, _ = norm_chunk(x2c, gain)
+    g2c = chunk(g3).astype(F32) + norm_grad(sum_chunk(dnorm3), x2c, inv3c, gain)
+    g2 = all_rows(g2c.astype(BF))
+
+    dy2 = g2
     dnorm2, (dq2, dk2, dv2) = backward(dy2, keep2, w)
-    g1 = (g2.astype(F32) + norm_grad(sum_chunk(dnorm2), x1, inv2, gain)).astype(BF)
 
     def weight_grad(left3, right3, left2, right2):
         left = jnp.concatenate([left3, left2], 0)
@@ -137,10 +175,10 @@
     part = jnp.sum(swap(grads, "y").astype(F32), 0).astype(BF)
     shard = jnp.sum(swap(part, "z").astype(F32), 0)
 
-    back_h = all_rows(h3)
-    back_g = all_rows(g1)
-    hidden_out = jnp.where(mine, back_h, hidden_in[0])
-    grad_in = jnp.where(mine, back_g, cotangent[0])
+    h3 = (x2 + sum_tile(mixed3)).astype(BF)
+    g1 = (g2.astype(F32) + norm_grad(sum_tile(dnorm2), x1, inv2, gain)).astype(BF)
+    hidden_out = jnp.where(mine, h3, hidden_in[0])
+    grad_in = jnp.where(mine, g1, cotangent[0])
     return (hidden_out[None], grad_in[None], shard[:3], shard[3].T)
 
 

time: 328 us -> 255 us (0.78)
  waiting for transfers between devices: 130 us -> 65.3 us
  starting transfers between devices: 77.5 us -> 110 us
  blocking collectives: 57.6 us -> 26.4 us
  local copies, waits for them, and re-layouts: 12 us -> 6.39 us
    all_to_all x14 -> x6, waiting for transfers between devices: 130 us -> 48.5 us  [swap(): return lax.all_to_all(x, axis, 0, 0)]
    ppermute x0 -> x20, starting transfers between devices: none -> 61.6 us  [the longest x8 25 us: from_pair(): return lax.ppermute(x, 'x', [(i, i ^ bit) for i in range(CTX // 2)])]
    all_to_all x2 -> x0, blocking collectives: 57.6 us -> none  [swap(): return lax.all_to_all(x, axis, 0, 0)]
    all_to_all x14 -> x6, starting transfers between devices: 77.5 us -> 48 us  [swap(): return lax.all_to_all(x, axis, 0, 0)]
    all_gather x0 -> x2, blocking collectives: none -> 26.4 us  [all_rows(): return lax.all_gather(chunk, CONTEXT, tiled=True)]
    ppermute x0 -> x20, waiting for transfers between devices: none -> 16.8 us  [the longest x8 16.7 us: from_pair(): return lax.ppermute(x, 'x', [(i, i ^ bit) for i in range(CTX // 2)])]
    broadcast_in_dim x8 -> x2, local copies, waits for them, and re-layouts: 6.11 us -> 1.51 us  [spread(): return swap(jnp.broadcast_to(x[None], (size,) + x.shape), axis)]
    broadcast_in_dim x4 -> x2, other arithmetic: 6.94 us -> 3.94 us  [on_device(): return (hidden_out[None], grad_in[None], shard[:3], shard[3].T)]
  transfers between devices with their start and end apart: 14 -> 26, of which waited for: 14 -> 10; matrix products, arithmetic and copies ran while one was open for 12% -> 16% of each run, Pallas kernels for 0% -> 0%
where the time goes in v2:
time: 255 us; the launch traced here: 252 us
  starting transfers between devices  110 us (43%)
  waiting for transfers between devices  65.3 us (26%)
  other arithmetic  27.2 us (11%)
  blocking collectives  26.4 us (10%)
  matrix products  15.9 us (6%)
  local copies, waits for them, and re-layouts  6.39 us (3%)
    all_to_all x6, waiting for transfers between devices, swap(): return lax.all_to_all(x, axis, 0, 0)  48.5 us
    all_to_all x6, starting transfers between devices, swap(): return lax.all_to_all(x, axis, 0, 0)  48 us
    all_gather x2, blocking collectives, all_rows(): return lax.all_gather(chunk, CONTEXT, tiled=True)  26.4 us
    ppermute x8, starting transfers between devices, from_pair(): return lax.ppermute(x, 'x', [(i, i ^ bit) for i in range(CTX // 2)])  25 us
    ppermute x6, starting transfers between devices, y_pieces(): got = lax.ppermute(part, 'y', [(i, (i + k) % NY) for i in range(NY)])  23.9 us
    ppermute x8, waiting for transfers between devices, from_pair(): return lax.ppermute(x, 'x', [(i, i ^ bit) for i in range(CTX // 2)])  16.7 us
    dot_general x32, matrix products, dot(): return lax.dot_general(a, b, (dims, ((), ())), preferred_element_type=F32)  15.9 us
    ppermute x6, starting transfers between devices, from_core(): return lax.ppermute(x, 'core', [(0, 1), (1, 0)])  12.8 us
  transfers between devices with their start and end apart: 26, of which 10 were waited for; matrix products, arithmetic and copies ran while one was open for 16% of the time, Pallas kernels for 0%

profile of v2, /device:TPU:6, one launch (start us, length us, event | category | flops | bytes accessed | tf_op | source)
XLA Modules:
  0.0 252.4 jit_solution(9228625839717395659)
XLA Ops:
  2.9 15.2 %all-to-all-start.1 = ((bf16[16,2,32,128]{3,2,1,0:T(8,128)(2,1)}), bf16[16,2,32,128]{3,2,1,0:T(8,128)(2,1)S(1)}, u32[]{:S(2)}, u32[]{:S(2)}) async-start(bf16[16,2,32,128]{3,2,1,0:T(8,128)(2,1)} %broadcast_in_dim.20), calls=%async_computation.1 | async-start | bytes 524288 | tf_op jit(solution)/shard_map/all_to_all | solution.py:20
  18.1 1.3 fusion.59
  19.4 1.7 bitcast_select_fusion.1
  21.1 1.9 collective-permute-start
  23.1 1.5 bitcast_select_fusion
  24.6 2.5 %collective-permute-start.13 = (bf16[128,2048]{1,0:T(8,128)(2,1)}, bf16[128,2048]{1,0:T(8,128)(2,1)S(1)}, u32[]{:S(2)}, u32[]{:S(2)}) collective-permute-start(bf16[128,2048]{1,0:T(8,128)(2,1)} %bitcast_select_fusion), channel_id=1, source_target_pairs={{0,1},{1,0},{2,3},{3,2},{4,5},{5,4},{6,7},{7,6},{8,9},{9,8},{10,11... | collective-permute-start | bytes 1572872 | tf_op jit(solution)/shard_map/ppermute | solution.py:36
  27.1 9.4 %all-to-all-done.1 = bf16[16,2,32,128]{3,2,1,0:T(8,128)(2,1)S(1)} async-done(((bf16[16,2,32,128]{3,2,1,0:T(8,128)(2,1)}), bf16[16,2,32,128]{3,2,1,0:T(8,128)(2,1)S(1)}, u32[]{:S(2)}, u32[]{:S(2)}) %all-to-all-start.1) | async-done | bytes 262176 | tf_op jit(solution)/shard_map/all_to_all | solution.py:20
  37.2 5.8 %all-to-all-start = ((bf16[16,2,32,128]{3,2,1,0:T(8,128)(2,1)}), bf16[16,2,32,128]{3,2,1,0:T(8,128)(2,1)S(1)}, u32[]{:S(2)}, u32[]{:S(2)}) async-start(bf16[16,2,32,128]{3,2,1,0:T(8,128)(2,1)} %broadcast_in_dim.17), calls=%async_computation | async-start | bytes 524288 | tf_op jit(solution)/shard_map/all_to_all | solution.py:20
  43.8 2.7 %collective-permute-start.1 = (bf16[128,2048]{1,0:T(8,128)(2,1)S(1)}, bf16[128,2048]{1,0:T(8,128)(2,1)S(1)}, u32[]{:S(2)}, u32[]{:S(2)}) collective-permute-start(bf16[128,2048]{1,0:T(8,128)(2,1)S(1)} %fusion.129), channel_id=1, source_target_pairs={{0,2},{2,0},{4,6},{6,4},{1,3},{3,1},{5,7},{7,5},{8,10},{10,8},{12,... | collective-permute-start | bytes 1572872 | tf_op jit(solution)/shard_map/ppermute | solution.py:40
  47.2 3.1 %collective-permute-start.14 = (bf16[128,2048]{1,0:T(8,128)(2,1)S(1)}, bf16[128,2048]{1,0:T(8,128)(2,1)S(1)}, u32[]{:S(2)}, u32[]{:S(2)}) collective-permute-start(bf16[128,2048]{1,0:T(8,128)(2,1)S(1)} %fusion.128), channel_id=1, source_target_pairs={{0,2},{2,0},{4,6},{6,4},{1,3},{3,1},{5,7},{7,5},{8,10},{10,8},{12,... | collective-permute-start | bytes 1572872 | tf_op jit(solution)/shard_map/ppermute | solution.py:40
  51.0 3.5 %collective-permute-start.6 = (bf16[2,16,1,32,128]{4,3,2,1,0:T(8,128)(2,1)S(1)}, bf16[2,16,1,32,128]{4,3,2,1,0:T(8,128)(2,1)S(1)}, u32[]{:S(2)}, u32[]{:S(2)}) collective-permute-start(bf16[2,16,1,32,128]{4,3,2,1,0:T(8,128)(2,1)S(1)} %bitcast.159), channel_id=1, source_target_pairs={{0,8},{8,16},{16,24},{24,0},{1,9},{9,17},{17,25},{25,1},{2,10},{10... | collective-permute-start | bytes 786440 | tf_op jit(solution)/shard_map/ppermute | solution.py:49
  54.5 4.8 %collective-permute-start.7 = (bf16[2,16,1,32,128]{4,3,2,1,0:T(8,128)(2,1)S(1)}, bf16[2,16,1,32,128]{4,3,2,1,0:T(8,128)(2,1)S(1)}, u32[]{:S(2)}, u32[]{:S(2)}) collective-permute-start(bf16[2,16,1,32,128]{4,3,2,1,0:T(8,128)(2,1)S(1)} %bitcast.160), channel_id=1, source_target_pairs={{0,16},{8,24},{16,0},{24,8},{1,17},{9,25},{17,1},{25,9},{2,18},{10... | collective-permute-start | bytes 786440 | tf_op jit(solution)/shard_map/ppermute | solution.py:49
  59.3 2.1 all-to-all-done
  61.4 3.5 %collective-permute-start.3 = (bf16[2,16,1,32,128]{4,3,2,1,0:T(8,128)(2,1)S(1)}, bf16[2,16,1,32,128]{4,3,2,1,0:T(8,128)(2,1)S(1)}, u32[]{:S(2)}, u32[]{:S(2)}) collective-permute-start(bf16[2,16,1,32,128]{4,3,2,1,0:T(8,128)(2,1)S(1)} %bitcast.162), channel_id=1, source_target_pairs={{0,8},{8,16},{16,24},{24,0},{1,9},{9,17},{17,25},{25,1},{2,10},{10... | collective-permute-start | bytes 786440 | tf_op jit(solution)/shard_map/ppermute | solution.py:49
  65.5 4.8 %collective-permute-start.4 = (bf16[2,16,1,32,128]{4,3,2,1,0:T(8,128)(2,1)S(1)}, bf16[2,16,1,32,128]{4,3,2,1,0:T(8,128)(2,1)S(1)}, u32[]{:S(2)}, u32[]{:S(2)}) collective-permute-start(bf16[2,16,1,32,128]{4,3,2,1,0:T(8,128)(2,1)S(1)} %bitcast.163), channel_id=1, source_target_pairs={{0,16},{8,24},{16,0},{24,8},{1,17},{9,25},{17,1},{25,9},{2,18},{10... | collective-permute-start | bytes 786440 | tf_op jit(solution)/shard_map/ppermute | solution.py:49
  70.5 4.6 %collective-permute-start.8 = (bf16[2,16,1,32,128]{4,3,2,1,0:T(8,128)(2,1)S(1)}, bf16[2,16,1,32,128]{4,3,2,1,0:T(8,128)(2,1)S(1)}, u32[]{:S(2)}, u32[]{:S(2)}) collective-permute-start(bf16[2,16,1,32,128]{4,3,2,1,0:T(8,128)(2,1)S(1)} %bitcast.161), channel_id=1, source_target_pairs={{0,24},{8,0},{16,8},{24,16},{1,25},{9,1},{17,9},{25,17},{2,26},{10... | collective-permute-start | bytes 786440 | tf_op jit(solution)/shard_map/ppermute | solution.py:49
  76.0 2.6 %collective-permute-start.5 = (bf16[2,16,1,32,128]{4,3,2,1,0:T(8,128)(2,1)S(1)}, bf16[2,16,1,32,128]{4,3,2,1,0:T(8,128)(2,1)S(1)}, u32[]{:S(2)}, u32[]{:S(2)}) collective-permute-start(bf16[2,16,1,32,128]{4,3,2,1,0:T(8,128)(2,1)S(1)} %bitcast.164), channel_id=1, source_target_pairs={{0,24},{8,0},{16,8},{24,16},{1,25},{9,1},{17,9},{25,17},{2,26},{10... | collective-permute-start | bytes 786440 | tf_op jit(solution)/shard_map/ppermute | solution.py:49
  78.8 2.4 collective-permute-start.2
  81.2 4.7 %collective-permute-start.15 = (bf16[128,2048]{1,0:T(8,128)(2,1)}, bf16[128,2048]{1,0:T(8,128)(2,1)}, u32[]{:S(2)}, u32[]{:S(2)}) collective-permute-start(bf16[128,2048]{1,0:T(8,128)(2,1)} %add.164), channel_id=1, source_target_pairs={{0,6},{2,4},{4,2},{6,0},{1,7},{3,5},{5,3},{7,1},{8,14},{10,12},{12... | collective-permute-start | bytes 1572872 | tf_op jit(solution)/shard_map/ppermute | solution.py:40
  86.3 10.4 %collective-permute-done.2 = bf16[128,2048]{1,0:T(8,128)(2,1)S(1)} collective-permute-done((bf16[128,2048]{1,0:T(8,128)(2,1)S(1)}, bf16[128,2048]{1,0:T(8,128)(2,1)S(1)}, u32[]{:S(2)}, u32[]{:S(2)}) %collective-permute-start.2) | collective-permute-done | bytes 524320 | tf_op jit(solution)/shard_map/ppermute | solution.py:40
  100.2 4.5 %all-to-all-start.2 = ((bf16[8,16,2048]{2,1,0:T(8,128)(2,1)}), bf16[8,16,2048]{2,1,0:T(8,128)(2,1)}, u32[]{:S(2)}, u32[]{:S(2)}) async-start(bf16[8,16,2048]{2,1,0:T(8,128)(2,1)} %bitcast.153), calls=%async_computation.2 | async-start | bytes 1048576 | tf_op jit(solution)/shard_map/all_to_all | solution.py:20
  105.0 2.7 %broadcast_select_fusion = (bf16[128,2048]{1,0:T(8,128)(2,1)S(1)}, bf16[128,2048]{1,0:T(8,128)(2,1)}) fusion(pred[]{:T(512)} %compare_reduce_fusion, bf16[128,2048]{1,0:T(8,128)(2,1)} %add.164, bf16[128,2048]{1,0:T(8,128)(2,1)} %collective-permute-done.15), kind=kLoop, calls=%fused_computation.85 | loop fusion | flops 524288 | bytes 2097153 | tf_op jit(solution)/shard_map/jit(_where)/select_n | solution.py:141
  108.0 5.1 %all-to-all-done.2 = bf16[8,16,2048]{2,1,0:T(8,128)(2,1)} async-done(((bf16[8,16,2048]{2,1,0:T(8,128)(2,1)}), bf16[8,16,2048]{2,1,0:T(8,128)(2,1)}, u32[]{:S(2)}, u32[]{:S(2)}) %all-to-all-start.2) | async-done | bytes 524320 | tf_op jit(solution)/shard_map/all_to_all | solution.py:20
  114.3 13.1 %all_gather.6 = bf16[128,2048]{1,0:T(8,128)(2,1)S(1)} all-gather(bf16[16,2048]{1,0:T(8,128)(2,1)S(1)} %fusion.40), channel_id=1, replica_groups=mesh['z'=16,'y'=4,'x'=4,'core'=2] {'x','core'}, dimensions={0}, use_global_device_ids=true | all-gather | bytes 589824 | tf_op jit(solution)/shard_map/all_gather | solution.py:86
  132.3 2.3 collective-permute-start.9
  135.7 6.1 %all-to-all-start.3 = ((bf16[8,16,2048]{2,1,0:T(8,128)(2,1)}), bf16[8,16,2048]{2,1,0:T(8,128)(2,1)}, u32[]{:S(2)}, u32[]{:S(2)}) async-start(bf16[8,16,2048]{2,1,0:T(8,128)(2,1)} %bitcast.150), calls=%async_computation.3 | async-start | bytes 1048576 | tf_op jit(solution)/shard_map/all_to_all | solution.py:20
  142.9 2.8 %collective-permute-start.10 = (bf16[64,2048]{1,0:T(8,128)(2,1)S(1)}, bf16[64,2048]{1,0:T(8,128)(2,1)}, u32[]{:S(2)}, u32[]{:S(2)}) collective-permute-start(bf16[64,2048]{1,0:T(8,128)(2,1)S(1)} %fusion.33), channel_id=1, source_target_pairs={{0,2},{2,0},{4,6},{6,4},{1,3},{3,1},{5,7},{7,5},{8,10},{10,8},{12,... | collective-permute-start | bytes 786440 | tf_op jit(solution)/shard_map/ppermute | solution.py:40
  145.7 5.0 %all-to-all-done.3 = bf16[8,16,2048]{2,1,0:T(8,128)(2,1)} async-done(((bf16[8,16,2048]{2,1,0:T(8,128)(2,1)}), bf16[8,16,2048]{2,1,0:T(8,128)(2,1)}, u32[]{:S(2)}, u32[]{:S(2)}) %all-to-all-start.3) | async-done | bytes 524320 | tf_op jit(solution)/shard_map/all_to_all | solution.py:20
  153.0 13.3 %all_gather.7 = bf16[128,2048]{1,0:T(8,128)(2,1)S(1)} all-gather(bf16[16,2048]{1,0:T(8,128)(2,1)S(1)} %fusion.38), channel_id=1, replica_groups=mesh['z'=16,'y'=4,'x'=4,'core'=2] {'x','core'}, dimensions={0}, use_global_device_ids=true | all-gather | bytes 589824 | tf_op jit(solution)/shard_map/all_gather | solution.py:86
  166.3 1.2 multiply_reduce_fusion
  170.6 1.3 fusion.74
  172.4 1.3 fusion.75
  174.2 1.9 copy_bitcast_fusion
  176.1 4.6 %all-to-all-start.4 = ((bf16[4,16,4,32,128]{4,3,1,2,0:T(8,128)(2,1)}), bf16[4,16,4,32,128]{4,3,1,2,0:T(8,128)(2,1)}, u32[]{:S(2)}, u32[]{:S(2)}) async-start(bf16[4,16,4,32,128]{4,3,1,2,0:T(8,128)(2,1)} %copy_bitcast_fusion), calls=%async_computation.4 | async-start | bytes 4194304 | tf_op jit(solution)/shard_map/all_to_all | solution.py:20
  180.7 1.5 fusion.3
  182.2 2.3 collective-permute-start.16
  185.5 4.0 %collective-permute-start.11 = (bf16[64,2048]{1,0:T(8,128)(2,1)S(1)}, bf16[64,2048]{1,0:T(8,128)(2,1)S(1)}, u32[]{:S(2)}, u32[]{:S(2)}) collective-permute-start(bf16[64,2048]{1,0:T(8,128)(2,1)S(1)} %add_convert_fusion.3), channel_id=1, source_target_pairs={{0,6},{2,4},{4,2},{6,0},{1,7},{3,5},{5,3},{7,1},{8,14},{10,12},{12... | collective-permute-start | bytes 786440 | tf_op jit(solution)/shard_map/ppermute | solution.py:40
  189.6 1.9 collective-permute-start.17
  191.6 5.5 %collective-permute-done.11 = bf16[64,2048]{1,0:T(8,128)(2,1)S(1)} collective-permute-done((bf16[64,2048]{1,0:T(8,128)(2,1)S(1)}, bf16[64,2048]{1,0:T(8,128)(2,1)S(1)}, u32[]{:S(2)}, u32[]{:S(2)}) %collective-permute-start.11) | collective-permute-done | bytes 262176 | tf_op jit(solution)/shard_map/ppermute | solution.py:40
  197.1 1.9 collective-permute-start.12
  199.7 3.4 %collective-permute-start.18 = (bf16[64,2048]{1,0:T(8,128)(2,1)S(1)}, bf16[64,2048]{1,0:T(8,128)(2,1)S(1)}, u32[]{:S(2)}, u32[]{:S(2)}) collective-permute-start(bf16[64,2048]{1,0:T(8,128)(2,1)S(1)} %add_convert_fusion.1), channel_id=1, source_target_pairs={{0,6},{2,4},{4,2},{6,0},{1,7},{3,5},{5,3},{7,1},{8,14},{10,12},{12... | collective-permute-start | bytes 786440 | tf_op jit(solution)/shard_map/ppermute | solution.py:40
  203.2 4.7 %all-to-all-done.4 = bf16[4,16,4,32,128]{4,3,1,2,0:T(8,128)(2,1)} async-done(((bf16[4,16,4,32,128]{4,3,1,2,0:T(8,128)(2,1)}), bf16[4,16,4,32,128]{4,3,1,2,0:T(8,128)(2,1)}, u32[]{:S(2)}, u32[]{:S(2)}) %all-to-all-start.4) | async-done | bytes 2097184 | tf_op jit(solution)/shard_map/all_to_all | solution.py:20
  207.8 2.0 reduce_sum.131
  210.7 11.7 %all-to-all-start.5 = ((bf16[16,4,32,128]{3,2,1,0:T(8,128)(2,1)}), bf16[16,4,32,128]{3,2,1,0:T(8,128)(2,1)S(1)}, u32[]{:S(2)}, u32[]{:S(2)}) async-start(bf16[16,4,32,128]{3,2,1,0:T(8,128)(2,1)} %copy.45), calls=%async_computation.5 | async-start | bytes 1048576 | tf_op jit(solution)/shard_map/all_to_all | solution.py:20
  222.5 1.9 collective-permute-start.19
  224.5 1.8 fusion.30
  226.6 2.2 fusion.28
  228.8 22.3 %all-to-all-done.5 = bf16[16,4,32,128]{3,2,1,0:T(8,128)(2,1)S(1)} async-done(((bf16[16,4,32,128]{3,2,1,0:T(8,128)(2,1)}), bf16[16,4,32,128]{3,2,1,0:T(8,128)(2,1)S(1)}, u32[]{:S(2)}, u32[]{:S(2)}) %all-to-all-start.5) | async-done | bytes 524320 | tf_op jit(solution)/shard_map/all_to_all | solution.py:20
  (165 shorter events, 30.0 us)
Async XLA Ops:
  0.6 35.8 %slice-start = ((bf16[3,32,128]{2,1,0:T(8,128)(2,1)}), bf16[2,32,128]{2,1,0:T(8,128)(2,1)S(1)}, s32[]{:S(2)}) async-start(bf16[3,32,128]{2,1,0:T(8,128)(2,1)} %param.9), calls=%async_computation.6 | async-start | bytes 32768 | tf_op jit(solution)/shard_map/slice | solution.py:55
  0.6 42.4 %copy-start.4 = (bf16[1,128,2048]{2,1,0:T(8,128)(2,1)S(1)}, bf16[1,128,2048]{2,1,0:T(8,128)(2,1)}, u32[]{:S(2)}) copy-start(bf16[1,128,2048]{2,1,0:T(8,128)(2,1)} %param.6) | copy-start | bytes 1572868
  0.7 22.4 %copy-start.6 = (bf16[1,128,2048]{2,1,0:T(8,128)(2,1)S(1)}, bf16[1,128,2048]{2,1,0:T(8,128)(2,1)}, u32[]{:S(2)}) copy-start(bf16[1,128,2048]{2,1,0:T(8,128)(2,1)} %param.7) | copy-start | bytes 1572868
  2.9 33.6 %all-to-all-start.1 = ((bf16[16,2,32,128]{3,2,1,0:T(8,128)(2,1)}), bf16[16,2,32,128]{3,2,1,0:T(8,128)(2,1)S(1)}, u32[]{:S(2)}, u32[]{:S(2)}) async-start(bf16[16,2,32,128]{3,2,1,0:T(8,128)(2,1)} %broadcast_in_dim.20), calls=%async_computation.1 | async-start | bytes 524288 | tf_op jit(solution)/shard_map/all_to_all | solution.py:20
  21.1 21.9 %collective-permute-start = (bf16[128,2048]{1,0:T(8,128)(2,1)S(1)}, bf16[128,2048]{1,0:T(8,128)(2,1)S(1)}, u32[]{:S(2)}, u32[]{:S(2)}) collective-permute-start(bf16[128,2048]{1,0:T(8,128)(2,1)S(1)} %bitcast_select_fusion.1), channel_id=1, source_target_pairs={{0,1},{1,0},{2,3},{3,2},{4,5},{5,4},{6,7},{7,6},{8,9},{9,8},{10,11... | collective-permute-start | bytes 1572872 | tf_op jit(solution)/shard_map/ppermute | solution.py:36
  24.6 25.8 %copy-start.31 = (s32[1,8]{1,0:T(1,128)S(1)}, s32[1,8]{1,0:T(1,128)}, u32[]{:S(2)}) copy-start(s32[1,8]{1,0:T(1,128)} %param.8) | copy-start | bytes 100
  24.6 21.9 %collective-permute-start.13 = (bf16[128,2048]{1,0:T(8,128)(2,1)}, bf16[128,2048]{1,0:T(8,128)(2,1)S(1)}, u32[]{:S(2)}, u32[]{:S(2)}) collective-permute-start(bf16[128,2048]{1,0:T(8,128)(2,1)} %bitcast_select_fusion), channel_id=1, source_target_pairs={{0,1},{1,0},{2,3},{3,2},{4,5},{5,4},{6,7},{7,6},{8,9},{9,8},{10,11... | collective-permute-start | bytes 1572872 | tf_op jit(solution)/shard_map/ppermute | solution.py:36
  37.2 24.2 %all-to-all-start = ((bf16[16,2,32,128]{3,2,1,0:T(8,128)(2,1)}), bf16[16,2,32,128]{3,2,1,0:T(8,128)(2,1)S(1)}, u32[]{:S(2)}, u32[]{:S(2)}) async-start(bf16[16,2,32,128]{3,2,1,0:T(8,128)(2,1)} %broadcast_in_dim.17), calls=%async_computation | async-start | bytes 524288 | tf_op jit(solution)/shard_map/all_to_all | solution.py:20
  43.8 21.8 %collective-permute-start.1 = (bf16[128,2048]{1,0:T(8,128)(2,1)S(1)}, bf16[128,2048]{1,0:T(8,128)(2,1)S(1)}, u32[]{:S(2)}, u32[]{:S(2)}) collective-permute-start(bf16[128,2048]{1,0:T(8,128)(2,1)S(1)} %fusion.129), channel_id=1, source_target_pairs={{0,2},{2,0},{4,6},{6,4},{1,3},{3,1},{5,7},{7,5},{8,10},{10,8},{12,... | collective-permute-start | bytes 1572872 | tf_op jit(solution)/shard_map/ppermute | solution.py:40
  47.2 23.2 %collective-permute-start.14 = (bf16[128,2048]{1,0:T(8,128)(2,1)S(1)}, bf16[128,2048]{1,0:T(8,128)(2,1)S(1)}, u32[]{:S(2)}, u32[]{:S(2)}) collective-permute-start(bf16[128,2048]{1,0:T(8,128)(2,1)S(1)} %fusion.128), channel_id=1, source_target_pairs={{0,2},{2,0},{4,6},{6,4},{1,3},{3,1},{5,7},{7,5},{8,10},{10,8},{12,... | collective-permute-start | bytes 1572872 | tf_op jit(solution)/shard_map/ppermute | solution.py:40
  51.0 25.0 %collective-permute-start.6 = (bf16[2,16,1,32,128]{4,3,2,1,0:T(8,128)(2,1)S(1)}, bf16[2,16,1,32,128]{4,3,2,1,0:T(8,128)(2,1)S(1)}, u32[]{:S(2)}, u32[]{:S(2)}) collective-permute-start(bf16[2,16,1,32,128]{4,3,2,1,0:T(8,128)(2,1)S(1)} %bitcast.159), channel_id=1, source_target_pairs={{0,8},{8,16},{16,24},{24,0},{1,9},{9,17},{17,25},{25,1},{2,10},{10... | collective-permute-start | bytes 786440 | tf_op jit(solution)/shard_map/ppermute | solution.py:49
  54.5 26.7 %collective-permute-start.7 = (bf16[2,16,1,32,128]{4,3,2,1,0:T(8,128)(2,1)S(1)}, bf16[2,16,1,32,128]{4,3,2,1,0:T(8,128)(2,1)S(1)}, u32[]{:S(2)}, u32[]{:S(2)}) collective-permute-start(bf16[2,16,1,32,128]{4,3,2,1,0:T(8,128)(2,1)S(1)} %bitcast.160), channel_id=1, source_target_pairs={{0,16},{8,24},{16,0},{24,8},{1,17},{9,25},{17,1},{25,9},{2,18},{10... | collective-permute-start | bytes 786440 | tf_op jit(solution)/shard_map/ppermute | solution.py:49
  61.4 17.3 %collective-permute-start.3 = (bf16[2,16,1,32,128]{4,3,2,1,0:T(8,128)(2,1)S(1)}, bf16[2,16,1,32,128]{4,3,2,1,0:T(8,128)(2,1)S(1)}, u32[]{:S(2)}, u32[]{:S(2)}) collective-permute-start(bf16[2,16,1,32,128]{4,3,2,1,0:T(8,128)(2,1)S(1)} %bitcast.162), channel_id=1, source_target_pairs={{0,8},{8,16},{16,24},{24,0},{1,9},{9,17},{17,25},{25,1},{2,10},{10... | collective-permute-start | bytes 786440 | tf_op jit(solution)/shard_map/ppermute | solution.py:49
  65.5 20.4 %collective-permute-start.4 = (bf16[2,16,1,32,128]{4,3,2,1,0:T(8,128)(2,1)S(1)}, bf16[2,16,1,32,128]{4,3,2,1,0:T(8,128)(2,1)S(1)}, u32[]{:S(2)}, u32[]{:S(2)}) collective-permute-start(bf16[2,16,1,32,128]{4,3,2,1,0:T(8,128)(2,1)S(1)} %bitcast.163), channel_id=1, source_target_pairs={{0,16},{8,24},{16,0},{24,8},{1,17},{9,25},{17,1},{25,9},{2,18},{10... | collective-permute-start | bytes 786440 | tf_op jit(solution)/shard_map/ppermute | solution.py:49
  70.5 15.5 %collective-permute-start.8 = (bf16[2,16,1,32,128]{4,3,2,1,0:T(8,128)(2,1)S(1)}, bf16[2,16,1,32,128]{4,3,2,1,0:T(8,128)(2,1)S(1)}, u32[]{:S(2)}, u32[]{:S(2)}) collective-permute-start(bf16[2,16,1,32,128]{4,3,2,1,0:T(8,128)(2,1)S(1)} %bitcast.161), channel_id=1, source_target_pairs={{0,24},{8,0},{16,8},{24,16},{1,25},{9,1},{17,9},{25,17},{2,26},{10... | collective-permute-start | bytes 786440 | tf_op jit(solution)/shard_map/ppermute | solution.py:49
  76.0 10.0 %collective-permute-start.5 = (bf16[2,16,1,32,128]{4,3,2,1,0:T(8,128)(2,1)S(1)}, bf16[2,16,1,32,128]{4,3,2,1,0:T(8,128)(2,1)S(1)}, u32[]{:S(2)}, u32[]{:S(2)}) collective-permute-start(bf16[2,16,1,32,128]{4,3,2,1,0:T(8,128)(2,1)S(1)} %bitcast.164), channel_id=1, source_target_pairs={{0,24},{8,0},{16,8},{24,16},{1,25},{9,1},{17,9},{25,17},{2,26},{10... | collective-permute-start | bytes 786440 | tf_op jit(solution)/shard_map/ppermute | solution.py:49
  78.8 18.0 %collective-permute-start.2 = (bf16[128,2048]{1,0:T(8,128)(2,1)S(1)}, bf16[128,2048]{1,0:T(8,128)(2,1)S(1)}, u32[]{:S(2)}, u32[]{:S(2)}) collective-permute-start(bf16[128,2048]{1,0:T(8,128)(2,1)S(1)} %add.144), channel_id=1, source_target_pairs={{0,6},{2,4},{4,2},{6,0},{1,7},{3,5},{5,3},{7,1},{8,14},{10,12},{12... | collective-permute-start | bytes 1572872 | tf_op jit(solution)/shard_map/ppermute | solution.py:40
  81.2 23.8 %collective-permute-start.15 = (bf16[128,2048]{1,0:T(8,128)(2,1)}, bf16[128,2048]{1,0:T(8,128)(2,1)}, u32[]{:S(2)}, u32[]{:S(2)}) collective-permute-start(bf16[128,2048]{1,0:T(8,128)(2,1)} %add.164), channel_id=1, source_target_pairs={{0,6},{2,4},{4,2},{6,0},{1,7},{3,5},{5,3},{7,1},{8,14},{10,12},{12... | collective-permute-start | bytes 1572872 | tf_op jit(solution)/shard_map/ppermute | solution.py:40
  86.2 11.4 %copy-start.14 = (f32[2048]{0:T(1024)S(1)}, f32[2048]{0:T(1024)}, u32[]{:S(2)}) copy-start(f32[2048]{0:T(1024)} %param.11) | copy-start | bytes 24580
  98.7 9.1 %copy-start.23 = (bf16[128,128]{1,0:T(8,128)(2,1)}, bf16[128,128]{1,0:T(8,128)(2,1)S(1)}, u32[]{:S(2)}) copy-start(bf16[128,128]{1,0:T(8,128)(2,1)S(1)} %convolution_convert_fusion.19) | copy-start | bytes 98308
  98.9 8.8 %copy-start.30 = (f32[128]{0:T(128)}, f32[128]{0:T(128)S(1)}, u32[]{:S(2)}) copy-start(f32[128]{0:T(128)S(1)} %fusion.54) | copy-start | bytes 1540
  99.1 8.6 %copy-start.19 = (bf16[128,128]{1,0:T(8,128)(2,1)}, bf16[128,128]{1,0:T(8,128)(2,1)S(1)}, u32[]{:S(2)}) copy-start(bf16[128,128]{1,0:T(8,128)(2,1)S(1)} %convolution_convert_fusion.18) | copy-start | bytes 98308
  100.2 12.9 %all-to-all-start.2 = ((bf16[8,16,2048]{2,1,0:T(8,128)(2,1)}), bf16[8,16,2048]{2,1,0:T(8,128)(2,1)}, u32[]{:S(2)}, u32[]{:S(2)}) async-start(bf16[8,16,2048]{2,1,0:T(8,128)(2,1)} %bitcast.153), calls=%async_computation.2 | async-start | bytes 1048576 | tf_op jit(solution)/shard_map/all_to_all | solution.py:20
  107.7 6.5 %copy-start.11 = (bf16[128,2048]{1,0:T(8,128)(2,1)}, bf16[128,2048]{1,0:T(8,128)(2,1)S(1)}, u32[]{:S(2)}) copy-start(bf16[128,2048]{1,0:T(8,128)(2,1)S(1)} %get-tuple-element.6) | copy-start | bytes 1572868
  130.2 4.3 %copy-start.15 = (bf16[128,128]{1,0:T(8,128)(2,1)}, bf16[128,128]{1,0:T(8,128)(2,1)S(1)}, u32[]{:S(2)}) copy-start(bf16[128,128]{1,0:T(8,128)(2,1)S(1)} %convolution_convert_fusion.12) | copy-start | bytes 98308
  132.3 9.5 %collective-permute-start.9 = (bf16[64,2048]{1,0:T(8,128)(2,1)S(1)}, bf16[64,2048]{1,0:T(8,128)(2,1)}, u32[]{:S(2)}, u32[]{:S(2)}) collective-permute-start(bf16[64,2048]{1,0:T(8,128)(2,1)S(1)} %dynamic-slice_bitcast_fusion.1), channel_id=1, source_target_pairs={{0,1},{1,0},{2,3},{3,2},{4,5},{5,4},{6,7},{7,6},{8,9},{9,8},{10,11... | collective-permute-start | bytes 786440 | tf_op jit(solution)/shard_map/ppermute | solution.py:36
  135.7 15.0 %all-to-all-start.3 = ((bf16[8,16,2048]{2,1,0:T(8,128)(2,1)}), bf16[8,16,2048]{2,1,0:T(8,128)(2,1)}, u32[]{:S(2)}, u32[]{:S(2)}) async-start(bf16[8,16,2048]{2,1,0:T(8,128)(2,1)} %bitcast.150), calls=%async_computation.3 | async-start | bytes 1048576 | tf_op jit(solution)/shard_map/all_to_all | solution.py:20
  142.9 41.6 %collective-permute-start.10 = (bf16[64,2048]{1,0:T(8,128)(2,1)S(1)}, bf16[64,2048]{1,0:T(8,128)(2,1)}, u32[]{:S(2)}, u32[]{:S(2)}) collective-permute-start(bf16[64,2048]{1,0:T(8,128)(2,1)S(1)} %fusion.33), channel_id=1, source_target_pairs={{0,2},{2,0},{4,6},{6,4},{1,3},{3,1},{5,7},{7,5},{8,10},{10,8},{12,... | collective-permute-start | bytes 786440 | tf_op jit(solution)/shard_map/ppermute | solution.py:40
  150.7 16.9 %copy-start.24 = (bf16[128,128]{1,0:T(8,128)(2,1)S(1)}, bf16[128,128]{1,0:T(8,128)(2,1)}, u32[]{:S(2)}) copy-start(bf16[128,128]{1,0:T(8,128)(2,1)} %copy-done.23) | copy-start | bytes 98308
  150.7 18.9 %copy-start.12 = (bf16[128,2048]{1,0:T(8,128)(2,1)S(1)}, bf16[128,2048]{1,0:T(8,128)(2,1)}, u32[]{:S(2)}) copy-start(bf16[128,2048]{1,0:T(8,128)(2,1)} %copy-done.11) | copy-start | bytes 1572868
  150.7 18.9 %copy-start.20 = (bf16[128,128]{1,0:T(8,128)(2,1)S(1)}, bf16[128,128]{1,0:T(8,128)(2,1)}, u32[]{:S(2)}) copy-start(bf16[128,128]{1,0:T(8,128)(2,1)} %copy-done.19) | copy-start | bytes 98308
  150.7 18.9 %copy-start.26 = (bf16[128,128]{1,0:T(8,128)(2,1)S(1)}, bf16[128,128]{1,0:T(8,128)(2,1)}, u32[]{:S(2)}) copy-start(bf16[128,128]{1,0:T(8,128)(2,1)} %copy-done.25) | copy-start | bytes 98308
  166.3 4.3 %copy-start.8 = (bf16[128,2048]{1,0:T(8,128)(2,1)}, bf16[128,2048]{1,0:T(8,128)(2,1)S(1)}, u32[]{:S(2)}) copy-start(bf16[128,2048]{1,0:T(8,128)(2,1)S(1)} %all_gather.7) | copy-start | bytes 1572868
  166.3 3.8 %copy-start.1 = (bf16[128,2048]{1,0:T(8,128)(2,1)S(1)}, bf16[128,2048]{1,0:T(8,128)(2,1)}, u32[]{:S(2)}) copy-start(bf16[128,2048]{1,0:T(8,128)(2,1)} %copy-done) | copy-start | bytes 1572868
  166.3 3.8 %copy-start.3 = (bf16[128,2048]{1,0:T(8,128)(2,1)S(1)}, bf16[128,2048]{1,0:T(8,128)(2,1)}, u32[]{:S(2)}) copy-start(bf16[128,2048]{1,0:T(8,128)(2,1)} %copy-done.2) | copy-start | bytes 1572868
  166.3 3.8 %copy-start.22 = (bf16[128,128]{1,0:T(8,128)(2,1)S(1)}, bf16[128,128]{1,0:T(8,128)(2,1)}, u32[]{:S(2)}) copy-start(bf16[128,128]{1,0:T(8,128)(2,1)} %copy-done.21) | copy-start | bytes 98308
  168.6 5.1 %copy-start.17 = (bf16[128,128]{1,0:T(8,128)(2,1)}, bf16[128,128]{1,0:T(8,128)(2,1)S(1)}, u32[]{:S(2)}) copy-start(bf16[128,128]{1,0:T(8,128)(2,1)S(1)} %convolution_convert_fusion.8) | copy-start | bytes 98308
  176.1 4.6 %copy-start.10 = (f32[128,2048]{1,0:T(8,128)S(1)}, f32[128,2048]{1,0:T(8,128)}, u32[]{:S(2)}) copy-start(f32[128,2048]{1,0:T(8,128)} %fusion.74) | copy-start | bytes 3145732
  176.1 4.6 %copy-start.18 = (bf16[128,128]{1,0:T(8,128)(2,1)S(1)}, bf16[128,128]{1,0:T(8,128)(2,1)}, u32[]{:S(2)}) copy-start(bf16[128,128]{1,0:T(8,128)(2,1)} %copy-done.17) | copy-start | bytes 98308
  176.1 31.8 %all-to-all-start.4 = ((bf16[4,16,4,32,128]{4,3,1,2,0:T(8,128)(2,1)}), bf16[4,16,4,32,128]{4,3,1,2,0:T(8,128)(2,1)}, u32[]{:S(2)}, u32[]{:S(2)}) async-start(bf16[4,16,4,32,128]{4,3,1,2,0:T(8,128)(2,1)} %copy_bitcast_fusion), calls=%async_computation.4 | async-start | bytes 4194304 | tf_op jit(solution)/shard_map/all_to_all | solution.py:20
  182.2 7.3 %collective-permute-start.16 = (bf16[64,2048]{1,0:T(8,128)(2,1)S(1)}, bf16[64,2048]{1,0:T(8,128)(2,1)S(1)}, u32[]{:S(2)}, u32[]{:S(2)}) collective-permute-start(bf16[64,2048]{1,0:T(8,128)(2,1)S(1)} %dynamic-slice_bitcast_fusion), channel_id=1, source_target_pairs={{0,1},{1,0},{2,3},{3,2},{4,5},{5,4},{6,7},{7,6},{8,9},{9,8},{10,11... | collective-permute-start | bytes 786440 | tf_op jit(solution)/shard_map/ppermute | solution.py:36
  185.5 11.5 %collective-permute-start.11 = (bf16[64,2048]{1,0:T(8,128)(2,1)S(1)}, bf16[64,2048]{1,0:T(8,128)(2,1)S(1)}, u32[]{:S(2)}, u32[]{:S(2)}) collective-permute-start(bf16[64,2048]{1,0:T(8,128)(2,1)S(1)} %add_convert_fusion.3), channel_id=1, source_target_pairs={{0,6},{2,4},{4,2},{6,0},{1,7},{3,5},{5,3},{7,1},{8,14},{10,12},{12... | collective-permute-start | bytes 786440 | tf_op jit(solution)/shard_map/ppermute | solution.py:40
  189.6 10.0 %collective-permute-start.17 = (bf16[64,2048]{1,0:T(8,128)(2,1)S(1)}, bf16[64,2048]{1,0:T(8,128)(2,1)S(1)}, u32[]{:S(2)}, u32[]{:S(2)}) collective-permute-start(bf16[64,2048]{1,0:T(8,128)(2,1)S(1)} %fusion.32), channel_id=1, source_target_pairs={{0,2},{2,0},{4,6},{6,4},{1,3},{3,1},{5,7},{7,5},{8,10},{10,8},{12,... | collective-permute-start | bytes 786440 | tf_op jit(solution)/shard_map/ppermute | solution.py:40
  197.1 6.0 %collective-permute-start.12 = (bf16[64,2048]{1,0:T(8,128)(2,1)S(1)}, bf16[64,2048]{1,0:T(8,128)(2,1)S(1)}, u32[]{:S(2)}, u32[]{:S(2)}) collective-permute-start(bf16[64,2048]{1,0:T(8,128)(2,1)S(1)} %add_convert_fusion.2), channel_id=1, source_target_pairs={{0,1},{1,0},{2,3},{3,2},{4,5},{5,4},{6,7},{7,6},{8,9},{9,8},{10,11... | collective-permute-start | bytes 786440 | tf_op jit(solution)/shard_map/ppermute | solution.py:36
  199.7 22.8 %collective-permute-start.18 = (bf16[64,2048]{1,0:T(8,128)(2,1)S(1)}, bf16[64,2048]{1,0:T(8,128)(2,1)S(1)}, u32[]{:S(2)}, u32[]{:S(2)}) collective-permute-start(bf16[64,2048]{1,0:T(8,128)(2,1)S(1)} %add_convert_fusion.1), channel_id=1, source_target_pairs={{0,6},{2,4},{4,2},{6,0},{1,7},{3,5},{5,3},{7,1},{8,14},{10,12},{12... | collective-permute-start | bytes 786440 | tf_op jit(solution)/shard_map/ppermute | solution.py:40
  209.8 14.6 %copy-start.5 = (bf16[1,128,2048]{2,1,0:T(8,128)(2,1)S(1)}, bf16[1,128,2048]{2,1,0:T(8,128)(2,1)}, u32[]{:S(2)}) copy-start(bf16[1,128,2048]{2,1,0:T(8,128)(2,1)} %param.6) | copy-start | bytes 1572868
  210.7 40.4 %all-to-all-start.5 = ((bf16[16,4,32,128]{3,2,1,0:T(8,128)(2,1)}), bf16[16,4,32,128]{3,2,1,0:T(8,128)(2,1)S(1)}, u32[]{:S(2)}, u32[]{:S(2)}) async-start(bf16[16,4,32,128]{3,2,1,0:T(8,128)(2,1)} %copy.45), calls=%async_computation.5 | async-start | bytes 1048576 | tf_op jit(solution)/shard_map/all_to_all | solution.py:20
  222.5 3.7 %collective-permute-start.19 = (bf16[64,2048]{1,0:T(8,128)(2,1)S(1)}, bf16[64,2048]{1,0:T(8,128)(2,1)S(1)}, u32[]{:S(2)}, u32[]{:S(2)}) collective-permute-start(bf16[64,2048]{1,0:T(8,128)(2,1)S(1)} %add_convert_fusion), channel_id=1, source_target_pairs={{0,1},{1,0},{2,3},{3,2},{4,5},{5,4},{6,7},{7,6},{8,9},{9,8},{10,11... | collective-permute-start | bytes 786440 | tf_op jit(solution)/shard_map/ppermute | solution.py:36
  (11 other events, 18.6 us)

commit v3 on v2

--- a/solution.py
+++ b/solution.py
@@ -40,22 +40,46 @@
     return lax.ppermute(x, "x", [(i, i ^ bit) for i in range(CTX // 2)])
 
 
-def y_pieces(part):
+def from_zpair(x):
+    return lax.ppermute(x, "zq", [(0, 1), (1, 0)])
+
+
+def y_others(pieces):
     y = lax.axis_index("y")
-    part = part.transpose(1, 0, 2, 3)[:, :, None]
-    full = jnp.zeros((part.shape[0], NZ, NY, 32, HD), BF)
-    full = lax.dynamic_update_index_in_dim(full, part, y, 2)
+    out = []
     for k in range(1, NY):
-        got = lax.ppermute(part, "y", [(i, (i + k) % NY) for i in range(NY)])
-        full = lax.dynamic_update_index_in_dim(full, got, (y - k) % NY, 2)
-    return full.reshape(-1, D, HD)
+        got = lax.ppermute(pieces(k), "y", [(i, (i + k) % NY) for i in range(NY)])
+        out.append(((y - k) % NY, got))
+    return out
 
 
 def gather_weights(w_qkv, w_out):
-    first = spread(w_qkv[:2], "z", NZ)
-    second = spread(jnp.stack([w_qkv[2], w_out.T]), "z", NZ)
-    wa, wb = y_pieces(first), y_pieces(second)
-    return wa[0], wa[1], wb[0], wb[1]
+    y, zq = lax.axis_index("y"), lax.axis_index("zq")
+    shard = jnp.concatenate([w_qkv, w_out.T[None]], 0)
+    near = spread(shard, "zp", NZ // 2)
+    full = jnp.zeros((4, NZ // 2, 2, NY, 32, HD), BF)
+    for parity, part in ((zq, near), (1 - zq, from_zpair(near))):
+        for source, piece in [(y, part)] + y_others(lambda k: part):
+            piece = piece.transpose(1, 0, 2, 3)[:, :, None, None]
+            full = lax.dynamic_update_slice(full, piece, (0, 0, parity, source, 0, 0))
+    return full.reshape(4, D, HD)
+
+
+def by_feature(x):
+    return x.reshape(NZ, NY, 32, x.shape[-1])
+
+
+def for_y(blocks, k):
+    return lax.dynamic_index_in_dim(blocks, (lax.axis_index("y") + k) % NY, 1, keepdims=False)
+
+
+def scatter_z(quarter):
+    zq = lax.axis_index("zq")
+    pairs = quarter.reshape(NZ // 2, 2, 4, 32, HD)
+    mine = lax.dynamic_index_in_dim(pairs, zq, 1, keepdims=False)
+    other = lax.dynamic_index_in_dim(pairs, 1 - zq, 1, keepdims=False)
+    part = mine + from_zpair(other.astype(BF)).astype(F32)
+    return jnp.sum(swap(part.astype(BF), "zp").astype(F32), 0)
 
 
 def from_owner(tile, mine):
@@ -65,12 +89,16 @@
     return kept + from_pair(kept, 3)
 
 
-def sum_tile(terms):
+def sum_begin(terms):
     core = lax.axis_index("core")
     halves = terms.astype(BF).reshape(2, TILE // 2, D)
     part = lax.dynamic_index_in_dim(halves, core, 0, keepdims=False)
     part = add(part, from_core(lax.dynamic_index_in_dim(halves, 1 - core, 0, keepdims=False)))
-    part = add(part, from_pair(part, 1))
+    return add(part, from_pair(part, 1))
+
+
+def sum_end(part):
+    core = lax.axis_index("core")
     part = add(part, from_pair(part, 3))
     other = from_core(part)
     low, high = jnp.where(core == 0, part, other), jnp.where(core == 0, other, part)
@@ -136,55 +164,70 @@
     def chunk(tile):
         return lax.dynamic_index_in_dim(tile.reshape(CTX, CHUNK, D), me, 0, keepdims=False)
 
+    tokens = ((0,), (0,))
     h1 = from_owner(hidden_in[0], mine)
     g3 = from_owner(cotangent[0], mine)
-    dy3 = jnp.where(live3, g3, jnp.zeros_like(g3))
 
     x1 = h1.astype(F32)
     inv2, rows2 = norm_chunk(x1, gain)
     mixed2, keep2 = forward(rows2, w)
+    attn2 = keep2[-1]
+    rows2t = by_feature(rows2.T)
+    rows_in = y_others(lambda k: for_y(rows2t, k))
     h2 = all_rows((chunk(h1).astype(F32) + sum_chunk(mixed2)).astype(BF))
+    h2, rows_in = lax.optimization_barrier((h2, rows_in))
 
     x2 = h2.astype(F32)
     inv3, normed3 = norm_chunk(x2, gain)
     rows3 = jnp.where(live3, normed3, jnp.zeros_like(normed3))
+    dy3 = jnp.where(live3, g3, jnp.zeros_like(g3))
     mixed3, keep3 = forward(rows3, w)
+    h3_part = sum_begin(mixed3)
     dnorm3, (dq3, dk3, dv3) = backward(dy3, keep3, w)
+    dnorm3, dq3, dk3, dv3 = lax.optimization_barrier((dnorm3.astype(BF), dq3, dk3, dv3))
+    early = jnp.stack(
+        [by_feature(dot(rows3, d, tokens)) for d in (dq3, dk3, dv3)]
+        + [by_feature(dot(dy3, keep3[-1], tokens))],
+        2,
+    )
+    early_in = y_others(lambda k: for_y(early, k).astype(BF))
     x2c = chunk(h2).astype(F32)
     inv3c, _ = norm_chunk(x2c, gain)
     g2c = chunk(g3).astype(F32) + norm_grad(sum_chunk(dnorm3), x2c, inv3c, gain)
-    g2 = all_rows(g2c.astype(BF))
-
-    dy2 = g2
-    dnorm2, (dq2, dk2, dv2) = backward(dy2, keep2, w)
-
-    def weight_grad(left3, right3, left2, right2):
-        left = jnp.concatenate([left3, left2], 0)
-        right = jnp.concatenate([right3, right2], 0)
-        return dot(left, right, ((0,), (0,))).astype(BF)
-
-    grads = jnp.stack(
-        [
-            weight_grad(rows3, dq3, rows2, dq2),
-            weight_grad(rows3, dk3, rows2, dk2),
-            weight_grad(rows3, dv3, rows2, dv2),
-            weight_grad(dy3, keep3[-1], dy2, keep2[-1]),
-        ]
-    )
-    grads = grads.reshape(4, NZ, NY, 32, HD).transpose(2, 1, 0, 3, 4)
-    part = jnp.sum(swap(grads, "y").astype(F32), 0).astype(BF)
-    shard = jnp.sum(swap(part, "z").astype(F32), 0)
-
-    h3 = (x2 + sum_tile(mixed3)).astype(BF)
-    g1 = (g2.astype(F32) + norm_grad(sum_tile(dnorm2), x1, inv2, gain)).astype(BF)
+    g2 = spread(g2c.astype(BF), CONTEXT, CTX).reshape(TILE, D)
+    g2, h3_part = lax.optimization_barrier((g2, h3_part))
+
+    dnorm2, (dq2, dk2, dv2) = backward(g2, keep2, w)
+    dnorm2 = dnorm2.astype(BF)
+    g1_part = sum_begin(dnorm2)
+    out2 = dot(g2, attn2, tokens)
+    dqkv2 = jnp.broadcast_to(jnp.concatenate([dq2, dk2, dv2], 0)[None], (NY, 3 * TILE, HD))
+    out2y = by_feature(out2).transpose(1, 0, 2, 3).reshape(NY, D // NY, HD).astype(BF)
+    late, early_in = lax.optimization_barrier((jnp.concatenate([dqkv2, out2y], 1), early_in))
+    late = swap(late, "y")
+
+    y = lax.axis_index("y")
+    left = jnp.zeros((D // NY, NY, TILE), BF)
+    for source, piece in [(y, for_y(rows2t, 0))] + rows_in:
+        left = lax.dynamic_update_slice(left, piece.reshape(D // NY, 1, TILE), (0, source, 0))
+    right = late[:, : 3 * TILE].reshape(NY, 3, TILE, HD)
+    quarter = jnp.einsum("dyr,ytrc->dtc", left, right, preferred_element_type=F32)
+    quarter = quarter.reshape(NZ, 32, 3, HD).transpose(0, 2, 1, 3)
+    last = jnp.sum(late[:, 3 * TILE :].astype(F32), 0).reshape(NZ, 1, 32, HD)
+    quarter = jnp.concatenate([quarter, last], 1)
+    quarter = quarter + for_y(early, 0) + sum(x.astype(F32) for _, x in early_in)
+    shard = scatter_z(quarter)
+
+    h3 = (x2 + sum_end(h3_part)).astype(BF)
+    g1 = (g2.astype(F32) + norm_grad(sum_end(g1_part), x1, inv2, gain)).astype(BF)
     hidden_out = jnp.where(mine, h3, hidden_in[0])
     grad_in = jnp.where(mine, g1, cotangent[0])
     return (hidden_out[None], grad_in[None], shard[:3], shard[3].T)
 
 
 def solution(mesh):
-    grid = Mesh(mesh.devices.reshape(NZ, NY, CTX // 2, 2), ("z", "y") + CONTEXT)
-    dp = ("z", "y")
+    grid = Mesh(mesh.devices.reshape(NZ // 2, 2, NY, CTX // 2, 2), ("zp", "zq", "y") + CONTEXT)
+    dp = ("zp", "zq", "y")
     in_specs = (
         P(dp, CONTEXT, None),
         P(dp, CONTEXT, None),

time: 255 us -> 272 us (1.067)
  local copies, waits for them, and re-layouts: 6.39 us -> 25.5 us
  blocking collectives: 26.4 us -> 13.1 us
  starting transfers between devices: 110 us -> 123 us
  waiting for transfers between devices: 65.3 us -> 52.3 us
  matrix products: 15.9 us -> 22.2 us
  other arithmetic: 27.2 us -> 31 us
    ppermute x6 -> x14, starting transfers between devices: 23.9 us -> 46.2 us  [the longest x12 40.4 us: y_others(): got = lax.ppermute(pieces(k), 'y', [(i, (i + k) % NY) for i in range(NY)])]
    all_gather x2 -> x1, blocking collectives: 26.4 us -> 13.1 us  [all_rows(): return lax.all_gather(chunk, CONTEXT, tiled=True)]
    ppermute x8, waiting for transfers between devices: 16.7 us -> 5.25 us  [from_pair(): return lax.ppermute(x, 'x', [(i, i ^ bit) for i in range(CTX // 2)])]
    all_to_all x6, waiting for transfers between devices: 48.5 us -> 39.2 us  [swap(): return lax.all_to_all(x, axis, 0, 0)]
    all_to_all x6, starting transfers between devices: 48 us -> 39 us  [swap(): return lax.all_to_all(x, axis, 0, 0)]
    ppermute x6 -> x14, waiting for transfers between devices: 0.02 us -> 7.77 us  [the longest x12 6.74 us: y_others(): got = lax.ppermute(pieces(k), 'y', [(i, (i + k) % NY) for i in range(NY)])]
    dynamic_update_slice x7 -> x12, local copies, waits for them, and re-layouts: 0.32 us -> 7.61 us  [the longest x4 5.38 us: on_device(): lax.dynamic_update_slice(left, piece.reshape(D // NY, 1, TILE), (0, sourc...]
    dot_general x32 -> x33, matrix products: 15.9 us -> 20.7 us  [dot(): return lax.dot_general(a, b, (dims, ((), ())), preferred_element_type=F32)]
  transfers between devices with their start and end apart: 26 -> 34, of which waited for: 10 -> 6; matrix products, arithmetic and copies ran while one was open for 16% -> 24% of each run, Pallas kernels for 0% -> 0%
where the time goes in v3:
time: 272 us; the launch traced here: 268 us
  starting transfers between devices  123 us (45%)
  waiting for transfers between devices  52.3 us (19%)
  other arithmetic  31 us (11%)
  local copies, waits for them, and re-layouts  25.5 us (9%)
  matrix products  22.2 us (8%)
  blocking collectives  13.1 us (5%)
    ppermute x12, starting transfers between devices, y_others(): got = lax.ppermute(pieces(k), 'y', [(i, (i + k) % NY) for i in range(NY)])  40.4 us
    all_to_all x6, waiting for transfers between devices, swap(): return lax.all_to_all(x, axis, 0, 0)  39.2 us
    all_to_all x6, starting transfers between devices, swap(): return lax.all_to_all(x, axis, 0, 0)  39 us
    ppermute x8, starting transfers between devices, from_pair(): return lax.ppermute(x, 'x', [(i, i ^ bit) for i in range(CTX // 2)])  24.6 us
    dot_general x33, matrix products, dot(): return lax.dot_general(a, b, (dims, ((), ())), preferred_element_type=F32)  20.7 us
    all_gather x1, blocking collectives, all_rows(): return lax.all_gather(chunk, CONTEXT, tiled=True)  13.1 us
    ppermute x6, starting transfers between devices, from_core(): return lax.ppermute(x, 'core', [(0, 1), (1, 0)])  12.7 us
    ppermute x12, waiting for transfers between devices, y_others(): got = lax.ppermute(pieces(k), 'y', [(i, (i + k) % NY) for i in range(NY)])  6.74 us
  transfers between devices with their start and end apart: 34, of which 6 were waited for; matrix products, arithmetic and copies ran while one was open for 24% of the time, Pallas kernels for 0%

profile of v3, /device:TPU:6, one launch (start us, length us, event | category | flops | bytes accessed | tf_op | source)
XLA Modules:
  0.0 268.3 jit_solution(18397139784779941785)
XLA Ops:
  2.0 1.8 bitcast_select_fusion.1
  3.8 1.9 collective-permute-start
  5.7 2.5 bitcast_select_fusion
  8.3 2.4 collective-permute-start.13
  11.4 15.2 %all-to-all-start = ((bf16[8,4,32,128]{3,2,1,0:T(8,128)(2,1)}), bf16[8,4,32,128]{3,2,1,0:T(8,128)(2,1)S(1)}, u32[]{:S(2)}, u32[]{:S(2)}) async-start(bf16[8,4,32,128]{3,2,1,0:T(8,128)(2,1)} %broadcast_in_dim.41), calls=%async_computation | async-start | bytes 524288 | tf_op jit(solution)/shard_map/all_to_all | solution.py:20
  27.4 2.7 %collective-permute-start.1 = (bf16[128,2048]{1,0:T(8,128)(2,1)S(1)}, bf16[128,2048]{1,0:T(8,128)(2,1)S(1)}, u32[]{:S(2)}, u32[]{:S(2)}) collective-permute-start(bf16[128,2048]{1,0:T(8,128)(2,1)S(1)} %fusion.135), channel_id=1, source_target_pairs={{0,2},{2,0},{4,6},{6,4},{1,3},{3,1},{5,7},{7,5},{8,10},{10,8},{12,... | collective-permute-start | bytes 1572872 | tf_op jit(solution)/shard_map/ppermute | solution.py:40
  30.9 3.1 %collective-permute-start.14 = (bf16[128,2048]{1,0:T(8,128)(2,1)S(1)}, bf16[128,2048]{1,0:T(8,128)(2,1)S(1)}, u32[]{:S(2)}, u32[]{:S(2)}) collective-permute-start(bf16[128,2048]{1,0:T(8,128)(2,1)S(1)} %fusion.134), channel_id=1, source_target_pairs={{0,2},{2,0},{4,6},{6,4},{1,3},{3,1},{5,7},{7,5},{8,10},{10,8},{12,... | collective-permute-start | bytes 1572872 | tf_op jit(solution)/shard_map/ppermute | solution.py:40
  34.0 14.2 %all-to-all-done = bf16[8,4,32,128]{3,2,1,0:T(8,128)(2,1)S(1)} async-done(((bf16[8,4,32,128]{3,2,1,0:T(8,128)(2,1)}), bf16[8,4,32,128]{3,2,1,0:T(8,128)(2,1)S(1)}, u32[]{:S(2)}, u32[]{:S(2)}) %all-to-all-start) | async-done | bytes 262176 | tf_op jit(solution)/shard_map/all_to_all | solution.py:20
  48.9 3.5 %collective-permute-start.3 = (bf16[8,4,32,128]{3,2,0,1:T(8,128)(2,1)}, bf16[8,4,32,128]{3,2,0,1:T(8,128)(2,1)}, u32[]{:S(2)}, u32[]{:S(2)}) collective-permute-start(bf16[8,4,32,128]{3,2,0,1:T(8,128)(2,1)} %copy.75), channel_id=1, source_target_pairs={{0,8},{8,16},{16,24},{24,0},{1,9},{9,17},{17,25},{25,1},{2,10},{10... | collective-permute-start | bytes 786440 | tf_op jit(solution)/shard_map/ppermute | solution.py:51
  52.4 1.9 collective-permute-start.6
  55.1 4.8 %collective-permute-start.4 = (bf16[8,4,32,128]{3,2,0,1:T(8,128)(2,1)}, bf16[8,4,32,128]{3,2,0,1:T(8,128)(2,1)S(1)}, u32[]{:S(2)}, u32[]{:S(2)}) collective-permute-start(bf16[8,4,32,128]{3,2,0,1:T(8,128)(2,1)} %copy.75), channel_id=1, source_target_pairs={{0,16},{8,24},{16,0},{24,8},{1,17},{9,25},{17,1},{25,9},{2,18},{10... | collective-permute-start | bytes 786440 | tf_op jit(solution)/shard_map/ppermute | solution.py:51
  60.4 3.3 %collective-permute-start.5 = (bf16[8,4,32,128]{3,2,0,1:T(8,128)(2,1)}, bf16[8,4,32,128]{3,2,0,1:T(8,128)(2,1)S(1)}, u32[]{:S(2)}, u32[]{:S(2)}) collective-permute-start(bf16[8,4,32,128]{3,2,0,1:T(8,128)(2,1)} %copy.75), channel_id=1, source_target_pairs={{0,24},{8,0},{16,8},{24,16},{1,25},{9,1},{17,9},{25,17},{2,26},{10... | collective-permute-start | bytes 786440 | tf_op jit(solution)/shard_map/ppermute | solution.py:51
  63.8 2.4 collective-permute-start.2
  67.2 4.7 %collective-permute-start.15 = (bf16[128,2048]{1,0:T(8,128)(2,1)}, bf16[128,2048]{1,0:T(8,128)(2,1)}, u32[]{:S(2)}, u32[]{:S(2)}) collective-permute-start(bf16[128,2048]{1,0:T(8,128)(2,1)} %add.261), channel_id=1, source_target_pairs={{0,6},{2,4},{4,2},{6,0},{1,7},{3,5},{5,3},{7,1},{8,14},{10,12},{12... | collective-permute-start | bytes 1572872 | tf_op jit(solution)/shard_map/ppermute | solution.py:40
  71.9 1.9 collective-permute-start.9
  74.8 4.6 %collective-permute-start.8 = (bf16[8,4,32,128]{3,2,0,1:T(8,128)(2,1)}, bf16[8,4,32,128]{3,2,0,1:T(8,128)(2,1)S(1)}, u32[]{:S(2)}, u32[]{:S(2)}) collective-permute-start(bf16[8,4,32,128]{3,2,0,1:T(8,128)(2,1)} %collective-permute-done.6), channel_id=1, source_target_pairs={{0,16},{8,24},{16,0},{24,8},{1,17},{9,25},{17,1},{25,9},{2,18},{10... | collective-permute-start | bytes 786440 | tf_op jit(solution)/shard_map/ppermute | solution.py:51
  79.5 1.9 collective-permute-start.7
  82.5 6.7 %collective-permute-done.7 = bf16[8,4,32,128]{3,2,0,1:T(8,128)(2,1)S(1)} collective-permute-done((bf16[8,4,32,128]{3,2,0,1:T(8,128)(2,1)}, bf16[8,4,32,128]{3,2,0,1:T(8,128)(2,1)S(1)}, u32[]{:S(2)}, u32[]{:S(2)}) %collective-permute-start.7) | collective-permute-done | bytes 262176 | tf_op jit(solution)/shard_map/ppermute | solution.py:51
  92.4 2.0 copy.83
  97.9 4.5 %all-to-all-start.1 = ((bf16[8,16,2048]{2,1,0:T(8,128)(2,1)}), bf16[8,16,2048]{2,1,0:T(8,128)(2,1)}, u32[]{:S(2)}, u32[]{:S(2)}) async-start(bf16[8,16,2048]{2,1,0:T(8,128)(2,1)} %bitcast.29), calls=%async_computation.1 | async-start | bytes 1048576 | tf_op jit(solution)/shard_map/all_to_all | solution.py:20
  103.2 2.6 collective-permute-start.12
  105.9 2.9 %collective-permute-start.11 = (bf16[16,32,128]{2,1,0:T(8,128)(2,1)}, bf16[16,32,128]{2,1,0:T(8,128)(2,1)}, u32[]{:S(2)}, u32[]{:S(2)}) collective-permute-start(bf16[16,32,128]{2,1,0:T(8,128)(2,1)} %get-tuple-element.55), channel_id=1, source_target_pairs={{0,16},{8,24},{16,0},{24,8},{1,17},{9,25},{17,1},{25,9},{2,18},{10... | collective-permute-start | bytes 393224 | tf_op jit(solution)/shard_map/ppermute | solution.py:51
  108.7 2.8 %collective-permute-start.10 = (bf16[16,32,128]{2,1,0:T(8,128)(2,1)}, bf16[16,32,128]{2,1,0:T(8,128)(2,1)}, u32[]{:S(2)}, u32[]{:S(2)}) collective-permute-start(bf16[16,32,128]{2,1,0:T(8,128)(2,1)} %get-tuple-element.56), channel_id=1, source_target_pairs={{0,8},{8,16},{16,24},{24,0},{1,9},{9,17},{17,25},{25,1},{2,10},{10... | collective-permute-start | bytes 393224 | tf_op jit(solution)/shard_map/ppermute | solution.py:51
  117.3 13.1 %all_gather.3 = bf16[128,2048]{1,0:T(8,128)(2,1)S(1)} all-gather(bf16[16,2048]{1,0:T(8,128)(2,1)S(1)} %fusion.49), channel_id=1, replica_groups=mesh['zp'=8,'zq'=2,'y'=4,'x'=4,'core'=2] {'x','core'}, dimensions={0}, use_global_device_ids=true | all-gather | bytes 589824 | tf_op jit(solution)/shard_map/all_gather | solution.py:114
  136.0 1.9 fusion.35
  138.0 1.7 dynamic-slice_bitcast_fusion.1
  139.7 2.4 collective-permute-start.16
  143.9 4.5 %all-to-all-start.2 = ((bf16[8,16,2048]{2,1,0:T(8,128)(2,1)}), bf16[8,16,2048]{2,1,0:T(8,128)(2,1)S(1)}, u32[]{:S(2)}, u32[]{:S(2)}) async-start(bf16[8,16,2048]{2,1,0:T(8,128)(2,1)} %bitcast.249), calls=%async_computation.2 | async-start | bytes 1048576 | tf_op jit(solution)/shard_map/all_to_all | solution.py:20
  156.4 3.6 %collective-permute-start.24 = (bf16[16,4,32,128]{3,2,1,0:T(8,128)(2,1)}, bf16[16,4,32,128]{3,2,1,0:T(8,128)(2,1)}, u32[]{:S(2)}, u32[]{:S(2)}) collective-permute-start(bf16[16,4,32,128]{3,2,1,0:T(8,128)(2,1)} %bitcast.212), channel_id=1, source_target_pairs={{0,8},{8,16},{16,24},{24,0},{1,9},{9,17},{17,25},{25,1},{2,10},{10... | collective-permute-start | bytes 1572872 | tf_op jit(solution)/shard_map/ppermute | solution.py:51
  160.0 4.1 %collective-permute-start.25 = (bf16[16,4,32,128]{3,2,1,0:T(8,128)(2,1)}, bf16[16,4,32,128]{3,2,1,0:T(8,128)(2,1)}, u32[]{:S(2)}, u32[]{:S(2)}) collective-permute-start(bf16[16,4,32,128]{3,2,1,0:T(8,128)(2,1)} %bitcast.213), channel_id=1, source_target_pairs={{0,16},{8,24},{16,0},{24,8},{1,17},{9,25},{17,1},{25,9},{2,18},{10... | collective-permute-start | bytes 1572872 | tf_op jit(solution)/shard_map/ppermute | solution.py:51
  164.0 4.5 %collective-permute-start.26 = (bf16[16,4,32,128]{3,2,1,0:T(8,128)(2,1)}, bf16[16,4,32,128]{3,2,1,0:T(8,128)(2,1)}, u32[]{:S(2)}, u32[]{:S(2)}) collective-permute-start(bf16[16,4,32,128]{3,2,1,0:T(8,128)(2,1)} %bitcast.214), channel_id=1, source_target_pairs={{0,24},{8,0},{16,8},{24,16},{1,25},{9,1},{17,9},{25,17},{2,26},{10... | collective-permute-start | bytes 1572872 | tf_op jit(solution)/shard_map/ppermute | solution.py:51
  174.4 2.8 %collective-permute-start.17 = (bf16[64,2048]{1,0:T(8,128)(2,1)S(1)}, bf16[64,2048]{1,0:T(8,128)(2,1)}, u32[]{:S(2)}, u32[]{:S(2)}) collective-permute-start(bf16[64,2048]{1,0:T(8,128)(2,1)S(1)} %fusion.32), channel_id=1, source_target_pairs={{0,2},{2,0},{4,6},{6,4},{1,3},{3,1},{5,7},{7,5},{8,10},{10,8},{12,... | collective-permute-start | bytes 786440 | tf_op jit(solution)/shard_map/ppermute | solution.py:40
  179.2 5.1 %all-to-all-start.3 = ((bf16[8,16,2048]{2,1,0:T(8,128)(2,1)}), bf16[8,16,2048]{2,1,0:T(8,128)(2,1)S(1)}, u32[]{:S(2)}, u32[]{:S(2)}) async-start(bf16[8,16,2048]{2,1,0:T(8,128)(2,1)} %broadcast_in_dim.96), calls=%async_computation.3 | async-start | bytes 1048576 | tf_op jit(solution)/shard_map/all_to_all | solution.py:20
  185.4 7.2 %all-to-all-done.3 = bf16[8,16,2048]{2,1,0:T(8,128)(2,1)S(1)} async-done(((bf16[8,16,2048]{2,1,0:T(8,128)(2,1)}), bf16[8,16,2048]{2,1,0:T(8,128)(2,1)S(1)}, u32[]{:S(2)}, u32[]{:S(2)}) %all-to-all-start.3) | async-done | bytes 524320 | tf_op jit(solution)/shard_map/all_to_all | solution.py:20
  197.9 1.9 collective-permute-start.20
  200.2 4.0 %collective-permute-start.18 = (bf16[64,2048]{1,0:T(8,128)(2,1)S(1)}, bf16[64,2048]{1,0:T(8,128)(2,1)}, u32[]{:S(2)}, u32[]{:S(2)}) collective-permute-start(bf16[64,2048]{1,0:T(8,128)(2,1)S(1)} %add_convert_fusion.3), channel_id=1, source_target_pairs={{0,6},{2,4},{4,2},{6,0},{1,7},{3,5},{5,3},{7,1},{8,14},{10,12},{12... | collective-permute-start | bytes 786440 | tf_op jit(solution)/shard_map/ppermute | solution.py:40
  205.3 4.2 %all-to-all-start.4 = ((bf16[4,896,128]{2,1,0:T(8,128)(2,1)}), bf16[4,896,128]{2,1,0:T(8,128)(2,1)}, u32[]{:S(2)}, u32[]{:S(2)}) async-start(bf16[4,896,128]{2,1,0:T(8,128)(2,1)} %pad_maximum_fusion.1), calls=%async_computation.4 | async-start | bytes 1835008 | tf_op jit(solution)/shard_map/all_to_all | solution.py:20
  210.7 1.9 collective-permute-start.21
  213.6 2.1 collective-permute-start.19
  215.8 5.2 %collective-permute-done.21 = bf16[64,2048]{1,0:T(8,128)(2,1)S(1)} collective-permute-done((bf16[64,2048]{1,0:T(8,128)(2,1)S(1)}, bf16[64,2048]{1,0:T(8,128)(2,1)S(1)}, u32[]{:S(2)}, u32[]{:S(2)}) %collective-permute-start.21) | collective-permute-done | bytes 262176 | tf_op jit(solution)/shard_map/ppermute | solution.py:40
  221.1 3.1 %collective-permute-start.22 = (bf16[64,2048]{1,0:T(8,128)(2,1)S(1)}, bf16[64,2048]{1,0:T(8,128)(2,1)}, u32[]{:S(2)}, u32[]{:S(2)}) collective-permute-start(bf16[64,2048]{1,0:T(8,128)(2,1)S(1)} %add_convert_fusion.1), channel_id=1, source_target_pairs={{0,6},{2,4},{4,2},{6,0},{1,7},{3,5},{5,3},{7,1},{8,14},{10,12},{12... | collective-permute-start | bytes 786440 | tf_op jit(solution)/shard_map/ppermute | solution.py:40
  228.7 2.2 fusion.22
  230.9 3.9 %collective-permute-start.27 = (bf16[8,4,32,128]{3,2,1,0:T(8,128)(2,1)S(1)}, bf16[8,4,32,128]{3,2,1,0:T(8,128)(2,1)S(1)}, u32[]{:S(2)}, u32[]{:S(2)}) collective-permute-start(bf16[8,4,32,128]{3,2,1,0:T(8,128)(2,1)S(1)} %fusion.38), channel_id=1, source_target_pairs={{0,32},{32,0},{1,33},{33,1},{2,34},{34,2},{3,35},{35,3},{4,36},{36... | collective-permute-start | bytes 786440 | tf_op jit(solution)/shard_map/ppermute | solution.py:44
  235.9 1.9 collective-permute-start.23
  237.8 1.7 fusion.29
  241.3 5.4 %all-to-all-start.5 = ((bf16[8,4,32,128]{3,2,1,0:T(8,128)(2,1)}), bf16[8,4,32,128]{3,2,1,0:T(8,128)(2,1)S(1)}, u32[]{:S(2)}, u32[]{:S(2)}) async-start(bf16[8,4,32,128]{3,2,1,0:T(8,128)(2,1)} %fusion.33), calls=%async_computation.5 | async-start | bytes 524288 | tf_op jit(solution)/shard_map/all_to_all | solution.py:20
  247.1 2.1 fusion.27
  249.2 17.8 %all-to-all-done.5 = bf16[8,4,32,128]{3,2,1,0:T(8,128)(2,1)S(1)} async-done(((bf16[8,4,32,128]{3,2,1,0:T(8,128)(2,1)}), bf16[8,4,32,128]{3,2,1,0:T(8,128)(2,1)S(1)}, u32[]{:S(2)}, u32[]{:S(2)}) %all-to-all-start.5) | async-done | bytes 262176 | tf_op jit(solution)/shard_map/all_to_all | solution.py:20
  (189 shorter events, 63.7 us)
Async XLA Ops:
  0.6 26.0 %copy-start.1 = (bf16[1,128,2048]{2,1,0:T(8,128)(2,1)S(1)}, bf16[1,128,2048]{2,1,0:T(8,128)(2,1)}, u32[]{:S(2)}) copy-start(bf16[1,128,2048]{2,1,0:T(8,128)(2,1)} %param.6) | copy-start | bytes 1572868
  0.6 10.0 %copy-start.24 = (bf16[128,32]{0,1:T(8,128)(2,1)S(1)}, bf16[128,32]{0,1:T(8,128)(2,1)}, u32[]{:S(2)}) copy-start(bf16[128,32]{0,1:T(8,128)(2,1)} %param.10) | copy-start | bytes 24580
  0.7 10.0 %copy-start.23 = (bf16[3,32,128]{2,1,0:T(8,128)(2,1)S(1)}, bf16[3,32,128]{2,1,0:T(8,128)(2,1)}, u32[]{:S(2)}) copy-start(bf16[3,32,128]{2,1,0:T(8,128)(2,1)} %param.9) | copy-start | bytes 73732
  2.0 28.1 %copy-start.2 = (bf16[1,128,2048]{2,1,0:T(8,128)(2,1)S(1)}, bf16[1,128,2048]{2,1,0:T(8,128)(2,1)}, u32[]{:S(2)}) copy-start(bf16[1,128,2048]{2,1,0:T(8,128)(2,1)} %param.7) | copy-start | bytes 1572868
  3.8 22.9 %collective-permute-start = (bf16[128,2048]{1,0:T(8,128)(2,1)S(1)}, bf16[128,2048]{1,0:T(8,128)(2,1)S(1)}, u32[]{:S(2)}, u32[]{:S(2)}) collective-permute-start(bf16[128,2048]{1,0:T(8,128)(2,1)S(1)} %bitcast_select_fusion.1), channel_id=1, source_target_pairs={{0,1},{1,0},{2,3},{3,2},{4,5},{5,4},{6,7},{7,6},{8,9},{9,8},{10,11... | collective-permute-start | bytes 1572872 | tf_op jit(solution)/shard_map/ppermute | solution.py:36
  8.3 21.9 %collective-permute-start.13 = (bf16[128,2048]{1,0:T(8,128)(2,1)}, bf16[128,2048]{1,0:T(8,128)(2,1)S(1)}, u32[]{:S(2)}, u32[]{:S(2)}) collective-permute-start(bf16[128,2048]{1,0:T(8,128)(2,1)} %bitcast_select_fusion), channel_id=1, source_target_pairs={{0,1},{1,0},{2,3},{3,2},{4,5},{5,4},{6,7},{7,6},{8,9},{9,8},{10,11... | collective-permute-start | bytes 1572872 | tf_op jit(solution)/shard_map/ppermute | solution.py:36
  11.4 42.9 %copy-start.27 = (s32[1,8]{1,0:T(1,128)S(1)}, s32[1,8]{1,0:T(1,128)}, u32[]{:S(2)}) copy-start(s32[1,8]{1,0:T(1,128)} %param.8) | copy-start | bytes 100
  11.4 36.8 %all-to-all-start = ((bf16[8,4,32,128]{3,2,1,0:T(8,128)(2,1)}), bf16[8,4,32,128]{3,2,1,0:T(8,128)(2,1)S(1)}, u32[]{:S(2)}, u32[]{:S(2)}) async-start(bf16[8,4,32,128]{3,2,1,0:T(8,128)(2,1)} %broadcast_in_dim.41), calls=%async_computation | async-start | bytes 524288 | tf_op jit(solution)/shard_map/all_to_all | solution.py:20
  27.4 33.0 %collective-permute-start.1 = (bf16[128,2048]{1,0:T(8,128)(2,1)S(1)}, bf16[128,2048]{1,0:T(8,128)(2,1)S(1)}, u32[]{:S(2)}, u32[]{:S(2)}) collective-permute-start(bf16[128,2048]{1,0:T(8,128)(2,1)S(1)} %fusion.135), channel_id=1, source_target_pairs={{0,2},{2,0},{4,6},{6,4},{1,3},{3,1},{5,7},{7,5},{8,10},{10,8},{12,... | collective-permute-start | bytes 1572872 | tf_op jit(solution)/shard_map/ppermute | solution.py:40
  30.9 33.0 %collective-permute-start.14 = (bf16[128,2048]{1,0:T(8,128)(2,1)S(1)}, bf16[128,2048]{1,0:T(8,128)(2,1)S(1)}, u32[]{:S(2)}, u32[]{:S(2)}) collective-permute-start(bf16[128,2048]{1,0:T(8,128)(2,1)S(1)} %fusion.134), channel_id=1, source_target_pairs={{0,2},{2,0},{4,6},{6,4},{1,3},{3,1},{5,7},{7,5},{8,10},{10,8},{12,... | collective-permute-start | bytes 1572872 | tf_op jit(solution)/shard_map/ppermute | solution.py:40
  48.9 18.2 %collective-permute-start.3 = (bf16[8,4,32,128]{3,2,0,1:T(8,128)(2,1)}, bf16[8,4,32,128]{3,2,0,1:T(8,128)(2,1)}, u32[]{:S(2)}, u32[]{:S(2)}) collective-permute-start(bf16[8,4,32,128]{3,2,0,1:T(8,128)(2,1)} %copy.75), channel_id=1, source_target_pairs={{0,8},{8,16},{16,24},{24,0},{1,9},{9,17},{17,25},{25,1},{2,10},{10... | collective-permute-start | bytes 786440 | tf_op jit(solution)/shard_map/ppermute | solution.py:51
  52.4 19.4 %collective-permute-start.6 = (bf16[8,4,32,128]{3,2,0,1:T(8,128)(2,1)}, bf16[8,4,32,128]{3,2,0,1:T(8,128)(2,1)}, u32[]{:S(2)}, u32[]{:S(2)}) collective-permute-start(bf16[8,4,32,128]{3,2,0,1:T(8,128)(2,1)} %copy.75), channel_id=1, source_target_pairs={{0,32},{32,0},{1,33},{33,1},{2,34},{34,2},{3,35},{35,3},{4,36},{36... | collective-permute-start | bytes 786440 | tf_op jit(solution)/shard_map/ppermute | solution.py:44
  55.1 19.7 %collective-permute-start.4 = (bf16[8,4,32,128]{3,2,0,1:T(8,128)(2,1)}, bf16[8,4,32,128]{3,2,0,1:T(8,128)(2,1)S(1)}, u32[]{:S(2)}, u32[]{:S(2)}) collective-permute-start(bf16[8,4,32,128]{3,2,0,1:T(8,128)(2,1)} %copy.75), channel_id=1, source_target_pairs={{0,16},{8,24},{16,0},{24,8},{1,17},{9,25},{17,1},{25,9},{2,18},{10... | collective-permute-start | bytes 786440 | tf_op jit(solution)/shard_map/ppermute | solution.py:51
  60.4 19.1 %collective-permute-start.5 = (bf16[8,4,32,128]{3,2,0,1:T(8,128)(2,1)}, bf16[8,4,32,128]{3,2,0,1:T(8,128)(2,1)S(1)}, u32[]{:S(2)}, u32[]{:S(2)}) collective-permute-start(bf16[8,4,32,128]{3,2,0,1:T(8,128)(2,1)} %copy.75), channel_id=1, source_target_pairs={{0,24},{8,0},{16,8},{24,16},{1,25},{9,1},{17,9},{25,17},{2,26},{10... | collective-permute-start | bytes 786440 | tf_op jit(solution)/shard_map/ppermute | solution.py:51
  63.8 26.7 %collective-permute-start.2 = (bf16[128,2048]{1,0:T(8,128)(2,1)S(1)}, bf16[128,2048]{1,0:T(8,128)(2,1)S(1)}, u32[]{:S(2)}, u32[]{:S(2)}) collective-permute-start(bf16[128,2048]{1,0:T(8,128)(2,1)S(1)} %add.237), channel_id=1, source_target_pairs={{0,6},{2,4},{4,2},{6,0},{1,7},{3,5},{5,3},{7,1},{8,14},{10,12},{12... | collective-permute-start | bytes 1572872 | tf_op jit(solution)/shard_map/ppermute | solution.py:40
  67.2 44.3 %collective-permute-start.15 = (bf16[128,2048]{1,0:T(8,128)(2,1)}, bf16[128,2048]{1,0:T(8,128)(2,1)}, u32[]{:S(2)}, u32[]{:S(2)}) collective-permute-start(bf16[128,2048]{1,0:T(8,128)(2,1)} %add.261), channel_id=1, source_target_pairs={{0,6},{2,4},{4,2},{6,0},{1,7},{3,5},{5,3},{7,1},{8,14},{10,12},{12... | collective-permute-start | bytes 1572872 | tf_op jit(solution)/shard_map/ppermute | solution.py:40
  71.9 17.4 %collective-permute-start.9 = (bf16[8,4,32,128]{3,2,0,1:T(8,128)(2,1)}, bf16[8,4,32,128]{3,2,0,1:T(8,128)(2,1)S(1)}, u32[]{:S(2)}, u32[]{:S(2)}) collective-permute-start(bf16[8,4,32,128]{3,2,0,1:T(8,128)(2,1)} %collective-permute-done.6), channel_id=1, source_target_pairs={{0,24},{8,0},{16,8},{24,16},{1,25},{9,1},{17,9},{25,17},{2,26},{10... | collective-permute-start | bytes 786440 | tf_op jit(solution)/shard_map/ppermute | solution.py:51
  74.8 14.4 %collective-permute-start.8 = (bf16[8,4,32,128]{3,2,0,1:T(8,128)(2,1)}, bf16[8,4,32,128]{3,2,0,1:T(8,128)(2,1)S(1)}, u32[]{:S(2)}, u32[]{:S(2)}) collective-permute-start(bf16[8,4,32,128]{3,2,0,1:T(8,128)(2,1)} %collective-permute-done.6), channel_id=1, source_target_pairs={{0,16},{8,24},{16,0},{24,8},{1,17},{9,25},{17,1},{25,9},{2,18},{10... | collective-permute-start | bytes 786440 | tf_op jit(solution)/shard_map/ppermute | solution.py:51
  79.5 9.7 %collective-permute-start.7 = (bf16[8,4,32,128]{3,2,0,1:T(8,128)(2,1)}, bf16[8,4,32,128]{3,2,0,1:T(8,128)(2,1)S(1)}, u32[]{:S(2)}, u32[]{:S(2)}) collective-permute-start(bf16[8,4,32,128]{3,2,0,1:T(8,128)(2,1)} %collective-permute-done.6), channel_id=1, source_target_pairs={{0,8},{8,16},{16,24},{24,0},{1,9},{9,17},{17,25},{25,1},{2,10},{10... | collective-permute-start | bytes 786440 | tf_op jit(solution)/shard_map/ppermute | solution.py:51
  90.5 51.6 %copy-start.3 = (bf16[1,8,2,4,32,128]{5,4,3,2,1,0:T(8,128)(2,1)}, bf16[1,8,2,4,32,128]{5,4,3,2,1,0:T(8,128)(2,1)S(1)}, u32[]{:S(2)}) copy-start(bf16[1,8,2,4,32,128]{5,4,3,2,1,0:T(8,128)(2,1)S(1)} %get-tuple-element.51) | copy-start | bytes 1572868
  95.2 7.2 %copy-start.16 = (bf16[2048,128]{1,0:T(8,128)(2,1)S(1)}, bf16[2048,128]{1,0:T(8,128)(2,1)}, u32[]{:S(2)}) copy-start(bf16[2048,128]{1,0:T(8,128)(2,1)} %copy.83) | copy-start | bytes 1572868
  96.5 5.9 %copy-start.26 = (f32[128]{0:T(128)}, f32[128]{0:T(128)S(1)}, u32[]{:S(2)}) copy-start(f32[128]{0:T(128)S(1)} %fusion.53) | copy-start | bytes 1540
  97.9 18.2 %all-to-all-start.1 = ((bf16[8,16,2048]{2,1,0:T(8,128)(2,1)}), bf16[8,16,2048]{2,1,0:T(8,128)(2,1)}, u32[]{:S(2)}, u32[]{:S(2)}) async-start(bf16[8,16,2048]{2,1,0:T(8,128)(2,1)} %bitcast.29), calls=%async_computation.1 | async-start | bytes 1048576 | tf_op jit(solution)/shard_map/all_to_all | solution.py:20
  103.2 27.2 %collective-permute-start.12 = (bf16[16,32,128]{2,1,0:T(8,128)(2,1)}, bf16[16,32,128]{2,1,0:T(8,128)(2,1)}, u32[]{:S(2)}, u32[]{:S(2)}) collective-permute-start(bf16[16,32,128]{2,1,0:T(8,128)(2,1)} %get-tuple-element.54), channel_id=1, source_target_pairs={{0,24},{8,0},{16,8},{24,16},{1,25},{9,1},{17,9},{25,17},{2,26},{10... | collective-permute-start | bytes 393224 | tf_op jit(solution)/shard_map/ppermute | solution.py:51
  105.9 24.5 %collective-permute-start.11 = (bf16[16,32,128]{2,1,0:T(8,128)(2,1)}, bf16[16,32,128]{2,1,0:T(8,128)(2,1)}, u32[]{:S(2)}, u32[]{:S(2)}) collective-permute-start(bf16[16,32,128]{2,1,0:T(8,128)(2,1)} %get-tuple-element.55), channel_id=1, source_target_pairs={{0,16},{8,24},{16,0},{24,8},{1,17},{9,25},{17,1},{25,9},{2,18},{10... | collective-permute-start | bytes 393224 | tf_op jit(solution)/shard_map/ppermute | solution.py:51
  108.7 21.6 %collective-permute-start.10 = (bf16[16,32,128]{2,1,0:T(8,128)(2,1)}, bf16[16,32,128]{2,1,0:T(8,128)(2,1)}, u32[]{:S(2)}, u32[]{:S(2)}) collective-permute-start(bf16[16,32,128]{2,1,0:T(8,128)(2,1)} %get-tuple-element.56), channel_id=1, source_target_pairs={{0,8},{8,16},{16,24},{24,0},{1,9},{9,17},{17,25},{25,1},{2,10},{10... | collective-permute-start | bytes 393224 | tf_op jit(solution)/shard_map/ppermute | solution.py:51
  138.0 4.5 %copy-start.11 = (bf16[1,8,2,4,32,128]{5,4,3,2,1,0:T(8,128)(2,1)S(1)}, bf16[1,8,2,4,32,128]{5,4,3,2,1,0:T(8,128)(2,1)}, u32[]{:S(2)}) copy-start(bf16[1,8,2,4,32,128]{5,4,3,2,1,0:T(8,128)(2,1)} %get-tuple-element.52) | copy-start | bytes 1572868
  139.7 33.6 %collective-permute-start.16 = (bf16[64,2048]{1,0:T(8,128)(2,1)}, bf16[64,2048]{1,0:T(8,128)(2,1)}, u32[]{:S(2)}, u32[]{:S(2)}) collective-permute-start(bf16[64,2048]{1,0:T(8,128)(2,1)} %dynamic-slice_bitcast_fusion.1), channel_id=1, source_target_pairs={{0,1},{1,0},{2,3},{3,2},{4,5},{5,4},{6,7},{7,6},{8,9},{9,8},{10,11... | collective-permute-start | bytes 786440 | tf_op jit(solution)/shard_map/ppermute | solution.py:36
  143.9 33.3 %all-to-all-start.2 = ((bf16[8,16,2048]{2,1,0:T(8,128)(2,1)}), bf16[8,16,2048]{2,1,0:T(8,128)(2,1)S(1)}, u32[]{:S(2)}, u32[]{:S(2)}) async-start(bf16[8,16,2048]{2,1,0:T(8,128)(2,1)} %bitcast.249), calls=%async_computation.2 | async-start | bytes 1048576 | tf_op jit(solution)/shard_map/all_to_all | solution.py:20
  156.4 48.9 %collective-permute-start.24 = (bf16[16,4,32,128]{3,2,1,0:T(8,128)(2,1)}, bf16[16,4,32,128]{3,2,1,0:T(8,128)(2,1)}, u32[]{:S(2)}, u32[]{:S(2)}) collective-permute-start(bf16[16,4,32,128]{3,2,1,0:T(8,128)(2,1)} %bitcast.212), channel_id=1, source_target_pairs={{0,8},{8,16},{16,24},{24,0},{1,9},{9,17},{17,25},{25,1},{2,10},{10... | collective-permute-start | bytes 1572872 | tf_op jit(solution)/shard_map/ppermute | solution.py:51
  160.0 45.3 %collective-permute-start.25 = (bf16[16,4,32,128]{3,2,1,0:T(8,128)(2,1)}, bf16[16,4,32,128]{3,2,1,0:T(8,128)(2,1)}, u32[]{:S(2)}, u32[]{:S(2)}) collective-permute-start(bf16[16,4,32,128]{3,2,1,0:T(8,128)(2,1)} %bitcast.213), channel_id=1, source_target_pairs={{0,16},{8,24},{16,0},{24,8},{1,17},{9,25},{17,1},{25,9},{2,18},{10... | collective-permute-start | bytes 1572872 | tf_op jit(solution)/shard_map/ppermute | solution.py:51
  164.0 41.3 %collective-permute-start.26 = (bf16[16,4,32,128]{3,2,1,0:T(8,128)(2,1)}, bf16[16,4,32,128]{3,2,1,0:T(8,128)(2,1)}, u32[]{:S(2)}, u32[]{:S(2)}) collective-permute-start(bf16[16,4,32,128]{3,2,1,0:T(8,128)(2,1)} %bitcast.214), channel_id=1, source_target_pairs={{0,24},{8,0},{16,8},{24,16},{1,25},{9,1},{17,9},{25,17},{2,26},{10... | collective-permute-start | bytes 1572872 | tf_op jit(solution)/shard_map/ppermute | solution.py:51
  174.4 10.0 %copy-start.18 = (bf16[64,2048]{1,0:T(8,128)(2,1)}, bf16[64,2048]{1,0:T(8,128)(2,1)S(1)}, u32[]{:S(2)}) copy-start(bf16[64,2048]{1,0:T(8,128)(2,1)S(1)} %fusion.32) | copy-start | bytes 786436
  174.4 9.9 %collective-permute-start.17 = (bf16[64,2048]{1,0:T(8,128)(2,1)S(1)}, bf16[64,2048]{1,0:T(8,128)(2,1)}, u32[]{:S(2)}, u32[]{:S(2)}) collective-permute-start(bf16[64,2048]{1,0:T(8,128)(2,1)S(1)} %fusion.32), channel_id=1, source_target_pairs={{0,2},{2,0},{4,6},{6,4},{1,3},{3,1},{5,7},{7,5},{8,10},{10,8},{12,... | collective-permute-start | bytes 786440 | tf_op jit(solution)/shard_map/ppermute | solution.py:40
  179.2 13.4 %all-to-all-start.3 = ((bf16[8,16,2048]{2,1,0:T(8,128)(2,1)}), bf16[8,16,2048]{2,1,0:T(8,128)(2,1)S(1)}, u32[]{:S(2)}, u32[]{:S(2)}) async-start(bf16[8,16,2048]{2,1,0:T(8,128)(2,1)} %broadcast_in_dim.96), calls=%async_computation.3 | async-start | bytes 1048576 | tf_op jit(solution)/shard_map/all_to_all | solution.py:20
  197.1 7.1 %copy-start.17 = (bf16[128,2048]{1,0:T(8,128)(2,1)}, bf16[128,2048]{1,0:T(8,128)(2,1)S(1)}, u32[]{:S(2)}) copy-start(bf16[128,2048]{1,0:T(8,128)(2,1)S(1)} %fusion.1) | copy-start | bytes 1572868
  197.9 11.7 %collective-permute-start.20 = (bf16[64,2048]{1,0:T(8,128)(2,1)}, bf16[64,2048]{1,0:T(8,128)(2,1)}, u32[]{:S(2)}, u32[]{:S(2)}) collective-permute-start(bf16[64,2048]{1,0:T(8,128)(2,1)} %dynamic-slice_bitcast_fusion), channel_id=1, source_target_pairs={{0,1},{1,0},{2,3},{3,2},{4,5},{5,4},{6,7},{7,6},{8,9},{9,8},{10,11... | collective-permute-start | bytes 786440 | tf_op jit(solution)/shard_map/ppermute | solution.py:36
  200.2 12.4 %collective-permute-start.18 = (bf16[64,2048]{1,0:T(8,128)(2,1)S(1)}, bf16[64,2048]{1,0:T(8,128)(2,1)}, u32[]{:S(2)}, u32[]{:S(2)}) collective-permute-start(bf16[64,2048]{1,0:T(8,128)(2,1)S(1)} %add_convert_fusion.3), channel_id=1, source_target_pairs={{0,6},{2,4},{4,2},{6,0},{1,7},{3,5},{5,3},{7,1},{8,14},{10,12},{12... | collective-permute-start | bytes 786440 | tf_op jit(solution)/shard_map/ppermute | solution.py:40
  205.3 19.7 %all-to-all-start.4 = ((bf16[4,896,128]{2,1,0:T(8,128)(2,1)}), bf16[4,896,128]{2,1,0:T(8,128)(2,1)}, u32[]{:S(2)}, u32[]{:S(2)}) async-start(bf16[4,896,128]{2,1,0:T(8,128)(2,1)} %pad_maximum_fusion.1), calls=%async_computation.4 | async-start | bytes 1835008 | tf_op jit(solution)/shard_map/all_to_all | solution.py:20
  210.7 10.3 %collective-permute-start.21 = (bf16[64,2048]{1,0:T(8,128)(2,1)S(1)}, bf16[64,2048]{1,0:T(8,128)(2,1)S(1)}, u32[]{:S(2)}, u32[]{:S(2)}) collective-permute-start(bf16[64,2048]{1,0:T(8,128)(2,1)S(1)} %fusion.31), channel_id=1, source_target_pairs={{0,2},{2,0},{4,6},{6,4},{1,3},{3,1},{5,7},{7,5},{8,10},{10,8},{12,... | collective-permute-start | bytes 786440 | tf_op jit(solution)/shard_map/ppermute | solution.py:40
  213.6 10.5 %collective-permute-start.19 = (bf16[64,2048]{1,0:T(8,128)(2,1)S(1)}, bf16[64,2048]{1,0:T(8,128)(2,1)S(1)}, u32[]{:S(2)}, u32[]{:S(2)}) collective-permute-start(bf16[64,2048]{1,0:T(8,128)(2,1)S(1)} %add_convert_fusion.2), channel_id=1, source_target_pairs={{0,1},{1,0},{2,3},{3,2},{4,5},{5,4},{6,7},{7,6},{8,9},{9,8},{10,11... | collective-permute-start | bytes 786440 | tf_op jit(solution)/shard_map/ppermute | solution.py:36
  221.1 13.8 %collective-permute-start.22 = (bf16[64,2048]{1,0:T(8,128)(2,1)S(1)}, bf16[64,2048]{1,0:T(8,128)(2,1)}, u32[]{:S(2)}, u32[]{:S(2)}) collective-permute-start(bf16[64,2048]{1,0:T(8,128)(2,1)S(1)} %add_convert_fusion.1), channel_id=1, source_target_pairs={{0,6},{2,4},{4,2},{6,0},{1,7},{3,5},{5,3},{7,1},{8,14},{10,12},{12... | collective-permute-start | bytes 786440 | tf_op jit(solution)/shard_map/ppermute | solution.py:40
  228.7 9.2 %copy-start.19 = (bf16[64,2048]{1,0:T(8,128)(2,1)S(1)}, bf16[64,2048]{1,0:T(8,128)(2,1)}, u32[]{:S(2)}) copy-start(bf16[64,2048]{1,0:T(8,128)(2,1)} %get-tuple-element.59) | copy-start | bytes 786436
  228.7 9.2 %copy-start.20 = (bf16[64,2048]{1,0:T(8,128)(2,1)S(1)}, bf16[64,2048]{1,0:T(8,128)(2,1)}, u32[]{:S(2)}) copy-start(bf16[64,2048]{1,0:T(8,128)(2,1)} %get-tuple-element.60) | copy-start | bytes 786436
  230.9 9.6 %collective-permute-start.27 = (bf16[8,4,32,128]{3,2,1,0:T(8,128)(2,1)S(1)}, bf16[8,4,32,128]{3,2,1,0:T(8,128)(2,1)S(1)}, u32[]{:S(2)}, u32[]{:S(2)}) collective-permute-start(bf16[8,4,32,128]{3,2,1,0:T(8,128)(2,1)S(1)} %fusion.38), channel_id=1, source_target_pairs={{0,32},{32,0},{1,33},{33,1},{2,34},{34,2},{3,35},{35,3},{4,36},{36... | collective-permute-start | bytes 786440 | tf_op jit(solution)/shard_map/ppermute | solution.py:44
  235.9 10.8 %collective-permute-start.23 = (bf16[64,2048]{1,0:T(8,128)(2,1)S(1)}, bf16[64,2048]{1,0:T(8,128)(2,1)S(1)}, u32[]{:S(2)}, u32[]{:S(2)}) collective-permute-start(bf16[64,2048]{1,0:T(8,128)(2,1)S(1)} %add_convert_fusion), channel_id=1, source_target_pairs={{0,1},{1,0},{2,3},{3,2},{4,5},{5,4},{6,7},{7,6},{8,9},{9,8},{10,11... | collective-permute-start | bytes 786440 | tf_op jit(solution)/shard_map/ppermute | solution.py:36
  239.5 7.5 %copy-start.25 = (f32[128]{0:T(128)S(1)}, f32[128]{0:T(128)}, u32[]{:S(2)}) copy-start(f32[128]{0:T(128)} %get-tuple-element.61) | copy-start | bytes 1540
  241.3 25.7 %all-to-all-start.5 = ((bf16[8,4,32,128]{3,2,1,0:T(8,128)(2,1)}), bf16[8,4,32,128]{3,2,1,0:T(8,128)(2,1)S(1)}, u32[]{:S(2)}, u32[]{:S(2)}) async-start(bf16[8,4,32,128]{3,2,1,0:T(8,128)(2,1)} %fusion.33), calls=%async_computation.5 | async-start | bytes 524288 | tf_op jit(solution)/shard_map/all_to_all | solution.py:20
  (16 other events, 40.8 us)

commit v4 on v2

--- a/solution.py
+++ b/solution.py
@@ -7,8 +7,9 @@
 TILE = 128
 D = 2048
 CTX = 8
-NZ = 16
-NY = 4
+NP = 8
+NN = 8
+NEAR = ("zq", "y")
 CHUNK = TILE // CTX
 SCALE = HD**-0.5
 CONTEXT = ("x", "core")
@@ -40,41 +41,26 @@
     return lax.ppermute(x, "x", [(i, i ^ bit) for i in range(CTX // 2)])
 
 
-def y_pieces(part):
-    y = lax.axis_index("y")
-    part = part.transpose(1, 0, 2, 3)[:, :, None]
-    full = jnp.zeros((part.shape[0], NZ, NY, 32, HD), BF)
-    full = lax.dynamic_update_index_in_dim(full, part, y, 2)
-    for k in range(1, NY):
-        got = lax.ppermute(part, "y", [(i, (i + k) % NY) for i in range(NY)])
-        full = lax.dynamic_update_index_in_dim(full, got, (y - k) % NY, 2)
-    return full.reshape(-1, D, HD)
-
-
-def gather_weights(w_qkv, w_out):
-    first = spread(w_qkv[:2], "z", NZ)
-    second = spread(jnp.stack([w_qkv[2], w_out.T]), "z", NZ)
-    wa, wb = y_pieces(first), y_pieces(second)
-    return wa[0], wa[1], wb[0], wb[1]
-
-
-def from_owner(tile, mine):
-    kept = jnp.where(mine, tile, jnp.zeros_like(tile))
-    kept = kept + from_core(kept)
-    kept = kept + from_pair(kept, 1)
-    return kept + from_pair(kept, 3)
-
-
-def sum_tile(terms):
+def for_near(x):
+    return x.reshape(NP, NN, 32, x.shape[-1]).transpose(1, 0, 2, 3).reshape(NN, D // NN, -1)
+
+
+def sum_begin(terms):
     core = lax.axis_index("core")
     halves = terms.astype(BF).reshape(2, TILE // 2, D)
     part = lax.dynamic_index_in_dim(halves, core, 0, keepdims=False)
     part = add(part, from_core(lax.dynamic_index_in_dim(halves, 1 - core, 0, keepdims=False)))
-    part = add(part, from_pair(part, 1))
+    return add(part, from_pair(part, 1))
+
+
+def sum_end(parts):
+    core = lax.axis_index("core")
+    part = jnp.stack(parts)
     part = add(part, from_pair(part, 3))
     other = from_core(part)
     low, high = jnp.where(core == 0, part, other), jnp.where(core == 0, other, part)
-    return jnp.concatenate([low, high], 0).astype(F32)
+    whole = jnp.concatenate([low, high], 1).astype(F32)
+    return whole[0], whole[1]
 
 
 def norm_chunk(x32, gain):
@@ -131,60 +117,82 @@
     live3 = jnp.any(depth >= 3)
     mine = jnp.any(alive & (places == me))
 
-    w = gather_weights(w_qkv, w_out)
-
     def chunk(tile):
         return lax.dynamic_index_in_dim(tile.reshape(CTX, CHUNK, D), me, 0, keepdims=False)
 
-    h1 = from_owner(hidden_in[0], mine)
-    g3 = from_owner(cotangent[0], mine)
-    dy3 = jnp.where(live3, g3, jnp.zeros_like(g3))
+    tokens = ((0,), (0,))
+    core = lax.axis_index("core")
+    none = jnp.zeros_like(hidden_in[0])
+    h_part = jnp.where(mine, hidden_in[0], none)
+    g_part = jnp.where(mine, cotangent[0], none)
+    tile = jnp.where(core == 0, h_part, g_part) + from_core(jnp.where(core == 0, g_part, h_part))
+    tile = tile + from_pair(tile, 1)
+
+    near = spread(jnp.concatenate([w_qkv, w_out.T[None]], 0), "zp", NP)
+    near, tile = lax.optimization_barrier((near, tile))
+    w = spread(near, NEAR, NN).transpose(2, 1, 0, 3, 4).reshape(4, D, HD)
+    tile = tile + from_pair(tile, 3)
+    other = from_core(tile)
+    h1, g3 = jnp.where(core == 0, tile, other), jnp.where(core == 0, other, tile)
 
     x1 = h1.astype(F32)
     inv2, rows2 = norm_chunk(x1, gain)
     mixed2, keep2 = forward(rows2, w)
-    h2 = all_rows((chunk(h1).astype(F32) + sum_chunk(mixed2)).astype(BF))
+    attn2 = keep2[-1]
+    h2c = (chunk(h1).astype(F32) + sum_chunk(mixed2)).astype(BF)
+    h2c, rows2t = lax.optimization_barrier((h2c, for_near(rows2.T)))
+    rows_in = swap(rows2t, NEAR)
+    h2 = all_rows(h2c)
+    h2, rows_in = lax.optimization_barrier((h2, rows_in))
 
     x2 = h2.astype(F32)
     inv3, normed3 = norm_chunk(x2, gain)
     rows3 = jnp.where(live3, normed3, jnp.zeros_like(normed3))
+    dy3 = jnp.where(live3, g3, jnp.zeros_like(g3))
     mixed3, keep3 = forward(rows3, w)
     dnorm3, (dq3, dk3, dv3) = backward(dy3, keep3, w)
+    dnorm3, dq3, dk3, dv3 = lax.optimization_barrier((dnorm3.astype(BF), dq3, dk3, dv3))
+    h3_part = sum_begin(mixed3)
+    early = jnp.concatenate(
+        [for_near(dot(rows3, d, tokens).astype(BF)) for d in (dq3, dk3, dv3)]
+        + [for_near(dot(dy3, keep3[-1], tokens).astype(BF))],
+        -1,
+    )
     x2c = chunk(h2).astype(F32)
     inv3c, _ = norm_chunk(x2c, gain)
     g2c = chunk(g3).astype(F32) + norm_grad(sum_chunk(dnorm3), x2c, inv3c, gain)
-    g2 = all_rows(g2c.astype(BF))
-
-    dy2 = g2
-    dnorm2, (dq2, dk2, dv2) = backward(dy2, keep2, w)
-
-    def weight_grad(left3, right3, left2, right2):
-        left = jnp.concatenate([left3, left2], 0)
-        right = jnp.concatenate([right3, right2], 0)
-        return dot(left, right, ((0,), (0,))).astype(BF)
-
-    grads = jnp.stack(
-        [
-            weight_grad(rows3, dq3, rows2, dq2),
-            weight_grad(rows3, dk3, rows2, dk2),
-            weight_grad(rows3, dv3, rows2, dv2),
-            weight_grad(dy3, keep3[-1], dy2, keep2[-1]),
-        ]
-    )
-    grads = grads.reshape(4, NZ, NY, 32, HD).transpose(2, 1, 0, 3, 4)
-    part = jnp.sum(swap(grads, "y").astype(F32), 0).astype(BF)
-    shard = jnp.sum(swap(part, "z").astype(F32), 0)
-
-    h3 = (x2 + sum_tile(mixed3)).astype(BF)
-    g1 = (g2.astype(F32) + norm_grad(sum_tile(dnorm2), x1, inv2, gain)).astype(BF)
+    g2c, early = lax.optimization_barrier((g2c.astype(BF), early))
+    early_in = swap(early, NEAR)
+    g2 = all_rows(g2c)
+    g2, h3_part = lax.optimization_barrier((g2, h3_part))
+
+    dnorm2, (dq2, dk2, dv2) = backward(g2, keep2, w)
+    dnorm2 = dnorm2.astype(BF)
+    out2 = for_near(dot(g2, attn2, tokens).astype(BF))
+    dqkv2 = jnp.broadcast_to(jnp.concatenate([dq2, dk2, dv2], 0)[None], (NN, 3 * TILE, HD))
+    late = jnp.concatenate([dqkv2, out2], 1)
+    late, early_in = lax.optimization_barrier((late, early_in))
+    late = swap(late, NEAR)
+
+    right = late[:, : 3 * TILE].reshape(NN, 3, TILE, HD)
+    part = jnp.einsum("ndr,ntrc->dtc", rows_in, right, preferred_element_type=F32)
+    last = jnp.sum(late[:, 3 * TILE :].astype(F32), 0)
+    part = jnp.concatenate([part.reshape(D // NN, 3 * HD), last], 1)
+    part = (part + jnp.sum(early_in.astype(F32), 0)).astype(BF)
+    part = part.reshape(NP, 32, 4, HD).transpose(0, 2, 1, 3)
+    shard = jnp.sum(swap(part, "zp").astype(F32), 0)
+
+    sum3, sum2 = sum_end([h3_part, sum_begin(dnorm2)])
+    h3 = (x2 + sum3).astype(BF)
+    g1 = (g2.astype(F32) + norm_grad(sum2, x1, inv2, gain)).astype(BF)
     hidden_out = jnp.where(mine, h3, hidden_in[0])
     grad_in = jnp.where(mine, g1, cotangent[0])
     return (hidden_out[None], grad_in[None], shard[:3], shard[3].T)
 
 
 def solution(mesh):
-    grid = Mesh(mesh.devices.reshape(NZ, NY, CTX // 2, 2), ("z", "y") + CONTEXT)
-    dp = ("z", "y")
+    grid = Mesh(mesh.devices.reshape(NP, 2, NN // 2, CTX // 2, 2), ("zp", "zq", "y") + CONTEXT)
+    dp = ("zp", "zq", "y")
     in_specs = (
         P(dp, CONTEXT, None),
         P(dp, CONTEXT, None),

time: 255 us -> 257 us (level)
  starting transfers between devices: 110 us -> 75.1 us
  waiting for transfers between devices: 65.3 us -> 85.2 us
  local copies, waits for them, and re-layouts: 6.39 us -> 17.6 us
  matrix products: 15.9 us -> 20.9 us
  other arithmetic: 27.2 us -> 23.3 us
  blocking collectives: 26.4 us -> 29.5 us
    ppermute x8 -> x5, waiting for transfers between devices: 16.7 us -> 47.1 us  [from_pair(): return lax.ppermute(x, 'x', [(i, i ^ bit) for i in range(CTX // 2)])]
    ppermute x6 -> x0, starting transfers between devices: 23.9 us -> none  [y_pieces(): got = lax.ppermute(part, 'y', [(i, (i + k) % NY) for i in range(NY)])]
    all_to_all x6 -> x8, waiting for transfers between devices: 48.5 us -> 31.1 us  [swap(): return lax.all_to_all(x, axis, 0, 0)]
    ppermute x8 -> x5, starting transfers between devices: 25 us -> 13.8 us  [from_pair(): return lax.ppermute(x, 'x', [(i, i ^ bit) for i in range(CTX // 2)])]
    ppermute x6 -> x5, waiting for transfers between devices: 0.02 us -> 6.97 us  [from_core(): return lax.ppermute(x, 'core', [(0, 1), (1, 0)])]
    all_to_all x6 -> x8, starting transfers between devices: 48 us -> 51.6 us  [swap(): return lax.all_to_all(x, axis, 0, 0)]
    select_n x6 -> x3, other arithmetic: 6.84 us -> 3.31 us  [the longest x1 1.91 us: on_device(): jnp.where(core == 0, g_part, h_part)]
    concatenate x0 -> x4, other arithmetic: none -> 3.52 us  [the longest x1 1.59 us: on_device(): jnp.concatenate([for_near(dot(rows3, d, tokens).astype(BF)) for d in (dq3...]
  transfers between devices with their start and end apart: 26 -> 18, of which waited for: 10 -> 13; matrix products, arithmetic and copies ran while one was open for 16% -> 12% of each run, Pallas kernels for 0% -> 0%
where the time goes in v4:
time: 257 us; the launch traced here: 253 us
  waiting for transfers between devices  85.2 us (33%)
  starting transfers between devices  75.1 us (29%)
  blocking collectives  29.5 us (11%)
  other arithmetic  23.3 us (9%)
  matrix products  20.9 us (8%)
  local copies, waits for them, and re-layouts  17.6 us (7%)
    all_to_all x8, starting transfers between devices, swap(): return lax.all_to_all(x, axis, 0, 0)  51.6 us
    ppermute x5, waiting for transfers between devices, from_pair(): return lax.ppermute(x, 'x', [(i, i ^ bit) for i in range(CTX // 2)])  47.1 us
    all_to_all x8, waiting for transfers between devices, swap(): return lax.all_to_all(x, axis, 0, 0)  31.1 us
    all_gather x2, blocking collectives, all_rows(): return lax.all_gather(chunk, CONTEXT, tiled=True)  29.5 us
    dot_general x33, matrix products, dot(): return lax.dot_general(a, b, (dims, ((), ())), preferred_element_type=F32)  19.2 us
    ppermute x5, starting transfers between devices, from_pair(): return lax.ppermute(x, 'x', [(i, i ^ bit) for i in range(CTX // 2)])  13.8 us
    ppermute x5, starting transfers between devices, from_core(): return lax.ppermute(x, 'core', [(0, 1), (1, 0)])  9.66 us
    ppermute x5, waiting for transfers between devices, from_core(): return lax.ppermute(x, 'core', [(0, 1), (1, 0)])  6.97 us
  transfers between devices with their start and end apart: 18, of which 13 were waited for; matrix products, arithmetic and copies ran while one was open for 12% of the time, Pallas kernels for 0%

profile of v4, /device:TPU:6, one launch (start us, length us, event | category | flops | bytes accessed | tf_op | source)
XLA Modules:
  0.0 253.1 jit_solution(11067987862900353491)
XLA Ops:
  0.7 1.4 fusion.47
  2.0 1.9 broadcast_select_fusion.5
  4.0 1.9 collective-permute-start
  7.4 15.1 %all-to-all-start = ((bf16[8,4,32,128]{3,2,1,0:T(8,128)(2,1)}), bf16[8,4,32,128]{3,2,1,0:T(8,128)(2,1)S(1)}, u32[]{:S(2)}, u32[]{:S(2)}) async-start(bf16[8,4,32,128]{3,2,1,0:T(8,128)(2,1)} %broadcast_in_dim.18), calls=%async_computation | async-start | bytes 524288 | tf_op jit(solution)/shard_map/all_to_all | solution.py:21
  23.2 2.7 %collective-permute-start.1 = (bf16[128,2048]{1,0:T(8,128)(2,1)S(1)}, bf16[128,2048]{1,0:T(8,128)(2,1)S(1)}, u32[]{:S(2)}, u32[]{:S(2)}) collective-permute-start(bf16[128,2048]{1,0:T(8,128)(2,1)S(1)} %select_add_fusion), channel_id=1, source_target_pairs={{0,2},{2,0},{4,6},{6,4},{1,3},{3,1},{5,7},{7,5},{8,10},{10,8},{12,... | collective-permute-start | bytes 1572872 | tf_op jit(solution)/shard_map/ppermute | solution.py:41
  26.0 13.2 %collective-permute-done.1 = bf16[128,2048]{1,0:T(8,128)(2,1)S(1)} collective-permute-done((bf16[128,2048]{1,0:T(8,128)(2,1)S(1)}, bf16[128,2048]{1,0:T(8,128)(2,1)S(1)}, u32[]{:S(2)}, u32[]{:S(2)}) %collective-permute-start.1) | collective-permute-done | bytes 524320 | tf_op jit(solution)/shard_map/ppermute | solution.py:41
  39.3 5.2 %all-to-all-done = bf16[8,4,32,128]{3,2,1,0:T(8,128)(2,1)S(1)} async-done(((bf16[8,4,32,128]{3,2,1,0:T(8,128)(2,1)}), bf16[8,4,32,128]{3,2,1,0:T(8,128)(2,1)S(1)}, u32[]{:S(2)}, u32[]{:S(2)}) %all-to-all-start) | async-done | bytes 262176 | tf_op jit(solution)/shard_map/all_to_all | solution.py:21
  44.5 1.8 broadcast_in_dim.19
  46.3 4.5 %all-to-all-start.1 = ((bf16[8,8,4,32,128]{4,3,1,2,0:T(8,128)(2,1)}), bf16[8,8,4,32,128]{4,3,1,2,0:T(8,128)(2,1)S(1)}, u32[]{:S(2)}, u32[]{:S(2)}) async-start(bf16[8,8,4,32,128]{4,3,1,2,0:T(8,128)(2,1)} %broadcast_in_dim.19), calls=%async_computation.1 | async-start | bytes 4194304 | tf_op jit(solution)/shard_map/all_to_all | solution.py:21
  50.8 2.4 collective-permute-start.2
  53.2 14.2 %collective-permute-done.2 = bf16[128,2048]{1,0:T(8,128)(2,1)S(1)} collective-permute-done((bf16[128,2048]{1,0:T(8,128)(2,1)S(1)}, bf16[128,2048]{1,0:T(8,128)(2,1)S(1)}, u32[]{:S(2)}, u32[]{:S(2)}) %collective-permute-start.2) | collective-permute-done | bytes 524320 | tf_op jit(solution)/shard_map/ppermute | solution.py:41
  67.5 1.9 collective-permute-start.3
  69.4 2.0 collective-permute-done.3
  72.3 4.6 %all-to-all-done.1 = bf16[8,8,4,32,128]{4,3,1,2,0:T(8,128)(2,1)S(1)} async-done(((bf16[8,8,4,32,128]{4,3,1,2,0:T(8,128)(2,1)}), bf16[8,8,4,32,128]{4,3,1,2,0:T(8,128)(2,1)S(1)}, u32[]{:S(2)}, u32[]{:S(2)}) %all-to-all-start.1) | async-done | bytes 2097184 | tf_op jit(solution)/shard_map/all_to_all | solution.py:21
  80.9 4.8 %all-to-all-start.2 = ((bf16[8,16,2048]{2,1,0:T(8,128)(2,1)}), bf16[8,16,2048]{2,1,0:T(8,128)(2,1)}, u32[]{:S(2)}, u32[]{:S(2)}) async-start(bf16[8,16,2048]{2,1,0:T(8,128)(2,1)} %bitcast.12), calls=%async_computation.2 | async-start | bytes 1048576 | tf_op jit(solution)/shard_map/all_to_all | solution.py:21
  86.7 2.1 copy.44
  88.8 1.9 copy.45
  90.7 3.4 %all-to-all-done.2 = bf16[8,16,2048]{2,1,0:T(8,128)(2,1)} async-done(((bf16[8,16,2048]{2,1,0:T(8,128)(2,1)}), bf16[8,16,2048]{2,1,0:T(8,128)(2,1)}, u32[]{:S(2)}, u32[]{:S(2)}) %all-to-all-start.2) | async-done | bytes 524320 | tf_op jit(solution)/shard_map/all_to_all | solution.py:21
  95.2 4.2 %all-to-all-start.3 = ((bf16[8,256,128]{2,1,0:T(8,128)(2,1)}), bf16[8,256,128]{2,1,0:T(8,128)(2,1)}, u32[]{:S(2)}, u32[]{:S(2)}) async-start(bf16[8,256,128]{2,1,0:T(8,128)(2,1)} %bitcast.200), calls=%async_computation.3 | async-start | bytes 1048576 | tf_op jit(solution)/shard_map/all_to_all | solution.py:21
  103.0 13.1 %all_gather.6 = bf16[128,2048]{1,0:T(8,128)(2,1)S(1)} all-gather(bf16[16,2048]{1,0:T(8,128)(2,1)S(1)} %fusion.40), channel_id=1, replica_groups=mesh['zp'=8,'zq'=2,'y'=4,'x'=4,'core'=2] {'x','core'}, dimensions={0}, use_global_device_ids=true | all-gather | bytes 589824 | tf_op jit(solution)/shard_map/all_gather | solution.py:72
  123.0 5.6 %all-to-all-start.4 = ((bf16[8,16,2048]{2,1,0:T(8,128)(2,1)}), bf16[8,16,2048]{2,1,0:T(8,128)(2,1)S(1)}, u32[]{:S(2)}, u32[]{:S(2)}) async-start(bf16[8,16,2048]{2,1,0:T(8,128)(2,1)} %bitcast.21), calls=%async_computation.4 | async-start | bytes 1048576 | tf_op jit(solution)/shard_map/all_to_all | solution.py:21
  133.2 1.6 pad_maximum_fusion
  134.8 2.1 all-to-all-done.4
  137.9 5.6 %all-to-all-start.5 = ((bf16[8,256,512]{2,1,0:T(8,128)(2,1)}), bf16[8,256,512]{2,1,0:T(8,128)(2,1)S(1)}, u32[]{:S(2)}, u32[]{:S(2)}) async-start(bf16[8,256,512]{2,1,0:T(8,128)(2,1)} %pad_maximum_fusion), calls=%async_computation.5 | async-start | bytes 4194304 | tf_op jit(solution)/shard_map/all_to_all | solution.py:21
  144.7 1.9 collective-permute-start.4
  146.6 1.6 collective-permute-done.4
  149.3 1.9 collective-permute-start.5
  151.2 16.4 %all_gather.7 = bf16[128,2048]{1,0:T(8,128)(2,1)S(1)} all-gather(bf16[16,2048]{1,0:T(8,128)(2,1)} %fusion.38), channel_id=1, replica_groups=mesh['zp'=8,'zq'=2,'y'=4,'x'=4,'core'=2] {'x','core'}, dimensions={0}, use_global_device_ids=true | all-gather | bytes 589824 | tf_op jit(solution)/shard_map/all_gather | solution.py:72
  169.3 1.1 pad_maximum_fusion.1
  170.7 1.3 convolution_add_fusion.1
  172.0 5.7 %all-to-all-start.6 = ((bf16[8,640,128]{2,1,0:T(8,128)(2,1)}), bf16[8,640,128]{2,1,0:T(8,128)(2,1)}, u32[]{:S(2)}, u32[]{:S(2)}) async-start(bf16[8,640,128]{2,1,0:T(8,128)(2,1)} %pad_maximum_fusion.1), calls=%async_computation.6 | async-start | bytes 2621440 | tf_op jit(solution)/shard_map/all_to_all | solution.py:21
  177.7 1.5 fusion.1
  179.3 2.0 collective-permute-start.6
  181.3 1.4 collective-permute-done.6
  182.8 2.8 %collective-permute-start.7 = (bf16[64,2048]{1,0:T(8,128)(2,1)S(1)}, bf16[64,2048]{1,0:T(8,128)(2,1)S(1)}, u32[]{:S(2)}, u32[]{:S(2)}) collective-permute-start(bf16[64,2048]{1,0:T(8,128)(2,1)S(1)} %fusion.29), channel_id=1, source_target_pairs={{0,2},{2,0},{4,6},{6,4},{1,3},{3,1},{5,7},{7,5},{8,10},{10,8},{12,... | collective-permute-start | bytes 786440 | tf_op jit(solution)/shard_map/ppermute | solution.py:41
  185.6 7.4 %collective-permute-done.7 = bf16[64,2048]{1,0:T(8,128)(2,1)S(1)} collective-permute-done((bf16[64,2048]{1,0:T(8,128)(2,1)S(1)}, bf16[64,2048]{1,0:T(8,128)(2,1)S(1)}, u32[]{:S(2)}, u32[]{:S(2)}) %collective-permute-start.7) | collective-permute-done | bytes 262176 | tf_op jit(solution)/shard_map/ppermute | solution.py:41
  193.2 4.0 %collective-permute-start.8 = (bf16[2,64,2048]{2,1,0:T(8,128)(2,1)S(1)}, bf16[2,64,2048]{2,1,0:T(8,128)(2,1)S(1)}, u32[]{:S(2)}, u32[]{:S(2)}) collective-permute-start(bf16[2,64,2048]{2,1,0:T(8,128)(2,1)S(1)} %pad_maximum_fusion.2), channel_id=1, source_target_pairs={{0,6},{2,4},{4,2},{6,0},{1,7},{3,5},{5,3},{7,1},{8,14},{10,12},{12... | collective-permute-start | bytes 1572872 | tf_op jit(solution)/shard_map/ppermute | solution.py:41
  197.2 12.3 %collective-permute-done.8 = bf16[2,64,2048]{2,1,0:T(8,128)(2,1)S(1)} collective-permute-done((bf16[2,64,2048]{2,1,0:T(8,128)(2,1)S(1)}, bf16[2,64,2048]{2,1,0:T(8,128)(2,1)S(1)}, u32[]{:S(2)}, u32[]{:S(2)}) %collective-permute-start.8) | collective-permute-done | bytes 524320 | tf_op jit(solution)/shard_map/ppermute | solution.py:41
  209.7 1.9 collective-permute-start.9
  211.6 1.9 collective-permute-done.9
  214.0 1.3 copy-done.1
  216.5 2.1 slice.62
  218.6 2.3 copy.53
  220.9 1.7 convolution_bitcast_fusion
  223.8 1.2 fusion.28
  225.7 6.2 %all-to-all-start.7 = ((bf16[8,4,32,128]{3,1,2,0:T(4,128)(2,1)}), bf16[8,4,32,128]{3,1,2,0:T(4,128)(2,1)S(1)}, u32[]{:S(2)}, u32[]{:S(2)}) async-start(bf16[8,4,32,128]{3,1,2,0:T(4,128)(2,1)} %bitcast.212), calls=%async_computation.7 | async-start | bytes 524288 | tf_op jit(solution)/shard_map/all_to_all | solution.py:21
  232.1 3.8 %fusion.24 = (bf16[1,128,2048]{2,1,0:T(8,128)(2,1)}, bf16[1,128,2048]{2,1,0:T(8,128)(2,1)}) fusion(bf16[128,2048]{1,0:T(8,128)(2,1)S(1)} %get-tuple-element.47, f32[2,128,2048]{2,1,0:T(8,128)S(1)} %maximum_convert_fusion, bf16[128,2048]{1,0:T(8,128)(2,1)S(1)} %copy-done.3, bf16[1,128,2048]{2,1,0:T(8,128)(2,1)} %param.7, f32[128]{0:T(128)S(1)} %broadcast_multiply_fusion.1, ...), kind=kLoop, calls=%fused_computation.74 | loop fusion | flops 3670016 | bytes 5776897 | tf_op jit(solution)/shard_map/broadcast_in_dim | solution.py:190
  235.9 15.8 %all-to-all-done.7 = bf16[8,4,32,128]{3,1,2,0:T(4,128)(2,1)S(1)} async-done(((bf16[8,4,32,128]{3,1,2,0:T(4,128)(2,1)}), bf16[8,4,32,128]{3,1,2,0:T(4,128)(2,1)S(1)}, u32[]{:S(2)}, u32[]{:S(2)}) %all-to-all-start.7) | async-done | bytes 262176 | tf_op jit(solution)/shard_map/all_to_all | solution.py:21
  (143 shorter events, 34.8 us)
Async XLA Ops:
  0.6 21.9 %copy-start.9 = (bf16[1,128,2048]{2,1,0:T(8,128)(2,1)S(1)}, bf16[1,128,2048]{2,1,0:T(8,128)(2,1)}, u32[]{:S(2)}) copy-start(bf16[1,128,2048]{2,1,0:T(8,128)(2,1)} %param.6) | copy-start | bytes 1572868
  0.6 21.9 %copy-start.10 = (bf16[1,128,2048]{2,1,0:T(8,128)(2,1)S(1)}, bf16[1,128,2048]{2,1,0:T(8,128)(2,1)}, u32[]{:S(2)}) copy-start(bf16[1,128,2048]{2,1,0:T(8,128)(2,1)} %param.7) | copy-start | bytes 1572868
  4.0 18.5 %collective-permute-start = (bf16[128,2048]{1,0:T(8,128)(2,1)S(1)}, bf16[128,2048]{1,0:T(8,128)(2,1)S(1)}, u32[]{:S(2)}, u32[]{:S(2)}) collective-permute-start(bf16[128,2048]{1,0:T(8,128)(2,1)S(1)} %broadcast_select_fusion.5), channel_id=1, source_target_pairs={{0,1},{1,0},{2,3},{3,2},{4,5},{5,4},{6,7},{7,6},{8,9},{9,8},{10,11... | collective-permute-start | bytes 1572872 | tf_op jit(solution)/shard_map/ppermute | solution.py:37
  7.4 37.1 %all-to-all-start = ((bf16[8,4,32,128]{3,2,1,0:T(8,128)(2,1)}), bf16[8,4,32,128]{3,2,1,0:T(8,128)(2,1)S(1)}, u32[]{:S(2)}, u32[]{:S(2)}) async-start(bf16[8,4,32,128]{3,2,1,0:T(8,128)(2,1)} %broadcast_in_dim.18), calls=%async_computation | async-start | bytes 524288 | tf_op jit(solution)/shard_map/all_to_all | solution.py:21
  23.2 15.9 %collective-permute-start.1 = (bf16[128,2048]{1,0:T(8,128)(2,1)S(1)}, bf16[128,2048]{1,0:T(8,128)(2,1)S(1)}, u32[]{:S(2)}, u32[]{:S(2)}) collective-permute-start(bf16[128,2048]{1,0:T(8,128)(2,1)S(1)} %select_add_fusion), channel_id=1, source_target_pairs={{0,2},{2,0},{4,6},{6,4},{1,3},{3,1},{5,7},{7,5},{8,10},{10,8},{12,... | collective-permute-start | bytes 1572872 | tf_op jit(solution)/shard_map/ppermute | solution.py:41
  46.3 30.6 %all-to-all-start.1 = ((bf16[8,8,4,32,128]{4,3,1,2,0:T(8,128)(2,1)}), bf16[8,8,4,32,128]{4,3,1,2,0:T(8,128)(2,1)S(1)}, u32[]{:S(2)}, u32[]{:S(2)}) async-start(bf16[8,8,4,32,128]{4,3,1,2,0:T(8,128)(2,1)} %broadcast_in_dim.19), calls=%async_computation.1 | async-start | bytes 4194304 | tf_op jit(solution)/shard_map/all_to_all | solution.py:21
  50.8 16.5 %collective-permute-start.2 = (bf16[128,2048]{1,0:T(8,128)(2,1)S(1)}, bf16[128,2048]{1,0:T(8,128)(2,1)S(1)}, u32[]{:S(2)}, u32[]{:S(2)}) collective-permute-start(bf16[128,2048]{1,0:T(8,128)(2,1)S(1)} %add.104), channel_id=1, source_target_pairs={{0,6},{2,4},{4,2},{6,0},{1,7},{3,5},{5,3},{7,1},{8,14},{10,12},{12... | collective-permute-start | bytes 1572872 | tf_op jit(solution)/shard_map/ppermute | solution.py:41
  67.5 10.0 %copy-start.5 = (bf16[128,2048]{1,0:T(8,128)(2,1)}, bf16[128,2048]{1,0:T(8,128)(2,1)S(1)}, u32[]{:S(2)}) copy-start(bf16[128,2048]{1,0:T(8,128)(2,1)S(1)} %add.105) | copy-start | bytes 1572868
  67.5 3.9 %collective-permute-start.3 = (bf16[128,2048]{1,0:T(8,128)(2,1)S(1)}, bf16[128,2048]{1,0:T(8,128)(2,1)}, u32[]{:S(2)}, u32[]{:S(2)}) collective-permute-start(bf16[128,2048]{1,0:T(8,128)(2,1)S(1)} %add.105), channel_id=1, source_target_pairs={{0,1},{1,0},{2,3},{3,2},{4,5},{5,4},{6,7},{7,6},{8,9},{9,8},{10,11... | collective-permute-start | bytes 1572872 | tf_op jit(solution)/shard_map/ppermute | solution.py:37
  77.5 0.7 copy-start.18
  78.0 43.3 %copy-start.7 = (bf16[1,8,8,32,128]{4,3,2,1,0:T(8,128)(2,1)}, bf16[1,8,8,32,128]{4,3,2,1,0:T(8,128)(2,1)S(1)}, u32[]{:S(2)}) copy-start(bf16[1,8,8,32,128]{4,3,2,1,0:T(8,128)(2,1)S(1)} %get-tuple-element.53) | copy-start | bytes 1572868
  78.0 43.6 %copy-start.13 = (bf16[1,8,8,32,128]{4,3,2,1,0:T(8,128)(2,1)}, bf16[1,8,8,32,128]{4,3,2,1,0:T(8,128)(2,1)S(1)}, u32[]{:S(2)}) copy-start(bf16[1,8,8,32,128]{4,3,2,1,0:T(8,128)(2,1)S(1)} %get-tuple-element.52) | copy-start | bytes 1572868
  78.0 43.9 %copy-start.11 = (bf16[1,8,8,32,128]{4,3,2,1,0:T(8,128)(2,1)}, bf16[1,8,8,32,128]{4,3,2,1,0:T(8,128)(2,1)S(1)}, u32[]{:S(2)}) copy-start(bf16[1,8,8,32,128]{4,3,2,1,0:T(8,128)(2,1)S(1)} %get-tuple-element.51) | copy-start | bytes 1572868
  78.6 2.3 copy-start.27
  79.3 9.5 %copy-start.19 = (bf16[128,128]{1,0:T(8,128)(2,1)}, bf16[128,128]{1,0:T(8,128)(2,1)S(1)}, u32[]{:S(2)}) copy-start(bf16[128,128]{1,0:T(8,128)(2,1)S(1)} %convolution_convert_fusion.21) | copy-start | bytes 98308
  79.5 9.3 %copy-start.21 = (f32[128]{0:T(128)}, f32[128]{0:T(128)S(1)}, u32[]{:S(2)}) copy-start(f32[128]{0:T(128)S(1)} %fusion.42) | copy-start | bytes 1540
  80.9 13.2 %all-to-all-start.2 = ((bf16[8,16,2048]{2,1,0:T(8,128)(2,1)}), bf16[8,16,2048]{2,1,0:T(8,128)(2,1)}, u32[]{:S(2)}, u32[]{:S(2)}) async-start(bf16[8,16,2048]{2,1,0:T(8,128)(2,1)} %bitcast.12), calls=%async_computation.2 | async-start | bytes 1048576 | tf_op jit(solution)/shard_map/all_to_all | solution.py:21
  86.6 12.7 %copy-start.24 = (s32[1,8]{1,0:T(1,128)S(1)}, s32[1,8]{1,0:T(1,128)}, u32[]{:S(2)}) copy-start(s32[1,8]{1,0:T(1,128)} %param.8) | copy-start | bytes 100
  86.7 13.4 %copy-start.6 = (bf16[128,2048]{1,0:T(8,128)(2,1)S(1)}, bf16[128,2048]{1,0:T(8,128)(2,1)}, u32[]{:S(2)}) copy-start(bf16[128,2048]{1,0:T(8,128)(2,1)} %copy-done.5) | copy-start | bytes 1572868
  95.2 20.9 %all-to-all-start.3 = ((bf16[8,256,128]{2,1,0:T(8,128)(2,1)}), bf16[8,256,128]{2,1,0:T(8,128)(2,1)}, u32[]{:S(2)}, u32[]{:S(2)}) async-start(bf16[8,256,128]{2,1,0:T(8,128)(2,1)} %bitcast.200), calls=%async_computation.3 | async-start | bytes 1048576 | tf_op jit(solution)/shard_map/all_to_all | solution.py:21
  101.2 0.8 copy-start.15
  103.0 16.9 %copy-start.29 = (bf16[128,128]{0,1:T(8,128)(2,1)}, bf16[128,128]{0,1:T(8,128)(2,1)S(1)}, u32[]{:S(2)}) copy-start(bf16[128,128]{0,1:T(8,128)(2,1)S(1)} %convolution_convert_fusion.16) | copy-start | bytes 98308
  116.1 21.1 %copy-start.4 = (bf16[128,2048]{1,0:T(8,128)(2,1)}, bf16[128,2048]{1,0:T(8,128)(2,1)S(1)}, u32[]{:S(2)}) copy-start(bf16[128,2048]{1,0:T(8,128)(2,1)S(1)} %all_gather.6) | copy-start | bytes 1572868
  116.3 3.1 %copy-start.25 = (f32[128]{0:T(128)}, f32[128]{0:T(128)S(1)}, u32[]{:S(2)}) copy-start(f32[128]{0:T(128)S(1)} %add_rsqrt_fusion) | copy-start | bytes 1540
  121.9 6.8 %copy-start.26 = (f32[128]{0:T(128)S(1)}, f32[128]{0:T(128)}, u32[]{:S(2)}) copy-start(f32[128]{0:T(128)} %copy-done.25) | copy-start | bytes 1540
  123.0 7.9 %copy-start.16 = (bf16[128,2048]{1,0:T(8,128)(2,1)S(1)}, bf16[128,2048]{1,0:T(8,128)(2,1)}, u32[]{:S(2)}) copy-start(bf16[128,2048]{1,0:T(8,128)(2,1)} %copy-done.15) | copy-start | bytes 1572868
  123.0 13.9 %all-to-all-start.4 = ((bf16[8,16,2048]{2,1,0:T(8,128)(2,1)}), bf16[8,16,2048]{2,1,0:T(8,128)(2,1)S(1)}, u32[]{:S(2)}, u32[]{:S(2)}) async-start(bf16[8,16,2048]{2,1,0:T(8,128)(2,1)} %bitcast.21), calls=%async_computation.4 | async-start | bytes 1048576 | tf_op jit(solution)/shard_map/all_to_all | solution.py:21
  137.9 34.1 %all-to-all-start.5 = ((bf16[8,256,512]{2,1,0:T(8,128)(2,1)}), bf16[8,256,512]{2,1,0:T(8,128)(2,1)S(1)}, u32[]{:S(2)}, u32[]{:S(2)}) async-start(bf16[8,256,512]{2,1,0:T(8,128)(2,1)} %pad_maximum_fusion), calls=%async_computation.5 | async-start | bytes 4194304 | tf_op jit(solution)/shard_map/all_to_all | solution.py:21
  143.8 0.8 copy-start.17
  144.7 3.6 %collective-permute-start.4 = (bf16[64,2048]{1,0:T(8,128)(2,1)S(1)}, bf16[64,2048]{1,0:T(8,128)(2,1)}, u32[]{:S(2)}, u32[]{:S(2)}) collective-permute-start(bf16[64,2048]{1,0:T(8,128)(2,1)S(1)} %dynamic-slice_bitcast_fusion.1), channel_id=1, source_target_pairs={{0,1},{1,0},{2,3},{3,2},{4,5},{5,4},{6,7},{7,6},{8,9},{9,8},{10,11... | collective-permute-start | bytes 786440 | tf_op jit(solution)/shard_map/ppermute | solution.py:37
  149.3 18.3 %collective-permute-start.5 = (bf16[64,2048]{1,0:T(8,128)(2,1)S(1)}, bf16[64,2048]{1,0:T(8,128)(2,1)S(1)}, u32[]{:S(2)}, u32[]{:S(2)}) collective-permute-start(bf16[64,2048]{1,0:T(8,128)(2,1)S(1)} %fusion.30), channel_id=1, source_target_pairs={{0,2},{2,0},{4,6},{6,4},{1,3},{3,1},{5,7},{7,5},{8,10},{10,8},{12,... | collective-permute-start | bytes 786440 | tf_op jit(solution)/shard_map/ppermute | solution.py:41
  167.6 1.0 copy-start.2
  167.6 0.9 copy-start.22
  167.6 0.9 copy-start.28
  167.6 1.0 copy-start.20
  168.6 1.8 copy-start.8
  169.3 1.5 copy-start.14
  170.7 7.0 %copy-start.12 = (bf16[1,8,8,32,128]{4,3,2,1,0:T(8,128)(2,1)S(1)}, bf16[1,8,8,32,128]{4,3,2,1,0:T(8,128)(2,1)}, u32[]{:S(2)}) copy-start(bf16[1,8,8,32,128]{4,3,2,1,0:T(8,128)(2,1)} %copy-done.11) | copy-start | bytes 1572868
  172.0 7.2 %copy-start = (bf16[8,256,512]{2,1,0:T(8,128)(2,1)}, bf16[8,256,512]{2,1,0:T(8,128)(2,1)S(1)}, u32[]{:S(2)}) copy-start(bf16[8,256,512]{2,1,0:T(8,128)(2,1)S(1)} %all-to-all-done.5) | copy-start | bytes 6291460
  172.0 44.4 %all-to-all-start.6 = ((bf16[8,640,128]{2,1,0:T(8,128)(2,1)}), bf16[8,640,128]{2,1,0:T(8,128)(2,1)}, u32[]{:S(2)}, u32[]{:S(2)}) async-start(bf16[8,640,128]{2,1,0:T(8,128)(2,1)} %pad_maximum_fusion.1), calls=%async_computation.6 | async-start | bytes 2621440 | tf_op jit(solution)/shard_map/all_to_all | solution.py:21
  179.3 3.4 %collective-permute-start.6 = (bf16[64,2048]{1,0:T(8,128)(2,1)S(1)}, bf16[64,2048]{1,0:T(8,128)(2,1)S(1)}, u32[]{:S(2)}, u32[]{:S(2)}) collective-permute-start(bf16[64,2048]{1,0:T(8,128)(2,1)S(1)} %dynamic-slice_bitcast_fusion), channel_id=1, source_target_pairs={{0,1},{1,0},{2,3},{3,2},{4,5},{5,4},{6,7},{7,6},{8,9},{9,8},{10,11... | collective-permute-start | bytes 786440 | tf_op jit(solution)/shard_map/ppermute | solution.py:37
  182.8 10.2 %collective-permute-start.7 = (bf16[64,2048]{1,0:T(8,128)(2,1)S(1)}, bf16[64,2048]{1,0:T(8,128)(2,1)S(1)}, u32[]{:S(2)}, u32[]{:S(2)}) collective-permute-start(bf16[64,2048]{1,0:T(8,128)(2,1)S(1)} %fusion.29), channel_id=1, source_target_pairs={{0,2},{2,0},{4,6},{6,4},{1,3},{3,1},{5,7},{7,5},{8,10},{10,8},{12,... | collective-permute-start | bytes 786440 | tf_op jit(solution)/shard_map/ppermute | solution.py:41
  193.2 16.3 %collective-permute-start.8 = (bf16[2,64,2048]{2,1,0:T(8,128)(2,1)S(1)}, bf16[2,64,2048]{2,1,0:T(8,128)(2,1)S(1)}, u32[]{:S(2)}, u32[]{:S(2)}) collective-permute-start(bf16[2,64,2048]{2,1,0:T(8,128)(2,1)S(1)} %pad_maximum_fusion.2), channel_id=1, source_target_pairs={{0,6},{2,4},{4,2},{6,0},{1,7},{3,5},{5,3},{7,1},{8,14},{10,12},{12... | collective-permute-start | bytes 1572872 | tf_op jit(solution)/shard_map/ppermute | solution.py:41
  209.7 3.8 %collective-permute-start.9 = (bf16[2,64,2048]{2,1,0:T(8,128)(2,1)S(1)}, bf16[2,64,2048]{2,1,0:T(8,128)(2,1)S(1)}, u32[]{:S(2)}, u32[]{:S(2)}) collective-permute-start(bf16[2,64,2048]{2,1,0:T(8,128)(2,1)S(1)} %add_convert_fusion), channel_id=1, source_target_pairs={{0,1},{1,0},{2,3},{3,2},{4,5},{5,4},{6,7},{7,6},{8,9},{9,8},{10,11... | collective-permute-start | bytes 1572872 | tf_op jit(solution)/shard_map/ppermute | solution.py:37
  213.8 1.6 copy-start.1
  223.8 8.3 %copy-start.3 = (bf16[128,2048]{1,0:T(8,128)(2,1)S(1)}, bf16[128,2048]{1,0:T(8,128)(2,1)}, u32[]{:S(2)}) copy-start(bf16[128,2048]{1,0:T(8,128)(2,1)} %copy-done.2) | copy-start | bytes 1572868
  223.8 8.3 %copy-start.23 = (f32[128]{0:T(128)S(1)}, f32[128]{0:T(128)}, u32[]{:S(2)}) copy-start(f32[128]{0:T(128)} %get-tuple-element.56) | copy-start | bytes 1540
  225.7 26.0 %all-to-all-start.7 = ((bf16[8,4,32,128]{3,1,2,0:T(4,128)(2,1)}), bf16[8,4,32,128]{3,1,2,0:T(4,128)(2,1)S(1)}, u32[]{:S(2)}, u32[]{:S(2)}) async-start(bf16[8,4,32,128]{3,1,2,0:T(4,128)(2,1)} %bitcast.212), calls=%async_computation.7 | async-start | bytes 524288 | tf_op jit(solution)/shard_map/all_to_all | solution.py:21

commit v5 on v4

--- a/solution.py
+++ b/solution.py
@@ -41,28 +41,6 @@
     return lax.ppermute(x, "x", [(i, i ^ bit) for i in range(CTX // 2)])
 
 
-def for_near(x):
-    return x.reshape(NP, NN, 32, x.shape[-1]).transpose(1, 0, 2, 3).reshape(NN, D // NN, -1)
-
-
-def sum_begin(terms):
-    core = lax.axis_index("core")
-    halves = terms.astype(BF).reshape(2, TILE // 2, D)
-    part = lax.dynamic_index_in_dim(halves, core, 0, keepdims=False)
-    part = add(part, from_core(lax.dynamic_index_in_dim(halves, 1 - core, 0, keepdims=False)))
-    return add(part, from_pair(part, 1))
-
-
-def sum_end(parts):
-    core = lax.axis_index("core")
-    part = jnp.stack(parts)
-    part = add(part, from_pair(part, 3))
-    other = from_core(part)
-    low, high = jnp.where(core == 0, part, other), jnp.where(core == 0, other, part)
-    whole = jnp.concatenate([low, high], 1).astype(F32)
-    return whole[0], whole[1]
-
-
 def norm_chunk(x32, gain):
     inv = lax.rsqrt(jnp.mean(x32 * x32, -1, keepdims=True) + 1e-06)
     return inv, (x32 * inv * gain).astype(BF)
@@ -100,8 +78,13 @@
     dq = dot(dscore, k, ((1,), (0,))).astype(BF)
     dk = dot(dscore, q, ((0,), (0,))).astype(BF)
     dv = dot(probb, dattn, ((0,), (0,))).astype(BF)
-    dnorm = dot(dq, w[0], ((1,), (1,))) + dot(dk, w[1], ((1,), (1,))) + dot(dv, w[2], ((1,), (1,)))
-    return dnorm, (dq, dk, dv)
+    return dq, dk, dv
+
+
+def norm_terms(dqkv, w):
+    dq, dk, dv = dqkv
+    total = dot(dq, w[0], ((1,), (1,))) + dot(dk, w[1], ((1,), (1,))) + dot(dv, w[2], ((1,), (1,)))
+    return total.astype(BF)
 
 
 def norm_grad(e, x32, inv, gain):
@@ -140,51 +123,46 @@
     mixed2, keep2 = forward(rows2, w)
     attn2 = keep2[-1]
     h2c = (chunk(h1).astype(F32) + sum_chunk(mixed2)).astype(BF)
-    h2c, rows2t = lax.optimization_barrier((h2c, for_near(rows2.T)))
-    rows_in = swap(rows2t, NEAR)
     h2 = all_rows(h2c)
-    h2, rows_in = lax.optimization_barrier((h2, rows_in))
 
     x2 = h2.astype(F32)
     inv3, normed3 = norm_chunk(x2, gain)
     rows3 = jnp.where(live3, normed3, jnp.zeros_like(normed3))
     dy3 = jnp.where(live3, g3, jnp.zeros_like(g3))
     mixed3, keep3 = forward(rows3, w)
-    dnorm3, (dq3, dk3, dv3) = backward(dy3, keep3, w)
-    dnorm3, dq3, dk3, dv3 = lax.optimization_barrier((dnorm3.astype(BF), dq3, dk3, dv3))
-    h3_part = sum_begin(mixed3)
-    early = jnp.concatenate(
-        [for_near(dot(rows3, d, tokens).astype(BF)) for d in (dq3, dk3, dv3)]
-        + [for_near(dot(dy3, keep3[-1], tokens).astype(BF))],
-        -1,
-    )
+    dqkv3 = backward(dy3, keep3, w)
+    dnorm3, dqkv3 = lax.optimization_barrier((norm_terms(dqkv3, w), dqkv3))
+
+    def products(rows, dqkv, dy, attn):
+        terms = [dot(rows, d, tokens) for d in dqkv] + [dot(dy, attn, tokens)]
+        return jnp.stack([x.reshape(NP, NN, 32, HD) for x in terms], 2)
+
+    early = products(rows3, dqkv3, dy3, keep3[-1])
     x2c = chunk(h2).astype(F32)
     inv3c, _ = norm_chunk(x2c, gain)
     g2c = chunk(g3).astype(F32) + norm_grad(sum_chunk(dnorm3), x2c, inv3c, gain)
     g2c, early = lax.optimization_barrier((g2c.astype(BF), early))
-    early_in = swap(early, NEAR)
     g2 = all_rows(g2c)
-    g2, h3_part = lax.optimization_barrier((g2, h3_part))
 
-    dnorm2, (dq2, dk2, dv2) = backward(g2, keep2, w)
-    dnorm2 = dnorm2.astype(BF)
-    out2 = for_near(dot(g2, attn2, tokens).astype(BF))
-    dqkv2 = jnp.broadcast_to(jnp.concatenate([dq2, dk2, dv2], 0)[None], (NN, 3 * TILE, HD))
-    late = jnp.concatenate([dqkv2, out2], 1)
-    late, early_in = lax.optimization_barrier((late, early_in))
-    late = swap(late, NEAR)
+    dqkv2 = backward(g2, keep2, w)
+    terms = (early + products(rows2, dqkv2, g2, attn2)).astype(BF).transpose(1, 0, 2, 3, 4)
+    terms, dqkv2 = lax.optimization_barrier((terms, dqkv2))
+    terms = swap(terms, NEAR)
+    dnorm2 = norm_terms(dqkv2, w)
 
-    right = late[:, : 3 * TILE].reshape(NN, 3, TILE, HD)
-    part = jnp.einsum("ndr,ntrc->dtc", rows_in, right, preferred_element_type=F32)
-    last = jnp.sum(late[:, 3 * TILE :].astype(F32), 0)
-    part = jnp.concatenate([part.reshape(D // NN, 3 * HD), last], 1)
-    part = (part + jnp.sum(early_in.astype(F32), 0)).astype(BF)
-    part = part.reshape(NP, 32, 4, HD).transpose(0, 2, 1, 3)
+    mixed3 = mixed3.astype(BF)
+    tile = add(jnp.where(core == 0, mixed3, dnorm2), from_core(jnp.where(core == 0, dnorm2, mixed3)))
+    tile = add(tile, from_pair(tile, 1))
+    terms, tile = lax.optimization_barrier((terms, tile))
+
+    part = jnp.sum(terms.astype(F32), 0).astype(BF)
     shard = jnp.sum(swap(part, "zp").astype(F32), 0)
 
-    sum3, sum2 = sum_end([h3_part, sum_begin(dnorm2)])
-    h3 = (x2 + sum3).astype(BF)
-    g1 = (g2.astype(F32) + norm_grad(sum2, x1, inv2, gain)).astype(BF)
+    tile = add(tile, from_pair(tile, 3))
+    other = from_core(tile)
+    sum3, sum2 = jnp.where(core == 0, tile, other), jnp.where(core == 0, other, tile)
+    h3 = (x2 + sum3.astype(F32)).astype(BF)
+    g1 = (g2.astype(F32) + norm_grad(sum2.astype(F32), x1, inv2, gain)).astype(BF)
     hidden_out = jnp.where(mine, h3, hidden_in[0])
     grad_in = jnp.where(mine, g1, cotangent[0])
     return (hidden_out[None], grad_in[None], shard[:3], shard[3].T)

time: 257 us -> 221 us (0.86); the launches traced: 253 us -> 220 us
  starting transfers between devices: 75.1 us -> 61.6 us
  local copies, waits for them, and re-layouts: 17.6 us -> 9.03 us
  waiting for transfers between devices: 85.2 us -> 81.2 us
  blocking collectives: 29.5 us -> 26.4 us
    all_to_all x8 -> x6, starting transfers between devices: 51.6 us -> 41.5 us  [swap(): return lax.all_to_all(x, axis, 0, 0)]
    ppermute x5 -> x4, waiting for transfers between devices: 6.97 us -> 2.9 us  [from_core(): return lax.ppermute(x, 'core', [(0, 1), (1, 0)])]
    all_to_all x8 -> x6, waiting for transfers between devices: 31.1 us -> 34.8 us  [swap(): return lax.all_to_all(x, axis, 0, 0)]
    ppermute x5 -> x4, waiting for transfers between devices: 47.1 us -> 43.5 us  [from_pair(): return lax.ppermute(x, 'x', [(i, i ^ bit) for i in range(CTX // 2)])]
    transpose x2 -> x1, local copies, waits for them, and re-layouts: 4.02 us -> 0.61 us  [on_device(): return (hidden_out[None], grad_in[None], shard[:3], shard[3].T)]
    all_gather x2, blocking collectives: 29.5 us -> 26.4 us  [all_rows(): return lax.all_gather(chunk, CONTEXT, tiled=True)]
    unnamed x61 -> x24, local copies, waits for them, and re-layouts: 3.85 us -> 0.84 us
    concatenate x3 -> x0, other arithmetic: 2.76 us -> none  [the longest x1 1.59 us: on_device(): jnp.concatenate([for_near(dot(rows3, d, tokens).astype(BF)) for d in (dq3...]
  transfers between devices with their start and end apart: 18 -> 14, of which waited for: 13 -> 12; matrix products, arithmetic and copies ran while one was open for 12% -> 10% of each run, Pallas kernels for 0% -> 0%
where the time goes in v5:
time: 221 us; the launch traced here: 220 us
  waiting for transfers between devices  81.2 us (37%)
  starting transfers between devices  61.6 us (28%)
  blocking collectives  26.4 us (12%)
  other arithmetic  20.8 us (9%)
  matrix products  19.4 us (9%)
  local copies, waits for them, and re-layouts  9.03 us (4%)
    ppermute x4, waiting for transfers between devices, from_pair(): return lax.ppermute(x, 'x', [(i, i ^ bit) for i in range(CTX // 2)])  43.5 us
    all_to_all x6, starting transfers between devices, swap(): return lax.all_to_all(x, axis, 0, 0)  41.5 us
    all_to_all x6, waiting for transfers between devices, swap(): return lax.all_to_all(x, axis, 0, 0)  34.8 us
    all_gather x2, blocking collectives, all_rows(): return lax.all_gather(chunk, CONTEXT, tiled=True)  26.4 us
    dot_general x36, matrix products, dot(): return lax.dot_general(a, b, (dims, ((), ())), preferred_element_type=F32)  19.4 us
    ppermute x4, starting transfers between devices, from_pair(): return lax.ppermute(x, 'x', [(i, i ^ bit) for i in range(CTX // 2)])  12 us
    ppermute x4, starting transfers between devices, from_core(): return lax.ppermute(x, 'core', [(0, 1), (1, 0)])  8.03 us
  transfers between devices with their start and end apart: 14, of which 12 were waited for; matrix products, arithmetic and copies ran while one was open for 10% of the time, Pallas kernels for 0%

profile of v5, /device:TPU:6, one launch (start us, length us, event | category | flops | bytes accessed | tf_op | source)
XLA Modules:
  0.0 219.6 jit_solution(7241335969171056493)
XLA Ops:
  0.6 1.3 fusion.45
  1.9 1.8 broadcast_select_fusion.5
  3.7 1.9 collective-permute-start
  7.2 15.1 %all-to-all-start = ((bf16[8,4,32,128]{3,2,1,0:T(8,128)(2,1)}), bf16[8,4,32,128]{3,2,1,0:T(8,128)(2,1)S(1)}, u32[]{:S(2)}, u32[]{:S(2)}) async-start(bf16[8,4,32,128]{3,2,1,0:T(8,128)(2,1)} %broadcast_in_dim.16), calls=%async_computation | async-start | bytes 524288 | tf_op jit(solution)/shard_map/all_to_all | solution.py:21
  22.2 1.8 select_add_fusion
  24.1 2.7 %collective-permute-start.1 = (bf16[128,2048]{1,0:T(8,128)(2,1)S(1)}, bf16[128,2048]{1,0:T(8,128)(2,1)S(1)}, u32[]{:S(2)}, u32[]{:S(2)}) collective-permute-start(bf16[128,2048]{1,0:T(8,128)(2,1)S(1)} %select_add_fusion), channel_id=1, source_target_pairs={{0,2},{2,0},{4,6},{6,4},{1,3},{3,1},{5,7},{7,5},{8,10},{10,8},{12,... | collective-permute-start | bytes 1572872 | tf_op jit(solution)/shard_map/ppermute | solution.py:41
  26.8 13.2 %collective-permute-done.1 = bf16[128,2048]{1,0:T(8,128)(2,1)S(1)} collective-permute-done((bf16[128,2048]{1,0:T(8,128)(2,1)S(1)}, bf16[128,2048]{1,0:T(8,128)(2,1)S(1)}, u32[]{:S(2)}, u32[]{:S(2)}) %collective-permute-start.1) | collective-permute-done | bytes 524320 | tf_op jit(solution)/shard_map/ppermute | solution.py:41
  40.2 4.1 %all-to-all-done = bf16[8,4,32,128]{3,2,1,0:T(8,128)(2,1)S(1)} async-done(((bf16[8,4,32,128]{3,2,1,0:T(8,128)(2,1)}), bf16[8,4,32,128]{3,2,1,0:T(8,128)(2,1)S(1)}, u32[]{:S(2)}, u32[]{:S(2)}) %all-to-all-start) | async-done | bytes 262176 | tf_op jit(solution)/shard_map/all_to_all | solution.py:21
  44.3 1.8 broadcast_in_dim.17
  46.1 4.5 %all-to-all-start.1 = ((bf16[8,8,4,32,128]{4,3,1,2,0:T(8,128)(2,1)}), bf16[8,8,4,32,128]{4,3,1,2,0:T(8,128)(2,1)S(1)}, u32[]{:S(2)}, u32[]{:S(2)}) async-start(bf16[8,8,4,32,128]{4,3,1,2,0:T(8,128)(2,1)} %broadcast_in_dim.17), calls=%async_computation.1 | async-start | bytes 4194304 | tf_op jit(solution)/shard_map/all_to_all | solution.py:21
  50.6 2.4 %collective-permute-start.2 = (bf16[128,2048]{1,0:T(8,128)(2,1)S(1)}, bf16[128,2048]{1,0:T(8,128)(2,1)S(1)}, u32[]{:S(2)}, u32[]{:S(2)}) collective-permute-start(bf16[128,2048]{1,0:T(8,128)(2,1)S(1)} %add.86), channel_id=1, source_target_pairs={{0,6},{2,4},{4,2},{6,0},{1,7},{3,5},{5,3},{7,1},{8,14},{10,12},{12... | collective-permute-start | bytes 1572872 | tf_op jit(solution)/shard_map/ppermute | solution.py:41
  53.0 14.2 %collective-permute-done.2 = bf16[128,2048]{1,0:T(8,128)(2,1)S(1)} collective-permute-done((bf16[128,2048]{1,0:T(8,128)(2,1)S(1)}, bf16[128,2048]{1,0:T(8,128)(2,1)S(1)}, u32[]{:S(2)}, u32[]{:S(2)}) %collective-permute-start.2) | collective-permute-done | bytes 524320 | tf_op jit(solution)/shard_map/ppermute | solution.py:41
  67.3 1.9 collective-permute-start.3
  69.9 1.4 collective-permute-done.3
  71.5 5.2 %all-to-all-done.1 = bf16[8,8,4,32,128]{4,3,1,2,0:T(8,128)(2,1)S(1)} async-done(((bf16[8,8,4,32,128]{4,3,1,2,0:T(8,128)(2,1)}), bf16[8,8,4,32,128]{4,3,1,2,0:T(8,128)(2,1)S(1)}, u32[]{:S(2)}, u32[]{:S(2)}) %all-to-all-start.1) | async-done | bytes 2097184 | tf_op jit(solution)/shard_map/all_to_all | solution.py:21
  79.4 1.1 convolution_convert_fusion.1
  80.5 4.8 %all-to-all-start.2 = ((bf16[8,16,2048]{2,1,0:T(8,128)(2,1)}), bf16[8,16,2048]{2,1,0:T(8,128)(2,1)}, u32[]{:S(2)}, u32[]{:S(2)}) async-start(bf16[8,16,2048]{2,1,0:T(8,128)(2,1)} %bitcast.145), calls=%async_computation.2 | async-start | bytes 1048576 | tf_op jit(solution)/shard_map/all_to_all | solution.py:21
  85.3 1.1 broadcast_select_fusion.3
  88.1 5.5 %all-to-all-done.2 = bf16[8,16,2048]{2,1,0:T(8,128)(2,1)} async-done(((bf16[8,16,2048]{2,1,0:T(8,128)(2,1)}), bf16[8,16,2048]{2,1,0:T(8,128)(2,1)}, u32[]{:S(2)}, u32[]{:S(2)}) %all-to-all-start.2) | async-done | bytes 524320 | tf_op jit(solution)/shard_map/all_to_all | solution.py:21
  93.6 1.1 convert_reduce_fusion.1
  94.8 13.1 %all_gather.6 = bf16[128,2048]{1,0:T(8,128)(2,1)S(1)} all-gather(bf16[16,2048]{1,0:T(8,128)(2,1)S(1)} %fusion.38), channel_id=1, replica_groups=mesh['zp'=8,'zq'=2,'y'=4,'x'=4,'core'=2] {'x','core'}, dimensions={0}, use_global_device_ids=true | all-gather | bytes 589824 | tf_op jit(solution)/shard_map/all_gather | solution.py:50
  108.1 2.1 convolution_convert_fusion.12
  110.2 1.0 convolution_convert_fusion.10
  111.2 1.0 convolution_convert_fusion.13
  114.0 1.1 fusion.1
  115.1 5.5 %all-to-all-start.3 = ((bf16[8,16,2048]{2,1,0:T(8,128)(2,1)}), bf16[8,16,2048]{2,1,0:T(8,128)(2,1)S(1)}, u32[]{:S(2)}, u32[]{:S(2)}) async-start(bf16[8,16,2048]{2,1,0:T(8,128)(2,1)} %bitcast.146), calls=%async_computation.3 | async-start | bytes 1048576 | tf_op jit(solution)/shard_map/all_to_all | solution.py:21
  120.6 1.1 fusion.65
  121.7 1.1 fusion.63
  122.7 1.1 fusion.61
  125.5 2.6 %copy.43 = f32[8,8,4,32,128]{4,3,0,2,1:T(8,128)} copy(f32[8,8,4,32,128]{4,3,1,0,2:T(8,128)S(1)} %pad_maximum_fusion) | data formatting | bytes 8388608 | tf_op jit(solution)/shard_map/stack | solution.py:138
  129.2 13.3 %all_gather.7 = bf16[128,2048]{1,0:T(8,128)(2,1)S(1)} all-gather(bf16[16,2048]{1,0:T(8,128)(2,1)S(1)} %fusion.36), channel_id=1, replica_groups=mesh['zp'=8,'zq'=2,'y'=4,'x'=4,'core'=2] {'x','core'}, dimensions={0}, use_global_device_ids=true | all-gather | bytes 589824 | tf_op jit(solution)/shard_map/all_gather | solution.py:50
  145.1 2.0 fusion.3
  147.1 4.5 %all-to-all-start.4 = ((bf16[8,8,4,32,128]{4,3,1,2,0:T(8,128)(2,1)}), bf16[8,8,4,32,128]{4,3,1,2,0:T(8,128)(2,1)}, u32[]{:S(2)}, u32[]{:S(2)}) async-start(bf16[8,8,4,32,128]{4,3,1,2,0:T(8,128)(2,1)} %fusion.3), calls=%async_computation.4 | async-start | bytes 4194304 | tf_op jit(solution)/shard_map/all_to_all | solution.py:21
  152.2 1.3 convolution_add_fusion.1
  153.9 2.3 %collective-permute-start.4 = (bf16[128,2048]{1,0:T(8,128)(2,1)S(1)}, bf16[128,2048]{1,0:T(8,128)(2,1)S(1)}, u32[]{:S(2)}, u32[]{:S(2)}) collective-permute-start(bf16[128,2048]{1,0:T(8,128)(2,1)S(1)} %get-tuple-element.54), channel_id=1, source_target_pairs={{0,1},{1,0},{2,3},{3,2},{4,5},{5,4},{6,7},{7,6},{8,9},{9,8},{10,11... | collective-permute-start | bytes 1572872 | tf_op jit(solution)/shard_map/ppermute | solution.py:37
  156.1 1.5 collective-permute-done.4
  158.0 2.9 %collective-permute-start.5 = (bf16[128,2048]{1,0:T(8,128)(2,1)S(1)}, bf16[128,2048]{1,0:T(8,128)(2,1)S(1)}, u32[]{:S(2)}, u32[]{:S(2)}) collective-permute-start(bf16[128,2048]{1,0:T(8,128)(2,1)S(1)} %add_convert_fusion.2), channel_id=1, source_target_pairs={{0,2},{2,0},{4,6},{6,4},{1,3},{3,1},{5,7},{7,5},{8,10},{10,8},{12,... | collective-permute-start | bytes 1572872 | tf_op jit(solution)/shard_map/ppermute | solution.py:41
  160.9 13.3 %collective-permute-done.5 = bf16[128,2048]{1,0:T(8,128)(2,1)S(1)} collective-permute-done((bf16[128,2048]{1,0:T(8,128)(2,1)S(1)}, bf16[128,2048]{1,0:T(8,128)(2,1)S(1)}, u32[]{:S(2)}, u32[]{:S(2)}) %collective-permute-start.5) | collective-permute-done | bytes 524320 | tf_op jit(solution)/shard_map/ppermute | solution.py:41
  174.3 4.1 %all-to-all-done.4 = bf16[8,8,4,32,128]{4,3,1,2,0:T(8,128)(2,1)} async-done(((bf16[8,8,4,32,128]{4,3,1,2,0:T(8,128)(2,1)}), bf16[8,8,4,32,128]{4,3,1,2,0:T(8,128)(2,1)}, u32[]{:S(2)}, u32[]{:S(2)}) %all-to-all-start.4) | async-done | bytes 2097184 | tf_op jit(solution)/shard_map/all_to_all | solution.py:21
  178.4 4.0 %collective-permute-start.6 = (bf16[128,2048]{1,0:T(8,128)(2,1)S(1)}, bf16[128,2048]{1,0:T(8,128)(2,1)}, u32[]{:S(2)}, u32[]{:S(2)}) collective-permute-start(bf16[128,2048]{1,0:T(8,128)(2,1)S(1)} %add_convert_fusion.1), channel_id=1, source_target_pairs={{0,6},{2,4},{4,2},{6,0},{1,7},{3,5},{5,3},{7,1},{8,14},{10,12},{12... | collective-permute-start | bytes 1572872 | tf_op jit(solution)/shard_map/ppermute | solution.py:41
  182.4 1.9 reduce_sum.131
  185.1 7.3 %all-to-all-start.5 = ((bf16[8,4,32,128]{3,2,1,0:T(8,128)(2,1)}), bf16[8,4,32,128]{3,2,1,0:T(8,128)(2,1)S(1)}, u32[]{:S(2)}, u32[]{:S(2)}) async-start(bf16[8,4,32,128]{3,2,1,0:T(8,128)(2,1)} %copy.40), calls=%async_computation.5 | async-start | bytes 524288 | tf_op jit(solution)/shard_map/all_to_all | solution.py:21
  192.3 2.9 %collective-permute-done.6 = bf16[128,2048]{1,0:T(8,128)(2,1)} collective-permute-done((bf16[128,2048]{1,0:T(8,128)(2,1)S(1)}, bf16[128,2048]{1,0:T(8,128)(2,1)}, u32[]{:S(2)}, u32[]{:S(2)}) %collective-permute-start.6) | collective-permute-done | bytes 524320 | tf_op jit(solution)/shard_map/ppermute | solution.py:41
  195.2 1.3 add_convert_fusion
  196.5 1.9 collective-permute-start.7
  198.5 15.1 %all-to-all-done.5 = bf16[8,4,32,128]{3,2,1,0:T(8,128)(2,1)S(1)} async-done(((bf16[8,4,32,128]{3,2,1,0:T(8,128)(2,1)}), bf16[8,4,32,128]{3,2,1,0:T(8,128)(2,1)S(1)}, u32[]{:S(2)}, u32[]{:S(2)}) %all-to-all-start.5) | async-done | bytes 262176 | tf_op jit(solution)/shard_map/all_to_all | solution.py:21
  214.9 1.4 fusion.23
  216.3 3.4 %fusion.25 = (bf16[1,128,2048]{2,1,0:T(8,128)(2,1)}, bf16[1,128,2048]{2,1,0:T(8,128)(2,1)}) fusion(bf16[128,2048]{1,0:T(8,128)(2,1)S(1)} %get-tuple-element.35, bf16[128,2048]{1,0:T(8,128)(2,1)S(1)} %all_gather.7, bf16[1,128,2048]{2,1,0:T(8,128)(2,1)S(1)} %copy-done.2, f32[128]{0:T(128)S(1)} %broadcast_multiply_fusion.1, f32[128]{0:T(128)S(1)} %get-tuple-element.42, ...), kind=kLoop, calls=%fused_computation.68 | loop fusion | flops 4718592 | bytes 4728322 | tf_op jit(solution)/shard_map/broadcast_in_dim | solution.py:168
  (81 shorter events, 17.6 us)
Async XLA Ops:
  3.7 18.5 %collective-permute-start = (bf16[128,2048]{1,0:T(8,128)(2,1)S(1)}, bf16[128,2048]{1,0:T(8,128)(2,1)S(1)}, u32[]{:S(2)}, u32[]{:S(2)}) collective-permute-start(bf16[128,2048]{1,0:T(8,128)(2,1)S(1)} %broadcast_select_fusion.5), channel_id=1, source_target_pairs={{0,1},{1,0},{2,3},{3,2},{4,5},{5,4},{6,7},{7,6},{8,9},{9,8},{10,11... | collective-permute-start | bytes 1572872 | tf_op jit(solution)/shard_map/ppermute | solution.py:37
  7.2 37.1 %all-to-all-start = ((bf16[8,4,32,128]{3,2,1,0:T(8,128)(2,1)}), bf16[8,4,32,128]{3,2,1,0:T(8,128)(2,1)S(1)}, u32[]{:S(2)}, u32[]{:S(2)}) async-start(bf16[8,4,32,128]{3,2,1,0:T(8,128)(2,1)} %broadcast_in_dim.16), calls=%async_computation | async-start | bytes 524288 | tf_op jit(solution)/shard_map/all_to_all | solution.py:21
  24.1 15.9 %collective-permute-start.1 = (bf16[128,2048]{1,0:T(8,128)(2,1)S(1)}, bf16[128,2048]{1,0:T(8,128)(2,1)S(1)}, u32[]{:S(2)}, u32[]{:S(2)}) collective-permute-start(bf16[128,2048]{1,0:T(8,128)(2,1)S(1)} %select_add_fusion), channel_id=1, source_target_pairs={{0,2},{2,0},{4,6},{6,4},{1,3},{3,1},{5,7},{7,5},{8,10},{10,8},{12,... | collective-permute-start | bytes 1572872 | tf_op jit(solution)/shard_map/ppermute | solution.py:41
  44.3 24.9 %copy-start.11 = (s32[1,8]{1,0:T(1,128)S(1)}, s32[1,8]{1,0:T(1,128)}, u32[]{:S(2)}) copy-start(s32[1,8]{1,0:T(1,128)} %param.8) | copy-start | bytes 100
  46.1 30.6 %all-to-all-start.1 = ((bf16[8,8,4,32,128]{4,3,1,2,0:T(8,128)(2,1)}), bf16[8,8,4,32,128]{4,3,1,2,0:T(8,128)(2,1)S(1)}, u32[]{:S(2)}, u32[]{:S(2)}) async-start(bf16[8,8,4,32,128]{4,3,1,2,0:T(8,128)(2,1)} %broadcast_in_dim.17), calls=%async_computation.1 | async-start | bytes 4194304 | tf_op jit(solution)/shard_map/all_to_all | solution.py:21
  50.6 16.5 %collective-permute-start.2 = (bf16[128,2048]{1,0:T(8,128)(2,1)S(1)}, bf16[128,2048]{1,0:T(8,128)(2,1)S(1)}, u32[]{:S(2)}, u32[]{:S(2)}) collective-permute-start(bf16[128,2048]{1,0:T(8,128)(2,1)S(1)} %add.86), channel_id=1, source_target_pairs={{0,6},{2,4},{4,2},{6,0},{1,7},{3,5},{5,3},{7,1},{8,14},{10,12},{12... | collective-permute-start | bytes 1572872 | tf_op jit(solution)/shard_map/ppermute | solution.py:41
  67.3 3.9 %collective-permute-start.3 = (bf16[128,2048]{1,0:T(8,128)(2,1)S(1)}, bf16[128,2048]{1,0:T(8,128)(2,1)}, u32[]{:S(2)}, u32[]{:S(2)}) collective-permute-start(bf16[128,2048]{1,0:T(8,128)(2,1)S(1)} %add.87), channel_id=1, source_target_pairs={{0,1},{1,0},{2,3},{3,2},{4,5},{5,4},{6,7},{7,6},{8,9},{9,8},{10,11... | collective-permute-start | bytes 1572872 | tf_op jit(solution)/shard_map/ppermute | solution.py:37
  71.5 6.3 %copy-start.10 = (f32[2048]{0:T(1024)S(1)}, f32[2048]{0:T(1024)}, u32[]{:S(2)}) copy-start(f32[2048]{0:T(1024)} %param.11) | copy-start | bytes 24580
  77.8 17.0 %copy-start.5 = (bf16[1,8,8,32,128]{4,3,2,1,0:T(8,128)(2,1)}, bf16[1,8,8,32,128]{4,3,2,1,0:T(8,128)(2,1)S(1)}, u32[]{:S(2)}) copy-start(bf16[1,8,8,32,128]{4,3,2,1,0:T(8,128)(2,1)S(1)} %get-tuple-element.38) | copy-start | bytes 1572868
  77.8 36.2 %copy-start.3 = (bf16[1,8,8,32,128]{4,3,2,1,0:T(8,128)(2,1)}, bf16[1,8,8,32,128]{4,3,2,1,0:T(8,128)(2,1)S(1)}, u32[]{:S(2)}) copy-start(bf16[1,8,8,32,128]{4,3,2,1,0:T(8,128)(2,1)S(1)} %get-tuple-element.37) | copy-start | bytes 1572868
  80.5 13.1 %all-to-all-start.2 = ((bf16[8,16,2048]{2,1,0:T(8,128)(2,1)}), bf16[8,16,2048]{2,1,0:T(8,128)(2,1)}, u32[]{:S(2)}, u32[]{:S(2)}) async-start(bf16[8,16,2048]{2,1,0:T(8,128)(2,1)} %bitcast.145), calls=%async_computation.2 | async-start | bytes 1048576 | tf_op jit(solution)/shard_map/all_to_all | solution.py:21
  86.4 0.8 copy-start.7
  108.1 5.5 %copy-start.6 = (bf16[1,8,8,32,128]{4,3,2,1,0:T(8,128)(2,1)S(1)}, bf16[1,8,8,32,128]{4,3,2,1,0:T(8,128)(2,1)}, u32[]{:S(2)}) copy-start(bf16[1,8,8,32,128]{4,3,2,1,0:T(8,128)(2,1)} %copy-done.5) | copy-start | bytes 1572868
  114.0 9.8 %copy-start.8 = (bf16[128,2048]{1,0:T(8,128)(2,1)S(1)}, bf16[128,2048]{1,0:T(8,128)(2,1)}, u32[]{:S(2)}) copy-start(bf16[128,2048]{1,0:T(8,128)(2,1)} %copy-done.7) | copy-start | bytes 1572868
  115.1 13.8 %all-to-all-start.3 = ((bf16[8,16,2048]{2,1,0:T(8,128)(2,1)}), bf16[8,16,2048]{2,1,0:T(8,128)(2,1)S(1)}, u32[]{:S(2)}, u32[]{:S(2)}) async-start(bf16[8,16,2048]{2,1,0:T(8,128)(2,1)} %bitcast.146), calls=%async_computation.3 | async-start | bytes 1048576 | tf_op jit(solution)/shard_map/all_to_all | solution.py:21
  142.5 2.6 %copy-start = (f32[8,8,4,32,128]{4,3,0,2,1:T(8,128)S(1)}, f32[8,8,4,32,128]{4,3,0,2,1:T(8,128)}, u32[]{:S(2)}) copy-start(f32[8,8,4,32,128]{4,3,0,2,1:T(8,128)} %copy.43) | copy-start | bytes 12582916
  147.1 6.5 %copy-start.4 = (bf16[1,8,8,32,128]{4,3,2,1,0:T(8,128)(2,1)S(1)}, bf16[1,8,8,32,128]{4,3,2,1,0:T(8,128)(2,1)}, u32[]{:S(2)}) copy-start(bf16[1,8,8,32,128]{4,3,2,1,0:T(8,128)(2,1)} %copy-done.3) | copy-start | bytes 1572868
  147.1 31.3 %all-to-all-start.4 = ((bf16[8,8,4,32,128]{4,3,1,2,0:T(8,128)(2,1)}), bf16[8,8,4,32,128]{4,3,1,2,0:T(8,128)(2,1)}, u32[]{:S(2)}, u32[]{:S(2)}) async-start(bf16[8,8,4,32,128]{4,3,1,2,0:T(8,128)(2,1)} %fusion.3), calls=%async_computation.4 | async-start | bytes 4194304 | tf_op jit(solution)/shard_map/all_to_all | solution.py:21
  153.9 3.8 %collective-permute-start.4 = (bf16[128,2048]{1,0:T(8,128)(2,1)S(1)}, bf16[128,2048]{1,0:T(8,128)(2,1)S(1)}, u32[]{:S(2)}, u32[]{:S(2)}) collective-permute-start(bf16[128,2048]{1,0:T(8,128)(2,1)S(1)} %get-tuple-element.54), channel_id=1, source_target_pairs={{0,1},{1,0},{2,3},{3,2},{4,5},{5,4},{6,7},{7,6},{8,9},{9,8},{10,11... | collective-permute-start | bytes 1572872 | tf_op jit(solution)/shard_map/ppermute | solution.py:37
  157.9 58.3 %copy-start.1 = (bf16[1,128,2048]{2,1,0:T(8,128)(2,1)S(1)}, bf16[1,128,2048]{2,1,0:T(8,128)(2,1)}, u32[]{:S(2)}) copy-start(bf16[1,128,2048]{2,1,0:T(8,128)(2,1)} %param.6) | copy-start | bytes 1572868
  157.9 58.3 %copy-start.2 = (bf16[1,128,2048]{2,1,0:T(8,128)(2,1)S(1)}, bf16[1,128,2048]{2,1,0:T(8,128)(2,1)}, u32[]{:S(2)}) copy-start(bf16[1,128,2048]{2,1,0:T(8,128)(2,1)} %param.7) | copy-start | bytes 1572868
  158.0 16.2 %collective-permute-start.5 = (bf16[128,2048]{1,0:T(8,128)(2,1)S(1)}, bf16[128,2048]{1,0:T(8,128)(2,1)S(1)}, u32[]{:S(2)}, u32[]{:S(2)}) collective-permute-start(bf16[128,2048]{1,0:T(8,128)(2,1)S(1)} %add_convert_fusion.2), channel_id=1, source_target_pairs={{0,2},{2,0},{4,6},{6,4},{1,3},{3,1},{5,7},{7,5},{8,10},{10,8},{12,... | collective-permute-start | bytes 1572872 | tf_op jit(solution)/shard_map/ppermute | solution.py:41
  174.3 18.0 %copy-start.9 = (bf16[128,2048]{1,0:T(8,128)(2,1)}, bf16[128,2048]{1,0:T(8,128)(2,1)S(1)}, u32[]{:S(2)}) copy-start(bf16[128,2048]{1,0:T(8,128)(2,1)S(1)} %add_convert_fusion.1) | copy-start | bytes 1572868
  178.4 16.8 %collective-permute-start.6 = (bf16[128,2048]{1,0:T(8,128)(2,1)S(1)}, bf16[128,2048]{1,0:T(8,128)(2,1)}, u32[]{:S(2)}, u32[]{:S(2)}) collective-permute-start(bf16[128,2048]{1,0:T(8,128)(2,1)S(1)} %add_convert_fusion.1), channel_id=1, source_target_pairs={{0,6},{2,4},{4,2},{6,0},{1,7},{3,5},{5,3},{7,1},{8,14},{10,12},{12... | collective-permute-start | bytes 1572872 | tf_op jit(solution)/shard_map/ppermute | solution.py:41
  185.1 28.6 %all-to-all-start.5 = ((bf16[8,4,32,128]{3,2,1,0:T(8,128)(2,1)}), bf16[8,4,32,128]{3,2,1,0:T(8,128)(2,1)S(1)}, u32[]{:S(2)}, u32[]{:S(2)}) async-start(bf16[8,4,32,128]{3,2,1,0:T(8,128)(2,1)} %copy.40), calls=%async_computation.5 | async-start | bytes 524288 | tf_op jit(solution)/shard_map/all_to_all | solution.py:21
  196.5 18.3 %collective-permute-start.7 = (bf16[128,2048]{1,0:T(8,128)(2,1)S(1)}, bf16[128,2048]{1,0:T(8,128)(2,1)}, u32[]{:S(2)}, u32[]{:S(2)}) collective-permute-start(bf16[128,2048]{1,0:T(8,128)(2,1)S(1)} %add_convert_fusion), channel_id=1, source_target_pairs={{0,1},{1,0},{2,3},{3,2},{4,5},{5,4},{6,7},{7,6},{8,9},{9,8},{10,11... | collective-permute-start | bytes 1572872 | tf_op jit(solution)/shard_map/ppermute | solution.py:37

commit v6 on v5

--- a/solution.py
+++ b/solution.py
@@ -10,7 +10,6 @@
 NP = 8
 NN = 8
 NEAR = ("zq", "y")
-CHUNK = TILE // CTX
 SCALE = HD**-0.5
 CONTEXT = ("x", "core")
 BF = jnp.bfloat16
@@ -46,12 +45,22 @@
     return inv, (x32 * inv * gain).astype(BF)
 
 
-def all_rows(chunk):
-    return lax.all_gather(chunk, CONTEXT, tiled=True)
+def core_half(x):
+    low, high = x[: TILE // 2], x[TILE // 2 :]
+    first = lax.axis_index("core") == 0
+    return jnp.where(first, low, high), jnp.where(first, high, low)
 
 
-def sum_chunk(terms):
-    return jnp.sum(swap(terms.astype(BF).reshape(CTX, CHUNK, D), CONTEXT).astype(F32), 0)
+def sum_half(terms):
+    mine, other = core_half(terms)
+    pair = add(mine, from_core(other))
+    return jnp.sum(spread(pair, "x", CTX // 2).astype(F32), 0)
+
+
+def both_halves(half):
+    other = from_core(half)
+    first = lax.axis_index("core") == 0
+    return jnp.concatenate([jnp.where(first, half, other), jnp.where(first, other, half)], 0)
 
 
 def forward(rows, w):
@@ -100,18 +109,17 @@
     live3 = jnp.any(depth >= 3)
     mine = jnp.any(alive & (places == me))
 
-    def chunk(tile):
-        return lax.dynamic_index_in_dim(tile.reshape(CTX, CHUNK, D), me, 0, keepdims=False)
-
     tokens = ((0,), (0,))
     core = lax.axis_index("core")
     none = jnp.zeros_like(hidden_in[0])
+    shard = jnp.concatenate([w_qkv, w_out.T[None]], 0)
+    shard, mine = lax.optimization_barrier((jnp.broadcast_to(shard[None], (NP,) + shard.shape), mine))
+    near = swap(shard, "zp")
     h_part = jnp.where(mine, hidden_in[0], none)
     g_part = jnp.where(mine, cotangent[0], none)
     tile = jnp.where(core == 0, h_part, g_part) + from_core(jnp.where(core == 0, g_part, h_part))
     tile = tile + from_pair(tile, 1)
 
-    near = spread(jnp.concatenate([w_qkv, w_out.T[None]], 0), "zp", NP)
     near, tile = lax.optimization_barrier((near, tile))
     w = spread(near, NEAR, NN).transpose(2, 1, 0, 3, 4).reshape(4, D, HD)
     tile = tile + from_pair(tile, 3)
@@ -122,8 +130,7 @@
     inv2, rows2 = norm_chunk(x1, gain)
     mixed2, keep2 = forward(rows2, w)
     attn2 = keep2[-1]
-    h2c = (chunk(h1).astype(F32) + sum_chunk(mixed2)).astype(BF)
-    h2 = all_rows(h2c)
+    h2 = both_halves((core_half(h1)[0].astype(F32) + sum_half(mixed2.astype(BF))).astype(BF))
 
     x2 = h2.astype(F32)
     inv3, normed3 = norm_chunk(x2, gain)
@@ -138,11 +145,11 @@
         return jnp.stack([x.reshape(NP, NN, 32, HD) for x in terms], 2)
 
     early = products(rows3, dqkv3, dy3, keep3[-1])
-    x2c = chunk(h2).astype(F32)
+    x2c = core_half(h2)[0].astype(F32)
     inv3c, _ = norm_chunk(x2c, gain)
-    g2c = chunk(g3).astype(F32) + norm_grad(sum_chunk(dnorm3), x2c, inv3c, gain)
+    g2c = core_half(g3)[0].astype(F32) + norm_grad(sum_half(dnorm3), x2c, inv3c, gain)
     g2c, early = lax.optimization_barrier((g2c.astype(BF), early))
-    g2 = all_rows(g2c)
+    g2 = both_halves(g2c)
 
     dqkv2 = backward(g2, keep2, w)
     terms = (early + products(rows2, dqkv2, g2, attn2)).astype(BF).transpose(1, 0, 2, 3, 4)
@@ -154,9 +161,8 @@
     tile = add(jnp.where(core == 0, mixed3, dnorm2), from_core(jnp.where(core == 0, dnorm2, mixed3)))
     tile = add(tile, from_pair(tile, 1))
     terms, tile = lax.optimization_barrier((terms, tile))
-
     part = jnp.sum(terms.astype(F32), 0).astype(BF)
-    shard = jnp.sum(swap(part, "zp").astype(F32), 0)
+    shards = swap(part, "zp")
 
     tile = add(tile, from_pair(tile, 3))
     other = from_core(tile)
@@ -165,6 +171,7 @@
     g1 = (g2.astype(F32) + norm_grad(sum2.astype(F32), x1, inv2, gain)).astype(BF)
     hidden_out = jnp.where(mine, h3, hidden_in[0])
     grad_in = jnp.where(mine, g1, cotangent[0])
+    shard = jnp.sum(shards.astype(F32), 0)
     return (hidden_out[None], grad_in[None], shard[:3], shard[3].T)
 
 

time: 221 us -> 221 us (level)
  blocking collectives: 26.4 us -> 0 us
  waiting for transfers between devices: 81.2 us -> 95.1 us
  starting transfers between devices: 61.6 us -> 67.8 us
  local copies, waits for them, and re-layouts: 9.03 us -> 12.1 us
    all_gather x2 -> x0, blocking collectives: 26.4 us -> none  [all_rows(): return lax.all_gather(chunk, CONTEXT, tiled=True)]
    all_to_all x6, waiting for transfers between devices: 34.8 us -> 44.5 us  [swap(): return lax.all_to_all(x, axis, 0, 0)]
    ppermute x4 -> x8, starting transfers between devices: 8.03 us -> 15.8 us  [from_core(): return lax.ppermute(x, 'core', [(0, 1), (1, 0)])]
    ppermute x4 -> x8, waiting for transfers between devices: 2.9 us -> 6.48 us  [from_core(): return lax.ppermute(x, 'core', [(0, 1), (1, 0)])]
  transfers between devices with their start and end apart: 14 -> 18, of which waited for: 12 -> 14; matrix products, arithmetic and copies ran while one was open for 10% -> 12% of each run, Pallas kernels for 0% -> 0%
where the time goes in v6:
time: 221 us; the launch traced here: 219 us
  waiting for transfers between devices  95.1 us (43%)
  starting transfers between devices  67.8 us (31%)
  other arithmetic  22.4 us (10%)
  matrix products  20.4 us (9%)
  local copies, waits for them, and re-layouts  12.1 us (5%)
    all_to_all x6, waiting for transfers between devices, swap(): return lax.all_to_all(x, axis, 0, 0)  44.5 us
    ppermute x4, waiting for transfers between devices, from_pair(): return lax.ppermute(x, 'x', [(i, i ^ bit) for i in range(CTX // 2)])  44.2 us
    all_to_all x6, starting transfers between devices, swap(): return lax.all_to_all(x, axis, 0, 0)  40.9 us
    dot_general x36, matrix products, dot(): return lax.dot_general(a, b, (dims, ((), ())), preferred_element_type=F32)  20.4 us
    ppermute x8, starting transfers between devices, from_core(): return lax.ppermute(x, 'core', [(0, 1), (1, 0)])  15.8 us
    ppermute x4, starting transfers between devices, from_pair(): return lax.ppermute(x, 'x', [(i, i ^ bit) for i in range(CTX // 2)])  11.1 us
    ppermute x8, waiting for transfers between devices, from_core(): return lax.ppermute(x, 'core', [(0, 1), (1, 0)])  6.48 us
  transfers between devices with their start and end apart: 18, of which 14 were waited for; matrix products, arithmetic and copies ran while one was open for 12% of the time, Pallas kernels for 0%

profile of v6, /device:TPU:6, one launch (start us, length us, event | category | flops | bytes accessed | tf_op | source)
XLA Modules:
  0.0 219.4 jit_solution(17211720954935785276)
XLA Ops:
  0.6 1.3 fusion.45
  3.4 1.8 broadcast_select_fusion.5
  5.2 1.9 collective-permute-start
  7.1 15.1 %all-to-all-start = ((bf16[8,4,32,128]{3,2,1,0:T(8,128)(2,1)}), bf16[8,4,32,128]{3,2,1,0:T(8,128)(2,1)S(1)}, u32[]{:S(2)}, u32[]{:S(2)}) async-start(bf16[8,4,32,128]{3,2,1,0:T(8,128)(2,1)} %broadcast_in_dim.20), calls=%async_computation | async-start | bytes 524288 | tf_op jit(solution)/shard_map/all_to_all | solution.py:20
  22.3 1.8 select_add_fusion
  24.1 2.7 %collective-permute-start.1 = (bf16[128,2048]{1,0:T(8,128)(2,1)S(1)}, bf16[128,2048]{1,0:T(8,128)(2,1)S(1)}, u32[]{:S(2)}, u32[]{:S(2)}) collective-permute-start(bf16[128,2048]{1,0:T(8,128)(2,1)S(1)} %select_add_fusion), channel_id=1, source_target_pairs={{0,2},{2,0},{4,6},{6,4},{1,3},{3,1},{5,7},{7,5},{8,10},{10,8},{12,... | collective-permute-start | bytes 1572872 | tf_op jit(solution)/shard_map/ppermute | solution.py:40
  26.8 13.2 %collective-permute-done.1 = bf16[128,2048]{1,0:T(8,128)(2,1)S(1)} collective-permute-done((bf16[128,2048]{1,0:T(8,128)(2,1)S(1)}, bf16[128,2048]{1,0:T(8,128)(2,1)S(1)}, u32[]{:S(2)}, u32[]{:S(2)}) %collective-permute-start.1) | collective-permute-done | bytes 524320 | tf_op jit(solution)/shard_map/ppermute | solution.py:40
  40.2 4.1 %all-to-all-done = bf16[8,4,32,128]{3,2,1,0:T(8,128)(2,1)S(1)} async-done(((bf16[8,4,32,128]{3,2,1,0:T(8,128)(2,1)}), bf16[8,4,32,128]{3,2,1,0:T(8,128)(2,1)S(1)}, u32[]{:S(2)}, u32[]{:S(2)}) %all-to-all-start) | async-done | bytes 262176 | tf_op jit(solution)/shard_map/all_to_all | solution.py:20
  44.3 1.8 broadcast_in_dim.21
  46.1 4.5 %all-to-all-start.1 = ((bf16[8,8,4,32,128]{4,3,1,2,0:T(8,128)(2,1)}), bf16[8,8,4,32,128]{4,3,1,2,0:T(8,128)(2,1)S(1)}, u32[]{:S(2)}, u32[]{:S(2)}) async-start(bf16[8,8,4,32,128]{4,3,1,2,0:T(8,128)(2,1)} %broadcast_in_dim.21), calls=%async_computation.1 | async-start | bytes 4194304 | tf_op jit(solution)/shard_map/all_to_all | solution.py:20
  50.6 2.4 %collective-permute-start.2 = (bf16[128,2048]{1,0:T(8,128)(2,1)S(1)}, bf16[128,2048]{1,0:T(8,128)(2,1)S(1)}, u32[]{:S(2)}, u32[]{:S(2)}) collective-permute-start(bf16[128,2048]{1,0:T(8,128)(2,1)S(1)} %add.89), channel_id=1, source_target_pairs={{0,6},{2,4},{4,2},{6,0},{1,7},{3,5},{5,3},{7,1},{8,14},{10,12},{12... | collective-permute-start | bytes 1572872 | tf_op jit(solution)/shard_map/ppermute | solution.py:40
  53.0 14.2 %collective-permute-done.2 = bf16[128,2048]{1,0:T(8,128)(2,1)S(1)} collective-permute-done((bf16[128,2048]{1,0:T(8,128)(2,1)S(1)}, bf16[128,2048]{1,0:T(8,128)(2,1)S(1)}, u32[]{:S(2)}, u32[]{:S(2)}) %collective-permute-start.2) | collective-permute-done | bytes 524320 | tf_op jit(solution)/shard_map/ppermute | solution.py:40
  67.3 1.9 collective-permute-start.3
  69.2 1.9 collective-permute-done.3
  72.4 4.2 %all-to-all-done.1 = bf16[8,8,4,32,128]{4,3,1,2,0:T(8,128)(2,1)S(1)} async-done(((bf16[8,8,4,32,128]{4,3,1,2,0:T(8,128)(2,1)}), bf16[8,8,4,32,128]{4,3,1,2,0:T(8,128)(2,1)S(1)}, u32[]{:S(2)}, u32[]{:S(2)}) %all-to-all-start.1) | async-done | bytes 2097184 | tf_op jit(solution)/shard_map/all_to_all | solution.py:20
  79.8 1.9 collective-permute-start.4
  81.7 1.5 collective-permute-done.4
  84.4 4.8 %all-to-all-start.2 = ((bf16[4,64,2048]{2,1,0:T(8,128)(2,1)}), bf16[4,64,2048]{2,1,0:T(8,128)(2,1)}, u32[]{:S(2)}, u32[]{:S(2)}) async-start(bf16[4,64,2048]{2,1,0:T(8,128)(2,1)} %broadcast_in_dim.23), calls=%async_computation.2 | async-start | bytes 2097152 | tf_op jit(solution)/shard_map/all_to_all | solution.py:20
  89.8 13.0 %all-to-all-done.2 = bf16[4,64,2048]{2,1,0:T(8,128)(2,1)} async-done(((bf16[4,64,2048]{2,1,0:T(8,128)(2,1)}), bf16[4,64,2048]{2,1,0:T(8,128)(2,1)}, u32[]{:S(2)}, u32[]{:S(2)}) %all-to-all-start.2) | async-done | bytes 1048608 | tf_op jit(solution)/shard_map/all_to_all | solution.py:20
  102.8 1.5 convert_reduce_fusion.1
  104.4 2.1 collective-permute-start.5
  114.0 1.9 collective-permute-start.6
  115.9 2.1 fusion.65
  119.2 5.6 %all-to-all-start.3 = ((bf16[4,64,2048]{2,1,0:T(8,128)(2,1)}), bf16[4,64,2048]{2,1,0:T(8,128)(2,1)S(1)}, u32[]{:S(2)}, u32[]{:S(2)}) async-start(bf16[4,64,2048]{2,1,0:T(8,128)(2,1)} %broadcast_in_dim.24), calls=%async_computation.3 | async-start | bytes 2097152 | tf_op jit(solution)/shard_map/all_to_all | solution.py:20
  124.7 1.9 fusion.63
  126.7 1.8 fusion.67
  130.2 2.6 %copy.57 = f32[8,8,4,32,128]{4,3,0,2,1:T(8,128)} copy(f32[8,8,4,32,128]{4,3,1,0,2:T(8,128)S(1)} %pad_maximum_fusion) | data formatting | bytes 8388608 | tf_op jit(solution)/shard_map/stack | solution.py:145
  132.8 5.9 %all-to-all-done.3 = bf16[4,64,2048]{2,1,0:T(8,128)(2,1)S(1)} async-done(((bf16[4,64,2048]{2,1,0:T(8,128)(2,1)}), bf16[4,64,2048]{2,1,0:T(8,128)(2,1)S(1)}, u32[]{:S(2)}, u32[]{:S(2)}) %all-to-all-start.3) | async-done | bytes 1048608 | tf_op jit(solution)/shard_map/all_to_all | solution.py:20
  139.4 2.1 collective-permute-start.7
  141.5 1.3 collective-permute-done.7
  145.5 2.0 fusion.3
  147.6 3.8 %all-to-all-start.4 = ((bf16[8,8,4,32,128]{4,3,1,2,0:T(8,128)(2,1)}), bf16[8,8,4,32,128]{4,3,1,2,0:T(8,128)(2,1)S(1)}, u32[]{:S(2)}, u32[]{:S(2)}) async-start(bf16[8,8,4,32,128]{4,3,1,2,0:T(8,128)(2,1)} %fusion.3), calls=%async_computation.4 | async-start | bytes 4194304 | tf_op jit(solution)/shard_map/all_to_all | solution.py:20
  151.4 1.4 convolution_convert_fusion
  153.1 1.3 convolution_add_fusion.1
  154.8 2.0 collective-permute-start.8
  156.8 1.8 collective-permute-done.8
  158.9 2.1 collective-permute-start.9
  160.9 13.9 %collective-permute-done.9 = bf16[128,2048]{1,0:T(8,128)(2,1)S(1)} collective-permute-done((bf16[128,2048]{1,0:T(8,128)(2,1)S(1)}, bf16[128,2048]{1,0:T(8,128)(2,1)S(1)}, u32[]{:S(2)}, u32[]{:S(2)}) %collective-permute-start.9) | collective-permute-done | bytes 524320 | tf_op jit(solution)/shard_map/ppermute | solution.py:40
  175.8 2.1 all-to-all-done.4
  177.9 4.0 %collective-permute-start.10 = (bf16[128,2048]{1,0:T(8,128)(2,1)}, bf16[128,2048]{1,0:T(8,128)(2,1)}, u32[]{:S(2)}, u32[]{:S(2)}) collective-permute-start(bf16[128,2048]{1,0:T(8,128)(2,1)} %add_convert_fusion.1), channel_id=1, source_target_pairs={{0,6},{2,4},{4,2},{6,0},{1,7},{3,5},{5,3},{7,1},{8,14},{10,12},{12... | collective-permute-start | bytes 1572872 | tf_op jit(solution)/shard_map/ppermute | solution.py:40
  182.9 1.8 copy.54
  184.7 7.3 %all-to-all-start.5 = ((bf16[8,4,32,128]{3,2,1,0:T(8,128)(2,1)}), bf16[8,4,32,128]{3,2,1,0:T(8,128)(2,1)S(1)}, u32[]{:S(2)}, u32[]{:S(2)}) async-start(bf16[8,4,32,128]{3,2,1,0:T(8,128)(2,1)} %copy.54), calls=%async_computation.5 | async-start | bytes 524288 | tf_op jit(solution)/shard_map/all_to_all | solution.py:20
  191.9 2.9 %collective-permute-done.10 = bf16[128,2048]{1,0:T(8,128)(2,1)} collective-permute-done((bf16[128,2048]{1,0:T(8,128)(2,1)}, bf16[128,2048]{1,0:T(8,128)(2,1)}, u32[]{:S(2)}, u32[]{:S(2)}) %collective-permute-start.10) | collective-permute-done | bytes 524320 | tf_op jit(solution)/shard_map/ppermute | solution.py:40
  194.8 1.3 add_convert_fusion
  196.2 1.9 collective-permute-start.11
  198.1 15.2 %all-to-all-done.5 = bf16[8,4,32,128]{3,2,1,0:T(8,128)(2,1)S(1)} async-done(((bf16[8,4,32,128]{3,2,1,0:T(8,128)(2,1)}), bf16[8,4,32,128]{3,2,1,0:T(8,128)(2,1)S(1)}, u32[]{:S(2)}, u32[]{:S(2)}) %all-to-all-start.5) | async-done | bytes 262176 | tf_op jit(solution)/shard_map/all_to_all | solution.py:20
  214.6 1.4 fusion.23
  216.0 3.4 %fusion.31 = (bf16[1,128,2048]{2,1,0:T(8,128)(2,1)}, bf16[1,128,2048]{2,1,0:T(8,128)(2,1)}) fusion(bf16[128,2048]{1,0:T(8,128)(2,1)S(1)} %get-tuple-element.40, bf16[1,128,2048]{2,1,0:T(8,128)(2,1)S(1)} %copy-done.2, f32[128]{0:T(128)S(1)} %broadcast_multiply_fusion.1, f32[128]{0:T(128)S(1)} %copy-done.28, f32[2048]{0:T(1024)S(1)} %copy-done.19, ...), kind=kLoop, calls=%fused_computation.77 | loop fusion | flops 6291456 | bytes 4728322 | tf_op jit(solution)/shard_map/broadcast_in_dim | solution.py:175
  (141 shorter events, 25.7 us)
Async XLA Ops:
  5.2 17.0 %collective-permute-start = (bf16[128,2048]{1,0:T(8,128)(2,1)S(1)}, bf16[128,2048]{1,0:T(8,128)(2,1)S(1)}, u32[]{:S(2)}, u32[]{:S(2)}) collective-permute-start(bf16[128,2048]{1,0:T(8,128)(2,1)S(1)} %broadcast_select_fusion.5), channel_id=1, source_target_pairs={{0,1},{1,0},{2,3},{3,2},{4,5},{5,4},{6,7},{7,6},{8,9},{9,8},{10,11... | collective-permute-start | bytes 1572872 | tf_op jit(solution)/shard_map/ppermute | solution.py:36
  7.1 37.1 %all-to-all-start = ((bf16[8,4,32,128]{3,2,1,0:T(8,128)(2,1)}), bf16[8,4,32,128]{3,2,1,0:T(8,128)(2,1)S(1)}, u32[]{:S(2)}, u32[]{:S(2)}) async-start(bf16[8,4,32,128]{3,2,1,0:T(8,128)(2,1)} %broadcast_in_dim.20), calls=%async_computation | async-start | bytes 524288 | tf_op jit(solution)/shard_map/all_to_all | solution.py:20
  24.1 15.9 %collective-permute-start.1 = (bf16[128,2048]{1,0:T(8,128)(2,1)S(1)}, bf16[128,2048]{1,0:T(8,128)(2,1)S(1)}, u32[]{:S(2)}, u32[]{:S(2)}) collective-permute-start(bf16[128,2048]{1,0:T(8,128)(2,1)S(1)} %select_add_fusion), channel_id=1, source_target_pairs={{0,2},{2,0},{4,6},{6,4},{1,3},{3,1},{5,7},{7,5},{8,10},{10,8},{12,... | collective-permute-start | bytes 1572872 | tf_op jit(solution)/shard_map/ppermute | solution.py:40
  46.1 30.6 %all-to-all-start.1 = ((bf16[8,8,4,32,128]{4,3,1,2,0:T(8,128)(2,1)}), bf16[8,8,4,32,128]{4,3,1,2,0:T(8,128)(2,1)S(1)}, u32[]{:S(2)}, u32[]{:S(2)}) async-start(bf16[8,8,4,32,128]{4,3,1,2,0:T(8,128)(2,1)} %broadcast_in_dim.21), calls=%async_computation.1 | async-start | bytes 4194304 | tf_op jit(solution)/shard_map/all_to_all | solution.py:20
  50.6 16.5 %collective-permute-start.2 = (bf16[128,2048]{1,0:T(8,128)(2,1)S(1)}, bf16[128,2048]{1,0:T(8,128)(2,1)S(1)}, u32[]{:S(2)}, u32[]{:S(2)}) collective-permute-start(bf16[128,2048]{1,0:T(8,128)(2,1)S(1)} %add.89), channel_id=1, source_target_pairs={{0,6},{2,4},{4,2},{6,0},{1,7},{3,5},{5,3},{7,1},{8,14},{10,12},{12... | collective-permute-start | bytes 1572872 | tf_op jit(solution)/shard_map/ppermute | solution.py:40
  67.3 3.8 %collective-permute-start.3 = (bf16[128,2048]{1,0:T(8,128)(2,1)S(1)}, bf16[128,2048]{1,0:T(8,128)(2,1)S(1)}, u32[]{:S(2)}, u32[]{:S(2)}) collective-permute-start(bf16[128,2048]{1,0:T(8,128)(2,1)S(1)} %add.90), channel_id=1, source_target_pairs={{0,1},{1,0},{2,3},{3,2},{4,5},{5,4},{6,7},{7,6},{8,9},{9,8},{10,11... | collective-permute-start | bytes 1572872 | tf_op jit(solution)/shard_map/ppermute | solution.py:36
  72.4 5.3 %copy-start.19 = (f32[2048]{0:T(1024)S(1)}, f32[2048]{0:T(1024)}, u32[]{:S(2)}) copy-start(f32[2048]{0:T(1024)} %param.11) | copy-start | bytes 24580
  77.7 1.6 copy-start.6
  77.7 5.6 %copy-start.9 = (bf16[1,8,8,32,128]{4,3,2,1,0:T(8,128)(2,1)}, bf16[1,8,8,32,128]{4,3,2,1,0:T(8,128)(2,1)S(1)}, u32[]{:S(2)}) copy-start(bf16[1,8,8,32,128]{4,3,2,1,0:T(8,128)(2,1)S(1)} %get-tuple-element.43) | copy-start | bytes 1572868
  77.7 35.2 %copy-start.3 = (bf16[1,8,8,32,128]{4,3,2,1,0:T(8,128)(2,1)}, bf16[1,8,8,32,128]{4,3,2,1,0:T(8,128)(2,1)S(1)}, u32[]{:S(2)}) copy-start(bf16[1,8,8,32,128]{4,3,2,1,0:T(8,128)(2,1)S(1)} %get-tuple-element.44) | copy-start | bytes 1572868
  77.7 65.2 %copy-start.5 = (bf16[1,8,8,32,128]{4,3,2,1,0:T(8,128)(2,1)}, bf16[1,8,8,32,128]{4,3,2,1,0:T(8,128)(2,1)S(1)}, u32[]{:S(2)}) copy-start(bf16[1,8,8,32,128]{4,3,2,1,0:T(8,128)(2,1)S(1)} %get-tuple-element.41) | copy-start | bytes 1572868
  78.1 1.6 copy-start.33
  78.5 10.6 %copy-start.31 = (s32[1,8]{1,0:T(1,128)S(1)}, s32[1,8]{1,0:T(1,128)}, u32[]{:S(2)}) copy-start(s32[1,8]{1,0:T(1,128)} %param.8) | copy-start | bytes 100
  79.1 25.2 %copy-start.29 = (f32[128]{0:T(128)}, f32[128]{0:T(128)S(1)}, u32[]{:S(2)}) copy-start(f32[128]{0:T(128)S(1)} %fusion.40) | copy-start | bytes 1540
  79.8 3.4 %collective-permute-start.4 = (bf16[64,2048]{1,0:T(8,128)(2,1)S(1)}, bf16[64,2048]{1,0:T(8,128)(2,1)S(1)}, u32[]{:S(2)}, u32[]{:S(2)}) collective-permute-start(bf16[64,2048]{1,0:T(8,128)(2,1)S(1)} %broadcast_select_fusion.14), channel_id=1, source_target_pairs={{0,1},{1,0},{2,3},{3,2},{4,5},{5,4},{6,7},{7,6},{8,9},{9,8},{10,11... | collective-permute-start | bytes 786440 | tf_op jit(solution)/shard_map/ppermute | solution.py:36
  84.4 18.4 %all-to-all-start.2 = ((bf16[4,64,2048]{2,1,0:T(8,128)(2,1)}), bf16[4,64,2048]{2,1,0:T(8,128)(2,1)}, u32[]{:S(2)}, u32[]{:S(2)}) async-start(bf16[4,64,2048]{2,1,0:T(8,128)(2,1)} %broadcast_in_dim.23), calls=%async_computation.2 | async-start | bytes 2097152 | tf_op jit(solution)/shard_map/all_to_all | solution.py:20
  102.8 6.0 %copy-start.10 = (bf16[1,8,8,32,128]{4,3,2,1,0:T(8,128)(2,1)S(1)}, bf16[1,8,8,32,128]{4,3,2,1,0:T(8,128)(2,1)}, u32[]{:S(2)}) copy-start(bf16[1,8,8,32,128]{4,3,2,1,0:T(8,128)(2,1)} %copy-done.9) | copy-start | bytes 1572868
  104.3 5.6 %copy-start.7 = (bf16[1,8,8,32,128]{4,3,2,1,0:T(8,128)(2,1)S(1)}, bf16[1,8,8,32,128]{4,3,2,1,0:T(8,128)(2,1)}, u32[]{:S(2)}) copy-start(bf16[1,8,8,32,128]{4,3,2,1,0:T(8,128)(2,1)} %copy-done.6) | copy-start | bytes 1572868
  104.4 4.2 %collective-permute-start.5 = (bf16[64,2048]{1,0:T(8,128)(2,1)S(1)}, bf16[64,2048]{1,0:T(8,128)(2,1)S(1)}, u32[]{:S(2)}, u32[]{:S(2)}) collective-permute-start(bf16[64,2048]{1,0:T(8,128)(2,1)S(1)} %add_convert_fusion.4), channel_id=1, source_target_pairs={{0,1},{1,0},{2,3},{3,2},{4,5},{5,4},{6,7},{7,6},{8,9},{9,8},{10,11... | collective-permute-start | bytes 786440 | tf_op jit(solution)/shard_map/ppermute | solution.py:36
  108.6 30.3 %copy-start.11 = (bf16[64,2048]{1,0:T(8,128)(2,1)}, bf16[64,2048]{1,0:T(8,128)(2,1)S(1)}, u32[]{:S(2)}) copy-start(bf16[64,2048]{1,0:T(8,128)(2,1)S(1)} %get-tuple-element.50) | copy-start | bytes 786436
  108.8 7.1 %copy-start.32 = (f32[128]{0:T(128)}, f32[128]{0:T(128)S(1)}, u32[]{:S(2)}) copy-start(f32[128]{0:T(128)S(1)} %add_rsqrt_fusion) | copy-start | bytes 1540
  112.5 16.0 %copy-start.20 = (bf16[128,128]{0,1:T(8,128)(2,1)}, bf16[128,128]{0,1:T(8,128)(2,1)S(1)}, u32[]{:S(2)}) copy-start(bf16[128,128]{0,1:T(8,128)(2,1)S(1)} %get-tuple-element.60) | copy-start | bytes 98308
  114.0 4.0 %collective-permute-start.6 = (bf16[64,2048]{1,0:T(8,128)(2,1)S(1)}, bf16[64,2048]{1,0:T(8,128)(2,1)S(1)}, u32[]{:S(2)}, u32[]{:S(2)}) collective-permute-start(bf16[64,2048]{1,0:T(8,128)(2,1)S(1)} %broadcast_select_fusion.10), channel_id=1, source_target_pairs={{0,1},{1,0},{2,3},{3,2},{4,5},{5,4},{6,7},{7,6},{8,9},{9,8},{10,11... | collective-permute-start | bytes 786440 | tf_op jit(solution)/shard_map/ppermute | solution.py:36
  119.2 19.5 %all-to-all-start.3 = ((bf16[4,64,2048]{2,1,0:T(8,128)(2,1)}), bf16[4,64,2048]{2,1,0:T(8,128)(2,1)S(1)}, u32[]{:S(2)}, u32[]{:S(2)}) async-start(bf16[4,64,2048]{2,1,0:T(8,128)(2,1)} %broadcast_in_dim.24), calls=%async_computation.3 | async-start | bytes 2097152 | tf_op jit(solution)/shard_map/all_to_all | solution.py:20
  124.7 4.8 %copy-start.18 = (f32[2048,128]{1,0:T(8,128)S(1)}, f32[2048,128]{1,0:T(8,128)}, u32[]{:S(2)}) copy-start(f32[2048,128]{1,0:T(8,128)} %fusion.65) | copy-start | bytes 3145732
  138.7 4.6 %copy-start.30 = (f32[128]{0:T(128)S(1)}, f32[128]{0:T(128)}, u32[]{:S(2)}) copy-start(f32[128]{0:T(128)} %copy-done.29) | copy-start | bytes 1540
  138.7 4.7 %copy-start.34 = (bf16[128,128]{1,0:T(8,128)(2,1)S(1)}, bf16[128,128]{1,0:T(8,128)(2,1)}, u32[]{:S(2)}) copy-start(bf16[128,128]{1,0:T(8,128)(2,1)} %copy-done.33) | copy-start | bytes 98308
  138.7 4.9 %copy-start.26 = (bf16[128,128]{1,0:T(8,128)(2,1)S(1)}, bf16[128,128]{1,0:T(8,128)(2,1)}, u32[]{:S(2)}) copy-start(bf16[128,128]{1,0:T(8,128)(2,1)} %copy-done.25) | copy-start | bytes 98308
  138.7 5.0 %copy-start.24 = (bf16[128,128]{1,0:T(8,128)(2,1)S(1)}, bf16[128,128]{1,0:T(8,128)(2,1)}, u32[]{:S(2)}) copy-start(bf16[128,128]{1,0:T(8,128)(2,1)} %copy-done.23) | copy-start | bytes 98308
  139.4 3.4 %collective-permute-start.7 = (bf16[64,2048]{1,0:T(8,128)(2,1)S(1)}, bf16[64,2048]{1,0:T(8,128)(2,1)S(1)}, u32[]{:S(2)}, u32[]{:S(2)}) collective-permute-start(bf16[64,2048]{1,0:T(8,128)(2,1)S(1)} %fusion.28), channel_id=1, source_target_pairs={{0,1},{1,0},{2,3},{3,2},{4,5},{5,4},{6,7},{7,6},{8,9},{9,8},{10,11... | collective-permute-start | bytes 786440 | tf_op jit(solution)/shard_map/ppermute | solution.py:36
  142.9 2.6 %copy-start.13 = (bf16[64,2048]{1,0:T(8,128)(2,1)}, bf16[64,2048]{1,0:T(8,128)(2,1)S(1)}, u32[]{:S(2)}) copy-start(bf16[64,2048]{1,0:T(8,128)(2,1)S(1)} %get-tuple-element.47) | copy-start | bytes 786436
  142.9 2.6 %copy-start.15 = (bf16[64,2048]{1,0:T(8,128)(2,1)}, bf16[64,2048]{1,0:T(8,128)(2,1)S(1)}, u32[]{:S(2)}) copy-start(bf16[64,2048]{1,0:T(8,128)(2,1)S(1)} %get-tuple-element.48) | copy-start | bytes 786436
  142.9 2.6 %copy-start = (f32[8,8,4,32,128]{4,3,0,2,1:T(8,128)S(1)}, f32[8,8,4,32,128]{4,3,0,2,1:T(8,128)}, u32[]{:S(2)}) copy-start(f32[8,8,4,32,128]{4,3,0,2,1:T(8,128)} %copy.57) | copy-start | bytes 12582916
  147.6 3.8 %copy-start.21 = (bf16[128,128]{0,1:T(8,128)(2,1)S(1)}, bf16[128,128]{0,1:T(8,128)(2,1)}, u32[]{:S(2)}) copy-start(bf16[128,128]{0,1:T(8,128)(2,1)} %copy-done.20) | copy-start | bytes 98308
  147.6 5.2 %copy-start.4 = (bf16[1,8,8,32,128]{4,3,2,1,0:T(8,128)(2,1)S(1)}, bf16[1,8,8,32,128]{4,3,2,1,0:T(8,128)(2,1)}, u32[]{:S(2)}) copy-start(bf16[1,8,8,32,128]{4,3,2,1,0:T(8,128)(2,1)} %copy-done.3) | copy-start | bytes 1572868
  147.6 30.3 %all-to-all-start.4 = ((bf16[8,8,4,32,128]{4,3,1,2,0:T(8,128)(2,1)}), bf16[8,8,4,32,128]{4,3,1,2,0:T(8,128)(2,1)S(1)}, u32[]{:S(2)}, u32[]{:S(2)}) async-start(bf16[8,8,4,32,128]{4,3,1,2,0:T(8,128)(2,1)} %fusion.3), calls=%async_computation.4 | async-start | bytes 4194304 | tf_op jit(solution)/shard_map/all_to_all | solution.py:20
  151.4 3.1 %copy-start.8 = (bf16[1,8,8,32,128]{4,3,2,1,0:T(8,128)(2,1)S(1)}, bf16[1,8,8,32,128]{4,3,2,1,0:T(8,128)(2,1)}, u32[]{:S(2)}) copy-start(bf16[1,8,8,32,128]{4,3,2,1,0:T(8,128)(2,1)} %copy-done.6) | copy-start | bytes 1572868
  154.8 3.8 %collective-permute-start.8 = (bf16[128,2048]{1,0:T(8,128)(2,1)S(1)}, bf16[128,2048]{1,0:T(8,128)(2,1)S(1)}, u32[]{:S(2)}, u32[]{:S(2)}) collective-permute-start(bf16[128,2048]{1,0:T(8,128)(2,1)S(1)} %get-tuple-element.63), channel_id=1, source_target_pairs={{0,1},{1,0},{2,3},{3,2},{4,5},{5,4},{6,7},{7,6},{8,9},{9,8},{10,11... | collective-permute-start | bytes 1572872 | tf_op jit(solution)/shard_map/ppermute | solution.py:36
  158.8 57.1 %copy-start.1 = (bf16[1,128,2048]{2,1,0:T(8,128)(2,1)S(1)}, bf16[1,128,2048]{2,1,0:T(8,128)(2,1)}, u32[]{:S(2)}) copy-start(bf16[1,128,2048]{2,1,0:T(8,128)(2,1)} %param.6) | copy-start | bytes 1572868
  158.8 57.1 %copy-start.28 = (f32[128]{0:T(128)S(1)}, f32[128]{0:T(128)}, u32[]{:S(2)}) copy-start(f32[128]{0:T(128)} %get-tuple-element.51) | copy-start | bytes 1540
  158.9 16.0 %collective-permute-start.9 = (bf16[128,2048]{1,0:T(8,128)(2,1)S(1)}, bf16[128,2048]{1,0:T(8,128)(2,1)S(1)}, u32[]{:S(2)}, u32[]{:S(2)}) collective-permute-start(bf16[128,2048]{1,0:T(8,128)(2,1)S(1)} %add_convert_fusion.2), channel_id=1, source_target_pairs={{0,2},{2,0},{4,6},{6,4},{1,3},{3,1},{5,7},{7,5},{8,10},{10,8},{12,... | collective-permute-start | bytes 1572872 | tf_op jit(solution)/shard_map/ppermute | solution.py:40
  177.9 17.0 %collective-permute-start.10 = (bf16[128,2048]{1,0:T(8,128)(2,1)}, bf16[128,2048]{1,0:T(8,128)(2,1)}, u32[]{:S(2)}, u32[]{:S(2)}) collective-permute-start(bf16[128,2048]{1,0:T(8,128)(2,1)} %add_convert_fusion.1), channel_id=1, source_target_pairs={{0,6},{2,4},{4,2},{6,0},{1,7},{3,5},{5,3},{7,1},{8,14},{10,12},{12... | collective-permute-start | bytes 1572872 | tf_op jit(solution)/shard_map/ppermute | solution.py:40
  182.9 33.1 %copy-start.2 = (bf16[1,128,2048]{2,1,0:T(8,128)(2,1)S(1)}, bf16[1,128,2048]{2,1,0:T(8,128)(2,1)}, u32[]{:S(2)}) copy-start(bf16[1,128,2048]{2,1,0:T(8,128)(2,1)} %param.7) | copy-start | bytes 1572868
  182.9 33.1 %copy-start.12 = (bf16[64,2048]{1,0:T(8,128)(2,1)S(1)}, bf16[64,2048]{1,0:T(8,128)(2,1)}, u32[]{:S(2)}) copy-start(bf16[64,2048]{1,0:T(8,128)(2,1)} %copy-done.11) | copy-start | bytes 786436
  182.9 33.1 %copy-start.14 = (bf16[64,2048]{1,0:T(8,128)(2,1)S(1)}, bf16[64,2048]{1,0:T(8,128)(2,1)}, u32[]{:S(2)}) copy-start(bf16[64,2048]{1,0:T(8,128)(2,1)} %copy-done.13) | copy-start | bytes 786436
  182.9 33.1 %copy-start.16 = (bf16[64,2048]{1,0:T(8,128)(2,1)S(1)}, bf16[64,2048]{1,0:T(8,128)(2,1)}, u32[]{:S(2)}) copy-start(bf16[64,2048]{1,0:T(8,128)(2,1)} %copy-done.15) | copy-start | bytes 786436
  184.7 28.6 %all-to-all-start.5 = ((bf16[8,4,32,128]{3,2,1,0:T(8,128)(2,1)}), bf16[8,4,32,128]{3,2,1,0:T(8,128)(2,1)S(1)}, u32[]{:S(2)}, u32[]{:S(2)}) async-start(bf16[8,4,32,128]{3,2,1,0:T(8,128)(2,1)} %copy.54), calls=%async_computation.5 | async-start | bytes 524288 | tf_op jit(solution)/shard_map/all_to_all | solution.py:20
  196.2 18.4 %collective-permute-start.11 = (bf16[128,2048]{1,0:T(8,128)(2,1)S(1)}, bf16[128,2048]{1,0:T(8,128)(2,1)}, u32[]{:S(2)}, u32[]{:S(2)}) collective-permute-start(bf16[128,2048]{1,0:T(8,128)(2,1)S(1)} %add_convert_fusion), channel_id=1, source_target_pairs={{0,1},{1,0},{2,3},{3,2},{4,5},{5,4},{6,7},{7,6},{8,9},{9,8},{10,11... | collective-permute-start | bytes 1572872 | tf_op jit(solution)/shard_map/ppermute | solution.py:36
  (5 other events, 4.8 us)

commit v7 on v5

--- a/solution.py
+++ b/solution.py
@@ -1,6 +1,9 @@
 import jax
 import jax.numpy as jnp
 from jax import lax
+from jax.experimental import pallas as pl
+from jax.experimental.layout import Layout, with_layout_constraint
+from jax.experimental.pallas import tpu as pltpu
 from jax.sharding import Mesh, PartitionSpec as P
 
 HD = 128
@@ -92,13 +95,37 @@
     return inv * u - x32 * inv**3 * jnp.mean(x32 * u, -1, keepdims=True)
 
 
+def last_kernel(flags, tile, other, base_h, base_g, h1, inv, gain, out_h, out_g):
+    first, mine = flags[0] == 0, flags[1] == 1
+    a, b = tile[...].astype(F32), other[...].astype(F32)
+    old_h, old_g = base_h[...], base_g[...]
+    new_h = (old_h.astype(F32) + jnp.where(first, a, b)).astype(BF)
+    dx = norm_grad(jnp.where(first, b, a), h1[...].astype(F32), inv[...], gain[...])
+    new_g = (old_g.astype(F32) + dx).astype(BF)
+    out_h[...] = jnp.where(mine, new_h, old_h)
+    out_g[...] = jnp.where(mine, new_g, old_g)
+
+
+def last_step(flags, tile, other, base_h, base_g, h1, inv, gain):
+    steps = 4
+    rows = pl.BlockSpec((TILE // steps, D), lambda i: (i, 0))
+    return pl.pallas_call(
+        last_kernel,
+        grid=(steps,),
+        in_specs=[pl.BlockSpec(memory_space=pltpu.SMEM)]
+        + [rows] * 5
+        + [pl.BlockSpec((TILE // steps, 1), lambda i: (i, 0)), pl.BlockSpec((1, D), lambda i: (0, 0))],
+        out_specs=[rows, rows],
+        out_shape=[jax.ShapeDtypeStruct((TILE, D), BF)] * 2,
+        compiler_params=pltpu.CompilerParams(vmem_limit_bytes=16 * 2**20),
+    )(flags, tile, other, base_h, base_g, h1, inv, gain.reshape(1, D))
+
+
 def on_device(hidden_in, cotangent, tile_depth, w_qkv, w_out, gain):
     me = lax.axis_index("x") * 2 + lax.axis_index("core")
     depth = tile_depth[0]
-    places = jnp.arange(CTX, dtype=jnp.int32)
-    alive = depth >= 2
     live3 = jnp.any(depth >= 3)
-    mine = jnp.any(alive & (places == me))
+    mine = lax.dynamic_index_in_dim(depth, me, 0, keepdims=False) >= 2
 
     def chunk(tile):
         return lax.dynamic_index_in_dim(tile.reshape(CTX, CHUNK, D), me, 0, keepdims=False)
@@ -129,42 +156,43 @@
     inv3, normed3 = norm_chunk(x2, gain)
     rows3 = jnp.where(live3, normed3, jnp.zeros_like(normed3))
     dy3 = jnp.where(live3, g3, jnp.zeros_like(g3))
+    rows3 = lax.optimization_barrier(rows3)
     mixed3, keep3 = forward(rows3, w)
     dqkv3 = backward(dy3, keep3, w)
-    dnorm3, dqkv3 = lax.optimization_barrier((norm_terms(dqkv3, w), dqkv3))
-
-    def products(rows, dqkv, dy, attn):
-        terms = [dot(rows, d, tokens) for d in dqkv] + [dot(dy, attn, tokens)]
-        return jnp.stack([x.reshape(NP, NN, 32, HD) for x in terms], 2)
-
-    early = products(rows3, dqkv3, dy3, keep3[-1])
+    dnorm3 = norm_terms(dqkv3, w)
     x2c = chunk(h2).astype(F32)
     inv3c, _ = norm_chunk(x2c, gain)
     g2c = chunk(g3).astype(F32) + norm_grad(sum_chunk(dnorm3), x2c, inv3c, gain)
-    g2c, early = lax.optimization_barrier((g2c.astype(BF), early))
-    g2 = all_rows(g2c)
+    g2 = all_rows(g2c.astype(BF))
 
     dqkv2 = backward(g2, keep2, w)
-    terms = (early + products(rows2, dqkv2, g2, attn2)).astype(BF).transpose(1, 0, 2, 3, 4)
-    terms, dqkv2 = lax.optimization_barrier((terms, dqkv2))
+
+    def product(left3, right3, left2, right2):
+        both = dot(jnp.concatenate([left3, left2], 0), jnp.concatenate([right3, right2], 0), tokens)
+        return both.astype(BF).reshape(NP, NN, 32, HD)
+
+    terms = [product(rows3, d3, rows2, d2) for d3, d2 in zip(dqkv3, dqkv2)]
+    terms.append(product(dy3, keep3[-1], g2, attn2))
+    terms = jnp.stack(terms, 2).transpose(1, 0, 2, 3, 4)
+    terms = with_layout_constraint(terms, Layout((0, 1, 2, 3, 4)))
+    terms, dqkv2, old_h, old_g = lax.optimization_barrier((terms, dqkv2, h2, g2))
     terms = swap(terms, NEAR)
+    base_h = jnp.where(mine, old_h, hidden_in[0])
+    base_g = jnp.where(mine, old_g, cotangent[0])
     dnorm2 = norm_terms(dqkv2, w)
 
     mixed3 = mixed3.astype(BF)
     tile = add(jnp.where(core == 0, mixed3, dnorm2), from_core(jnp.where(core == 0, dnorm2, mixed3)))
     tile = add(tile, from_pair(tile, 1))
-    terms, tile = lax.optimization_barrier((terms, tile))
+    terms, tile, base_h, base_g = lax.optimization_barrier((terms, tile, base_h, base_g))
 
     part = jnp.sum(terms.astype(F32), 0).astype(BF)
     shard = jnp.sum(swap(part, "zp").astype(F32), 0)
 
     tile = add(tile, from_pair(tile, 3))
     other = from_core(tile)
-    sum3, sum2 = jnp.where(core == 0, tile, other), jnp.where(core == 0, other, tile)
-    h3 = (x2 + sum3.astype(F32)).astype(BF)
-    g1 = (g2.astype(F32) + norm_grad(sum2.astype(F32), x1, inv2, gain)).astype(BF)
-    hidden_out = jnp.where(mine, h3, hidden_in[0])
-    grad_in = jnp.where(mine, g1, cotangent[0])
+    flags = jnp.stack([core, mine.astype(jnp.int32)])
+    hidden_out, grad_in = last_step(flags, tile, other, base_h, base_g, h1, inv2, gain)
     return (hidden_out[None], grad_in[None], shard[:3], shard[3].T)
 
 

time: 221 us -> 213 us (0.964)
  blocking collectives: 26.4 us -> 39.2 us
  matrix products: 19.4 us -> 9.59 us
  starting transfers between devices: 61.6 us -> 55.2 us
  other arithmetic: 20.8 us -> 17.1 us
  local copies, waits for them, and re-layouts: 9.03 us -> 6.37 us
  Pallas kernels: 0 us -> 2.63 us
    all_to_all x0 -> x1, blocking collectives: none -> 12.9 us  [swap(): return lax.all_to_all(x, axis, 0, 0)]
    dot_general x36 -> x32, matrix products: 19.4 us -> 9.59 us  [dot(): return lax.dot_general(a, b, (dims, ((), ())), preferred_element_type=F32)]
    all_to_all x6 -> x5, starting transfers between devices: 41.5 us -> 35.2 us  [swap(): return lax.all_to_all(x, axis, 0, 0)]
    broadcast_in_dim x1 -> x0, other arithmetic: 3.37 us -> none  [on_device(): return (hidden_out[None], grad_in[None], shard[:3], shard[3].T)]
    select_n x1 -> x3, other arithmetic: 1.1 us -> 4.22 us  [the longest x1 2.55 us: on_device(): dy3 = jnp.where(live3, g3, jnp.zeros_like(g3))]
    pallas_call x0 -> x1, Pallas kernels: none -> 2.63 us  [last_step(): pl.pallas_call(last_kernel, grid=(steps,), in_specs=[pl.BlockSpec(memory_...]
    another operation x1 -> x0, local copies, waits for them, and re-layouts: 2.57 us -> none  [products(): return jnp.stack([x.reshape(NP, NN, 32, HD) for x in terms], 2)]
    all_to_all x6 -> x5, waiting for transfers between devices: 34.8 us -> 34 us  [swap(): return lax.all_to_all(x, axis, 0, 0)]
  transfers between devices with their start and end apart: 14 -> 13, of which waited for: 12 -> 11; matrix products, arithmetic and copies ran while one was open for 10% -> 6% of each run, Pallas kernels for 0% -> 0%
where the time goes in v7:
time: 213 us; the launch traced here: 212 us
  waiting for transfers between devices  80.3 us (38%)
  starting transfers between devices  55.2 us (26%)
  blocking collectives  39.2 us (18%)
  other arithmetic  17.1 us (8%)
  matrix products  9.59 us (5%)
  local copies, waits for them, and re-layouts  6.37 us (3%)
  Pallas kernels  2.63 us (1%)
    ppermute x4, waiting for transfers between devices, from_pair(): return lax.ppermute(x, 'x', [(i, i ^ bit) for i in range(CTX // 2)])  43.6 us
    all_to_all x5, starting transfers between devices, swap(): return lax.all_to_all(x, axis, 0, 0)  35.2 us
    all_to_all x5, waiting for transfers between devices, swap(): return lax.all_to_all(x, axis, 0, 0)  34 us
    all_gather x2, blocking collectives, all_rows(): return lax.all_gather(chunk, CONTEXT, tiled=True)  26.2 us
    all_to_all x1, blocking collectives, swap(): return lax.all_to_all(x, axis, 0, 0)  12.9 us
    ppermute x4, starting transfers between devices, from_pair(): return lax.ppermute(x, 'x', [(i, i ^ bit) for i in range(CTX // 2)])  11.9 us
    dot_general x32, matrix products, dot(): return lax.dot_general(a, b, (dims, ((), ())), preferred_element_type=F32)  9.59 us
    ppermute x4, starting transfers between devices, from_core(): return lax.ppermute(x, 'core', [(0, 1), (1, 0)])  8.15 us
  transfers between devices with their start and end apart: 13, of which 11 were waited for; matrix products, arithmetic and copies ran while one was open for 6% of the time, Pallas kernels for 0%

profile of v7, /device:TPU:6, one launch (start us, length us, event | category | flops | bytes accessed | tf_op | source)
XLA Modules:
  0.0 212.1 jit_solution(16925467318143055678)
XLA Ops:
  0.7 1.3 fusion.55
  2.0 1.9 broadcast_select_fusion.3
  3.9 1.9 collective-permute-start
  5.8 0.8 pad_maximum_fusion.5
  6.6 0.7 broadcast_in_dim.18
  7.3 15.1 %all-to-all-start = ((bf16[8,4,32,128]{3,2,1,0:T(8,128)(2,1)}), bf16[8,4,32,128]{3,2,1,0:T(8,128)(2,1)S(1)}, u32[]{:S(2)}, u32[]{:S(2)}) async-start(bf16[8,4,32,128]{3,2,1,0:T(8,128)(2,1)} %broadcast_in_dim.18), calls=%async_computation | async-start | bytes 524288 | tf_op jit(solution)/shard_map/all_to_all | solution.py:24
  22.5 0.7 select_add_fusion
  23.2 2.7 %collective-permute-start.1 = (bf16[128,2048]{1,0:T(8,128)(2,1)S(1)}, bf16[128,2048]{1,0:T(8,128)(2,1)S(1)}, u32[]{:S(2)}, u32[]{:S(2)}) collective-permute-start(bf16[128,2048]{1,0:T(8,128)(2,1)S(1)} %select_add_fusion), channel_id=1, source_target_pairs={{0,2},{2,0},{4,6},{6,4},{1,3},{3,1},{5,7},{7,5},{8,10},{10,8},{12,... | collective-permute-start | bytes 1572872 | tf_op jit(solution)/shard_map/ppermute | solution.py:44
  25.9 13.2 %collective-permute-done.1 = bf16[128,2048]{1,0:T(8,128)(2,1)S(1)} collective-permute-done((bf16[128,2048]{1,0:T(8,128)(2,1)S(1)}, bf16[128,2048]{1,0:T(8,128)(2,1)S(1)}, u32[]{:S(2)}, u32[]{:S(2)}) %collective-permute-start.1) | collective-permute-done | bytes 524320 | tf_op jit(solution)/shard_map/ppermute | solution.py:44
  39.3 5.2 %all-to-all-done = bf16[8,4,32,128]{3,2,1,0:T(8,128)(2,1)S(1)} async-done(((bf16[8,4,32,128]{3,2,1,0:T(8,128)(2,1)}), bf16[8,4,32,128]{3,2,1,0:T(8,128)(2,1)S(1)}, u32[]{:S(2)}, u32[]{:S(2)}) %all-to-all-start) | async-done | bytes 262176 | tf_op jit(solution)/shard_map/all_to_all | solution.py:24
  44.5 1.8 broadcast_in_dim.19
  46.3 4.6 %all-to-all-start.1 = ((bf16[8,8,4,32,128]{4,3,1,2,0:T(8,128)(2,1)}), bf16[8,8,4,32,128]{4,3,1,2,0:T(8,128)(2,1)S(1)}, u32[]{:S(2)}, u32[]{:S(2)}) async-start(bf16[8,8,4,32,128]{4,3,1,2,0:T(8,128)(2,1)} %broadcast_in_dim.19), calls=%async_computation.1 | async-start | bytes 4194304 | tf_op jit(solution)/shard_map/all_to_all | solution.py:24
  50.9 2.4 %collective-permute-start.2 = (bf16[128,2048]{1,0:T(8,128)(2,1)S(1)}, bf16[128,2048]{1,0:T(8,128)(2,1)S(1)}, u32[]{:S(2)}, u32[]{:S(2)}) collective-permute-start(bf16[128,2048]{1,0:T(8,128)(2,1)S(1)} %add.82), channel_id=1, source_target_pairs={{0,6},{2,4},{4,2},{6,0},{1,7},{3,5},{5,3},{7,1},{8,14},{10,12},{12... | collective-permute-start | bytes 1572872 | tf_op jit(solution)/shard_map/ppermute | solution.py:44
  53.3 14.2 %collective-permute-done.2 = bf16[128,2048]{1,0:T(8,128)(2,1)S(1)} collective-permute-done((bf16[128,2048]{1,0:T(8,128)(2,1)S(1)}, bf16[128,2048]{1,0:T(8,128)(2,1)S(1)}, u32[]{:S(2)}, u32[]{:S(2)}) %collective-permute-start.2) | collective-permute-done | bytes 524320 | tf_op jit(solution)/shard_map/ppermute | solution.py:44
  67.6 1.9 collective-permute-start.3
  69.5 0.7 compare_reduce_fusion
  70.2 1.2 collective-permute-done.3
  72.4 4.6 %all-to-all-done.1 = bf16[8,8,4,32,128]{4,3,1,2,0:T(8,128)(2,1)S(1)} async-done(((bf16[8,8,4,32,128]{4,3,1,2,0:T(8,128)(2,1)}), bf16[8,8,4,32,128]{4,3,1,2,0:T(8,128)(2,1)S(1)}, u32[]{:S(2)}, u32[]{:S(2)}) %all-to-all-start.1) | async-done | bytes 2097184 | tf_op jit(solution)/shard_map/all_to_all | solution.py:24
  77.0 0.6 copy.53
  77.6 0.5 fusion.54
  79.4 1.1 convolution_convert_fusion.5
  80.5 4.8 %all-to-all-start.2 = ((bf16[8,16,2048]{2,1,0:T(8,128)(2,1)}), bf16[8,16,2048]{2,1,0:T(8,128)(2,1)S(1)}, u32[]{:S(2)}, u32[]{:S(2)}) async-start(bf16[8,16,2048]{2,1,0:T(8,128)(2,1)} %bitcast.131), calls=%async_computation.2 | async-start | bytes 1048576 | tf_op jit(solution)/shard_map/all_to_all | solution.py:24
  85.3 2.5 %broadcast_select_fusion.4 = (bf16[128,2048]{1,0:T(8,128)(2,1)S(1)}, bf16[128,2048]{1,0:T(8,128)(2,1)}) fusion(pred[]{:T(512)} %compare_reduce_fusion, bf16[128,2048]{1,0:T(8,128)(2,1)} %copy-done.12, bf16[128,2048]{1,0:T(8,128)(2,1)} %copy-done.5, pred[]{:T(512)S(6)} %eq.2), kind=kLoop, calls=%fused_computation.73 | loop fusion | flops 524288 | bytes 2097154 | tf_op jit(solution)/shard_map/jit(_where)/select_n | solution.py:158
  87.8 0.8 copy-done.10
  88.9 4.7 %all-to-all-done.2 = bf16[8,16,2048]{2,1,0:T(8,128)(2,1)S(1)} async-done(((bf16[8,16,2048]{2,1,0:T(8,128)(2,1)}), bf16[8,16,2048]{2,1,0:T(8,128)(2,1)S(1)}, u32[]{:S(2)}, u32[]{:S(2)}) %all-to-all-start.2) | async-done | bytes 524320 | tf_op jit(solution)/shard_map/all_to_all | solution.py:24
  93.7 13.1 %all_gather.6 = bf16[128,2048]{1,0:T(8,128)(2,1)S(1)} all-gather(bf16[16,2048]{1,0:T(8,128)(2,1)S(1)} %fusion.26), channel_id=1, replica_groups=mesh['zp'=8,'zq'=2,'y'=4,'x'=4,'core'=2] {'x','core'}, dimensions={0}, use_global_device_ids=true | all-gather | bytes 589824 | tf_op jit(solution)/shard_map/all_gather | solution.py:53
  107.0 0.9 fusion.19
  110.8 12.9 %all_to_all.30 = bf16[8,16,2048]{2,1,0:T(8,128)(2,1)S(1)} all-to-all(bf16[8,16,2048]{2,1,0:T(8,128)(2,1)S(1)} %bitcast.132), channel_id=1, replica_groups=mesh['zp'=8,'zq'=2,'y'=4,'x'=4,'core'=2] {'x','core'}, dimensions={0} | all-to-all | bytes 1048576 | tf_op jit(solution)/shard_map/all_to_all | solution.py:24
  124.0 0.9 fusion.24
  124.9 13.1 %all_gather.7 = bf16[128,2048]{1,0:T(8,128)(2,1)S(1)} all-gather(bf16[16,2048]{1,0:T(8,128)(2,1)S(1)} %fusion.24), channel_id=1, replica_groups=mesh['zp'=8,'zq'=2,'y'=4,'x'=4,'core'=2] {'x','core'}, dimensions={0}, use_global_device_ids=true | all-gather | bytes 589824 | tf_op jit(solution)/shard_map/all_gather | solution.py:53
  140.0 0.5 convolution_convert_fusion.2
  141.1 1.8 copy_bitcast_fusion
  142.8 4.5 %all-to-all-start.4 = ((bf16[8,8,4,32,128]{4,3,2,1,0:T(8,128)(2,1)}), bf16[8,8,4,32,128]{4,3,2,1,0:T(8,128)(2,1)}, u32[]{:S(2)}, u32[]{:S(2)}) async-start(bf16[8,8,4,32,128]{4,3,2,1,0:T(8,128)(2,1)} %copy_bitcast_fusion), calls=%async_computation.4 | async-start | bytes 4194304 | tf_op jit(solution)/shard_map/all_to_all | solution.py:24
  148.6 2.4 %collective-permute-start.4 = (bf16[128,2048]{1,0:T(8,128)(2,1)S(1)}, bf16[128,2048]{1,0:T(8,128)(2,1)S(1)}, u32[]{:S(2)}, u32[]{:S(2)}) collective-permute-start(bf16[128,2048]{1,0:T(8,128)(2,1)S(1)} %get-tuple-element.54), channel_id=1, source_target_pairs={{0,1},{1,0},{2,3},{3,2},{4,5},{5,4},{6,7},{7,6},{8,9},{9,8},{10,11... | collective-permute-start | bytes 1572872 | tf_op jit(solution)/shard_map/ppermute | solution.py:40
  151.0 1.5 collective-permute-done.4
  152.8 2.8 %collective-permute-start.5 = (bf16[128,2048]{1,0:T(8,128)(2,1)S(1)}, bf16[128,2048]{1,0:T(8,128)(2,1)S(1)}, u32[]{:S(2)}, u32[]{:S(2)}) collective-permute-start(bf16[128,2048]{1,0:T(8,128)(2,1)S(1)} %add_convert_fusion.2), channel_id=1, source_target_pairs={{0,2},{2,0},{4,6},{6,4},{1,3},{3,1},{5,7},{7,5},{8,10},{10,8},{12,... | collective-permute-start | bytes 1572872 | tf_op jit(solution)/shard_map/ppermute | solution.py:44
  155.6 0.8 bitcast_select_fusion
  156.4 12.4 %collective-permute-done.5 = bf16[128,2048]{1,0:T(8,128)(2,1)S(1)} collective-permute-done((bf16[128,2048]{1,0:T(8,128)(2,1)S(1)}, bf16[128,2048]{1,0:T(8,128)(2,1)S(1)}, u32[]{:S(2)}, u32[]{:S(2)}) %collective-permute-start.5) | collective-permute-done | bytes 524320 | tf_op jit(solution)/shard_map/ppermute | solution.py:44
  169.0 5.0 %all-to-all-done.4 = bf16[8,8,4,32,128]{4,3,2,1,0:T(8,128)(2,1)} async-done(((bf16[8,8,4,32,128]{4,3,2,1,0:T(8,128)(2,1)}), bf16[8,8,4,32,128]{4,3,2,1,0:T(8,128)(2,1)}, u32[]{:S(2)}, u32[]{:S(2)}) %all-to-all-start.4) | async-done | bytes 2097184 | tf_op jit(solution)/shard_map/all_to_all | solution.py:24
  174.0 4.0 %collective-permute-start.6 = (bf16[128,2048]{1,0:T(8,128)(2,1)S(1)}, bf16[128,2048]{1,0:T(8,128)(2,1)S(1)}, u32[]{:S(2)}, u32[]{:S(2)}) collective-permute-start(bf16[128,2048]{1,0:T(8,128)(2,1)S(1)} %add_convert_fusion.1), channel_id=1, source_target_pairs={{0,6},{2,4},{4,2},{6,0},{1,7},{3,5},{5,3},{7,1},{8,14},{10,12},{12... | collective-permute-start | bytes 1572872 | tf_op jit(solution)/shard_map/ppermute | solution.py:44
  178.0 2.7 %reduce_sum.121 = bf16[8,4,32,128]{3,2,1,0:T(8,128)(2,1)} reduce(bf16[8,8,4,32,128]{4,3,2,1,0:T(8,128)(2,1)} %all-to-all-done.4, bf16[]{:T(256)} %constant.46.clone.1), dimensions={0}, to_apply=%region_13.14 | reduce | flops 917504 | bytes 2359298 | tf_op jit(solution)/shard_map/reduce_sum | solution.py:189
  180.7 6.2 %all-to-all-start.5 = ((bf16[8,4,32,128]{3,2,1,0:T(8,128)(2,1)}), bf16[8,4,32,128]{3,2,1,0:T(8,128)(2,1)S(1)}, u32[]{:S(2)}, u32[]{:S(2)}) async-start(bf16[8,4,32,128]{3,2,1,0:T(8,128)(2,1)} %reduce_sum.121), calls=%async_computation.5 | async-start | bytes 524288 | tf_op jit(solution)/shard_map/all_to_all | solution.py:24
  186.9 3.8 %collective-permute-done.6 = bf16[128,2048]{1,0:T(8,128)(2,1)S(1)} collective-permute-done((bf16[128,2048]{1,0:T(8,128)(2,1)S(1)}, bf16[128,2048]{1,0:T(8,128)(2,1)S(1)}, u32[]{:S(2)}, u32[]{:S(2)}) %collective-permute-start.6) | collective-permute-done | bytes 524320 | tf_op jit(solution)/shard_map/ppermute | solution.py:44
  190.8 1.9 collective-permute-start.7
  193.6 14.6 %all-to-all-done.5 = bf16[8,4,32,128]{3,2,1,0:T(8,128)(2,1)S(1)} async-done(((bf16[8,4,32,128]{3,2,1,0:T(8,128)(2,1)}), bf16[8,4,32,128]{3,2,1,0:T(8,128)(2,1)S(1)}, u32[]{:S(2)}, u32[]{:S(2)}) %all-to-all-start.5) | async-done | bytes 262176 | tf_op jit(solution)/shard_map/all_to_all | solution.py:24
  208.2 0.6 slice.44
  208.9 0.6 slice_bitcast_fusion
  209.5 2.6 %shard_map.93 = (bf16[128,2048]{1,0:T(8,128)(2,1)}, bf16[128,2048]{1,0:T(8,128)(2,1)}) custom-call(s32[2]{0:T(128)S(1)} %pad_add_fusion.flags, bf16[128,2048]{1,0:T(8,128)(2,1)S(1)} %add_convert_fusion.tile, bf16[128,2048]{1,0:T(8,128)(2,1)S(1)} %collective-permute-done.7.other, bf16[128,2048]{1,0:T(8,128)(2,1)S(1)} %get-tuple-element.27.base_h, ...), custom_call_target="tpu_custom_call" | custom-call | tf_op jit(solution)/shard_map/pallas_call | solution.py:112
  (81 shorter events, 10.7 us)
Async XLA Ops:
  0.6 21.8 %copy-start.6 = (bf16[1,128,2048]{2,1,0:T(8,128)(2,1)S(1)}, bf16[1,128,2048]{2,1,0:T(8,128)(2,1)}, u32[]{:S(2)}) copy-start(bf16[1,128,2048]{2,1,0:T(8,128)(2,1)} %param.6) | copy-start | bytes 1572868
  0.6 21.8 %copy-start.8 = (bf16[1,128,2048]{2,1,0:T(8,128)(2,1)S(1)}, bf16[1,128,2048]{2,1,0:T(8,128)(2,1)}, u32[]{:S(2)}) copy-start(bf16[1,128,2048]{2,1,0:T(8,128)(2,1)} %param.7) | copy-start | bytes 1572868
  3.9 18.5 %collective-permute-start = (bf16[128,2048]{1,0:T(8,128)(2,1)S(1)}, bf16[128,2048]{1,0:T(8,128)(2,1)S(1)}, u32[]{:S(2)}, u32[]{:S(2)}) collective-permute-start(bf16[128,2048]{1,0:T(8,128)(2,1)S(1)} %broadcast_select_fusion.3), channel_id=1, source_target_pairs={{0,1},{1,0},{2,3},{3,2},{4,5},{5,4},{6,7},{7,6},{8,9},{9,8},{10,11... | collective-permute-start | bytes 1572872 | tf_op jit(solution)/shard_map/ppermute | solution.py:40
  7.3 37.1 %all-to-all-start = ((bf16[8,4,32,128]{3,2,1,0:T(8,128)(2,1)}), bf16[8,4,32,128]{3,2,1,0:T(8,128)(2,1)S(1)}, u32[]{:S(2)}, u32[]{:S(2)}) async-start(bf16[8,4,32,128]{3,2,1,0:T(8,128)(2,1)} %broadcast_in_dim.18), calls=%async_computation | async-start | bytes 524288 | tf_op jit(solution)/shard_map/all_to_all | solution.py:24
  23.2 15.9 %collective-permute-start.1 = (bf16[128,2048]{1,0:T(8,128)(2,1)S(1)}, bf16[128,2048]{1,0:T(8,128)(2,1)S(1)}, u32[]{:S(2)}, u32[]{:S(2)}) collective-permute-start(bf16[128,2048]{1,0:T(8,128)(2,1)S(1)} %select_add_fusion), channel_id=1, source_target_pairs={{0,2},{2,0},{4,6},{6,4},{1,3},{3,1},{5,7},{7,5},{8,10},{10,8},{12,... | collective-permute-start | bytes 1572872 | tf_op jit(solution)/shard_map/ppermute | solution.py:44
  46.3 23.2 %copy-start.13 = (s32[1,8]{1,0:T(1,128)S(1)}, s32[1,8]{1,0:T(1,128)}, u32[]{:S(2)}) copy-start(s32[1,8]{1,0:T(1,128)} %param.8) | copy-start | bytes 100
  46.3 30.7 %all-to-all-start.1 = ((bf16[8,8,4,32,128]{4,3,1,2,0:T(8,128)(2,1)}), bf16[8,8,4,32,128]{4,3,1,2,0:T(8,128)(2,1)S(1)}, u32[]{:S(2)}, u32[]{:S(2)}) async-start(bf16[8,8,4,32,128]{4,3,1,2,0:T(8,128)(2,1)} %broadcast_in_dim.19), calls=%async_computation.1 | async-start | bytes 4194304 | tf_op jit(solution)/shard_map/all_to_all | solution.py:24
  50.9 21.3 %copy-start = (f32[2048]{0:T(1024)S(1)}, f32[2048]{0:T(1024)}, u32[]{:S(2)}) copy-start(f32[2048]{0:T(1024)} %param.11) | copy-start | bytes 24580
  50.9 16.5 %collective-permute-start.2 = (bf16[128,2048]{1,0:T(8,128)(2,1)S(1)}, bf16[128,2048]{1,0:T(8,128)(2,1)S(1)}, u32[]{:S(2)}, u32[]{:S(2)}) collective-permute-start(bf16[128,2048]{1,0:T(8,128)(2,1)S(1)} %add.82), channel_id=1, source_target_pairs={{0,6},{2,4},{4,2},{6,0},{1,7},{3,5},{5,3},{7,1},{8,14},{10,12},{12... | collective-permute-start | bytes 1572872 | tf_op jit(solution)/shard_map/ppermute | solution.py:44
  67.6 4.1 %copy-start.5 = (bf16[128,2048]{1,0:T(8,128)(2,1)}, bf16[128,2048]{1,0:T(8,128)(2,1)S(1)}, u32[]{:S(2)}) copy-start(bf16[128,2048]{1,0:T(8,128)(2,1)S(1)} %add.83) | copy-start | bytes 1572868
  67.6 3.8 %collective-permute-start.3 = (bf16[128,2048]{1,0:T(8,128)(2,1)S(1)}, bf16[128,2048]{1,0:T(8,128)(2,1)S(1)}, u32[]{:S(2)}, u32[]{:S(2)}) collective-permute-start(bf16[128,2048]{1,0:T(8,128)(2,1)S(1)} %add.83), channel_id=1, source_target_pairs={{0,1},{1,0},{2,3},{3,2},{4,5},{5,4},{6,7},{7,6},{8,9},{9,8},{10,11... | collective-permute-start | bytes 1572872 | tf_op jit(solution)/shard_map/ppermute | solution.py:40
  71.4 0.8 copy-start.12
  72.4 6.3 %copy-start.1 = (bf16[128,2048]{1,0:T(8,128)(2,1)}, bf16[128,2048]{1,0:T(8,128)(2,1)S(1)}, u32[]{:S(2)}) copy-start(bf16[128,2048]{1,0:T(8,128)(2,1)S(1)} %fusion.12) | copy-start | bytes 1572868
  80.5 13.1 %all-to-all-start.2 = ((bf16[8,16,2048]{2,1,0:T(8,128)(2,1)}), bf16[8,16,2048]{2,1,0:T(8,128)(2,1)S(1)}, u32[]{:S(2)}, u32[]{:S(2)}) async-start(bf16[8,16,2048]{2,1,0:T(8,128)(2,1)} %bitcast.131), calls=%async_computation.2 | async-start | bytes 1048576 | tf_op jit(solution)/shard_map/all_to_all | solution.py:24
  87.8 0.8 copy-start.10
  123.7 15.3 %copy-start.2 = (bf16[128,2048]{1,0:T(8,128)(2,1)S(1)}, bf16[128,2048]{1,0:T(8,128)(2,1)}, u32[]{:S(2)}) copy-start(bf16[128,2048]{1,0:T(8,128)(2,1)} %copy-done.1) | copy-start | bytes 1572868
  138.0 2.5 %copy-start.3 = (bf16[128,2048]{1,0:T(8,128)(2,1)}, bf16[128,2048]{1,0:T(8,128)(2,1)S(1)}, u32[]{:S(2)}) copy-start(bf16[128,2048]{1,0:T(8,128)(2,1)S(1)} %all_gather.7) | copy-start | bytes 1572868
  139.5 1.0 copy-start.11
  142.8 31.2 %all-to-all-start.4 = ((bf16[8,8,4,32,128]{4,3,2,1,0:T(8,128)(2,1)}), bf16[8,8,4,32,128]{4,3,2,1,0:T(8,128)(2,1)}, u32[]{:S(2)}, u32[]{:S(2)}) async-start(bf16[8,8,4,32,128]{4,3,2,1,0:T(8,128)(2,1)} %copy_bitcast_fusion), calls=%async_computation.4 | async-start | bytes 4194304 | tf_op jit(solution)/shard_map/all_to_all | solution.py:24
  148.3 7.3 %copy-start.4 = (bf16[128,2048]{1,0:T(8,128)(2,1)S(1)}, bf16[128,2048]{1,0:T(8,128)(2,1)}, u32[]{:S(2)}) copy-start(bf16[128,2048]{1,0:T(8,128)(2,1)} %copy-done.3) | copy-start | bytes 1572868
  148.3 7.3 %copy-start.7 = (bf16[1,128,2048]{2,1,0:T(8,128)(2,1)S(1)}, bf16[1,128,2048]{2,1,0:T(8,128)(2,1)}, u32[]{:S(2)}) copy-start(bf16[1,128,2048]{2,1,0:T(8,128)(2,1)} %param.6) | copy-start | bytes 1572868
  148.3 7.3 %copy-start.9 = (bf16[1,128,2048]{2,1,0:T(8,128)(2,1)S(1)}, bf16[1,128,2048]{2,1,0:T(8,128)(2,1)}, u32[]{:S(2)}) copy-start(bf16[1,128,2048]{2,1,0:T(8,128)(2,1)} %param.7) | copy-start | bytes 1572868
  148.6 3.9 %collective-permute-start.4 = (bf16[128,2048]{1,0:T(8,128)(2,1)S(1)}, bf16[128,2048]{1,0:T(8,128)(2,1)S(1)}, u32[]{:S(2)}, u32[]{:S(2)}) collective-permute-start(bf16[128,2048]{1,0:T(8,128)(2,1)S(1)} %get-tuple-element.54), channel_id=1, source_target_pairs={{0,1},{1,0},{2,3},{3,2},{4,5},{5,4},{6,7},{7,6},{8,9},{9,8},{10,11... | collective-permute-start | bytes 1572872 | tf_op jit(solution)/shard_map/ppermute | solution.py:40
  152.8 16.1 %collective-permute-start.5 = (bf16[128,2048]{1,0:T(8,128)(2,1)S(1)}, bf16[128,2048]{1,0:T(8,128)(2,1)S(1)}, u32[]{:S(2)}, u32[]{:S(2)}) collective-permute-start(bf16[128,2048]{1,0:T(8,128)(2,1)S(1)} %add_convert_fusion.2), channel_id=1, source_target_pairs={{0,2},{2,0},{4,6},{6,4},{1,3},{3,1},{5,7},{7,5},{8,10},{10,8},{12,... | collective-permute-start | bytes 1572872 | tf_op jit(solution)/shard_map/ppermute | solution.py:44
  174.0 16.7 %collective-permute-start.6 = (bf16[128,2048]{1,0:T(8,128)(2,1)S(1)}, bf16[128,2048]{1,0:T(8,128)(2,1)S(1)}, u32[]{:S(2)}, u32[]{:S(2)}) collective-permute-start(bf16[128,2048]{1,0:T(8,128)(2,1)S(1)} %add_convert_fusion.1), channel_id=1, source_target_pairs={{0,6},{2,4},{4,2},{6,0},{1,7},{3,5},{5,3},{7,1},{8,14},{10,12},{12... | collective-permute-start | bytes 1572872 | tf_op jit(solution)/shard_map/ppermute | solution.py:44
  180.7 27.5 %all-to-all-start.5 = ((bf16[8,4,32,128]{3,2,1,0:T(8,128)(2,1)}), bf16[8,4,32,128]{3,2,1,0:T(8,128)(2,1)S(1)}, u32[]{:S(2)}, u32[]{:S(2)}) async-start(bf16[8,4,32,128]{3,2,1,0:T(8,128)(2,1)} %reduce_sum.121), calls=%async_computation.5 | async-start | bytes 524288 | tf_op jit(solution)/shard_map/all_to_all | solution.py:24
  190.8 18.6 %collective-permute-start.7 = (bf16[128,2048]{1,0:T(8,128)(2,1)S(1)}, bf16[128,2048]{1,0:T(8,128)(2,1)S(1)}, u32[]{:S(2)}, u32[]{:S(2)}) collective-permute-start(bf16[128,2048]{1,0:T(8,128)(2,1)S(1)} %add_convert_fusion.tile), channel_id=1, source_target_pairs={{0,1},{1,0},{2,3},{3,2},{4,5},{5,4},{6,7},{7,6},{8,9},{9,8},{10,11... | collective-permute-start | bytes 1572872 | tf_op jit(solution)/shard_map/ppermute | solution.py:40

commit v8 on v7

--- a/solution.py
+++ b/solution.py
@@ -138,7 +138,7 @@
     tile = jnp.where(core == 0, h_part, g_part) + from_core(jnp.where(core == 0, g_part, h_part))
     tile = tile + from_pair(tile, 1)
 
-    near = spread(jnp.concatenate([w_qkv, w_out.T[None]], 0), "zp", NP)
+    near = lax.all_gather(jnp.concatenate([w_qkv, w_out.T[None]], 0), "zp")
     near, tile = lax.optimization_barrier((near, tile))
     w = spread(near, NEAR, NN).transpose(2, 1, 0, 3, 4).reshape(4, D, HD)
     tile = tile + from_pair(tile, 3)
@@ -187,12 +187,14 @@
     terms, tile, base_h, base_g = lax.optimization_barrier((terms, tile, base_h, base_g))
 
     part = jnp.sum(terms.astype(F32), 0).astype(BF)
-    shard = jnp.sum(swap(part, "zp").astype(F32), 0)
+    shards = swap(part, "zp")
 
     tile = add(tile, from_pair(tile, 3))
     other = from_core(tile)
     flags = jnp.stack([core, mine.astype(jnp.int32)])
     hidden_out, grad_in = last_step(flags, tile, other, base_h, base_g, h1, inv2, gain)
+    shards, hidden_out, grad_in = lax.optimization_barrier((shards, hidden_out, grad_in))
+    shard = jnp.sum(shards.astype(F32), 0)
     return (hidden_out[None], grad_in[None], shard[:3], shard[3].T)
 
 

time: 213 us -> 210 us (0.986)
  blocking collectives: 39.2 us -> 75 us
  waiting for transfers between devices: 80.3 us -> 54.2 us
  starting transfers between devices: 55.2 us -> 43.2 us
    all_gather x0 -> x1, blocking collectives: none -> 35.8 us  [on_device(): near = lax.all_gather(jnp.concatenate([w_qkv, w_out.T[None]], 0), 'zp')]
    ppermute x4, waiting for transfers between devices: 43.6 us -> 24.2 us  [from_pair(): return lax.ppermute(x, 'x', [(i, i ^ bit) for i in range(CTX // 2)])]
    all_to_all x5 -> x4, starting transfers between devices: 35.2 us -> 22.5 us  [swap(): return lax.all_to_all(x, axis, 0, 0)]
    all_to_all x5 -> x4, waiting for transfers between devices: 34 us -> 24.3 us  [swap(): return lax.all_to_all(x, axis, 0, 0)]
    ppermute x4, waiting for transfers between devices: 2.71 us -> 5.68 us  [from_core(): return lax.ppermute(x, 'core', [(0, 1), (1, 0)])]
  transfers between devices with their start and end apart: 13 -> 12, of which waited for: 11 -> 11; matrix products, arithmetic and copies ran while one was open for 6% -> 5% of each run, Pallas kernels for 0% -> 1%
where the time goes in v8:
time: 210 us; the launch traced here: 209 us
  blocking collectives  75 us (36%)
  waiting for transfers between devices  54.2 us (26%)
  starting transfers between devices  43.2 us (21%)
  other arithmetic  17.3 us (8%)
  matrix products  9.6 us (5%)
  local copies, waits for them, and re-layouts  5.62 us (3%)
  Pallas kernels  2.63 us (1%)
    all_gather x1, blocking collectives, on_device(): near = lax.all_gather(jnp.concatenate([w_qkv, w_out.T[None]], 0), 'zp')  35.8 us
    all_gather x2, blocking collectives, all_rows(): return lax.all_gather(chunk, CONTEXT, tiled=True)  26.2 us
    all_to_all x4, waiting for transfers between devices, swap(): return lax.all_to_all(x, axis, 0, 0)  24.3 us
    ppermute x4, waiting for transfers between devices, from_pair(): return lax.ppermute(x, 'x', [(i, i ^ bit) for i in range(CTX // 2)])  24.2 us
    all_to_all x4, starting transfers between devices, swap(): return lax.all_to_all(x, axis, 0, 0)  22.5 us
    all_to_all x1, blocking collectives, swap(): return lax.all_to_all(x, axis, 0, 0)  12.9 us
    ppermute x4, starting transfers between devices, from_pair(): return lax.ppermute(x, 'x', [(i, i ^ bit) for i in range(CTX // 2)])  12.5 us
    dot_general x32, matrix products, dot(): return lax.dot_general(a, b, (dims, ((), ())), preferred_element_type=F32)  9.6 us
  transfers between devices with their start and end apart: 12, of which 11 were waited for; matrix products, arithmetic and copies ran while one was open for 5% of the time, Pallas kernels for 1%

profile of v8, /device:TPU:6, one launch (start us, length us, event | category | flops | bytes accessed | tf_op | source)
XLA Modules:
  0.0 209.3 jit_solution(130269618014895483)
XLA Ops:
  0.7 1.2 fusion.55
  1.9 1.9 broadcast_select_fusion.3
  3.8 1.9 collective-permute-start
  5.7 1.9 collective-permute-done
  7.6 1.9 select_add_fusion
  9.5 2.7 %collective-permute-start.1 = (bf16[128,2048]{1,0:T(8,128)(2,1)S(1)}, bf16[128,2048]{1,0:T(8,128)(2,1)S(1)}, u32[]{:S(2)}, u32[]{:S(2)}) collective-permute-start(bf16[128,2048]{1,0:T(8,128)(2,1)S(1)} %select_add_fusion), channel_id=1, source_target_pairs={{0,2},{2,0},{4,6},{6,4},{1,3},{3,1},{5,7},{7,5},{8,10},{10,8},{12,... | collective-permute-start | bytes 1572872 | tf_op jit(solution)/shard_map/ppermute | solution.py:44
  12.3 35.8 %all-gather = bf16[32,32,128]{2,1,0:T(8,128)(2,1)S(1)} all-gather(bf16[4,32,128]{2,1,0:T(8,128)(2,1)S(1)} %pad_maximum_fusion.5), channel_id=2, replica_groups=mesh['zp'=8,'zq'=2,'y'=4,'x'=4,'core'=2] {'zp'}, dimensions={0}, use_global_device_ids=true | all-gather | bytes 294912 | tf_op jit(solution)/shard_map/all_gather | solution.py:141
  48.3 1.8 broadcast_in_dim.16
  50.1 5.4 %all-to-all-start = ((bf16[8,8,4,32,128]{4,3,1,2,0:T(8,128)(2,1)}), bf16[8,8,4,32,128]{4,3,1,2,0:T(8,128)(2,1)S(1)}, u32[]{:S(2)}, u32[]{:S(2)}) async-start(bf16[8,8,4,32,128]{4,3,1,2,0:T(8,128)(2,1)} %broadcast_in_dim.16), calls=%async_computation | async-start | bytes 4194304 | tf_op jit(solution)/shard_map/all_to_all | solution.py:24
  55.5 3.0 %collective-permute-start.2 = (bf16[128,2048]{1,0:T(8,128)(2,1)S(1)}, bf16[128,2048]{1,0:T(8,128)(2,1)S(1)}, u32[]{:S(2)}, u32[]{:S(2)}) collective-permute-start(bf16[128,2048]{1,0:T(8,128)(2,1)S(1)} %add.82), channel_id=1, source_target_pairs={{0,6},{2,4},{4,2},{6,0},{1,7},{3,5},{5,3},{7,1},{8,14},{10,12},{12... | collective-permute-start | bytes 1572872 | tf_op jit(solution)/shard_map/ppermute | solution.py:44
  58.6 9.2 %collective-permute-done.2 = bf16[128,2048]{1,0:T(8,128)(2,1)S(1)} collective-permute-done((bf16[128,2048]{1,0:T(8,128)(2,1)S(1)}, bf16[128,2048]{1,0:T(8,128)(2,1)S(1)}, u32[]{:S(2)}, u32[]{:S(2)}) %collective-permute-start.2) | collective-permute-done | bytes 524320 | tf_op jit(solution)/shard_map/ppermute | solution.py:44
  67.9 1.9 collective-permute-start.3
  69.9 0.6 compare_reduce_fusion
  70.5 1.2 collective-permute-done.3
  72.7 2.5 %all-to-all-done = bf16[8,8,4,32,128]{4,3,1,2,0:T(8,128)(2,1)S(1)} async-done(((bf16[8,8,4,32,128]{4,3,1,2,0:T(8,128)(2,1)}), bf16[8,8,4,32,128]{4,3,1,2,0:T(8,128)(2,1)S(1)}, u32[]{:S(2)}, u32[]{:S(2)}) %all-to-all-start) | async-done | bytes 2097184 | tf_op jit(solution)/shard_map/all_to_all | solution.py:24
  75.2 0.6 copy.54
  75.8 0.5 fusion.54
  77.6 1.1 convolution_convert_fusion.5
  78.7 5.1 %all-to-all-start.1 = ((bf16[8,16,2048]{2,1,0:T(8,128)(2,1)}), bf16[8,16,2048]{2,1,0:T(8,128)(2,1)S(1)}, u32[]{:S(2)}, u32[]{:S(2)}) async-start(bf16[8,16,2048]{2,1,0:T(8,128)(2,1)} %bitcast.132), calls=%async_computation.1 | async-start | bytes 1048576 | tf_op jit(solution)/shard_map/all_to_all | solution.py:24
  83.9 2.5 %broadcast_select_fusion.4 = (bf16[128,2048]{1,0:T(8,128)(2,1)S(1)}, bf16[128,2048]{1,0:T(8,128)(2,1)}) fusion(pred[]{:T(512)} %compare_reduce_fusion, bf16[128,2048]{1,0:T(8,128)(2,1)} %copy-done.10, bf16[128,2048]{1,0:T(8,128)(2,1)} %copy-done.5, pred[]{:T(512)S(6)} %eq.2), kind=kLoop, calls=%fused_computation.73 | loop fusion | flops 524288 | bytes 2097154 | tf_op jit(solution)/shard_map/jit(_where)/select_n | solution.py:158
  86.4 0.8 copy-done.8
  87.5 4.7 %all-to-all-done.1 = bf16[8,16,2048]{2,1,0:T(8,128)(2,1)S(1)} async-done(((bf16[8,16,2048]{2,1,0:T(8,128)(2,1)}), bf16[8,16,2048]{2,1,0:T(8,128)(2,1)S(1)}, u32[]{:S(2)}, u32[]{:S(2)}) %all-to-all-start.1) | async-done | bytes 524320 | tf_op jit(solution)/shard_map/all_to_all | solution.py:24
  92.3 13.1 %all_gather.14 = bf16[128,2048]{1,0:T(8,128)(2,1)S(1)} all-gather(bf16[16,2048]{1,0:T(8,128)(2,1)S(1)} %fusion.26), channel_id=1, replica_groups=mesh['zp'=8,'zq'=2,'y'=4,'x'=4,'core'=2] {'x','core'}, dimensions={0}, use_global_device_ids=true | all-gather | bytes 589824 | tf_op jit(solution)/shard_map/all_gather | solution.py:53
  105.6 0.8 fusion.19
  109.4 12.9 %all_to_all.25 = bf16[8,16,2048]{2,1,0:T(8,128)(2,1)S(1)} all-to-all(bf16[8,16,2048]{2,1,0:T(8,128)(2,1)S(1)} %bitcast.133), channel_id=1, replica_groups=mesh['zp'=8,'zq'=2,'y'=4,'x'=4,'core'=2] {'x','core'}, dimensions={0} | all-to-all | bytes 1048576 | tf_op jit(solution)/shard_map/all_to_all | solution.py:24
  122.5 0.9 fusion.24
  123.5 13.1 %all_gather.15 = bf16[128,2048]{1,0:T(8,128)(2,1)S(1)} all-gather(bf16[16,2048]{1,0:T(8,128)(2,1)S(1)} %fusion.24), channel_id=1, replica_groups=mesh['zp'=8,'zq'=2,'y'=4,'x'=4,'core'=2] {'x','core'}, dimensions={0}, use_global_device_ids=true | all-gather | bytes 589824 | tf_op jit(solution)/shard_map/all_gather | solution.py:53
  137.6 0.5 convolution_convert_fusion.4
  138.1 0.5 convolution_convert_fusion.3
  138.6 0.5 convolution_convert_fusion.2
  139.6 1.7 copy_bitcast_fusion
  141.4 4.5 %all-to-all-start.3 = ((bf16[8,8,4,32,128]{4,3,2,1,0:T(8,128)(2,1)}), bf16[8,8,4,32,128]{4,3,2,1,0:T(8,128)(2,1)}, u32[]{:S(2)}, u32[]{:S(2)}) async-start(bf16[8,8,4,32,128]{4,3,2,1,0:T(8,128)(2,1)} %copy_bitcast_fusion), calls=%async_computation.3 | async-start | bytes 4194304 | tf_op jit(solution)/shard_map/all_to_all | solution.py:24
  147.2 2.4 %collective-permute-start.4 = (bf16[128,2048]{1,0:T(8,128)(2,1)S(1)}, bf16[128,2048]{1,0:T(8,128)(2,1)S(1)}, u32[]{:S(2)}, u32[]{:S(2)}) collective-permute-start(bf16[128,2048]{1,0:T(8,128)(2,1)S(1)} %get-tuple-element.60), channel_id=1, source_target_pairs={{0,1},{1,0},{2,3},{3,2},{4,5},{5,4},{6,7},{7,6},{8,9},{9,8},{10,11... | collective-permute-start | bytes 1572872 | tf_op jit(solution)/shard_map/ppermute | solution.py:40
  149.6 1.5 collective-permute-done.4
  151.4 2.8 %collective-permute-start.5 = (bf16[128,2048]{1,0:T(8,128)(2,1)S(1)}, bf16[128,2048]{1,0:T(8,128)(2,1)S(1)}, u32[]{:S(2)}, u32[]{:S(2)}) collective-permute-start(bf16[128,2048]{1,0:T(8,128)(2,1)S(1)} %add_convert_fusion.2), channel_id=1, source_target_pairs={{0,2},{2,0},{4,6},{6,4},{1,3},{3,1},{5,7},{7,5},{8,10},{10,8},{12,... | collective-permute-start | bytes 1572872 | tf_op jit(solution)/shard_map/ppermute | solution.py:44
  154.2 0.8 bitcast_select_fusion
  155.0 12.4 %collective-permute-done.5 = bf16[128,2048]{1,0:T(8,128)(2,1)S(1)} collective-permute-done((bf16[128,2048]{1,0:T(8,128)(2,1)S(1)}, bf16[128,2048]{1,0:T(8,128)(2,1)S(1)}, u32[]{:S(2)}, u32[]{:S(2)}) %collective-permute-start.5) | collective-permute-done | bytes 524320 | tf_op jit(solution)/shard_map/ppermute | solution.py:44
  167.6 5.0 %all-to-all-done.3 = bf16[8,8,4,32,128]{4,3,2,1,0:T(8,128)(2,1)} async-done(((bf16[8,8,4,32,128]{4,3,2,1,0:T(8,128)(2,1)}), bf16[8,8,4,32,128]{4,3,2,1,0:T(8,128)(2,1)}, u32[]{:S(2)}, u32[]{:S(2)}) %all-to-all-start.3) | async-done | bytes 2097184 | tf_op jit(solution)/shard_map/all_to_all | solution.py:24
  172.6 4.0 %collective-permute-start.6 = (bf16[128,2048]{1,0:T(8,128)(2,1)S(1)}, bf16[128,2048]{1,0:T(8,128)(2,1)S(1)}, u32[]{:S(2)}, u32[]{:S(2)}) collective-permute-start(bf16[128,2048]{1,0:T(8,128)(2,1)S(1)} %add_convert_fusion.1), channel_id=1, source_target_pairs={{0,6},{2,4},{4,2},{6,0},{1,7},{3,5},{5,3},{7,1},{8,14},{10,12},{12... | collective-permute-start | bytes 1572872 | tf_op jit(solution)/shard_map/ppermute | solution.py:44
  176.5 2.8 %reduce_sum.121 = bf16[8,4,32,128]{3,2,1,0:T(8,128)(2,1)} reduce(bf16[8,8,4,32,128]{4,3,2,1,0:T(8,128)(2,1)} %all-to-all-done.3, bf16[]{:T(256)} %constant.46.clone.1), dimensions={0}, to_apply=%region_13.14 | reduce | flops 917504 | bytes 2359298 | tf_op jit(solution)/shard_map/reduce_sum | solution.py:189
  179.3 7.4 %all-to-all-start.4 = ((bf16[8,4,32,128]{3,2,1,0:T(8,128)(2,1)}), bf16[8,4,32,128]{3,2,1,0:T(8,128)(2,1)S(1)}, u32[]{:S(2)}, u32[]{:S(2)}) async-start(bf16[8,4,32,128]{3,2,1,0:T(8,128)(2,1)} %reduce_sum.121), calls=%async_computation.4 | async-start | bytes 524288 | tf_op jit(solution)/shard_map/all_to_all | solution.py:24
  186.7 2.5 %collective-permute-done.6 = bf16[128,2048]{1,0:T(8,128)(2,1)S(1)} collective-permute-done((bf16[128,2048]{1,0:T(8,128)(2,1)S(1)}, bf16[128,2048]{1,0:T(8,128)(2,1)S(1)}, u32[]{:S(2)}, u32[]{:S(2)}) %collective-permute-start.6) | collective-permute-done | bytes 524320 | tf_op jit(solution)/shard_map/ppermute | solution.py:44
  189.4 1.9 collective-permute-start.7
  192.2 1.0 collective-permute-done.7.other
  193.2 2.6 %shard_map.93 = (bf16[128,2048]{1,0:T(8,128)(2,1)}, bf16[128,2048]{1,0:T(8,128)(2,1)}) custom-call(s32[2]{0:T(128)S(1)} %pad_add_fusion.flags, bf16[128,2048]{1,0:T(8,128)(2,1)S(1)} %add_convert_fusion.tile, bf16[128,2048]{1,0:T(8,128)(2,1)S(1)} %collective-permute-done.7.other, bf16[128,2048]{1,0:T(8,128)(2,1)S(1)} %get-tuple-element.31.base_h, ...), custom_call_target="tpu_custom_call" | custom-call | tf_op jit(solution)/shard_map/pallas_call | solution.py:112
  195.8 12.2 %all-to-all-done.4 = bf16[8,4,32,128]{3,2,1,0:T(8,128)(2,1)S(1)} async-done(((bf16[8,4,32,128]{3,2,1,0:T(8,128)(2,1)}), bf16[8,4,32,128]{3,2,1,0:T(8,128)(2,1)S(1)}, u32[]{:S(2)}, u32[]{:S(2)}) %all-to-all-start.4) | async-done | bytes 262176 | tf_op jit(solution)/shard_map/all_to_all | solution.py:24
  208.1 0.6 slice.44
  208.7 0.6 slice_bitcast_fusion
  (79 shorter events, 9.7 us)
Async XLA Ops:
  0.6 11.7 %copy-start.12 = (bf16[128,32]{0,1:T(8,128)(2,1)S(1)}, bf16[128,32]{0,1:T(8,128)(2,1)}, u32[]{:S(2)}) copy-start(bf16[128,32]{0,1:T(8,128)(2,1)} %param.10) | copy-start | bytes 24580
  0.6 11.7 %copy-start.11 = (bf16[3,32,128]{2,1,0:T(8,128)(2,1)S(1)}, bf16[3,32,128]{2,1,0:T(8,128)(2,1)}, u32[]{:S(2)}) copy-start(bf16[3,32,128]{2,1,0:T(8,128)(2,1)} %param.9) | copy-start | bytes 73732
  3.8 3.8 %collective-permute-start = (bf16[128,2048]{1,0:T(8,128)(2,1)S(1)}, bf16[128,2048]{1,0:T(8,128)(2,1)S(1)}, u32[]{:S(2)}, u32[]{:S(2)}) collective-permute-start(bf16[128,2048]{1,0:T(8,128)(2,1)S(1)} %broadcast_select_fusion.3), channel_id=1, source_target_pairs={{0,1},{1,0},{2,3},{3,2},{4,5},{5,4},{6,7},{7,6},{8,9},{9,8},{10,11... | collective-permute-start | bytes 1572872 | tf_op jit(solution)/shard_map/ppermute | solution.py:40
  9.5 38.6 %collective-permute-start.1 = (bf16[128,2048]{1,0:T(8,128)(2,1)S(1)}, bf16[128,2048]{1,0:T(8,128)(2,1)S(1)}, u32[]{:S(2)}, u32[]{:S(2)}) collective-permute-start(bf16[128,2048]{1,0:T(8,128)(2,1)S(1)} %select_add_fusion), channel_id=1, source_target_pairs={{0,2},{2,0},{4,6},{6,4},{1,3},{3,1},{5,7},{7,5},{8,10},{10,8},{12,... | collective-permute-start | bytes 1572872 | tf_op jit(solution)/shard_map/ppermute | solution.py:44
  50.1 19.7 %copy-start.13 = (s32[1,8]{1,0:T(1,128)S(1)}, s32[1,8]{1,0:T(1,128)}, u32[]{:S(2)}) copy-start(s32[1,8]{1,0:T(1,128)} %param.8) | copy-start | bytes 100
  50.1 25.1 %all-to-all-start = ((bf16[8,8,4,32,128]{4,3,1,2,0:T(8,128)(2,1)}), bf16[8,8,4,32,128]{4,3,1,2,0:T(8,128)(2,1)S(1)}, u32[]{:S(2)}, u32[]{:S(2)}) async-start(bf16[8,8,4,32,128]{4,3,1,2,0:T(8,128)(2,1)} %broadcast_in_dim.16), calls=%async_computation | async-start | bytes 4194304 | tf_op jit(solution)/shard_map/all_to_all | solution.py:24
  55.5 17.0 %copy-start = (f32[2048]{0:T(1024)S(1)}, f32[2048]{0:T(1024)}, u32[]{:S(2)}) copy-start(f32[2048]{0:T(1024)} %param.11) | copy-start | bytes 24580
  55.5 12.3 %collective-permute-start.2 = (bf16[128,2048]{1,0:T(8,128)(2,1)S(1)}, bf16[128,2048]{1,0:T(8,128)(2,1)S(1)}, u32[]{:S(2)}, u32[]{:S(2)}) collective-permute-start(bf16[128,2048]{1,0:T(8,128)(2,1)S(1)} %add.82), channel_id=1, source_target_pairs={{0,6},{2,4},{4,2},{6,0},{1,7},{3,5},{5,3},{7,1},{8,14},{10,12},{12... | collective-permute-start | bytes 1572872 | tf_op jit(solution)/shard_map/ppermute | solution.py:44
  67.9 4.1 %copy-start.5 = (bf16[128,2048]{1,0:T(8,128)(2,1)}, bf16[128,2048]{1,0:T(8,128)(2,1)S(1)}, u32[]{:S(2)}) copy-start(bf16[128,2048]{1,0:T(8,128)(2,1)S(1)} %add.83) | copy-start | bytes 1572868
  67.9 3.8 %collective-permute-start.3 = (bf16[128,2048]{1,0:T(8,128)(2,1)S(1)}, bf16[128,2048]{1,0:T(8,128)(2,1)S(1)}, u32[]{:S(2)}, u32[]{:S(2)}) collective-permute-start(bf16[128,2048]{1,0:T(8,128)(2,1)S(1)} %add.83), channel_id=1, source_target_pairs={{0,1},{1,0},{2,3},{3,2},{4,5},{5,4},{6,7},{7,6},{8,9},{9,8},{10,11... | collective-permute-start | bytes 1572872 | tf_op jit(solution)/shard_map/ppermute | solution.py:40
  71.7 0.8 copy-start.10
  72.7 4.2 %copy-start.1 = (bf16[128,2048]{1,0:T(8,128)(2,1)}, bf16[128,2048]{1,0:T(8,128)(2,1)S(1)}, u32[]{:S(2)}) copy-start(bf16[128,2048]{1,0:T(8,128)(2,1)S(1)} %fusion.12) | copy-start | bytes 1572868
  78.7 13.4 %all-to-all-start.1 = ((bf16[8,16,2048]{2,1,0:T(8,128)(2,1)}), bf16[8,16,2048]{2,1,0:T(8,128)(2,1)S(1)}, u32[]{:S(2)}, u32[]{:S(2)}) async-start(bf16[8,16,2048]{2,1,0:T(8,128)(2,1)} %bitcast.132), calls=%async_computation.1 | async-start | bytes 1048576 | tf_op jit(solution)/shard_map/all_to_all | solution.py:24
  86.4 0.8 copy-start.8
  122.3 15.3 %copy-start.2 = (bf16[128,2048]{1,0:T(8,128)(2,1)S(1)}, bf16[128,2048]{1,0:T(8,128)(2,1)}, u32[]{:S(2)}) copy-start(bf16[128,2048]{1,0:T(8,128)(2,1)} %copy-done.1) | copy-start | bytes 1572868
  136.6 2.5 %copy-start.3 = (bf16[128,2048]{1,0:T(8,128)(2,1)}, bf16[128,2048]{1,0:T(8,128)(2,1)S(1)}, u32[]{:S(2)}) copy-start(bf16[128,2048]{1,0:T(8,128)(2,1)S(1)} %all_gather.15) | copy-start | bytes 1572868
  138.1 1.0 copy-start.9
  141.4 31.2 %all-to-all-start.3 = ((bf16[8,8,4,32,128]{4,3,2,1,0:T(8,128)(2,1)}), bf16[8,8,4,32,128]{4,3,2,1,0:T(8,128)(2,1)}, u32[]{:S(2)}, u32[]{:S(2)}) async-start(bf16[8,8,4,32,128]{4,3,2,1,0:T(8,128)(2,1)} %copy_bitcast_fusion), calls=%async_computation.3 | async-start | bytes 4194304 | tf_op jit(solution)/shard_map/all_to_all | solution.py:24
  146.8 7.3 %copy-start.4 = (bf16[128,2048]{1,0:T(8,128)(2,1)S(1)}, bf16[128,2048]{1,0:T(8,128)(2,1)}, u32[]{:S(2)}) copy-start(bf16[128,2048]{1,0:T(8,128)(2,1)} %copy-done.3) | copy-start | bytes 1572868
  146.8 7.3 %copy-start.6 = (bf16[1,128,2048]{2,1,0:T(8,128)(2,1)S(1)}, bf16[1,128,2048]{2,1,0:T(8,128)(2,1)}, u32[]{:S(2)}) copy-start(bf16[1,128,2048]{2,1,0:T(8,128)(2,1)} %param.6) | copy-start | bytes 1572868
  146.9 7.3 %copy-start.7 = (bf16[1,128,2048]{2,1,0:T(8,128)(2,1)S(1)}, bf16[1,128,2048]{2,1,0:T(8,128)(2,1)}, u32[]{:S(2)}) copy-start(bf16[1,128,2048]{2,1,0:T(8,128)(2,1)} %param.7) | copy-start | bytes 1572868
  147.2 3.9 %collective-permute-start.4 = (bf16[128,2048]{1,0:T(8,128)(2,1)S(1)}, bf16[128,2048]{1,0:T(8,128)(2,1)S(1)}, u32[]{:S(2)}, u32[]{:S(2)}) collective-permute-start(bf16[128,2048]{1,0:T(8,128)(2,1)S(1)} %get-tuple-element.60), channel_id=1, source_target_pairs={{0,1},{1,0},{2,3},{3,2},{4,5},{5,4},{6,7},{7,6},{8,9},{9,8},{10,11... | collective-permute-start | bytes 1572872 | tf_op jit(solution)/shard_map/ppermute | solution.py:40
  151.4 16.1 %collective-permute-start.5 = (bf16[128,2048]{1,0:T(8,128)(2,1)S(1)}, bf16[128,2048]{1,0:T(8,128)(2,1)S(1)}, u32[]{:S(2)}, u32[]{:S(2)}) collective-permute-start(bf16[128,2048]{1,0:T(8,128)(2,1)S(1)} %add_convert_fusion.2), channel_id=1, source_target_pairs={{0,2},{2,0},{4,6},{6,4},{1,3},{3,1},{5,7},{7,5},{8,10},{10,8},{12,... | collective-permute-start | bytes 1572872 | tf_op jit(solution)/shard_map/ppermute | solution.py:44
  172.6 16.7 %collective-permute-start.6 = (bf16[128,2048]{1,0:T(8,128)(2,1)S(1)}, bf16[128,2048]{1,0:T(8,128)(2,1)S(1)}, u32[]{:S(2)}, u32[]{:S(2)}) collective-permute-start(bf16[128,2048]{1,0:T(8,128)(2,1)S(1)} %add_convert_fusion.1), channel_id=1, source_target_pairs={{0,6},{2,4},{4,2},{6,0},{1,7},{3,5},{5,3},{7,1},{8,14},{10,12},{12... | collective-permute-start | bytes 1572872 | tf_op jit(solution)/shard_map/ppermute | solution.py:44
  179.3 28.7 %all-to-all-start.4 = ((bf16[8,4,32,128]{3,2,1,0:T(8,128)(2,1)}), bf16[8,4,32,128]{3,2,1,0:T(8,128)(2,1)S(1)}, u32[]{:S(2)}, u32[]{:S(2)}) async-start(bf16[8,4,32,128]{3,2,1,0:T(8,128)(2,1)} %reduce_sum.121), calls=%async_computation.4 | async-start | bytes 524288 | tf_op jit(solution)/shard_map/all_to_all | solution.py:24
  189.4 3.8 %collective-permute-start.7 = (bf16[128,2048]{1,0:T(8,128)(2,1)S(1)}, bf16[128,2048]{1,0:T(8,128)(2,1)S(1)}, u32[]{:S(2)}, u32[]{:S(2)}) collective-permute-start(bf16[128,2048]{1,0:T(8,128)(2,1)S(1)} %add_convert_fusion.tile), channel_id=1, source_target_pairs={{0,1},{1,0},{2,3},{3,2},{4,5},{5,4},{6,7},{7,6},{8,9},{9,8},{10,11... | collective-permute-start | bytes 1572872 | tf_op jit(solution)/shard_map/ppermute | solution.py:40

commit v9 on v8

--- a/solution.py
+++ b/solution.py
@@ -95,6 +95,81 @@
     return inv * u - x32 * inv**3 * jnp.mean(x32 * u, -1, keepdims=True)
 
 
+def first_kernel(places, depth, h, g, w_qkv, w_out, sent, shards):
+    first, live = places[0] == 0, depth[0, places[1]] >= 2
+    tile = jnp.where(first, g[...], h[...])
+    sent[...] = jnp.where(live, tile, jnp.zeros_like(tile))
+    for i in range(NP):
+        shards[i, :3] = w_qkv[...]
+        shards[i, 3] = w_out[...]
+
+
+def first_step(places, depth, h, g, w_qkv, w_out):
+    scalars = pl.BlockSpec(memory_space=pltpu.SMEM)
+    return pl.pallas_call(
+        first_kernel,
+        in_specs=[scalars, scalars] + [pl.BlockSpec(memory_space=pltpu.VMEM)] * 4,
+        out_specs=[pl.BlockSpec(memory_space=pltpu.VMEM)] * 2,
+        out_shape=[
+            jax.ShapeDtypeStruct((TILE, D), BF),
+            jax.ShapeDtypeStruct((NP, 4, 32, HD), BF),
+        ],
+        compiler_params=pltpu.CompilerParams(vmem_limit_bytes=16 * 2**20),
+    )(places, depth, h, g, w_qkv, w_out)
+
+
+def copies_kernel(near, out):
+    for t in range(4):
+        out[0, t] = near[:, t]
+
+
+def copies(near):
+    return pl.pallas_call(
+        copies_kernel,
+        grid=(NN,),
+        in_specs=[pl.BlockSpec((NP, 4, 32, HD), lambda i: (0, 0, 0, 0))],
+        out_specs=pl.BlockSpec((1, 4, NP, 32, HD), lambda i: (i, 0, 0, 0, 0)),
+        out_shape=jax.ShapeDtypeStruct((NN, 4, NP, 32, HD), BF),
+        compiler_params=pltpu.CompilerParams(vmem_limit_bytes=16 * 2**20),
+    )(near)
+
+
+def sum_kernel(terms, out):
+    total = terms[0].astype(F32)
+    for i in range(1, NN):
+        total = total + terms[i].astype(F32)
+    out[...] = total.astype(BF)
+
+
+def sum_terms(terms):
+    return pl.pallas_call(
+        sum_kernel,
+        grid=(NP // 2,),
+        in_specs=[pl.BlockSpec((NN, 2, 4, 32, HD), lambda i: (0, i, 0, 0, 0))],
+        out_specs=pl.BlockSpec((2, 4, 32, HD), lambda i: (i, 0, 0, 0)),
+        out_shape=jax.ShapeDtypeStruct((NP, 4, 32, HD), BF),
+        compiler_params=pltpu.CompilerParams(vmem_limit_bytes=16 * 2**20),
+    )(terms)
+
+
+def shards_kernel(terms, qkv, out):
+    total = terms[0].astype(F32)
+    for i in range(1, NP):
+        total = total + terms[i].astype(F32)
+    qkv[...] = total[:3]
+    out[...] = total[3]
+
+
+def weight_shards(terms):
+    return pl.pallas_call(
+        shards_kernel,
+        out_shape=[
+            jax.ShapeDtypeStruct((3, 32, HD), F32),
+            jax.ShapeDtypeStruct((32, HD), F32),
+        ],
+    )(terms)
+
+
 def last_kernel(flags, tile, other, base_h, base_g, h1, inv, gain, out_h, out_g):
     first, mine = flags[0] == 0, flags[1] == 1
     a, b = tile[...].astype(F32), other[...].astype(F32)
@@ -133,14 +208,15 @@
     tokens = ((0,), (0,))
     core = lax.axis_index("core")
     none = jnp.zeros_like(hidden_in[0])
-    h_part = jnp.where(mine, hidden_in[0], none)
-    g_part = jnp.where(mine, cotangent[0], none)
-    tile = jnp.where(core == 0, h_part, g_part) + from_core(jnp.where(core == 0, g_part, h_part))
+    places = jnp.stack([core, me])
+    sent, shards = first_step(places, tile_depth, hidden_in[0], cotangent[0], w_qkv, w_out.T)
+    kept = jnp.where(mine, jnp.where(core == 0, hidden_in[0], cotangent[0]), none)
+    tile = kept + from_core(sent)
     tile = tile + from_pair(tile, 1)
 
-    near = lax.all_gather(jnp.concatenate([w_qkv, w_out.T[None]], 0), "zp")
+    near = swap(shards, "zp")
     near, tile = lax.optimization_barrier((near, tile))
-    w = spread(near, NEAR, NN).transpose(2, 1, 0, 3, 4).reshape(4, D, HD)
+    w = swap(copies(near), NEAR).transpose(1, 2, 0, 3, 4).reshape(4, D, HD)
     tile = tile + from_pair(tile, 3)
     other = from_core(tile)
     h1, g3 = jnp.where(core == 0, tile, other), jnp.where(core == 0, other, tile)
@@ -184,18 +260,19 @@
     mixed3 = mixed3.astype(BF)
     tile = add(jnp.where(core == 0, mixed3, dnorm2), from_core(jnp.where(core == 0, dnorm2, mixed3)))
     tile = add(tile, from_pair(tile, 1))
-    terms, tile, base_h, base_g = lax.optimization_barrier((terms, tile, base_h, base_g))
-
-    part = jnp.sum(terms.astype(F32), 0).astype(BF)
+    pair = from_pair(tile, 3)
+
+    part = sum_terms(terms)
     shards = swap(part, "zp")
 
-    tile = add(tile, from_pair(tile, 3))
+    tile, pair, _ = lax.optimization_barrier((tile, pair, part))
+    tile = add(tile, pair)
     other = from_core(tile)
     flags = jnp.stack([core, mine.astype(jnp.int32)])
     hidden_out, grad_in = last_step(flags, tile, other, base_h, base_g, h1, inv2, gain)
     shards, hidden_out, grad_in = lax.optimization_barrier((shards, hidden_out, grad_in))
-    shard = jnp.sum(shards.astype(F32), 0)
-    return (hidden_out[None], grad_in[None], shard[:3], shard[3].T)
+    grad_qkv, grad_out = weight_shards(shards)
+    return (hidden_out[None], grad_in[None], grad_qkv, grad_out.T)
 
 
 def solution(mesh):

time: 210 us -> 215 us (1.024)
  blocking collectives: 75 us -> 39.1 us
  waiting for transfers between devices: 54.2 us -> 69.2 us
  starting transfers between devices: 43.2 us -> 56.5 us
  Pallas kernels: 2.63 us -> 10.2 us
  local copies, waits for them, and re-layouts: 5.62 us -> 8.42 us
    all_gather x1 -> x0, blocking collectives: 35.8 us -> none  [on_device(): near = lax.all_gather(jnp.concatenate([w_qkv, w_out.T[None]], 0), 'zp')]
    ppermute x4, waiting for transfers between devices: 24.2 us -> 42.3 us  [from_pair(): return lax.ppermute(x, 'x', [(i, i ^ bit) for i in range(CTX // 2)])]
    all_to_all x4 -> x5, starting transfers between devices: 22.5 us -> 36.7 us  [swap(): return lax.all_to_all(x, axis, 0, 0)]
    pallas_call x0 -> x4, Pallas kernels: none -> 7.56 us  [the longest x1 3.02 us: copies(): pl.pallas_call(copies_kernel, grid=(NN,), in_specs=[pl.BlockSpec((NP, 4,...]
    unnamed x28 -> x48, local copies, waits for them, and re-layouts: 1.36 us -> 7.79 us
    reduce_sum x2 -> x0, other arithmetic: 2.8 us -> none  [the longest x1 2.76 us: on_device(): part = jnp.sum(terms.astype(F32), 0).astype(BF)]
    all_to_all x4 -> x5, waiting for transfers between devices: 24.3 us -> 23.1 us  [swap(): return lax.all_to_all(x, axis, 0, 0)]
  transfers between devices with their start and end apart: 12 -> 13, of which waited for: 11 -> 11; matrix products, arithmetic and copies ran while one was open for 5% -> 6% of each run, Pallas kernels for 1% -> 2%
where the time goes in v9:
time: 215 us; the launch traced here: 212 us
  waiting for transfers between devices  69.2 us (32%)
  starting transfers between devices  56.5 us (26%)
  blocking collectives  39.1 us (18%)
  other arithmetic  16.4 us (8%)
  matrix products  10.7 us (5%)
  Pallas kernels  10.2 us (5%)
  local copies, waits for them, and re-layouts  8.42 us (4%)
    ppermute x4, waiting for transfers between devices, from_pair(): return lax.ppermute(x, 'x', [(i, i ^ bit) for i in range(CTX // 2)])  42.3 us
    all_to_all x5, starting transfers between devices, swap(): return lax.all_to_all(x, axis, 0, 0)  36.7 us
    all_gather x2, blocking collectives, all_rows(): return lax.all_gather(chunk, CONTEXT, tiled=True)  26.2 us
    all_to_all x5, waiting for transfers between devices, swap(): return lax.all_to_all(x, axis, 0, 0)  23.1 us
    all_to_all x1, blocking collectives, swap(): return lax.all_to_all(x, axis, 0, 0)  12.9 us
    ppermute x4, starting transfers between devices, from_pair(): return lax.ppermute(x, 'x', [(i, i ^ bit) for i in range(CTX // 2)])  11.9 us
    dot_general x32, matrix products, dot(): return lax.dot_general(a, b, (dims, ((), ())), preferred_element_type=F32)  10.7 us
    ppermute x4, starting transfers between devices, from_core(): return lax.ppermute(x, 'core', [(0, 1), (1, 0)])  7.98 us
  transfers between devices with their start and end apart: 13, of which 11 were waited for; matrix products, arithmetic and copies ran while one was open for 6% of the time, Pallas kernels for 2%

profile of v9, /device:TPU:6, one launch (start us, length us, event | category | flops | bytes accessed | tf_op | source)
XLA Modules:
  0.0 212.4 jit_solution(16926208488471729218)
XLA Ops:
  0.7 1.0 copy-done
  1.8 1.0 copy-done.2
  4.9 1.3 shard_map.93
  6.2 1.9 collective-permute-start
  8.1 15.1 %all-to-all-start = ((bf16[8,4,32,128]{3,2,1,0:T(8,128)(2,1)}), bf16[8,4,32,128]{3,2,1,0:T(8,128)(2,1)S(1)}, u32[]{:S(2)}, u32[]{:S(2)}) async-start(bf16[8,4,32,128]{3,2,1,0:T(8,128)(2,1)} %get-tuple-element.23), calls=%async_computation | async-start | bytes 524288 | tf_op jit(solution)/shard_map/all_to_all | solution.py:24
  23.2 1.2 fusion.55
  24.5 1.8 select_add_fusion
  26.2 2.7 %collective-permute-start.1 = (bf16[128,2048]{1,0:T(8,128)(2,1)S(1)}, bf16[128,2048]{1,0:T(8,128)(2,1)S(1)}, u32[]{:S(2)}, u32[]{:S(2)}) collective-permute-start(bf16[128,2048]{1,0:T(8,128)(2,1)S(1)} %select_add_fusion), channel_id=1, source_target_pairs={{0,2},{2,0},{4,6},{6,4},{1,3},{3,1},{5,7},{7,5},{8,10},{10,8},{12,... | collective-permute-start | bytes 1572872 | tf_op jit(solution)/shard_map/ppermute | solution.py:44
  29.0 13.2 %collective-permute-done.1 = bf16[128,2048]{1,0:T(8,128)(2,1)S(1)} collective-permute-done((bf16[128,2048]{1,0:T(8,128)(2,1)S(1)}, bf16[128,2048]{1,0:T(8,128)(2,1)S(1)}, u32[]{:S(2)}, u32[]{:S(2)}) %collective-permute-start.1) | collective-permute-done | bytes 524320 | tf_op jit(solution)/shard_map/ppermute | solution.py:44
  42.3 3.0 %all-to-all-done.near = bf16[8,4,32,128]{3,2,1,0:T(8,128)(2,1)S(1)} async-done(((bf16[8,4,32,128]{3,2,1,0:T(8,128)(2,1)}), bf16[8,4,32,128]{3,2,1,0:T(8,128)(2,1)S(1)}, u32[]{:S(2)}, u32[]{:S(2)}) %all-to-all-start) | async-done | bytes 262176 | tf_op jit(solution)/shard_map/all_to_all | solution.py:24
  45.3 3.0 %shard_map.94 = bf16[8,4,8,32,128]{4,3,2,1,0:T(8,128)(2,1)} custom-call(bf16[8,4,32,128]{3,2,1,0:T(8,128)(2,1)S(1)} %all-to-all-done.near), custom_call_target="tpu_custom_call" | custom-call | tf_op jit(solution)/shard_map/pallas_call | solution.py:127
  48.3 4.6 %all-to-all-start.1 = ((bf16[8,4,8,32,128]{4,3,2,1,0:T(8,128)(2,1)}), bf16[8,4,8,32,128]{4,3,2,1,0:T(8,128)(2,1)S(1)}, u32[]{:S(2)}, u32[]{:S(2)}) async-start(bf16[8,4,8,32,128]{4,3,2,1,0:T(8,128)(2,1)} %shard_map.94), calls=%async_computation.1 | async-start | bytes 4194304 | tf_op jit(solution)/shard_map/all_to_all | solution.py:24
  52.9 2.4 %collective-permute-start.2 = (bf16[128,2048]{1,0:T(8,128)(2,1)S(1)}, bf16[128,2048]{1,0:T(8,128)(2,1)S(1)}, u32[]{:S(2)}, u32[]{:S(2)}) collective-permute-start(bf16[128,2048]{1,0:T(8,128)(2,1)S(1)} %add.82), channel_id=1, source_target_pairs={{0,6},{2,4},{4,2},{6,0},{1,7},{3,5},{5,3},{7,1},{8,14},{10,12},{12... | collective-permute-start | bytes 1572872 | tf_op jit(solution)/shard_map/ppermute | solution.py:44
  55.3 14.2 %collective-permute-done.2 = bf16[128,2048]{1,0:T(8,128)(2,1)S(1)} collective-permute-done((bf16[128,2048]{1,0:T(8,128)(2,1)S(1)}, bf16[128,2048]{1,0:T(8,128)(2,1)S(1)}, u32[]{:S(2)}, u32[]{:S(2)}) %collective-permute-start.2) | collective-permute-done | bytes 524320 | tf_op jit(solution)/shard_map/ppermute | solution.py:44
  69.6 1.9 collective-permute-start.3
  72.2 1.2 collective-permute-done.3
  74.2 1.0 fusion.12
  75.2 3.8 %all-to-all-done.1 = bf16[8,4,8,32,128]{4,3,2,1,0:T(8,128)(2,1)S(1)} async-done(((bf16[8,4,8,32,128]{4,3,2,1,0:T(8,128)(2,1)}), bf16[8,4,8,32,128]{4,3,2,1,0:T(8,128)(2,1)S(1)}, u32[]{:S(2)}, u32[]{:S(2)}) %all-to-all-start.1) | async-done | bytes 2097184 | tf_op jit(solution)/shard_map/all_to_all | solution.py:24
  79.5 1.1 copy-done.15
  82.0 1.1 convolution_convert_fusion.5
  83.1 4.8 %all-to-all-start.2 = ((bf16[8,16,2048]{2,1,0:T(8,128)(2,1)}), bf16[8,16,2048]{2,1,0:T(8,128)(2,1)}, u32[]{:S(2)}, u32[]{:S(2)}) async-start(bf16[8,16,2048]{2,1,0:T(8,128)(2,1)} %bitcast.120), calls=%async_computation.2 | async-start | bytes 1048576 | tf_op jit(solution)/shard_map/all_to_all | solution.py:24
  87.9 2.5 %broadcast_select_fusion.5 = (bf16[128,2048]{1,0:T(8,128)(2,1)S(1)}, bf16[128,2048]{1,0:T(8,128)(2,1)}) fusion(pred[]{:T(512)} %compare_reduce_fusion, bf16[128,2048]{1,0:T(8,128)(2,1)} %copy-done.22, bf16[128,2048]{1,0:T(8,128)(2,1)S(1)} %copy-done.19, pred[]{:T(512)S(6)} %eq.2), kind=kLoop, calls=%fused_computation.68 | loop fusion | flops 524288 | bytes 2097154 | tf_op jit(solution)/shard_map/jit(_where)/select_n | solution.py:234
  90.4 0.8 copy-done.20
  91.5 4.7 %all-to-all-done.2 = bf16[8,16,2048]{2,1,0:T(8,128)(2,1)} async-done(((bf16[8,16,2048]{2,1,0:T(8,128)(2,1)}), bf16[8,16,2048]{2,1,0:T(8,128)(2,1)}, u32[]{:S(2)}, u32[]{:S(2)}) %all-to-all-start.2) | async-done | bytes 524320 | tf_op jit(solution)/shard_map/all_to_all | solution.py:24
  96.3 1.1 convert_reduce_fusion.1
  97.4 13.1 %all_gather.6 = bf16[128,2048]{1,0:T(8,128)(2,1)S(1)} all-gather(bf16[16,2048]{1,0:T(8,128)(2,1)S(1)} %fusion.26), channel_id=1, replica_groups=mesh['zp'=8,'zq'=2,'y'=4,'x'=4,'core'=2] {'x','core'}, dimensions={0}, use_global_device_ids=true | all-gather | bytes 589824 | tf_op jit(solution)/shard_map/all_gather | solution.py:53
  114.5 12.9 %all_to_all.30 = bf16[8,16,2048]{2,1,0:T(8,128)(2,1)S(1)} all-to-all(bf16[8,16,2048]{2,1,0:T(8,128)(2,1)S(1)} %bitcast.121), channel_id=1, replica_groups=mesh['zp'=8,'zq'=2,'y'=4,'x'=4,'core'=2] {'x','core'}, dimensions={0} | all-to-all | bytes 1048576 | tf_op jit(solution)/shard_map/all_to_all | solution.py:24
  127.7 0.9 fusion.24
  128.7 13.1 %all_gather.7 = bf16[128,2048]{1,0:T(8,128)(2,1)S(1)} all-gather(bf16[16,2048]{1,0:T(8,128)(2,1)S(1)} %fusion.24), channel_id=1, replica_groups=mesh['zp'=8,'zq'=2,'y'=4,'x'=4,'core'=2] {'x','core'}, dimensions={0}, use_global_device_ids=true | all-gather | bytes 589824 | tf_op jit(solution)/shard_map/all_gather | solution.py:53
  144.8 1.8 copy_bitcast_fusion
  146.6 3.6 %all-to-all-start.4 = ((bf16[8,8,4,32,128]{4,3,2,1,0:T(8,128)(2,1)}), bf16[8,8,4,32,128]{4,3,2,1,0:T(8,128)(2,1)S(1)}, u32[]{:S(2)}, u32[]{:S(2)}) async-start(bf16[8,8,4,32,128]{4,3,2,1,0:T(8,128)(2,1)} %copy_bitcast_fusion), calls=%async_computation.4 | async-start | bytes 4194304 | tf_op jit(solution)/shard_map/all_to_all | solution.py:24
  150.3 1.4 convolution_convert_fusion
  153.0 2.2 %collective-permute-start.4 = (bf16[128,2048]{1,0:T(8,128)(2,1)S(1)}, bf16[128,2048]{1,0:T(8,128)(2,1)S(1)}, u32[]{:S(2)}, u32[]{:S(2)}) collective-permute-start(bf16[128,2048]{1,0:T(8,128)(2,1)S(1)} %get-tuple-element.64), channel_id=1, source_target_pairs={{0,1},{1,0},{2,3},{3,2},{4,5},{5,4},{6,7},{7,6},{8,9},{9,8},{10,11... | collective-permute-start | bytes 1572872 | tf_op jit(solution)/shard_map/ppermute | solution.py:40
  155.2 1.6 collective-permute-done.4
  157.1 2.8 %collective-permute-start.5 = (bf16[128,2048]{1,0:T(8,128)(2,1)S(1)}, bf16[128,2048]{1,0:T(8,128)(2,1)S(1)}, u32[]{:S(2)}, u32[]{:S(2)}) collective-permute-start(bf16[128,2048]{1,0:T(8,128)(2,1)S(1)} %add_convert_fusion.2), channel_id=1, source_target_pairs={{0,2},{2,0},{4,6},{6,4},{1,3},{3,1},{5,7},{7,5},{8,10},{10,8},{12,... | collective-permute-start | bytes 1572872 | tf_op jit(solution)/shard_map/ppermute | solution.py:44
  159.8 13.3 %collective-permute-done.5 = bf16[128,2048]{1,0:T(8,128)(2,1)S(1)} collective-permute-done((bf16[128,2048]{1,0:T(8,128)(2,1)S(1)}, bf16[128,2048]{1,0:T(8,128)(2,1)S(1)}, u32[]{:S(2)}, u32[]{:S(2)}) %collective-permute-start.5) | collective-permute-done | bytes 524320 | tf_op jit(solution)/shard_map/ppermute | solution.py:44
  173.1 0.9 add_convert_fusion.1
  174.0 4.0 %collective-permute-start.6 = (bf16[128,2048]{1,0:T(8,128)(2,1)}, bf16[128,2048]{1,0:T(8,128)(2,1)}, u32[]{:S(2)}, u32[]{:S(2)}) collective-permute-start(bf16[128,2048]{1,0:T(8,128)(2,1)} %add_convert_fusion.1), channel_id=1, source_target_pairs={{0,6},{2,4},{4,2},{6,0},{1,7},{3,5},{5,3},{7,1},{8,14},{10,12},{12... | collective-permute-start | bytes 1572872 | tf_op jit(solution)/shard_map/ppermute | solution.py:44
  178.9 1.6 shard_map.95
  180.5 8.6 %all-to-all-start.5 = ((bf16[8,4,32,128]{3,2,1,0:T(8,128)(2,1)}), bf16[8,4,32,128]{3,2,1,0:T(8,128)(2,1)S(1)}, u32[]{:S(2)}, u32[]{:S(2)}) async-start(bf16[8,4,32,128]{3,2,1,0:T(8,128)(2,1)} %shard_map.95), calls=%async_computation.5 | async-start | bytes 524288 | tf_op jit(solution)/shard_map/all_to_all | solution.py:24
  189.1 1.7 collective-permute-done.6
  190.8 1.3 add_convert_fusion.tile
  192.1 1.9 collective-permute-start.7
  194.1 0.9 broadcast_select_fusion
  194.9 1.0 collective-permute-done.7.other
  195.9 2.6 %shard_map.96 = (bf16[128,2048]{1,0:T(8,128)(2,1)}, bf16[128,2048]{1,0:T(8,128)(2,1)}) custom-call(s32[2]{0:T(128)S(1)} %pad_add_fusion.1.flags, bf16[128,2048]{1,0:T(8,128)(2,1)S(1)} %add_convert_fusion.tile, bf16[128,2048]{1,0:T(8,128)(2,1)S(1)} %collective-permute-done.7.other, bf16[128,2048]{1,0:T(8,128)(2,1)S(1)} %get-tuple-element.67.base_h, ...), custom_call_target="tpu_custom_call" | custom-call | tf_op jit(solution)/shard_map/pallas_call | solution.py:187
  198.6 11.6 %all-to-all-done.5.terms = bf16[8,4,32,128]{3,2,1,0:T(8,128)(2,1)S(1)} async-done(((bf16[8,4,32,128]{3,2,1,0:T(8,128)(2,1)}), bf16[8,4,32,128]{3,2,1,0:T(8,128)(2,1)S(1)}, u32[]{:S(2)}, u32[]{:S(2)}) %all-to-all-start.5) | async-done | bytes 262176 | tf_op jit(solution)/shard_map/all_to_all | solution.py:24
  210.8 1.6 shard_map.97
  (100 shorter events, 15.5 us)
Async XLA Ops:
  0.7 1.0 copy-start
  1.8 1.0 copy-start.2
  2.8 0.7 copy-start.5
  3.5 0.7 copy-start.6
  4.2 0.7 copy-start.7
  6.2 18.3 %collective-permute-start = (bf16[128,2048]{1,0:T(8,128)(2,1)S(1)}, bf16[128,2048]{1,0:T(8,128)(2,1)S(1)}, u32[]{:S(2)}, u32[]{:S(2)}) collective-permute-start(bf16[128,2048]{1,0:T(8,128)(2,1)S(1)} %get-tuple-element.24), channel_id=1, source_target_pairs={{0,1},{1,0},{2,3},{3,2},{4,5},{5,4},{6,7},{7,6},{8,9},{9,8},{10,11... | collective-permute-start | bytes 1572872 | tf_op jit(solution)/shard_map/ppermute | solution.py:40
  8.1 37.1 %all-to-all-start = ((bf16[8,4,32,128]{3,2,1,0:T(8,128)(2,1)}), bf16[8,4,32,128]{3,2,1,0:T(8,128)(2,1)S(1)}, u32[]{:S(2)}, u32[]{:S(2)}) async-start(bf16[8,4,32,128]{3,2,1,0:T(8,128)(2,1)} %get-tuple-element.23), calls=%async_computation | async-start | bytes 524288 | tf_op jit(solution)/shard_map/all_to_all | solution.py:24
  26.2 15.9 %collective-permute-start.1 = (bf16[128,2048]{1,0:T(8,128)(2,1)S(1)}, bf16[128,2048]{1,0:T(8,128)(2,1)S(1)}, u32[]{:S(2)}, u32[]{:S(2)}) collective-permute-start(bf16[128,2048]{1,0:T(8,128)(2,1)S(1)} %select_add_fusion), channel_id=1, source_target_pairs={{0,2},{2,0},{4,6},{6,4},{1,3},{3,1},{5,7},{7,5},{8,10},{10,8},{12,... | collective-permute-start | bytes 1572872 | tf_op jit(solution)/shard_map/ppermute | solution.py:44
  48.3 23.2 %copy-start.8 = (s32[1,8]{1,0:T(1,128)S(1)}, s32[1,8]{1,0:T(1,128)}, u32[]{:S(2)}) copy-start(s32[1,8]{1,0:T(1,128)} %depth.1) | copy-start | bytes 100
  48.3 30.7 %all-to-all-start.1 = ((bf16[8,4,8,32,128]{4,3,2,1,0:T(8,128)(2,1)}), bf16[8,4,8,32,128]{4,3,2,1,0:T(8,128)(2,1)S(1)}, u32[]{:S(2)}, u32[]{:S(2)}) async-start(bf16[8,4,8,32,128]{4,3,2,1,0:T(8,128)(2,1)} %shard_map.94), calls=%async_computation.1 | async-start | bytes 4194304 | tf_op jit(solution)/shard_map/all_to_all | solution.py:24
  52.9 21.3 %copy-start.4 = (f32[2048]{0:T(1024)S(1)}, f32[2048]{0:T(1024)}, u32[]{:S(2)}) copy-start(f32[2048]{0:T(1024)} %param.11) | copy-start | bytes 24580
  52.9 16.5 %collective-permute-start.2 = (bf16[128,2048]{1,0:T(8,128)(2,1)S(1)}, bf16[128,2048]{1,0:T(8,128)(2,1)S(1)}, u32[]{:S(2)}, u32[]{:S(2)}) collective-permute-start(bf16[128,2048]{1,0:T(8,128)(2,1)S(1)} %add.82), channel_id=1, source_target_pairs={{0,6},{2,4},{4,2},{6,0},{1,7},{3,5},{5,3},{7,1},{8,14},{10,12},{12... | collective-permute-start | bytes 1572872 | tf_op jit(solution)/shard_map/ppermute | solution.py:44
  69.6 4.1 %copy-start.18 = (bf16[128,2048]{1,0:T(8,128)(2,1)}, bf16[128,2048]{1,0:T(8,128)(2,1)S(1)}, u32[]{:S(2)}) copy-start(bf16[128,2048]{1,0:T(8,128)(2,1)S(1)} %add.83) | copy-start | bytes 1572868
  69.6 3.8 %collective-permute-start.3 = (bf16[128,2048]{1,0:T(8,128)(2,1)S(1)}, bf16[128,2048]{1,0:T(8,128)(2,1)S(1)}, u32[]{:S(2)}, u32[]{:S(2)}) collective-permute-start(bf16[128,2048]{1,0:T(8,128)(2,1)S(1)} %add.83), channel_id=1, source_target_pairs={{0,1},{1,0},{2,3},{3,2},{4,5},{5,4},{6,7},{7,6},{8,9},{9,8},{10,11... | collective-permute-start | bytes 1572872 | tf_op jit(solution)/shard_map/ppermute | solution.py:40
  73.4 0.8 copy-start.22
  79.4 1.2 copy-start.15
  79.4 34.5 %copy-start.10 = (bf16[1,8,8,32,128]{4,3,2,1,0:T(8,128)(2,1)}, bf16[1,8,8,32,128]{4,3,2,1,0:T(8,128)(2,1)S(1)}, u32[]{:S(2)}) copy-start(bf16[1,8,8,32,128]{4,3,2,1,0:T(8,128)(2,1)S(1)} %copy.16) | copy-start | bytes 1572868
  81.2 33.0 %copy-start.12 = (bf16[1,8,8,32,128]{4,3,2,1,0:T(8,128)(2,1)}, bf16[1,8,8,32,128]{4,3,2,1,0:T(8,128)(2,1)S(1)}, u32[]{:S(2)}) copy-start(bf16[1,8,8,32,128]{4,3,2,1,0:T(8,128)(2,1)S(1)} %copy.17) | copy-start | bytes 1572868
  81.5 6.4 %copy-start.19 = (bf16[128,2048]{1,0:T(8,128)(2,1)S(1)}, bf16[128,2048]{1,0:T(8,128)(2,1)}, u32[]{:S(2)}) copy-start(bf16[128,2048]{1,0:T(8,128)(2,1)} %copy-done.18) | copy-start | bytes 1572868
  81.6 60.2 %copy-start.9 = (bf16[1,8,8,32,128]{4,3,2,1,0:T(8,128)(2,1)}, bf16[1,8,8,32,128]{4,3,2,1,0:T(8,128)(2,1)S(1)}, u32[]{:S(2)}) copy-start(bf16[1,8,8,32,128]{4,3,2,1,0:T(8,128)(2,1)S(1)} %copy.18) | copy-start | bytes 1572868
  83.1 13.2 %all-to-all-start.2 = ((bf16[8,16,2048]{2,1,0:T(8,128)(2,1)}), bf16[8,16,2048]{2,1,0:T(8,128)(2,1)}, u32[]{:S(2)}, u32[]{:S(2)}) async-start(bf16[8,16,2048]{2,1,0:T(8,128)(2,1)} %bitcast.120), calls=%async_computation.2 | async-start | bytes 1048576 | tf_op jit(solution)/shard_map/all_to_all | solution.py:24
  90.4 0.8 copy-start.20
  110.6 17.1 %copy-start.14 = (bf16[128,2048]{1,0:T(8,128)(2,1)}, bf16[128,2048]{1,0:T(8,128)(2,1)S(1)}, u32[]{:S(2)}) copy-start(bf16[128,2048]{1,0:T(8,128)(2,1)S(1)} %all_gather.6) | copy-start | bytes 1572868
  127.5 15.3 %copy-start.16 = (bf16[128,2048]{1,0:T(8,128)(2,1)S(1)}, bf16[128,2048]{1,0:T(8,128)(2,1)}, u32[]{:S(2)}) copy-start(bf16[128,2048]{1,0:T(8,128)(2,1)} %fusion.12) | copy-start | bytes 1572868
  141.8 2.5 %copy-start.17 = (bf16[128,2048]{1,0:T(8,128)(2,1)}, bf16[128,2048]{1,0:T(8,128)(2,1)S(1)}, u32[]{:S(2)}) copy-start(bf16[128,2048]{1,0:T(8,128)(2,1)S(1)} %all_gather.7) | copy-start | bytes 1572868
  143.3 1.0 copy-start.21
  146.6 32.3 %all-to-all-start.4 = ((bf16[8,8,4,32,128]{4,3,2,1,0:T(8,128)(2,1)}), bf16[8,8,4,32,128]{4,3,2,1,0:T(8,128)(2,1)S(1)}, u32[]{:S(2)}, u32[]{:S(2)}) async-start(bf16[8,8,4,32,128]{4,3,2,1,0:T(8,128)(2,1)} %copy_bitcast_fusion), calls=%async_computation.4 | async-start | bytes 4194304 | tf_op jit(solution)/shard_map/all_to_all | solution.py:24
  150.3 1.7 copy-start.11
  151.7 1.0 copy-start.13
  153.0 3.8 %collective-permute-start.4 = (bf16[128,2048]{1,0:T(8,128)(2,1)S(1)}, bf16[128,2048]{1,0:T(8,128)(2,1)S(1)}, u32[]{:S(2)}, u32[]{:S(2)}) collective-permute-start(bf16[128,2048]{1,0:T(8,128)(2,1)S(1)} %get-tuple-element.64), channel_id=1, source_target_pairs={{0,1},{1,0},{2,3},{3,2},{4,5},{5,4},{6,7},{7,6},{8,9},{9,8},{10,11... | collective-permute-start | bytes 1572872 | tf_op jit(solution)/shard_map/ppermute | solution.py:40
  157.1 16.0 %collective-permute-start.5 = (bf16[128,2048]{1,0:T(8,128)(2,1)S(1)}, bf16[128,2048]{1,0:T(8,128)(2,1)S(1)}, u32[]{:S(2)}, u32[]{:S(2)}) collective-permute-start(bf16[128,2048]{1,0:T(8,128)(2,1)S(1)} %add_convert_fusion.2), channel_id=1, source_target_pairs={{0,2},{2,0},{4,6},{6,4},{1,3},{3,1},{5,7},{7,5},{8,10},{10,8},{12,... | collective-permute-start | bytes 1572872 | tf_op jit(solution)/shard_map/ppermute | solution.py:44
  174.0 16.8 %collective-permute-start.6 = (bf16[128,2048]{1,0:T(8,128)(2,1)}, bf16[128,2048]{1,0:T(8,128)(2,1)}, u32[]{:S(2)}, u32[]{:S(2)}) collective-permute-start(bf16[128,2048]{1,0:T(8,128)(2,1)} %add_convert_fusion.1), channel_id=1, source_target_pairs={{0,6},{2,4},{4,2},{6,0},{1,7},{3,5},{5,3},{7,1},{8,14},{10,12},{12... | collective-permute-start | bytes 1572872 | tf_op jit(solution)/shard_map/ppermute | solution.py:44
  178.9 15.2 %copy-start.1 = (bf16[1,128,2048]{2,1,0:T(8,128)(2,1)S(1)}, bf16[1,128,2048]{2,1,0:T(8,128)(2,1)}, u32[]{:S(2)}) copy-start(bf16[1,128,2048]{2,1,0:T(8,128)(2,1)} %param.6) | copy-start | bytes 1572868
  180.5 13.6 %copy-start.3 = (bf16[1,128,2048]{2,1,0:T(8,128)(2,1)S(1)}, bf16[1,128,2048]{2,1,0:T(8,128)(2,1)}, u32[]{:S(2)}) copy-start(bf16[1,128,2048]{2,1,0:T(8,128)(2,1)} %param.7) | copy-start | bytes 1572868
  180.5 29.6 %all-to-all-start.5 = ((bf16[8,4,32,128]{3,2,1,0:T(8,128)(2,1)}), bf16[8,4,32,128]{3,2,1,0:T(8,128)(2,1)S(1)}, u32[]{:S(2)}, u32[]{:S(2)}) async-start(bf16[8,4,32,128]{3,2,1,0:T(8,128)(2,1)} %shard_map.95), calls=%async_computation.5 | async-start | bytes 524288 | tf_op jit(solution)/shard_map/all_to_all | solution.py:24
  192.1 3.8 %collective-permute-start.7 = (bf16[128,2048]{1,0:T(8,128)(2,1)S(1)}, bf16[128,2048]{1,0:T(8,128)(2,1)S(1)}, u32[]{:S(2)}, u32[]{:S(2)}) collective-permute-start(bf16[128,2048]{1,0:T(8,128)(2,1)S(1)} %add_convert_fusion.tile), channel_id=1, source_target_pairs={{0,1},{1,0},{2,3},{3,2},{4,5},{5,4},{6,7},{7,6},{8,9},{9,8},{10,11... | collective-permute-start | bytes 1572872 | tf_op jit(solution)/shard_map/ppermute | solution.py:40
  210.1 0.7 copy-start.23

commit v10 on v8

--- a/solution.py
+++ b/solution.py
@@ -95,6 +95,75 @@
     return inv * u - x32 * inv**3 * jnp.mean(x32 * u, -1, keepdims=True)
 
 
+def first_kernel(depth, h, g, w_qkv, w_out, sent, shards, qkv_in, out_in, sems):
+    core = lax.axis_index("core")
+    live = depth[0, lax.axis_index("x") * 2 + core] >= 2
+    weights = [
+        pltpu.make_async_copy(w_qkv, qkv_in, sems.at[0]),
+        pltpu.make_async_copy(w_out, out_in, sems.at[1]),
+    ]
+    for copy in weights:
+        copy.start()
+
+    @pl.when(live & (core == 0))
+    def _():
+        copy = pltpu.make_async_copy(g, sent, sems.at[2])
+        copy.start()
+        copy.wait()
+
+    @pl.when(live & (core == 1))
+    def _():
+        copy = pltpu.make_async_copy(h, sent, sems.at[3])
+        copy.start()
+        copy.wait()
+
+    @pl.when(jnp.logical_not(live))
+    def _():
+        sent[...] = jnp.zeros_like(sent)
+
+    for copy in weights:
+        copy.wait()
+    for i in range(NP):
+        shards[i, :3] = qkv_in[...]
+        shards[i, 3] = out_in[...]
+
+
+def first_step(depth, h, g, w_qkv, w_out):
+    return pl.pallas_call(
+        first_kernel,
+        in_specs=[pl.BlockSpec(memory_space=pltpu.SMEM)] + [pl.BlockSpec(memory_space=pl.ANY)] * 4,
+        out_specs=[pl.BlockSpec(memory_space=pltpu.VMEM)] * 2,
+        out_shape=[
+            jax.ShapeDtypeStruct((TILE, D), BF),
+            jax.ShapeDtypeStruct((NP, 4, 32, HD), BF),
+        ],
+        scratch_shapes=[
+            pltpu.VMEM((3, 32, HD), BF),
+            pltpu.VMEM((32, HD), BF),
+            pltpu.SemaphoreType.DMA((4,)),
+        ],
+        compiler_params=pltpu.CompilerParams(vmem_limit_bytes=60 * 2**20),
+    )(depth, h, g, w_qkv, w_out)
+
+
+def sum_kernel(terms, out):
+    total = terms[0].astype(F32)
+    for i in range(1, NN):
+        total = total + terms[i].astype(F32)
+    out[...] = total.astype(BF)
+
+
+def sum_terms(terms):
+    return pl.pallas_call(
+        sum_kernel,
+        grid=(NP // 2,),
+        in_specs=[pl.BlockSpec((NN, 2, 4, 32, HD), lambda i: (0, i, 0, 0, 0))],
+        out_specs=pl.BlockSpec((2, 4, 32, HD), lambda i: (i, 0, 0, 0)),
+        out_shape=jax.ShapeDtypeStruct((NP, 4, 32, HD), BF),
+        compiler_params=pltpu.CompilerParams(vmem_limit_bytes=16 * 2**20),
+    )(terms)
+
+
 def last_kernel(flags, tile, other, base_h, base_g, h1, inv, gain, out_h, out_g):
     first, mine = flags[0] == 0, flags[1] == 1
     a, b = tile[...].astype(F32), other[...].astype(F32)
@@ -133,12 +202,12 @@
     tokens = ((0,), (0,))
     core = lax.axis_index("core")
     none = jnp.zeros_like(hidden_in[0])
-    h_part = jnp.where(mine, hidden_in[0], none)
-    g_part = jnp.where(mine, cotangent[0], none)
-    tile = jnp.where(core == 0, h_part, g_part) + from_core(jnp.where(core == 0, g_part, h_part))
+    sent, shards = first_step(tile_depth, hidden_in[0], cotangent[0], w_qkv, w_out.T)
+    kept = jnp.where(mine, jnp.where(core == 0, hidden_in[0], cotangent[0]), none)
+    tile = kept + from_core(sent)
     tile = tile + from_pair(tile, 1)
 
-    near = lax.all_gather(jnp.concatenate([w_qkv, w_out.T[None]], 0), "zp")
+    near = swap(shards, "zp")
     near, tile = lax.optimization_barrier((near, tile))
     w = spread(near, NEAR, NN).transpose(2, 1, 0, 3, 4).reshape(4, D, HD)
     tile = tile + from_pair(tile, 3)
@@ -184,12 +253,13 @@
     mixed3 = mixed3.astype(BF)
     tile = add(jnp.where(core == 0, mixed3, dnorm2), from_core(jnp.where(core == 0, dnorm2, mixed3)))
     tile = add(tile, from_pair(tile, 1))
-    terms, tile, base_h, base_g = lax.optimization_barrier((terms, tile, base_h, base_g))
-
-    part = jnp.sum(terms.astype(F32), 0).astype(BF)
+    pair = from_pair(tile, 3)
+
+    part = sum_terms(terms)
     shards = swap(part, "zp")
 
-    tile = add(tile, from_pair(tile, 3))
+    tile, pair, _ = lax.optimization_barrier((tile, pair, part))
+    tile = add(tile, pair)
     other = from_core(tile)
     flags = jnp.stack([core, mine.astype(jnp.int32)])
     hidden_out, grad_in = last_step(flags, tile, other, base_h, base_g, h1, inv2, gain)

time: 210 us -> 208 us (level)
  blocking collectives: 75 us -> 39.2 us
  waiting for transfers between devices: 54.2 us -> 68.9 us
  starting transfers between devices: 43.2 us -> 56.7 us
  Pallas kernels: 2.63 us -> 6.56 us
    all_gather x1 -> x0, blocking collectives: 35.8 us -> none  [on_device(): near = lax.all_gather(jnp.concatenate([w_qkv, w_out.T[None]], 0), 'zp')]
    ppermute x4, waiting for transfers between devices: 24.2 us -> 42.4 us  [from_pair(): return lax.ppermute(x, 'x', [(i, i ^ bit) for i in range(CTX // 2)])]
    all_to_all x4 -> x5, starting transfers between devices: 22.5 us -> 36.9 us  [swap(): return lax.all_to_all(x, axis, 0, 0)]
    pallas_call x0 -> x2, Pallas kernels: none -> 3.9 us  [the longest x1 2.31 us: first_step(): pl.pallas_call(first_kernel, in_specs=[pl.BlockSpec(memory_space=pltpu.SM...]
    ppermute x4, waiting for transfers between devices: 5.68 us -> 2.79 us  [from_core(): return lax.ppermute(x, 'core', [(0, 1), (1, 0)])]
    reduce_sum x1 -> x0, other arithmetic: 2.76 us -> none  [on_device(): part = jnp.sum(terms.astype(F32), 0).astype(BF)]
    all_to_all x4 -> x5, waiting for transfers between devices: 24.3 us -> 23.7 us  [swap(): return lax.all_to_all(x, axis, 0, 0)]
  transfers between devices with their start and end apart: 12 -> 13, of which waited for: 11 -> 10; matrix products, arithmetic and copies ran while one was open for 5% -> 7% of each run, Pallas kernels for 1% -> 2%
where the time goes in v10:
time: 208 us; the launch traced here: 207 us
  waiting for transfers between devices  68.9 us (33%)
  starting transfers between devices  56.7 us (27%)
  blocking collectives  39.2 us (19%)
  other arithmetic  16.8 us (8%)
  matrix products  10.7 us (5%)
  Pallas kernels  6.56 us (3%)
  local copies, waits for them, and re-layouts  5.99 us (3%)
    ppermute x4, waiting for transfers between devices, from_pair(): return lax.ppermute(x, 'x', [(i, i ^ bit) for i in range(CTX // 2)])  42.4 us
    all_to_all x5, starting transfers between devices, swap(): return lax.all_to_all(x, axis, 0, 0)  36.9 us
    all_gather x2, blocking collectives, all_rows(): return lax.all_gather(chunk, CONTEXT, tiled=True)  26.2 us
    all_to_all x5, waiting for transfers between devices, swap(): return lax.all_to_all(x, axis, 0, 0)  23.7 us
    all_to_all x1, blocking collectives, swap(): return lax.all_to_all(x, axis, 0, 0)  12.9 us
    ppermute x4, starting transfers between devices, from_pair(): return lax.ppermute(x, 'x', [(i, i ^ bit) for i in range(CTX // 2)])  11.9 us
    dot_general x32, matrix products, dot(): return lax.dot_general(a, b, (dims, ((), ())), preferred_element_type=F32)  10.7 us
    ppermute x4, starting transfers between devices, from_core(): return lax.ppermute(x, 'core', [(0, 1), (1, 0)])  8.01 us
  transfers between devices with their start and end apart: 13, of which 10 were waited for; matrix products, arithmetic and copies ran while one was open for 7% of the time, Pallas kernels for 2%

profile of v10, /device:TPU:6, one launch (start us, length us, event | category | flops | bytes accessed | tf_op | source)
XLA Modules:
  0.0 206.6 jit_solution(7049436294233117476)
XLA Ops:
  0.6 2.3 %shard_map.93 = (bf16[128,2048]{1,0:T(8,128)(2,1)}, bf16[8,4,32,128]{3,2,1,0:T(8,128)(2,1)}) custom-call(s32[1,8]{1,0:T(1,128)} %depth.1, bf16[128,2048]{1,0:T(8,128)(2,1)} %bitcast.121, bf16[128,2048]{1,0:T(8,128)(2,1)} %bitcast.122, bf16[3,32,128]{2,1,0:T(8,128)(2,1)} %w_qkv.1, bf16[32,128]{1,0:T(8,128)(2,1)} %bitcast.130), custom_call_target="tpu_custom_call" | custom-call | tf_op jit(solution)/shard_map/pallas_call | solution.py:132
  3.0 1.9 collective-permute-start
  4.9 15.1 %all-to-all-start = ((bf16[8,4,32,128]{3,2,1,0:T(8,128)(2,1)}), bf16[8,4,32,128]{3,2,1,0:T(8,128)(2,1)S(1)}, u32[]{:S(2)}, u32[]{:S(2)}) async-start(bf16[8,4,32,128]{3,2,1,0:T(8,128)(2,1)} %get-tuple-element.21), calls=%async_computation | async-start | bytes 524288 | tf_op jit(solution)/shard_map/all_to_all | solution.py:24
  20.0 1.2 fusion.55
  21.2 1.9 select_add_fusion
  23.1 2.7 %collective-permute-start.1 = (bf16[128,2048]{1,0:T(8,128)(2,1)S(1)}, bf16[128,2048]{1,0:T(8,128)(2,1)S(1)}, u32[]{:S(2)}, u32[]{:S(2)}) collective-permute-start(bf16[128,2048]{1,0:T(8,128)(2,1)S(1)} %select_add_fusion), channel_id=1, source_target_pairs={{0,2},{2,0},{4,6},{6,4},{1,3},{3,1},{5,7},{7,5},{8,10},{10,8},{12,... | collective-permute-start | bytes 1572872 | tf_op jit(solution)/shard_map/ppermute | solution.py:44
  25.9 13.2 %collective-permute-done.1 = bf16[128,2048]{1,0:T(8,128)(2,1)S(1)} collective-permute-done((bf16[128,2048]{1,0:T(8,128)(2,1)S(1)}, bf16[128,2048]{1,0:T(8,128)(2,1)S(1)}, u32[]{:S(2)}, u32[]{:S(2)}) %collective-permute-start.1) | collective-permute-done | bytes 524320 | tf_op jit(solution)/shard_map/ppermute | solution.py:44
  39.2 2.8 %all-to-all-done = bf16[8,4,32,128]{3,2,1,0:T(8,128)(2,1)S(1)} async-done(((bf16[8,4,32,128]{3,2,1,0:T(8,128)(2,1)}), bf16[8,4,32,128]{3,2,1,0:T(8,128)(2,1)S(1)}, u32[]{:S(2)}, u32[]{:S(2)}) %all-to-all-start) | async-done | bytes 262176 | tf_op jit(solution)/shard_map/all_to_all | solution.py:24
  42.0 1.8 broadcast_in_dim.13
  43.8 4.6 %all-to-all-start.1 = ((bf16[8,8,4,32,128]{4,3,1,2,0:T(8,128)(2,1)}), bf16[8,8,4,32,128]{4,3,1,2,0:T(8,128)(2,1)S(1)}, u32[]{:S(2)}, u32[]{:S(2)}) async-start(bf16[8,8,4,32,128]{4,3,1,2,0:T(8,128)(2,1)} %broadcast_in_dim.13), calls=%async_computation.1 | async-start | bytes 4194304 | tf_op jit(solution)/shard_map/all_to_all | solution.py:24
  48.5 2.4 %collective-permute-start.2 = (bf16[128,2048]{1,0:T(8,128)(2,1)S(1)}, bf16[128,2048]{1,0:T(8,128)(2,1)S(1)}, u32[]{:S(2)}, u32[]{:S(2)}) collective-permute-start(bf16[128,2048]{1,0:T(8,128)(2,1)S(1)} %add.82), channel_id=1, source_target_pairs={{0,6},{2,4},{4,2},{6,0},{1,7},{3,5},{5,3},{7,1},{8,14},{10,12},{12... | collective-permute-start | bytes 1572872 | tf_op jit(solution)/shard_map/ppermute | solution.py:44
  50.8 14.2 %collective-permute-done.2 = bf16[128,2048]{1,0:T(8,128)(2,1)S(1)} collective-permute-done((bf16[128,2048]{1,0:T(8,128)(2,1)S(1)}, bf16[128,2048]{1,0:T(8,128)(2,1)S(1)}, u32[]{:S(2)}, u32[]{:S(2)}) %collective-permute-start.2) | collective-permute-done | bytes 524320 | tf_op jit(solution)/shard_map/ppermute | solution.py:44
  65.1 1.9 collective-permute-start.3
  67.1 0.6 compare_reduce_fusion
  67.7 1.2 collective-permute-done.3
  69.9 4.6 %all-to-all-done.1 = bf16[8,8,4,32,128]{4,3,1,2,0:T(8,128)(2,1)S(1)} async-done(((bf16[8,8,4,32,128]{4,3,1,2,0:T(8,128)(2,1)}), bf16[8,8,4,32,128]{4,3,1,2,0:T(8,128)(2,1)S(1)}, u32[]{:S(2)}, u32[]{:S(2)}) %all-to-all-start.1) | async-done | bytes 2097184 | tf_op jit(solution)/shard_map/all_to_all | solution.py:24
  74.5 0.6 copy.43
  75.1 0.5 fusion.54
  77.0 1.1 convolution_convert_fusion.5
  78.1 4.8 %all-to-all-start.2 = ((bf16[8,16,2048]{2,1,0:T(8,128)(2,1)}), bf16[8,16,2048]{2,1,0:T(8,128)(2,1)}, u32[]{:S(2)}, u32[]{:S(2)}) async-start(bf16[8,16,2048]{2,1,0:T(8,128)(2,1)} %bitcast.123), calls=%async_computation.2 | async-start | bytes 1048576 | tf_op jit(solution)/shard_map/all_to_all | solution.py:24
  82.8 2.5 %broadcast_select_fusion.5 = (bf16[128,2048]{1,0:T(8,128)(2,1)S(1)}, bf16[128,2048]{1,0:T(8,128)(2,1)}) fusion(pred[]{:T(512)} %compare_reduce_fusion, bf16[128,2048]{1,0:T(8,128)(2,1)} %copy-done.11, bf16[128,2048]{1,0:T(8,128)(2,1)} %copy-done.8, pred[]{:T(512)S(6)} %eq.2), kind=kLoop, calls=%fused_computation.70 | loop fusion | flops 524288 | bytes 2097154 | tf_op jit(solution)/shard_map/jit(_where)/select_n | solution.py:227
  85.3 0.8 copy-done.9
  86.4 4.8 %all-to-all-done.2 = bf16[8,16,2048]{2,1,0:T(8,128)(2,1)} async-done(((bf16[8,16,2048]{2,1,0:T(8,128)(2,1)}), bf16[8,16,2048]{2,1,0:T(8,128)(2,1)}, u32[]{:S(2)}, u32[]{:S(2)}) %all-to-all-start.2) | async-done | bytes 524320 | tf_op jit(solution)/shard_map/all_to_all | solution.py:24
  91.2 1.1 convert_reduce_fusion.1
  92.4 13.1 %all_gather.6 = bf16[128,2048]{1,0:T(8,128)(2,1)S(1)} all-gather(bf16[16,2048]{1,0:T(8,128)(2,1)S(1)} %fusion.26), channel_id=1, replica_groups=mesh['zp'=8,'zq'=2,'y'=4,'x'=4,'core'=2] {'x','core'}, dimensions={0}, use_global_device_ids=true | all-gather | bytes 589824 | tf_op jit(solution)/shard_map/all_gather | solution.py:53
  105.7 0.8 fusion.19
  109.4 12.9 %all_to_all.30 = bf16[8,16,2048]{2,1,0:T(8,128)(2,1)S(1)} all-to-all(bf16[8,16,2048]{2,1,0:T(8,128)(2,1)S(1)} %bitcast.124), channel_id=1, replica_groups=mesh['zp'=8,'zq'=2,'y'=4,'x'=4,'core'=2] {'x','core'}, dimensions={0} | all-to-all | bytes 1048576 | tf_op jit(solution)/shard_map/all_to_all | solution.py:24
  122.6 0.9 fusion.24
  123.6 13.1 %all_gather.7 = bf16[128,2048]{1,0:T(8,128)(2,1)S(1)} all-gather(bf16[16,2048]{1,0:T(8,128)(2,1)S(1)} %fusion.24), channel_id=1, replica_groups=mesh['zp'=8,'zq'=2,'y'=4,'x'=4,'core'=2] {'x','core'}, dimensions={0}, use_global_device_ids=true | all-gather | bytes 589824 | tf_op jit(solution)/shard_map/all_gather | solution.py:53
  139.7 1.8 copy_bitcast_fusion
  141.6 3.8 %all-to-all-start.4 = ((bf16[8,8,4,32,128]{4,3,2,1,0:T(8,128)(2,1)}), bf16[8,8,4,32,128]{4,3,2,1,0:T(8,128)(2,1)S(1)}, u32[]{:S(2)}, u32[]{:S(2)}) async-start(bf16[8,8,4,32,128]{4,3,2,1,0:T(8,128)(2,1)} %copy_bitcast_fusion), calls=%async_computation.4 | async-start | bytes 4194304 | tf_op jit(solution)/shard_map/all_to_all | solution.py:24
  145.4 1.4 convolution_convert_fusion
  148.1 2.3 %collective-permute-start.4 = (bf16[128,2048]{1,0:T(8,128)(2,1)S(1)}, bf16[128,2048]{1,0:T(8,128)(2,1)S(1)}, u32[]{:S(2)}, u32[]{:S(2)}) collective-permute-start(bf16[128,2048]{1,0:T(8,128)(2,1)S(1)} %get-tuple-element.60), channel_id=1, source_target_pairs={{0,1},{1,0},{2,3},{3,2},{4,5},{5,4},{6,7},{7,6},{8,9},{9,8},{10,11... | collective-permute-start | bytes 1572872 | tf_op jit(solution)/shard_map/ppermute | solution.py:40
  150.4 1.5 collective-permute-done.4
  152.2 2.8 %collective-permute-start.5 = (bf16[128,2048]{1,0:T(8,128)(2,1)S(1)}, bf16[128,2048]{1,0:T(8,128)(2,1)S(1)}, u32[]{:S(2)}, u32[]{:S(2)}) collective-permute-start(bf16[128,2048]{1,0:T(8,128)(2,1)S(1)} %add_convert_fusion.2), channel_id=1, source_target_pairs={{0,2},{2,0},{4,6},{6,4},{1,3},{3,1},{5,7},{7,5},{8,10},{10,8},{12,... | collective-permute-start | bytes 1572872 | tf_op jit(solution)/shard_map/ppermute | solution.py:44
  155.0 13.3 %collective-permute-done.5 = bf16[128,2048]{1,0:T(8,128)(2,1)S(1)} collective-permute-done((bf16[128,2048]{1,0:T(8,128)(2,1)S(1)}, bf16[128,2048]{1,0:T(8,128)(2,1)S(1)}, u32[]{:S(2)}, u32[]{:S(2)}) %collective-permute-start.5) | collective-permute-done | bytes 524320 | tf_op jit(solution)/shard_map/ppermute | solution.py:44
  168.2 0.9 add_convert_fusion.1
  169.2 4.0 %collective-permute-start.6 = (bf16[128,2048]{1,0:T(8,128)(2,1)}, bf16[128,2048]{1,0:T(8,128)(2,1)}, u32[]{:S(2)}, u32[]{:S(2)}) collective-permute-start(bf16[128,2048]{1,0:T(8,128)(2,1)} %add_convert_fusion.1), channel_id=1, source_target_pairs={{0,6},{2,4},{4,2},{6,0},{1,7},{3,5},{5,3},{7,1},{8,14},{10,12},{12... | collective-permute-start | bytes 1572872 | tf_op jit(solution)/shard_map/ppermute | solution.py:44
  174.0 1.6 shard_map.94
  175.6 8.6 %all-to-all-start.5 = ((bf16[8,4,32,128]{3,2,1,0:T(8,128)(2,1)}), bf16[8,4,32,128]{3,2,1,0:T(8,128)(2,1)S(1)}, u32[]{:S(2)}, u32[]{:S(2)}) async-start(bf16[8,4,32,128]{3,2,1,0:T(8,128)(2,1)} %shard_map.94), calls=%async_computation.5 | async-start | bytes 524288 | tf_op jit(solution)/shard_map/all_to_all | solution.py:24
  184.2 1.8 collective-permute-done.6
  185.9 1.3 add_convert_fusion.tile
  187.3 1.9 collective-permute-start.7
  189.2 2.0 broadcast_select_fusion
  191.2 2.7 %shard_map.95 = (bf16[128,2048]{1,0:T(8,128)(2,1)}, bf16[128,2048]{1,0:T(8,128)(2,1)}) custom-call(s32[2]{0:T(128)S(1)} %pad_add_fusion.flags, bf16[128,2048]{1,0:T(8,128)(2,1)S(1)} %add_convert_fusion.tile, bf16[128,2048]{1,0:T(8,128)(2,1)S(1)} %collective-permute-done.7.other, bf16[128,2048]{1,0:T(8,128)(2,1)S(1)} %get-tuple-element.63.base_h, ...), custom_call_target="tpu_custom_call" | custom-call | tf_op jit(solution)/shard_map/pallas_call | solution.py:181
  193.8 11.5 %all-to-all-done.5 = bf16[8,4,32,128]{3,2,1,0:T(8,128)(2,1)S(1)} async-done(((bf16[8,4,32,128]{3,2,1,0:T(8,128)(2,1)}), bf16[8,4,32,128]{3,2,1,0:T(8,128)(2,1)S(1)}, u32[]{:S(2)}, u32[]{:S(2)}) %all-to-all-start.5) | async-done | bytes 262176 | tf_op jit(solution)/shard_map/all_to_all | solution.py:24
  205.4 0.6 slice.44
  206.0 0.6 slice_bitcast_fusion
  (77 shorter events, 10.9 us)
Async XLA Ops:
  3.0 18.3 %collective-permute-start = (bf16[128,2048]{1,0:T(8,128)(2,1)}, bf16[128,2048]{1,0:T(8,128)(2,1)S(1)}, u32[]{:S(2)}, u32[]{:S(2)}) collective-permute-start(bf16[128,2048]{1,0:T(8,128)(2,1)} %get-tuple-element.22), channel_id=1, source_target_pairs={{0,1},{1,0},{2,3},{3,2},{4,5},{5,4},{6,7},{7,6},{8,9},{9,8},{10,11... | collective-permute-start | bytes 1572872 | tf_op jit(solution)/shard_map/ppermute | solution.py:40
  4.9 37.1 %all-to-all-start = ((bf16[8,4,32,128]{3,2,1,0:T(8,128)(2,1)}), bf16[8,4,32,128]{3,2,1,0:T(8,128)(2,1)S(1)}, u32[]{:S(2)}, u32[]{:S(2)}) async-start(bf16[8,4,32,128]{3,2,1,0:T(8,128)(2,1)} %get-tuple-element.21), calls=%async_computation | async-start | bytes 524288 | tf_op jit(solution)/shard_map/all_to_all | solution.py:24
  23.1 15.9 %collective-permute-start.1 = (bf16[128,2048]{1,0:T(8,128)(2,1)S(1)}, bf16[128,2048]{1,0:T(8,128)(2,1)S(1)}, u32[]{:S(2)}, u32[]{:S(2)}) collective-permute-start(bf16[128,2048]{1,0:T(8,128)(2,1)S(1)} %select_add_fusion), channel_id=1, source_target_pairs={{0,2},{2,0},{4,6},{6,4},{1,3},{3,1},{5,7},{7,5},{8,10},{10,8},{12,... | collective-permute-start | bytes 1572872 | tf_op jit(solution)/shard_map/ppermute | solution.py:44
  43.8 23.2 %copy-start.12 = (s32[1,8]{1,0:T(1,128)S(1)}, s32[1,8]{1,0:T(1,128)}, u32[]{:S(2)}) copy-start(s32[1,8]{1,0:T(1,128)} %depth.1) | copy-start | bytes 100
  43.8 30.7 %all-to-all-start.1 = ((bf16[8,8,4,32,128]{4,3,1,2,0:T(8,128)(2,1)}), bf16[8,8,4,32,128]{4,3,1,2,0:T(8,128)(2,1)S(1)}, u32[]{:S(2)}, u32[]{:S(2)}) async-start(bf16[8,8,4,32,128]{4,3,1,2,0:T(8,128)(2,1)} %broadcast_in_dim.13), calls=%async_computation.1 | async-start | bytes 4194304 | tf_op jit(solution)/shard_map/all_to_all | solution.py:24
  48.5 21.3 %copy-start = (f32[2048]{0:T(1024)S(1)}, f32[2048]{0:T(1024)}, u32[]{:S(2)}) copy-start(f32[2048]{0:T(1024)} %param.11) | copy-start | bytes 24580
  48.5 16.5 %collective-permute-start.2 = (bf16[128,2048]{1,0:T(8,128)(2,1)S(1)}, bf16[128,2048]{1,0:T(8,128)(2,1)S(1)}, u32[]{:S(2)}, u32[]{:S(2)}) collective-permute-start(bf16[128,2048]{1,0:T(8,128)(2,1)S(1)} %add.82), channel_id=1, source_target_pairs={{0,6},{2,4},{4,2},{6,0},{1,7},{3,5},{5,3},{7,1},{8,14},{10,12},{12... | collective-permute-start | bytes 1572872 | tf_op jit(solution)/shard_map/ppermute | solution.py:44
  65.1 4.1 %copy-start.8 = (bf16[128,2048]{1,0:T(8,128)(2,1)}, bf16[128,2048]{1,0:T(8,128)(2,1)S(1)}, u32[]{:S(2)}) copy-start(bf16[128,2048]{1,0:T(8,128)(2,1)S(1)} %add.83) | copy-start | bytes 1572868
  65.1 3.8 %collective-permute-start.3 = (bf16[128,2048]{1,0:T(8,128)(2,1)S(1)}, bf16[128,2048]{1,0:T(8,128)(2,1)S(1)}, u32[]{:S(2)}, u32[]{:S(2)}) collective-permute-start(bf16[128,2048]{1,0:T(8,128)(2,1)S(1)} %add.83), channel_id=1, source_target_pairs={{0,1},{1,0},{2,3},{3,2},{4,5},{5,4},{6,7},{7,6},{8,9},{9,8},{10,11... | collective-permute-start | bytes 1572872 | tf_op jit(solution)/shard_map/ppermute | solution.py:40
  69.0 0.8 copy-start.11
  75.6 33.2 %copy-start.4 = (bf16[1,8,8,32,128]{4,3,2,1,0:T(8,128)(2,1)}, bf16[1,8,8,32,128]{4,3,2,1,0:T(8,128)(2,1)S(1)}, u32[]{:S(2)}) copy-start(bf16[1,8,8,32,128]{4,3,2,1,0:T(8,128)(2,1)S(1)} %get-tuple-element.44) | copy-start | bytes 1572868
  75.6 33.5 %copy-start.2 = (bf16[1,8,8,32,128]{4,3,2,1,0:T(8,128)(2,1)}, bf16[1,8,8,32,128]{4,3,2,1,0:T(8,128)(2,1)S(1)}, u32[]{:S(2)}) copy-start(bf16[1,8,8,32,128]{4,3,2,1,0:T(8,128)(2,1)S(1)} %get-tuple-element.46) | copy-start | bytes 1572868
  75.7 61.0 %copy-start.1 = (bf16[1,8,8,32,128]{4,3,2,1,0:T(8,128)(2,1)}, bf16[1,8,8,32,128]{4,3,2,1,0:T(8,128)(2,1)S(1)}, u32[]{:S(2)}) copy-start(bf16[1,8,8,32,128]{4,3,2,1,0:T(8,128)(2,1)S(1)} %get-tuple-element.45) | copy-start | bytes 1572868
  78.1 13.2 %all-to-all-start.2 = ((bf16[8,16,2048]{2,1,0:T(8,128)(2,1)}), bf16[8,16,2048]{2,1,0:T(8,128)(2,1)}, u32[]{:S(2)}, u32[]{:S(2)}) async-start(bf16[8,16,2048]{2,1,0:T(8,128)(2,1)} %bitcast.123), calls=%async_computation.2 | async-start | bytes 1048576 | tf_op jit(solution)/shard_map/all_to_all | solution.py:24
  85.3 0.8 copy-start.9
  105.5 17.1 %copy-start.6 = (bf16[128,2048]{1,0:T(8,128)(2,1)}, bf16[128,2048]{1,0:T(8,128)(2,1)S(1)}, u32[]{:S(2)}) copy-start(bf16[128,2048]{1,0:T(8,128)(2,1)S(1)} %all_gather.6) | copy-start | bytes 1572868
  136.7 2.5 %copy-start.7 = (bf16[128,2048]{1,0:T(8,128)(2,1)}, bf16[128,2048]{1,0:T(8,128)(2,1)S(1)}, u32[]{:S(2)}) copy-start(bf16[128,2048]{1,0:T(8,128)(2,1)S(1)} %all_gather.7) | copy-start | bytes 1572868
  138.2 1.0 copy-start.10
  141.6 32.4 %all-to-all-start.4 = ((bf16[8,8,4,32,128]{4,3,2,1,0:T(8,128)(2,1)}), bf16[8,8,4,32,128]{4,3,2,1,0:T(8,128)(2,1)S(1)}, u32[]{:S(2)}, u32[]{:S(2)}) async-start(bf16[8,8,4,32,128]{4,3,2,1,0:T(8,128)(2,1)} %copy_bitcast_fusion), calls=%async_computation.4 | async-start | bytes 4194304 | tf_op jit(solution)/shard_map/all_to_all | solution.py:24
  145.4 1.7 copy-start.5
  146.8 1.0 copy-start.3
  148.1 3.8 %collective-permute-start.4 = (bf16[128,2048]{1,0:T(8,128)(2,1)S(1)}, bf16[128,2048]{1,0:T(8,128)(2,1)S(1)}, u32[]{:S(2)}, u32[]{:S(2)}) collective-permute-start(bf16[128,2048]{1,0:T(8,128)(2,1)S(1)} %get-tuple-element.60), channel_id=1, source_target_pairs={{0,1},{1,0},{2,3},{3,2},{4,5},{5,4},{6,7},{7,6},{8,9},{9,8},{10,11... | collective-permute-start | bytes 1572872 | tf_op jit(solution)/shard_map/ppermute | solution.py:40
  152.2 16.1 %collective-permute-start.5 = (bf16[128,2048]{1,0:T(8,128)(2,1)S(1)}, bf16[128,2048]{1,0:T(8,128)(2,1)S(1)}, u32[]{:S(2)}, u32[]{:S(2)}) collective-permute-start(bf16[128,2048]{1,0:T(8,128)(2,1)S(1)} %add_convert_fusion.2), channel_id=1, source_target_pairs={{0,2},{2,0},{4,6},{6,4},{1,3},{3,1},{5,7},{7,5},{8,10},{10,8},{12,... | collective-permute-start | bytes 1572872 | tf_op jit(solution)/shard_map/ppermute | solution.py:44
  169.2 16.8 %collective-permute-start.6 = (bf16[128,2048]{1,0:T(8,128)(2,1)}, bf16[128,2048]{1,0:T(8,128)(2,1)}, u32[]{:S(2)}, u32[]{:S(2)}) collective-permute-start(bf16[128,2048]{1,0:T(8,128)(2,1)} %add_convert_fusion.1), channel_id=1, source_target_pairs={{0,6},{2,4},{4,2},{6,0},{1,7},{3,5},{5,3},{7,1},{8,14},{10,12},{12... | collective-permute-start | bytes 1572872 | tf_op jit(solution)/shard_map/ppermute | solution.py:44
  175.6 29.8 %all-to-all-start.5 = ((bf16[8,4,32,128]{3,2,1,0:T(8,128)(2,1)}), bf16[8,4,32,128]{3,2,1,0:T(8,128)(2,1)S(1)}, u32[]{:S(2)}, u32[]{:S(2)}) async-start(bf16[8,4,32,128]{3,2,1,0:T(8,128)(2,1)} %shard_map.94), calls=%async_computation.5 | async-start | bytes 524288 | tf_op jit(solution)/shard_map/all_to_all | solution.py:24
  187.3 3.9 %collective-permute-start.7 = (bf16[128,2048]{1,0:T(8,128)(2,1)S(1)}, bf16[128,2048]{1,0:T(8,128)(2,1)S(1)}, u32[]{:S(2)}, u32[]{:S(2)}) collective-permute-start(bf16[128,2048]{1,0:T(8,128)(2,1)S(1)} %add_convert_fusion.tile), channel_id=1, source_target_pairs={{0,1},{1,0},{2,3},{3,2},{4,5},{5,4},{6,7},{7,6},{8,9},{9,8},{10,11... | collective-permute-start | bytes 1572872 | tf_op jit(solution)/shard_map/ppermute | solution.py:40

commit v11 on v10

--- a/solution.py
+++ b/solution.py
@@ -2,7 +2,6 @@
 import jax.numpy as jnp
 from jax import lax
 from jax.experimental import pallas as pl
-from jax.experimental.layout import Layout, with_layout_constraint
 from jax.experimental.pallas import tpu as pltpu
 from jax.sharding import Mesh, PartitionSpec as P
 
@@ -146,6 +145,40 @@
     )(depth, h, g, w_qkv, w_out)
 
 
+def products_kernel(rows_t, dqkv3, dq, dk, dv, out, terms, both, block, sems):
+    both[:TILE] = dqkv3[...]
+    for t, part in enumerate((dq, dk, dv)):
+        both[TILE:, t * HD : (t + 1) * HD] = part[...]
+    size = D // NP
+    parts = []
+    for p in range(NP):
+        grad = dot(rows_t[p * size : (p + 1) * size, :], both[...], ((1,), (0,))).astype(BF)
+        for n in range(NN):
+            rows = slice(n * 32, (n + 1) * 32)
+            for t in range(3):
+                block[p, n, t] = grad[rows, t * HD : (t + 1) * HD]
+            block[p, n, 3] = out[p * size + n * 32 : p * size + (n + 1) * 32, :]
+        parts.append(pltpu.make_async_copy(block.at[p], terms.at[:, p], sems.at[p]))
+        parts[-1].start()
+    for part in parts:
+        part.wait()
+
+
+def products(rows_t, dqkv3, dqkv2, out):
+    return pl.pallas_call(
+        products_kernel,
+        in_specs=[pl.BlockSpec(memory_space=pltpu.VMEM)] * 6,
+        out_specs=pl.BlockSpec(memory_space=pl.ANY),
+        out_shape=jax.ShapeDtypeStruct((NN, NP, 4, 32, HD), BF),
+        scratch_shapes=[
+            pltpu.VMEM((2 * TILE, 3 * HD), BF),
+            pltpu.VMEM((NP, NN, 4, 32, HD), BF),
+            pltpu.SemaphoreType.DMA((NP,)),
+        ],
+        compiler_params=pltpu.CompilerParams(vmem_limit_bytes=60 * 2**20),
+    )(rows_t, dqkv3, *dqkv2, out)
+
+
 def sum_kernel(terms, out):
     total = terms[0].astype(F32)
     for i in range(1, NN):
@@ -236,14 +269,10 @@
 
     dqkv2 = backward(g2, keep2, w)
 
-    def product(left3, right3, left2, right2):
-        both = dot(jnp.concatenate([left3, left2], 0), jnp.concatenate([right3, right2], 0), tokens)
-        return both.astype(BF).reshape(NP, NN, 32, HD)
-
-    terms = [product(rows3, d3, rows2, d2) for d3, d2 in zip(dqkv3, dqkv2)]
-    terms.append(product(dy3, keep3[-1], g2, attn2))
-    terms = jnp.stack(terms, 2).transpose(1, 0, 2, 3, 4)
-    terms = with_layout_constraint(terms, Layout((0, 1, 2, 3, 4)))
+    out = jnp.concatenate([dy3, g2], 0), jnp.concatenate([keep3[-1], attn2], 0)
+    out = dot(out[0], out[1], tokens).astype(BF)
+    rows_t = jnp.concatenate([rows3, rows2], 0).T
+    terms = products(rows_t, jnp.concatenate(dqkv3, 1), dqkv2, out)
     terms, dqkv2, old_h, old_g = lax.optimization_barrier((terms, dqkv2, h2, g2))
     terms = swap(terms, NEAR)
     base_h = jnp.where(mine, old_h, hidden_in[0])

time: 208 us -> 215 us (1.034)
  blocking collectives: 39.2 us -> 26.2 us
  starting transfers between devices: 56.7 us -> 62 us
  waiting for transfers between devices: 68.9 us -> 73.3 us
  local copies, waits for them, and re-layouts: 5.99 us -> 9.76 us
  Pallas kernels: 6.56 us -> 9.67 us
    all_to_all x1 -> x0, blocking collectives: 12.9 us -> none  [swap(): return lax.all_to_all(x, axis, 0, 0)]
    all_to_all x5 -> x6, starting transfers between devices: 36.9 us -> 42.1 us  [swap(): return lax.all_to_all(x, axis, 0, 0)]
    all_to_all x5 -> x6, waiting for transfers between devices: 23.7 us -> 27.8 us  [swap(): return lax.all_to_all(x, axis, 0, 0)]
    pallas_call x0 -> x1, Pallas kernels: none -> 3.09 us  [products(): pl.pallas_call(products_kernel, in_specs=[pl.BlockSpec(memory_space=pltpu...]
    transpose x0 -> x1, local copies, waits for them, and re-layouts: none -> 2.27 us  [on_device(): rows_t = jnp.concatenate([rows3, rows2], 0).T]
    dot_general x32 -> x29, matrix products: 10.7 us -> 12.7 us  [dot(): return lax.dot_general(a, b, (dims, ((), ())), preferred_element_type=F32)]
  transfers between devices with their start and end apart: 13 -> 14, of which waited for: 10 -> 11; matrix products, arithmetic and copies ran while one was open for 7% -> 9% of each run, Pallas kernels for 2% -> 2%
where the time goes in v11:
time: 215 us; the launch traced here: 213 us
  waiting for transfers between devices  73.3 us (34%)
  starting transfers between devices  62 us (29%)
  blocking collectives  26.2 us (12%)
  other arithmetic  17.8 us (8%)
  matrix products  12.7 us (6%)
  local copies, waits for them, and re-layouts  9.76 us (5%)
  Pallas kernels  9.67 us (4%)
    ppermute x4, waiting for transfers between devices, from_pair(): return lax.ppermute(x, 'x', [(i, i ^ bit) for i in range(CTX // 2)])  42.7 us
    all_to_all x6, starting transfers between devices, swap(): return lax.all_to_all(x, axis, 0, 0)  42.1 us
    all_to_all x6, waiting for transfers between devices, swap(): return lax.all_to_all(x, axis, 0, 0)  27.8 us
    all_gather x2, blocking collectives, all_rows(): return lax.all_gather(chunk, CONTEXT, tiled=True)  26.2 us
    dot_general x29, matrix products, dot(): return lax.dot_general(a, b, (dims, ((), ())), preferred_element_type=F32)  12.7 us
    ppermute x4, starting transfers between devices, from_pair(): return lax.ppermute(x, 'x', [(i, i ^ bit) for i in range(CTX // 2)])  11.9 us
    ppermute x4, starting transfers between devices, from_core(): return lax.ppermute(x, 'core', [(0, 1), (1, 0)])  8.02 us
  transfers between devices with their start and end apart: 14, of which 11 were waited for; matrix products, arithmetic and copies ran while one was open for 9% of the time, Pallas kernels for 2%

profile of v11, /device:TPU:6, one launch (start us, length us, event | category | flops | bytes accessed | tf_op | source)
XLA Modules:
  0.0 213.1 jit_solution(1356335094468207457)
XLA Ops:
  0.6 2.3 %shard_map.93 = (bf16[128,2048]{1,0:T(8,128)(2,1)}, bf16[8,4,32,128]{3,2,1,0:T(8,128)(2,1)}) custom-call(s32[1,8]{1,0:T(1,128)} %depth.1, bf16[128,2048]{1,0:T(8,128)(2,1)} %bitcast.117, bf16[128,2048]{1,0:T(8,128)(2,1)} %bitcast.118, bf16[3,32,128]{2,1,0:T(8,128)(2,1)} %w_qkv.1, bf16[32,128]{1,0:T(8,128)(2,1)} %bitcast.122), custom_call_target="tpu_custom_call" | custom-call | tf_op jit(solution)/shard_map/pallas_call | solution.py:131
  3.0 1.9 collective-permute-start
  4.9 15.1 %all-to-all-start = ((bf16[8,4,32,128]{3,2,1,0:T(8,128)(2,1)}), bf16[8,4,32,128]{3,2,1,0:T(8,128)(2,1)S(1)}, u32[]{:S(2)}, u32[]{:S(2)}) async-start(bf16[8,4,32,128]{3,2,1,0:T(8,128)(2,1)} %get-tuple-element.21), calls=%async_computation | async-start | bytes 524288 | tf_op jit(solution)/shard_map/all_to_all | solution.py:23
  20.0 1.3 fusion.43
  21.3 1.9 select_add_fusion
  23.2 2.7 %collective-permute-start.1 = (bf16[128,2048]{1,0:T(8,128)(2,1)S(1)}, bf16[128,2048]{1,0:T(8,128)(2,1)S(1)}, u32[]{:S(2)}, u32[]{:S(2)}) collective-permute-start(bf16[128,2048]{1,0:T(8,128)(2,1)S(1)} %select_add_fusion), channel_id=1, source_target_pairs={{0,2},{2,0},{4,6},{6,4},{1,3},{3,1},{5,7},{7,5},{8,10},{10,8},{12,... | collective-permute-start | bytes 1572872 | tf_op jit(solution)/shard_map/ppermute | solution.py:43
  25.9 13.2 %collective-permute-done.1 = bf16[128,2048]{1,0:T(8,128)(2,1)S(1)} collective-permute-done((bf16[128,2048]{1,0:T(8,128)(2,1)S(1)}, bf16[128,2048]{1,0:T(8,128)(2,1)S(1)}, u32[]{:S(2)}, u32[]{:S(2)}) %collective-permute-start.1) | collective-permute-done | bytes 524320 | tf_op jit(solution)/shard_map/ppermute | solution.py:43
  39.2 2.8 %all-to-all-done = bf16[8,4,32,128]{3,2,1,0:T(8,128)(2,1)S(1)} async-done(((bf16[8,4,32,128]{3,2,1,0:T(8,128)(2,1)}), bf16[8,4,32,128]{3,2,1,0:T(8,128)(2,1)S(1)}, u32[]{:S(2)}, u32[]{:S(2)}) %all-to-all-start) | async-done | bytes 262176 | tf_op jit(solution)/shard_map/all_to_all | solution.py:23
  42.0 1.8 broadcast_in_dim.13
  43.8 4.6 %all-to-all-start.1 = ((bf16[8,8,4,32,128]{4,3,1,2,0:T(8,128)(2,1)}), bf16[8,8,4,32,128]{4,3,1,2,0:T(8,128)(2,1)}, u32[]{:S(2)}, u32[]{:S(2)}) async-start(bf16[8,8,4,32,128]{4,3,1,2,0:T(8,128)(2,1)} %broadcast_in_dim.13), calls=%async_computation.1 | async-start | bytes 4194304 | tf_op jit(solution)/shard_map/all_to_all | solution.py:23
  48.4 2.4 %collective-permute-start.2 = (bf16[128,2048]{1,0:T(8,128)(2,1)S(1)}, bf16[128,2048]{1,0:T(8,128)(2,1)S(1)}, u32[]{:S(2)}, u32[]{:S(2)}) collective-permute-start(bf16[128,2048]{1,0:T(8,128)(2,1)S(1)} %add.82), channel_id=1, source_target_pairs={{0,6},{2,4},{4,2},{6,0},{1,7},{3,5},{5,3},{7,1},{8,14},{10,12},{12... | collective-permute-start | bytes 1572872 | tf_op jit(solution)/shard_map/ppermute | solution.py:43
  50.8 14.3 %collective-permute-done.2 = bf16[128,2048]{1,0:T(8,128)(2,1)S(1)} collective-permute-done((bf16[128,2048]{1,0:T(8,128)(2,1)S(1)}, bf16[128,2048]{1,0:T(8,128)(2,1)S(1)}, u32[]{:S(2)}, u32[]{:S(2)}) %collective-permute-start.2) | collective-permute-done | bytes 524320 | tf_op jit(solution)/shard_map/ppermute | solution.py:43
  65.3 1.9 collective-permute-start.3
  67.8 1.2 collective-permute-done.3
  70.1 4.7 %all-to-all-done.1 = bf16[8,8,4,32,128]{4,3,1,2,0:T(8,128)(2,1)} async-done(((bf16[8,8,4,32,128]{4,3,1,2,0:T(8,128)(2,1)}), bf16[8,8,4,32,128]{4,3,1,2,0:T(8,128)(2,1)}, u32[]{:S(2)}, u32[]{:S(2)}) %all-to-all-start.1) | async-done | bytes 2097184 | tf_op jit(solution)/shard_map/all_to_all | solution.py:23
  74.8 2.2 %copy.48 = bf16[8,8,4,32,128]{4,3,0,1,2:T(8,128)(2,1)S(1)} copy(bf16[8,8,4,32,128]{4,3,1,2,0:T(8,128)(2,1)} %all-to-all-done.1) | data formatting | bytes 4194304 | tf_op jit(solution)/shard_map/all_to_all | solution.py:23
  78.7 1.1 convolution_convert_fusion.2
  79.8 4.8 %all-to-all-start.2 = ((bf16[8,16,2048]{2,1,0:T(8,128)(2,1)}), bf16[8,16,2048]{2,1,0:T(8,128)(2,1)}, u32[]{:S(2)}, u32[]{:S(2)}) async-start(bf16[8,16,2048]{2,1,0:T(8,128)(2,1)} %bitcast.119), calls=%async_computation.2 | async-start | bytes 1048576 | tf_op jit(solution)/shard_map/all_to_all | solution.py:23
  84.6 2.6 %broadcast_select_fusion.5 = (bf16[128,2048]{1,0:T(8,128)(2,1)S(1)}, bf16[128,2048]{1,0:T(8,128)(2,1)}) fusion(pred[]{:T(512)} %compare_reduce_fusion, bf16[128,2048]{1,0:T(8,128)(2,1)} %copy-done.11, bf16[128,2048]{1,0:T(8,128)(2,1)S(1)} %add.83, pred[]{:T(512)S(6)} %eq.2), kind=kLoop, calls=%fused_computation.65 | loop fusion | flops 524288 | bytes 2097154 | tf_op jit(solution)/shard_map/jit(_where)/select_n | solution.py:260
  88.3 4.7 %all-to-all-done.2 = bf16[8,16,2048]{2,1,0:T(8,128)(2,1)} async-done(((bf16[8,16,2048]{2,1,0:T(8,128)(2,1)}), bf16[8,16,2048]{2,1,0:T(8,128)(2,1)}, u32[]{:S(2)}, u32[]{:S(2)}) %all-to-all-start.2) | async-done | bytes 524320 | tf_op jit(solution)/shard_map/all_to_all | solution.py:23
  93.0 1.2 convert_reduce_fusion.1
  94.2 13.1 %all_gather.6 = bf16[128,2048]{1,0:T(8,128)(2,1)S(1)} all-gather(bf16[16,2048]{1,0:T(8,128)(2,1)S(1)} %fusion.26), channel_id=1, replica_groups=mesh['zp'=8,'zq'=2,'y'=4,'x'=4,'core'=2] {'x','core'}, dimensions={0}, use_global_device_ids=true | all-gather | bytes 589824 | tf_op jit(solution)/shard_map/all_gather | solution.py:52
  111.1 1.1 fusion
  112.2 5.5 %all-to-all-start.3 = ((bf16[8,16,2048]{2,1,0:T(8,128)(2,1)}), bf16[8,16,2048]{2,1,0:T(8,128)(2,1)S(1)}, u32[]{:S(2)}, u32[]{:S(2)}) async-start(bf16[8,16,2048]{2,1,0:T(8,128)(2,1)} %bitcast.120), calls=%async_computation.3 | async-start | bytes 1048576 | tf_op jit(solution)/shard_map/all_to_all | solution.py:23
  117.7 1.0 maximum_bitcast_fusion
  118.7 2.3 %copy.38.rows_t = bf16[2048,256]{1,0:T(8,128)(2,1)} copy(bf16[2048,256]{0,1:T(8,128)(2,1)} %maximum_bitcast_fusion) | data formatting | bytes 2097152 | tf_op jit(solution)/shard_map/transpose | solution.py:274
  121.6 4.3 %all-to-all-done.3 = bf16[8,16,2048]{2,1,0:T(8,128)(2,1)S(1)} async-done(((bf16[8,16,2048]{2,1,0:T(8,128)(2,1)}), bf16[8,16,2048]{2,1,0:T(8,128)(2,1)S(1)}, u32[]{:S(2)}, u32[]{:S(2)}) %all-to-all-start.3) | async-done | bytes 524320 | tf_op jit(solution)/shard_map/all_to_all | solution.py:23
  126.0 1.0 fusion.20
  127.0 1.0 fusion.24
  128.0 13.1 %all_gather.7 = bf16[128,2048]{1,0:T(8,128)(2,1)S(1)} all-gather(bf16[16,2048]{1,0:T(8,128)(2,1)S(1)} %fusion.24), channel_id=1, replica_groups=mesh['zp'=8,'zq'=2,'y'=4,'x'=4,'core'=2] {'x','core'}, dimensions={0}, use_global_device_ids=true | all-gather | bytes 589824 | tf_op jit(solution)/shard_map/all_gather | solution.py:52
  144.0 1.3 convolution_convert_fusion.1.out
  145.2 3.1 %shard_map.94 = bf16[8,8,4,32,128]{4,3,2,1,0:T(8,128)(2,1)} custom-call(bf16[2048,256]{1,0:T(8,128)(2,1)} %copy.38.rows_t, bf16[128,384]{1,0:T(8,128)(2,1)} %pad_maximum_fusion.dqkv3, bf16[128,128]{1,0:T(8,128)(2,1)} %convolution_convert_fusion.5.dq, bf16[128,128]{1,0:T(8,128)(2,1)} %convolution_convert_fusion.4.dk, ...), custom_call_target="tpu_custom_call" | custom-call | tf_op jit(solution)/shard_map/pallas_call | solution.py:168
  148.4 3.6 %all-to-all-start.4 = ((bf16[8,8,4,32,128]{4,3,2,1,0:T(8,128)(2,1)}), bf16[8,8,4,32,128]{4,3,2,1,0:T(8,128)(2,1)S(1)}, u32[]{:S(2)}, u32[]{:S(2)}) async-start(bf16[8,8,4,32,128]{4,3,2,1,0:T(8,128)(2,1)} %shard_map.94), calls=%async_computation.4 | async-start | bytes 4194304 | tf_op jit(solution)/shard_map/all_to_all | solution.py:23
  152.0 1.4 convolution_convert_fusion
  154.8 2.3 %collective-permute-start.4 = (bf16[128,2048]{1,0:T(8,128)(2,1)S(1)}, bf16[128,2048]{1,0:T(8,128)(2,1)S(1)}, u32[]{:S(2)}, u32[]{:S(2)}) collective-permute-start(bf16[128,2048]{1,0:T(8,128)(2,1)S(1)} %get-tuple-element.60), channel_id=1, source_target_pairs={{0,1},{1,0},{2,3},{3,2},{4,5},{5,4},{6,7},{7,6},{8,9},{9,8},{10,11... | collective-permute-start | bytes 1572872 | tf_op jit(solution)/shard_map/ppermute | solution.py:39
  157.0 1.5 collective-permute-done.4
  158.8 2.8 %collective-permute-start.5 = (bf16[128,2048]{1,0:T(8,128)(2,1)S(1)}, bf16[128,2048]{1,0:T(8,128)(2,1)S(1)}, u32[]{:S(2)}, u32[]{:S(2)}) collective-permute-start(bf16[128,2048]{1,0:T(8,128)(2,1)S(1)} %add_convert_fusion.2), channel_id=1, source_target_pairs={{0,2},{2,0},{4,6},{6,4},{1,3},{3,1},{5,7},{7,5},{8,10},{10,8},{12,... | collective-permute-start | bytes 1572872 | tf_op jit(solution)/shard_map/ppermute | solution.py:43
  161.6 13.3 %collective-permute-done.5 = bf16[128,2048]{1,0:T(8,128)(2,1)S(1)} collective-permute-done((bf16[128,2048]{1,0:T(8,128)(2,1)S(1)}, bf16[128,2048]{1,0:T(8,128)(2,1)S(1)}, u32[]{:S(2)}, u32[]{:S(2)}) %collective-permute-start.5) | collective-permute-done | bytes 524320 | tf_op jit(solution)/shard_map/ppermute | solution.py:43
  174.9 0.9 add_convert_fusion.1
  175.8 4.0 %collective-permute-start.6 = (bf16[128,2048]{1,0:T(8,128)(2,1)}, bf16[128,2048]{1,0:T(8,128)(2,1)}, u32[]{:S(2)}, u32[]{:S(2)}) collective-permute-start(bf16[128,2048]{1,0:T(8,128)(2,1)} %add_convert_fusion.1), channel_id=1, source_target_pairs={{0,6},{2,4},{4,2},{6,0},{1,7},{3,5},{5,3},{7,1},{8,14},{10,12},{12... | collective-permute-start | bytes 1572872 | tf_op jit(solution)/shard_map/ppermute | solution.py:43
  180.6 1.6 shard_map.95
  182.2 8.5 %all-to-all-start.5 = ((bf16[8,4,32,128]{3,2,1,0:T(8,128)(2,1)}), bf16[8,4,32,128]{3,2,1,0:T(8,128)(2,1)S(1)}, u32[]{:S(2)}, u32[]{:S(2)}) async-start(bf16[8,4,32,128]{3,2,1,0:T(8,128)(2,1)} %shard_map.95), calls=%async_computation.5 | async-start | bytes 524288 | tf_op jit(solution)/shard_map/all_to_all | solution.py:23
  190.7 1.9 collective-permute-done.6
  192.6 1.3 add_convert_fusion.tile
  193.9 1.9 collective-permute-start.7
  195.9 1.9 broadcast_select_fusion
  197.8 2.7 %shard_map.96 = (bf16[128,2048]{1,0:T(8,128)(2,1)}, bf16[128,2048]{1,0:T(8,128)(2,1)}) custom-call(s32[2]{0:T(128)S(1)} %pad_add_fusion.flags, bf16[128,2048]{1,0:T(8,128)(2,1)S(1)} %add_convert_fusion.tile, bf16[128,2048]{1,0:T(8,128)(2,1)S(1)} %collective-permute-done.7.other, bf16[128,2048]{1,0:T(8,128)(2,1)S(1)} %get-tuple-element.63.base_h, ...), custom_call_target="tpu_custom_call" | custom-call | tf_op jit(solution)/shard_map/pallas_call | solution.py:214
  200.5 11.4 %all-to-all-done.5 = bf16[8,4,32,128]{3,2,1,0:T(8,128)(2,1)S(1)} async-done(((bf16[8,4,32,128]{3,2,1,0:T(8,128)(2,1)}), bf16[8,4,32,128]{3,2,1,0:T(8,128)(2,1)S(1)}, u32[]{:S(2)}, u32[]{:S(2)}) %all-to-all-start.5) | async-done | bytes 262176 | tf_op jit(solution)/shard_map/all_to_all | solution.py:23
  (84 shorter events, 15.0 us)
Async XLA Ops:
  3.0 18.3 %collective-permute-start = (bf16[128,2048]{1,0:T(8,128)(2,1)}, bf16[128,2048]{1,0:T(8,128)(2,1)S(1)}, u32[]{:S(2)}, u32[]{:S(2)}) collective-permute-start(bf16[128,2048]{1,0:T(8,128)(2,1)} %get-tuple-element.22), channel_id=1, source_target_pairs={{0,1},{1,0},{2,3},{3,2},{4,5},{5,4},{6,7},{7,6},{8,9},{9,8},{10,11... | collective-permute-start | bytes 1572872 | tf_op jit(solution)/shard_map/ppermute | solution.py:39
  4.9 37.1 %all-to-all-start = ((bf16[8,4,32,128]{3,2,1,0:T(8,128)(2,1)}), bf16[8,4,32,128]{3,2,1,0:T(8,128)(2,1)S(1)}, u32[]{:S(2)}, u32[]{:S(2)}) async-start(bf16[8,4,32,128]{3,2,1,0:T(8,128)(2,1)} %get-tuple-element.21), calls=%async_computation | async-start | bytes 524288 | tf_op jit(solution)/shard_map/all_to_all | solution.py:23
  23.2 15.9 %collective-permute-start.1 = (bf16[128,2048]{1,0:T(8,128)(2,1)S(1)}, bf16[128,2048]{1,0:T(8,128)(2,1)S(1)}, u32[]{:S(2)}, u32[]{:S(2)}) collective-permute-start(bf16[128,2048]{1,0:T(8,128)(2,1)S(1)} %select_add_fusion), channel_id=1, source_target_pairs={{0,2},{2,0},{4,6},{6,4},{1,3},{3,1},{5,7},{7,5},{8,10},{10,8},{12,... | collective-permute-start | bytes 1572872 | tf_op jit(solution)/shard_map/ppermute | solution.py:43
  43.8 23.4 %copy-start.15 = (s32[1,8]{1,0:T(1,128)S(1)}, s32[1,8]{1,0:T(1,128)}, u32[]{:S(2)}) copy-start(s32[1,8]{1,0:T(1,128)} %depth.1) | copy-start | bytes 100
  43.8 30.9 %all-to-all-start.1 = ((bf16[8,8,4,32,128]{4,3,1,2,0:T(8,128)(2,1)}), bf16[8,8,4,32,128]{4,3,1,2,0:T(8,128)(2,1)}, u32[]{:S(2)}, u32[]{:S(2)}) async-start(bf16[8,8,4,32,128]{4,3,1,2,0:T(8,128)(2,1)} %broadcast_in_dim.13), calls=%async_computation.1 | async-start | bytes 4194304 | tf_op jit(solution)/shard_map/all_to_all | solution.py:23
  48.4 21.5 %copy-start = (f32[2048]{0:T(1024)S(1)}, f32[2048]{0:T(1024)}, u32[]{:S(2)}) copy-start(f32[2048]{0:T(1024)} %param.11) | copy-start | bytes 24580
  48.4 16.7 %collective-permute-start.2 = (bf16[128,2048]{1,0:T(8,128)(2,1)S(1)}, bf16[128,2048]{1,0:T(8,128)(2,1)S(1)}, u32[]{:S(2)}, u32[]{:S(2)}) collective-permute-start(bf16[128,2048]{1,0:T(8,128)(2,1)S(1)} %add.82), channel_id=1, source_target_pairs={{0,6},{2,4},{4,2},{6,0},{1,7},{3,5},{5,3},{7,1},{8,14},{10,12},{12... | collective-permute-start | bytes 1572872 | tf_op jit(solution)/shard_map/ppermute | solution.py:43
  65.3 3.8 %collective-permute-start.3 = (bf16[128,2048]{1,0:T(8,128)(2,1)S(1)}, bf16[128,2048]{1,0:T(8,128)(2,1)S(1)}, u32[]{:S(2)}, u32[]{:S(2)}) collective-permute-start(bf16[128,2048]{1,0:T(8,128)(2,1)S(1)} %add.83), channel_id=1, source_target_pairs={{0,1},{1,0},{2,3},{3,2},{4,5},{5,4},{6,7},{7,6},{8,9},{9,8},{10,11... | collective-permute-start | bytes 1572872 | tf_op jit(solution)/shard_map/ppermute | solution.py:39
  69.1 0.8 copy-start.11
  77.4 2.4 %copy-start.4 = (bf16[1,8,8,32,128]{4,3,2,1,0:T(8,128)(2,1)}, bf16[1,8,8,32,128]{4,3,2,1,0:T(8,128)(2,1)S(1)}, u32[]{:S(2)}) copy-start(bf16[1,8,8,32,128]{4,3,2,1,0:T(8,128)(2,1)S(1)} %get-tuple-element.46) | copy-start | bytes 1572868
  77.4 33.7 %copy-start.2 = (bf16[1,8,8,32,128]{4,3,2,1,0:T(8,128)(2,1)}, bf16[1,8,8,32,128]{4,3,2,1,0:T(8,128)(2,1)S(1)}, u32[]{:S(2)}) copy-start(bf16[1,8,8,32,128]{4,3,2,1,0:T(8,128)(2,1)S(1)} %get-tuple-element.45) | copy-start | bytes 1572868
  77.4 63.7 %copy-start.1 = (bf16[1,8,8,32,128]{4,3,2,1,0:T(8,128)(2,1)}, bf16[1,8,8,32,128]{4,3,2,1,0:T(8,128)(2,1)S(1)}, u32[]{:S(2)}) copy-start(bf16[1,8,8,32,128]{4,3,2,1,0:T(8,128)(2,1)S(1)} %get-tuple-element.44) | copy-start | bytes 1572868
  79.8 13.2 %all-to-all-start.2 = ((bf16[8,16,2048]{2,1,0:T(8,128)(2,1)}), bf16[8,16,2048]{2,1,0:T(8,128)(2,1)}, u32[]{:S(2)}, u32[]{:S(2)}) async-start(bf16[8,16,2048]{2,1,0:T(8,128)(2,1)} %bitcast.119), calls=%async_computation.2 | async-start | bytes 1048576 | tf_op jit(solution)/shard_map/all_to_all | solution.py:23
  87.2 0.8 copy-start.9
  93.0 15.7 %copy-start.5 = (bf16[1,8,8,32,128]{4,3,2,1,0:T(8,128)(2,1)S(1)}, bf16[1,8,8,32,128]{4,3,2,1,0:T(8,128)(2,1)}, u32[]{:S(2)}) copy-start(bf16[1,8,8,32,128]{4,3,2,1,0:T(8,128)(2,1)} %copy-done.4) | copy-start | bytes 1572868
  107.3 2.0 copy-start.7
  112.2 13.8 %all-to-all-start.3 = ((bf16[8,16,2048]{2,1,0:T(8,128)(2,1)}), bf16[8,16,2048]{2,1,0:T(8,128)(2,1)S(1)}, u32[]{:S(2)}, u32[]{:S(2)}) async-start(bf16[8,16,2048]{2,1,0:T(8,128)(2,1)} %bitcast.120), calls=%async_computation.3 | async-start | bytes 1048576 | tf_op jit(solution)/shard_map/all_to_all | solution.py:23
  121.0 23.0 %copy-start.10 = (bf16[128,2048]{1,0:T(8,128)(2,1)S(1)}, bf16[128,2048]{1,0:T(8,128)(2,1)}, u32[]{:S(2)}) copy-start(bf16[128,2048]{1,0:T(8,128)(2,1)} %copy-done.9) | copy-start | bytes 1572868
  141.1 2.8 %copy-start.8 = (bf16[128,2048]{1,0:T(8,128)(2,1)}, bf16[128,2048]{1,0:T(8,128)(2,1)S(1)}, u32[]{:S(2)}) copy-start(bf16[128,2048]{1,0:T(8,128)(2,1)S(1)} %all_gather.7) | copy-start | bytes 1572868
  148.3 5.1 %copy-start.12 = (bf16[128,128]{1,0:T(8,128)(2,1)S(1)}, bf16[128,128]{1,0:T(8,128)(2,1)}, u32[]{:S(2)}) copy-start(bf16[128,128]{1,0:T(8,128)(2,1)} %convolution_convert_fusion.5.dq) | copy-start | bytes 98308
  148.4 32.3 %all-to-all-start.4 = ((bf16[8,8,4,32,128]{4,3,2,1,0:T(8,128)(2,1)}), bf16[8,8,4,32,128]{4,3,2,1,0:T(8,128)(2,1)S(1)}, u32[]{:S(2)}, u32[]{:S(2)}) async-start(bf16[8,8,4,32,128]{4,3,2,1,0:T(8,128)(2,1)} %shard_map.94), calls=%async_computation.4 | async-start | bytes 4194304 | tf_op jit(solution)/shard_map/all_to_all | solution.py:23
  152.0 1.8 copy-start.6
  152.0 1.8 copy-start.13
  153.4 1.0 copy-start.3
  153.4 1.0 copy-start.14
  154.8 3.8 %collective-permute-start.4 = (bf16[128,2048]{1,0:T(8,128)(2,1)S(1)}, bf16[128,2048]{1,0:T(8,128)(2,1)S(1)}, u32[]{:S(2)}, u32[]{:S(2)}) collective-permute-start(bf16[128,2048]{1,0:T(8,128)(2,1)S(1)} %get-tuple-element.60), channel_id=1, source_target_pairs={{0,1},{1,0},{2,3},{3,2},{4,5},{5,4},{6,7},{7,6},{8,9},{9,8},{10,11... | collective-permute-start | bytes 1572872 | tf_op jit(solution)/shard_map/ppermute | solution.py:39
  158.8 16.1 %collective-permute-start.5 = (bf16[128,2048]{1,0:T(8,128)(2,1)S(1)}, bf16[128,2048]{1,0:T(8,128)(2,1)S(1)}, u32[]{:S(2)}, u32[]{:S(2)}) collective-permute-start(bf16[128,2048]{1,0:T(8,128)(2,1)S(1)} %add_convert_fusion.2), channel_id=1, source_target_pairs={{0,2},{2,0},{4,6},{6,4},{1,3},{3,1},{5,7},{7,5},{8,10},{10,8},{12,... | collective-permute-start | bytes 1572872 | tf_op jit(solution)/shard_map/ppermute | solution.py:43
  175.8 16.8 %collective-permute-start.6 = (bf16[128,2048]{1,0:T(8,128)(2,1)}, bf16[128,2048]{1,0:T(8,128)(2,1)}, u32[]{:S(2)}, u32[]{:S(2)}) collective-permute-start(bf16[128,2048]{1,0:T(8,128)(2,1)} %add_convert_fusion.1), channel_id=1, source_target_pairs={{0,6},{2,4},{4,2},{6,0},{1,7},{3,5},{5,3},{7,1},{8,14},{10,12},{12... | collective-permute-start | bytes 1572872 | tf_op jit(solution)/shard_map/ppermute | solution.py:43
  182.2 29.6 %all-to-all-start.5 = ((bf16[8,4,32,128]{3,2,1,0:T(8,128)(2,1)}), bf16[8,4,32,128]{3,2,1,0:T(8,128)(2,1)S(1)}, u32[]{:S(2)}, u32[]{:S(2)}) async-start(bf16[8,4,32,128]{3,2,1,0:T(8,128)(2,1)} %shard_map.95), calls=%async_computation.5 | async-start | bytes 524288 | tf_op jit(solution)/shard_map/all_to_all | solution.py:23
  193.9 3.9 %collective-permute-start.7 = (bf16[128,2048]{1,0:T(8,128)(2,1)S(1)}, bf16[128,2048]{1,0:T(8,128)(2,1)S(1)}, u32[]{:S(2)}, u32[]{:S(2)}) collective-permute-start(bf16[128,2048]{1,0:T(8,128)(2,1)S(1)} %add_convert_fusion.tile), channel_id=1, source_target_pairs={{0,1},{1,0},{2,3},{3,2},{4,5},{5,4},{6,7},{7,6},{8,9},{9,8},{10,11... | collective-permute-start | bytes 1572872 | tf_op jit(solution)/shard_map/ppermute | solution.py:39

commit v12 on v10

--- a/solution.py
+++ b/solution.py
@@ -213,6 +213,8 @@
     tile = tile + from_pair(tile, 3)
     other = from_core(tile)
     h1, g3 = jnp.where(core == 0, tile, other), jnp.where(core == 0, other, tile)
+    dy3 = jnp.where(live3, g3, jnp.zeros_like(g3))
+    h1, g3, dy3 = lax.optimization_barrier((h1, g3, dy3))
 
     x1 = h1.astype(F32)
     inv2, rows2 = norm_chunk(x1, gain)
@@ -221,10 +223,10 @@
     h2c = (chunk(h1).astype(F32) + sum_chunk(mixed2)).astype(BF)
     h2 = all_rows(h2c)
 
+    h2, dy3 = lax.optimization_barrier((h2, dy3))
     x2 = h2.astype(F32)
     inv3, normed3 = norm_chunk(x2, gain)
     rows3 = jnp.where(live3, normed3, jnp.zeros_like(normed3))
-    dy3 = jnp.where(live3, g3, jnp.zeros_like(g3))
     rows3 = lax.optimization_barrier(rows3)
     mixed3, keep3 = forward(rows3, w)
     dqkv3 = backward(dy3, keep3, w)
@@ -264,8 +266,9 @@
     flags = jnp.stack([core, mine.astype(jnp.int32)])
     hidden_out, grad_in = last_step(flags, tile, other, base_h, base_g, h1, inv2, gain)
     shards, hidden_out, grad_in = lax.optimization_barrier((shards, hidden_out, grad_in))
-    shard = jnp.sum(shards.astype(F32), 0)
-    return (hidden_out[None], grad_in[None], shard[:3], shard[3].T)
+    grad_qkv = jnp.sum(shards[:, :3].astype(F32), 0)
+    grad_out = jnp.sum(shards[:, 3].astype(F32), 0).T
+    return (hidden_out[None], grad_in[None], grad_qkv, grad_out)
 
 
 def solution(mesh):

time: 208 us -> 207 us (level)
  blocking collectives: 39.2 us -> 52.1 us
  waiting for transfers between devices: 68.9 us -> 62.8 us
  starting transfers between devices: 56.7 us -> 52 us
  local copies, waits for them, and re-layouts: 5.99 us -> 3.36 us
    all_to_all x1 -> x2, blocking collectives: 12.9 us -> 25.8 us  [swap(): return lax.all_to_all(x, axis, 0, 0)]
    all_to_all x5 -> x4, waiting for transfers between devices: 23.7 us -> 17.7 us  [swap(): return lax.all_to_all(x, axis, 0, 0)]
    all_to_all x5 -> x4, starting transfers between devices: 36.9 us -> 32.1 us  [swap(): return lax.all_to_all(x, axis, 0, 0)]
  transfers between devices with their start and end apart: 13 -> 12, of which waited for: 10 -> 9; matrix products, arithmetic and copies ran while one was open for 7% -> 6% of each run, Pallas kernels for 2% -> 2%
where the time goes in v12:
time: 207 us; the launch traced here: 205 us
  waiting for transfers between devices  62.8 us (30%)
  blocking collectives  52.1 us (25%)
  starting transfers between devices  52 us (25%)
  other arithmetic  16.4 us (8%)
  matrix products  9.95 us (5%)
  Pallas kernels  6.57 us (3%)
  local copies, waits for them, and re-layouts  3.36 us (2%)
    ppermute x4, waiting for transfers between devices, from_pair(): return lax.ppermute(x, 'x', [(i, i ^ bit) for i in range(CTX // 2)])  42.4 us
    all_to_all x4, starting transfers between devices, swap(): return lax.all_to_all(x, axis, 0, 0)  32.1 us
    all_gather x2, blocking collectives, all_rows(): return lax.all_gather(chunk, CONTEXT, tiled=True)  26.2 us
    all_to_all x2, blocking collectives, swap(): return lax.all_to_all(x, axis, 0, 0)  25.8 us
    all_to_all x4, waiting for transfers between devices, swap(): return lax.all_to_all(x, axis, 0, 0)  17.7 us
    ppermute x4, starting transfers between devices, from_pair(): return lax.ppermute(x, 'x', [(i, i ^ bit) for i in range(CTX // 2)])  11.9 us
    dot_general x32, matrix products, dot(): return lax.dot_general(a, b, (dims, ((), ())), preferred_element_type=F32)  9.95 us
    ppermute x4, starting transfers between devices, from_core(): return lax.ppermute(x, 'core', [(0, 1), (1, 0)])  8.01 us
  transfers between devices with their start and end apart: 12, of which 9 were waited for; matrix products, arithmetic and copies ran while one was open for 6% of the time, Pallas kernels for 2%

profile of v12, /device:TPU:6, one launch (start us, length us, event | category | flops | bytes accessed | tf_op | source)
XLA Modules:
  0.0 204.9 jit_solution(11600194659983816082)
XLA Ops:
  0.6 2.3 %shard_map.93 = (bf16[128,2048]{1,0:T(8,128)(2,1)}, bf16[8,4,32,128]{3,2,1,0:T(8,128)(2,1)}) custom-call(s32[1,8]{1,0:T(1,128)} %depth.1, bf16[128,2048]{1,0:T(8,128)(2,1)} %bitcast.118, bf16[128,2048]{1,0:T(8,128)(2,1)} %bitcast.119, bf16[3,32,128]{2,1,0:T(8,128)(2,1)} %w_qkv.1, bf16[32,128]{1,0:T(8,128)(2,1)} %bitcast.128), custom_call_target="tpu_custom_call" | custom-call | tf_op jit(solution)/shard_map/pallas_call | solution.py:132
  3.0 1.9 collective-permute-start
  4.9 15.1 %all-to-all-start = ((bf16[8,4,32,128]{3,2,1,0:T(8,128)(2,1)}), bf16[8,4,32,128]{3,2,1,0:T(8,128)(2,1)S(1)}, u32[]{:S(2)}, u32[]{:S(2)}) async-start(bf16[8,4,32,128]{3,2,1,0:T(8,128)(2,1)} %get-tuple-element.26), calls=%async_computation | async-start | bytes 524288 | tf_op jit(solution)/shard_map/all_to_all | solution.py:24
  20.0 1.2 fusion.55
  21.2 1.9 select_add_fusion
  23.1 2.7 %collective-permute-start.1 = (bf16[128,2048]{1,0:T(8,128)(2,1)S(1)}, bf16[128,2048]{1,0:T(8,128)(2,1)S(1)}, u32[]{:S(2)}, u32[]{:S(2)}) collective-permute-start(bf16[128,2048]{1,0:T(8,128)(2,1)S(1)} %select_add_fusion), channel_id=1, source_target_pairs={{0,2},{2,0},{4,6},{6,4},{1,3},{3,1},{5,7},{7,5},{8,10},{10,8},{12,... | collective-permute-start | bytes 1572872 | tf_op jit(solution)/shard_map/ppermute | solution.py:44
  25.9 13.2 %collective-permute-done.1 = bf16[128,2048]{1,0:T(8,128)(2,1)S(1)} collective-permute-done((bf16[128,2048]{1,0:T(8,128)(2,1)S(1)}, bf16[128,2048]{1,0:T(8,128)(2,1)S(1)}, u32[]{:S(2)}, u32[]{:S(2)}) %collective-permute-start.1) | collective-permute-done | bytes 524320 | tf_op jit(solution)/shard_map/ppermute | solution.py:44
  39.2 2.8 %all-to-all-done = bf16[8,4,32,128]{3,2,1,0:T(8,128)(2,1)S(1)} async-done(((bf16[8,4,32,128]{3,2,1,0:T(8,128)(2,1)}), bf16[8,4,32,128]{3,2,1,0:T(8,128)(2,1)S(1)}, u32[]{:S(2)}, u32[]{:S(2)}) %all-to-all-start) | async-done | bytes 262176 | tf_op jit(solution)/shard_map/all_to_all | solution.py:24
  42.0 1.8 broadcast_in_dim.13
  43.9 4.6 %all-to-all-start.1 = ((bf16[8,8,4,32,128]{4,3,1,2,0:T(8,128)(2,1)}), bf16[8,8,4,32,128]{4,3,1,2,0:T(8,128)(2,1)S(1)}, u32[]{:S(2)}, u32[]{:S(2)}) async-start(bf16[8,8,4,32,128]{4,3,1,2,0:T(8,128)(2,1)} %broadcast_in_dim.13), calls=%async_computation.1 | async-start | bytes 4194304 | tf_op jit(solution)/shard_map/all_to_all | solution.py:24
  48.5 2.4 %collective-permute-start.2 = (bf16[128,2048]{1,0:T(8,128)(2,1)S(1)}, bf16[128,2048]{1,0:T(8,128)(2,1)S(1)}, u32[]{:S(2)}, u32[]{:S(2)}) collective-permute-start(bf16[128,2048]{1,0:T(8,128)(2,1)S(1)} %add.82), channel_id=1, source_target_pairs={{0,6},{2,4},{4,2},{6,0},{1,7},{3,5},{5,3},{7,1},{8,14},{10,12},{12... | collective-permute-start | bytes 1572872 | tf_op jit(solution)/shard_map/ppermute | solution.py:44
  50.9 14.2 %collective-permute-done.2 = bf16[128,2048]{1,0:T(8,128)(2,1)S(1)} collective-permute-done((bf16[128,2048]{1,0:T(8,128)(2,1)S(1)}, bf16[128,2048]{1,0:T(8,128)(2,1)S(1)}, u32[]{:S(2)}, u32[]{:S(2)}) %collective-permute-start.2) | collective-permute-done | bytes 524320 | tf_op jit(solution)/shard_map/ppermute | solution.py:44
  65.2 1.9 collective-permute-start.3
  67.1 0.7 compare_reduce_fusion
  67.8 1.1 collective-permute-done.3
  69.0 1.8 broadcast_select_fusion.5
  71.1 3.4 %all-to-all-done.1 = bf16[8,8,4,32,128]{4,3,1,2,0:T(8,128)(2,1)S(1)} async-done(((bf16[8,8,4,32,128]{4,3,1,2,0:T(8,128)(2,1)}), bf16[8,8,4,32,128]{4,3,1,2,0:T(8,128)(2,1)S(1)}, u32[]{:S(2)}, u32[]{:S(2)}) %all-to-all-start.1) | async-done | bytes 2097184 | tf_op jit(solution)/shard_map/all_to_all | solution.py:24
  74.6 0.6 copy.43
  77.2 12.9 %all_to_all.30 = bf16[8,16,2048]{2,1,0:T(8,128)(2,1)S(1)} all-to-all(bf16[8,16,2048]{2,1,0:T(8,128)(2,1)S(1)} %bitcast.120), channel_id=1, replica_groups=mesh['zp'=8,'zq'=2,'y'=4,'x'=4,'core'=2] {'x','core'}, dimensions={0} | all-to-all | bytes 1048576 | tf_op jit(solution)/shard_map/all_to_all | solution.py:24
  90.2 13.1 %all_gather.6 = bf16[128,2048]{1,0:T(8,128)(2,1)S(1)} all-gather(bf16[16,2048]{1,0:T(8,128)(2,1)S(1)} %fusion.26), channel_id=1, replica_groups=mesh['zp'=8,'zq'=2,'y'=4,'x'=4,'core'=2] {'x','core'}, dimensions={0}, use_global_device_ids=true | all-gather | bytes 589824 | tf_op jit(solution)/shard_map/all_gather | solution.py:53
  103.5 1.0 fusion.19
  107.8 12.9 %all_to_all.31 = bf16[8,16,2048]{2,1,0:T(8,128)(2,1)S(1)} all-to-all(bf16[8,16,2048]{2,1,0:T(8,128)(2,1)S(1)} %bitcast.121), channel_id=1, replica_groups=mesh['zp'=8,'zq'=2,'y'=4,'x'=4,'core'=2] {'x','core'}, dimensions={0} | all-to-all | bytes 1048576 | tf_op jit(solution)/shard_map/all_to_all | solution.py:24
  121.0 0.9 fusion.24
  121.9 13.1 %all_gather.7 = bf16[128,2048]{1,0:T(8,128)(2,1)S(1)} all-gather(bf16[16,2048]{1,0:T(8,128)(2,1)S(1)} %fusion.24), channel_id=1, replica_groups=mesh['zp'=8,'zq'=2,'y'=4,'x'=4,'core'=2] {'x','core'}, dimensions={0}, use_global_device_ids=true | all-gather | bytes 589824 | tf_op jit(solution)/shard_map/all_gather | solution.py:53
  136.0 0.5 convolution_convert_fusion.4
  136.5 0.5 convolution_convert_fusion.3
  137.0 0.5 convolution_convert_fusion.2
  137.6 0.5 convolution_convert_fusion.1
  138.0 1.8 copy_bitcast_fusion
  139.9 3.8 %all-to-all-start.4 = ((bf16[8,8,4,32,128]{4,3,2,1,0:T(8,128)(2,1)}), bf16[8,8,4,32,128]{4,3,2,1,0:T(8,128)(2,1)S(1)}, u32[]{:S(2)}, u32[]{:S(2)}) async-start(bf16[8,8,4,32,128]{4,3,2,1,0:T(8,128)(2,1)} %copy_bitcast_fusion), calls=%async_computation.4 | async-start | bytes 4194304 | tf_op jit(solution)/shard_map/all_to_all | solution.py:24
  143.7 1.4 convolution_convert_fusion
  145.7 0.4 copy-done.3
  146.4 2.3 %collective-permute-start.4 = (bf16[128,2048]{1,0:T(8,128)(2,1)S(1)}, bf16[128,2048]{1,0:T(8,128)(2,1)S(1)}, u32[]{:S(2)}, u32[]{:S(2)}) collective-permute-start(bf16[128,2048]{1,0:T(8,128)(2,1)S(1)} %get-tuple-element.69), channel_id=1, source_target_pairs={{0,1},{1,0},{2,3},{3,2},{4,5},{5,4},{6,7},{7,6},{8,9},{9,8},{10,11... | collective-permute-start | bytes 1572872 | tf_op jit(solution)/shard_map/ppermute | solution.py:40
  148.7 1.5 collective-permute-done.4
  150.5 2.8 %collective-permute-start.5 = (bf16[128,2048]{1,0:T(8,128)(2,1)S(1)}, bf16[128,2048]{1,0:T(8,128)(2,1)S(1)}, u32[]{:S(2)}, u32[]{:S(2)}) collective-permute-start(bf16[128,2048]{1,0:T(8,128)(2,1)S(1)} %add_convert_fusion.2), channel_id=1, source_target_pairs={{0,2},{2,0},{4,6},{6,4},{1,3},{3,1},{5,7},{7,5},{8,10},{10,8},{12,... | collective-permute-start | bytes 1572872 | tf_op jit(solution)/shard_map/ppermute | solution.py:44
  153.3 13.3 %collective-permute-done.5 = bf16[128,2048]{1,0:T(8,128)(2,1)S(1)} collective-permute-done((bf16[128,2048]{1,0:T(8,128)(2,1)S(1)}, bf16[128,2048]{1,0:T(8,128)(2,1)S(1)}, u32[]{:S(2)}, u32[]{:S(2)}) %collective-permute-start.5) | collective-permute-done | bytes 524320 | tf_op jit(solution)/shard_map/ppermute | solution.py:44
  166.6 0.9 add_convert_fusion.1
  167.5 4.0 %collective-permute-start.6 = (bf16[128,2048]{1,0:T(8,128)(2,1)}, bf16[128,2048]{1,0:T(8,128)(2,1)}, u32[]{:S(2)}, u32[]{:S(2)}) collective-permute-start(bf16[128,2048]{1,0:T(8,128)(2,1)} %add_convert_fusion.1), channel_id=1, source_target_pairs={{0,6},{2,4},{4,2},{6,0},{1,7},{3,5},{5,3},{7,1},{8,14},{10,12},{12... | collective-permute-start | bytes 1572872 | tf_op jit(solution)/shard_map/ppermute | solution.py:44
  172.3 1.6 shard_map.94
  173.9 8.6 %all-to-all-start.5 = ((bf16[8,4,32,128]{3,2,1,0:T(8,128)(2,1)}), bf16[8,4,32,128]{3,2,1,0:T(8,128)(2,1)S(1)}, u32[]{:S(2)}, u32[]{:S(2)}) async-start(bf16[8,4,32,128]{3,2,1,0:T(8,128)(2,1)} %shard_map.94), calls=%async_computation.5 | async-start | bytes 524288 | tf_op jit(solution)/shard_map/all_to_all | solution.py:24
  182.5 1.8 collective-permute-done.6
  184.3 1.3 add_convert_fusion.tile
  185.6 1.9 collective-permute-start.7
  187.5 2.0 broadcast_select_fusion
  189.5 2.7 %shard_map.95 = (bf16[128,2048]{1,0:T(8,128)(2,1)}, bf16[128,2048]{1,0:T(8,128)(2,1)}) custom-call(s32[2]{0:T(128)S(1)} %pad_add_fusion.flags, bf16[128,2048]{1,0:T(8,128)(2,1)S(1)} %add_convert_fusion.tile, bf16[128,2048]{1,0:T(8,128)(2,1)S(1)} %collective-permute-done.7.other, bf16[128,2048]{1,0:T(8,128)(2,1)S(1)} %get-tuple-element.72.base_h, ...), custom_call_target="tpu_custom_call" | custom-call | tf_op jit(solution)/shard_map/pallas_call | solution.py:181
  192.2 11.5 %all-to-all-done.5 = bf16[8,4,32,128]{3,2,1,0:T(8,128)(2,1)S(1)} async-done(((bf16[8,4,32,128]{3,2,1,0:T(8,128)(2,1)}), bf16[8,4,32,128]{3,2,1,0:T(8,128)(2,1)S(1)}, u32[]{:S(2)}, u32[]{:S(2)}) %all-to-all-start.5) | async-done | bytes 262176 | tf_op jit(solution)/shard_map/all_to_all | solution.py:24
  203.7 0.6 convert_reduce_fusion.2
  204.3 0.6 convert_reduce_fusion.3
  (69 shorter events, 8.7 us)
Async XLA Ops:
  3.0 18.3 %collective-permute-start = (bf16[128,2048]{1,0:T(8,128)(2,1)}, bf16[128,2048]{1,0:T(8,128)(2,1)S(1)}, u32[]{:S(2)}, u32[]{:S(2)}) collective-permute-start(bf16[128,2048]{1,0:T(8,128)(2,1)} %get-tuple-element.27), channel_id=1, source_target_pairs={{0,1},{1,0},{2,3},{3,2},{4,5},{5,4},{6,7},{7,6},{8,9},{9,8},{10,11... | collective-permute-start | bytes 1572872 | tf_op jit(solution)/shard_map/ppermute | solution.py:40
  4.9 37.1 %all-to-all-start = ((bf16[8,4,32,128]{3,2,1,0:T(8,128)(2,1)}), bf16[8,4,32,128]{3,2,1,0:T(8,128)(2,1)S(1)}, u32[]{:S(2)}, u32[]{:S(2)}) async-start(bf16[8,4,32,128]{3,2,1,0:T(8,128)(2,1)} %get-tuple-element.26), calls=%async_computation | async-start | bytes 524288 | tf_op jit(solution)/shard_map/all_to_all | solution.py:24
  23.1 15.9 %collective-permute-start.1 = (bf16[128,2048]{1,0:T(8,128)(2,1)S(1)}, bf16[128,2048]{1,0:T(8,128)(2,1)S(1)}, u32[]{:S(2)}, u32[]{:S(2)}) collective-permute-start(bf16[128,2048]{1,0:T(8,128)(2,1)S(1)} %select_add_fusion), channel_id=1, source_target_pairs={{0,2},{2,0},{4,6},{6,4},{1,3},{3,1},{5,7},{7,5},{8,10},{10,8},{12,... | collective-permute-start | bytes 1572872 | tf_op jit(solution)/shard_map/ppermute | solution.py:44
  43.9 23.2 %copy-start.9 = (s32[1,8]{1,0:T(1,128)S(1)}, s32[1,8]{1,0:T(1,128)}, u32[]{:S(2)}) copy-start(s32[1,8]{1,0:T(1,128)} %depth.1) | copy-start | bytes 100
  43.9 30.7 %all-to-all-start.1 = ((bf16[8,8,4,32,128]{4,3,1,2,0:T(8,128)(2,1)}), bf16[8,8,4,32,128]{4,3,1,2,0:T(8,128)(2,1)S(1)}, u32[]{:S(2)}, u32[]{:S(2)}) async-start(bf16[8,8,4,32,128]{4,3,1,2,0:T(8,128)(2,1)} %broadcast_in_dim.13), calls=%async_computation.1 | async-start | bytes 4194304 | tf_op jit(solution)/shard_map/all_to_all | solution.py:24
  48.5 22.4 %copy-start = (f32[2048]{0:T(1024)S(1)}, f32[2048]{0:T(1024)}, u32[]{:S(2)}) copy-start(f32[2048]{0:T(1024)} %param.11) | copy-start | bytes 24580
  48.5 16.5 %collective-permute-start.2 = (bf16[128,2048]{1,0:T(8,128)(2,1)S(1)}, bf16[128,2048]{1,0:T(8,128)(2,1)S(1)}, u32[]{:S(2)}, u32[]{:S(2)}) collective-permute-start(bf16[128,2048]{1,0:T(8,128)(2,1)S(1)} %add.82), channel_id=1, source_target_pairs={{0,6},{2,4},{4,2},{6,0},{1,7},{3,5},{5,3},{7,1},{8,14},{10,12},{12... | collective-permute-start | bytes 1572872 | tf_op jit(solution)/shard_map/ppermute | solution.py:44
  65.2 3.8 %collective-permute-start.3 = (bf16[128,2048]{1,0:T(8,128)(2,1)S(1)}, bf16[128,2048]{1,0:T(8,128)(2,1)S(1)}, u32[]{:S(2)}, u32[]{:S(2)}) collective-permute-start(bf16[128,2048]{1,0:T(8,128)(2,1)S(1)} %add.83), channel_id=1, source_target_pairs={{0,1},{1,0},{2,3},{3,2},{4,5},{5,4},{6,7},{7,6},{8,9},{9,8},{10,11... | collective-permute-start | bytes 1572872 | tf_op jit(solution)/shard_map/ppermute | solution.py:40
  75.5 31.6 %copy-start.4 = (bf16[1,8,8,32,128]{4,3,2,1,0:T(8,128)(2,1)}, bf16[1,8,8,32,128]{4,3,2,1,0:T(8,128)(2,1)S(1)}, u32[]{:S(2)}) copy-start(bf16[1,8,8,32,128]{4,3,2,1,0:T(8,128)(2,1)S(1)} %get-tuple-element.54) | copy-start | bytes 1572868
  75.5 31.9 %copy-start.2 = (bf16[1,8,8,32,128]{4,3,2,1,0:T(8,128)(2,1)}, bf16[1,8,8,32,128]{4,3,2,1,0:T(8,128)(2,1)S(1)}, u32[]{:S(2)}) copy-start(bf16[1,8,8,32,128]{4,3,2,1,0:T(8,128)(2,1)S(1)} %get-tuple-element.53) | copy-start | bytes 1572868
  75.5 59.5 %copy-start.1 = (bf16[1,8,8,32,128]{4,3,2,1,0:T(8,128)(2,1)}, bf16[1,8,8,32,128]{4,3,2,1,0:T(8,128)(2,1)S(1)}, u32[]{:S(2)}) copy-start(bf16[1,8,8,32,128]{4,3,2,1,0:T(8,128)(2,1)S(1)} %get-tuple-element.52) | copy-start | bytes 1572868
  103.3 17.7 %copy-start.6 = (bf16[128,2048]{1,0:T(8,128)(2,1)}, bf16[128,2048]{1,0:T(8,128)(2,1)S(1)}, u32[]{:S(2)}) copy-start(bf16[128,2048]{1,0:T(8,128)(2,1)S(1)} %all_gather.6) | copy-start | bytes 1572868
  103.5 1.9 copy-start.8
  135.0 2.5 %copy-start.7 = (bf16[128,2048]{1,0:T(8,128)(2,1)}, bf16[128,2048]{1,0:T(8,128)(2,1)S(1)}, u32[]{:S(2)}) copy-start(bf16[128,2048]{1,0:T(8,128)(2,1)S(1)} %all_gather.7) | copy-start | bytes 1572868
  139.9 32.4 %all-to-all-start.4 = ((bf16[8,8,4,32,128]{4,3,2,1,0:T(8,128)(2,1)}), bf16[8,8,4,32,128]{4,3,2,1,0:T(8,128)(2,1)S(1)}, u32[]{:S(2)}, u32[]{:S(2)}) async-start(bf16[8,8,4,32,128]{4,3,2,1,0:T(8,128)(2,1)} %copy_bitcast_fusion), calls=%async_computation.4 | async-start | bytes 4194304 | tf_op jit(solution)/shard_map/all_to_all | solution.py:24
  143.7 1.7 copy-start.5
  145.1 1.0 copy-start.3
  146.4 3.8 %collective-permute-start.4 = (bf16[128,2048]{1,0:T(8,128)(2,1)S(1)}, bf16[128,2048]{1,0:T(8,128)(2,1)S(1)}, u32[]{:S(2)}, u32[]{:S(2)}) collective-permute-start(bf16[128,2048]{1,0:T(8,128)(2,1)S(1)} %get-tuple-element.69), channel_id=1, source_target_pairs={{0,1},{1,0},{2,3},{3,2},{4,5},{5,4},{6,7},{7,6},{8,9},{9,8},{10,11... | collective-permute-start | bytes 1572872 | tf_op jit(solution)/shard_map/ppermute | solution.py:40
  150.5 16.1 %collective-permute-start.5 = (bf16[128,2048]{1,0:T(8,128)(2,1)S(1)}, bf16[128,2048]{1,0:T(8,128)(2,1)S(1)}, u32[]{:S(2)}, u32[]{:S(2)}) collective-permute-start(bf16[128,2048]{1,0:T(8,128)(2,1)S(1)} %add_convert_fusion.2), channel_id=1, source_target_pairs={{0,2},{2,0},{4,6},{6,4},{1,3},{3,1},{5,7},{7,5},{8,10},{10,8},{12,... | collective-permute-start | bytes 1572872 | tf_op jit(solution)/shard_map/ppermute | solution.py:44
  167.5 16.8 %collective-permute-start.6 = (bf16[128,2048]{1,0:T(8,128)(2,1)}, bf16[128,2048]{1,0:T(8,128)(2,1)}, u32[]{:S(2)}, u32[]{:S(2)}) collective-permute-start(bf16[128,2048]{1,0:T(8,128)(2,1)} %add_convert_fusion.1), channel_id=1, source_target_pairs={{0,6},{2,4},{4,2},{6,0},{1,7},{3,5},{5,3},{7,1},{8,14},{10,12},{12... | collective-permute-start | bytes 1572872 | tf_op jit(solution)/shard_map/ppermute | solution.py:44
  173.9 29.7 %all-to-all-start.5 = ((bf16[8,4,32,128]{3,2,1,0:T(8,128)(2,1)}), bf16[8,4,32,128]{3,2,1,0:T(8,128)(2,1)S(1)}, u32[]{:S(2)}, u32[]{:S(2)}) async-start(bf16[8,4,32,128]{3,2,1,0:T(8,128)(2,1)} %shard_map.94), calls=%async_computation.5 | async-start | bytes 524288 | tf_op jit(solution)/shard_map/all_to_all | solution.py:24
  185.6 3.9 %collective-permute-start.7 = (bf16[128,2048]{1,0:T(8,128)(2,1)S(1)}, bf16[128,2048]{1,0:T(8,128)(2,1)S(1)}, u32[]{:S(2)}, u32[]{:S(2)}) collective-permute-start(bf16[128,2048]{1,0:T(8,128)(2,1)S(1)} %add_convert_fusion.tile), channel_id=1, source_target_pairs={{0,1},{1,0},{2,3},{3,2},{4,5},{5,4},{6,7},{7,6},{8,9},{9,8},{10,11... | collective-permute-start | bytes 1572872 | tf_op jit(solution)/shard_map/ppermute | solution.py:40

commit v13 on v12

--- a/solution.py
+++ b/solution.py
@@ -95,55 +95,38 @@
     return inv * u - x32 * inv**3 * jnp.mean(x32 * u, -1, keepdims=True)
 
 
-def first_kernel(depth, h, g, w_qkv, w_out, sent, shards, qkv_in, out_in, sems):
+def first_kernel(h, g, w_qkv, w_out, sent, shards, sems, tile_sems):
+    parts = []
+    for i in range(NP):
+        parts.append(pltpu.make_async_copy(w_qkv, shards.at[i, pl.ds(0, 3)], sems.at[i, 0]))
+        parts.append(pltpu.make_async_copy(w_out, shards.at[i, 3], sems.at[i, 1]))
+    for part in parts:
+        part.start()
     core = lax.axis_index("core")
-    live = depth[0, lax.axis_index("x") * 2 + core] >= 2
-    weights = [
-        pltpu.make_async_copy(w_qkv, qkv_in, sems.at[0]),
-        pltpu.make_async_copy(w_out, out_in, sems.at[1]),
-    ]
-    for copy in weights:
-        copy.start()
-
-    @pl.when(live & (core == 0))
-    def _():
-        copy = pltpu.make_async_copy(g, sent, sems.at[2])
-        copy.start()
-        copy.wait()
-
-    @pl.when(live & (core == 1))
-    def _():
-        copy = pltpu.make_async_copy(h, sent, sems.at[3])
-        copy.start()
-        copy.wait()
-
-    @pl.when(jnp.logical_not(live))
-    def _():
-        sent[...] = jnp.zeros_like(sent)
-
-    for copy in weights:
-        copy.wait()
-    for i in range(NP):
-        shards[i, :3] = qkv_in[...]
-        shards[i, 3] = out_in[...]
-
-
-def first_step(depth, h, g, w_qkv, w_out):
+    for i, tile in enumerate((g, h)):
+
+        @pl.when(core == i)
+        def _(i=i, tile=tile):
+            copy = pltpu.make_async_copy(tile, sent, tile_sems.at[i])
+            copy.start()
+            copy.wait()
+
+    for part in parts:
+        part.wait()
+
+
+def first_step(h, g, w_qkv, w_out):
     return pl.pallas_call(
         first_kernel,
-        in_specs=[pl.BlockSpec(memory_space=pltpu.SMEM)] + [pl.BlockSpec(memory_space=pl.ANY)] * 4,
-        out_specs=[pl.BlockSpec(memory_space=pltpu.VMEM)] * 2,
+        in_specs=[pl.BlockSpec(memory_space=pl.ANY)] * 4,
+        out_specs=[pl.BlockSpec(memory_space=pl.ANY)] * 2,
         out_shape=[
             jax.ShapeDtypeStruct((TILE, D), BF),
             jax.ShapeDtypeStruct((NP, 4, 32, HD), BF),
         ],
-        scratch_shapes=[
-            pltpu.VMEM((3, 32, HD), BF),
-            pltpu.VMEM((32, HD), BF),
-            pltpu.SemaphoreType.DMA((4,)),
-        ],
+        scratch_shapes=[pltpu.SemaphoreType.DMA((NP, 2)), pltpu.SemaphoreType.DMA((2,))],
         compiler_params=pltpu.CompilerParams(vmem_limit_bytes=60 * 2**20),
-    )(depth, h, g, w_qkv, w_out)
+    )(h, g, w_qkv, w_out)
 
 
 def sum_kernel(terms, out):
@@ -202,9 +185,10 @@
     tokens = ((0,), (0,))
     core = lax.axis_index("core")
     none = jnp.zeros_like(hidden_in[0])
-    sent, shards = first_step(tile_depth, hidden_in[0], cotangent[0], w_qkv, w_out.T)
+    sent, shards = first_step(hidden_in[0], cotangent[0], w_qkv, w_out.T)
+    near_mine = lax.dynamic_index_in_dim(depth, me + 1 - 2 * core, 0, keepdims=False) >= 2
     kept = jnp.where(mine, jnp.where(core == 0, hidden_in[0], cotangent[0]), none)
-    tile = kept + from_core(sent)
+    tile = jnp.where(near_mine, from_core(sent), kept)
     tile = tile + from_pair(tile, 1)
 
     near = swap(shards, "zp")

time: 207 us -> 229 us (1.11)
  Pallas kernels: 6.57 us -> 29.3 us
  other arithmetic: 16.4 us -> 13.8 us
    pallas_call x1, Pallas kernels: 2.31 us -> 25.1 us  [first_step(): pl.pallas_call(first_kernel, in_specs=[pl.BlockSpec(memory_space=pl.ANY)]...]
  transfers between devices with their start and end apart: 12 -> 12, of which waited for: 9 -> 10; matrix products, arithmetic and copies ran while one was open for 6% -> 5% of each run, Pallas kernels for 2% -> 2%
where the time goes in v13:
time: 229 us; the launch traced here: 228 us
  waiting for transfers between devices  62.8 us (27%)
  starting transfers between devices  52.8 us (23%)
  blocking collectives  52.1 us (23%)
  Pallas kernels  29.3 us (13%)
  other arithmetic  13.8 us (6%)
  matrix products  9.95 us (4%)
  local copies, waits for them, and re-layouts  4.74 us (2%)
  between operations  2.45 us (1%)
    ppermute x4, waiting for transfers between devices, from_pair(): return lax.ppermute(x, 'x', [(i, i ^ bit) for i in range(CTX // 2)])  42.2 us
    all_to_all x4, starting transfers between devices, swap(): return lax.all_to_all(x, axis, 0, 0)  32.9 us
    all_gather x2, blocking collectives, all_rows(): return lax.all_gather(chunk, CONTEXT, tiled=True)  26.2 us
    all_to_all x2, blocking collectives, swap(): return lax.all_to_all(x, axis, 0, 0)  25.8 us
    pallas_call x1, Pallas kernels, first_step(): pl.pallas_call(first_kernel, in_specs=[pl.BlockSpec(memory_space=pl.ANY)]...  25.1 us
    all_to_all x4, waiting for transfers between devices, swap(): return lax.all_to_all(x, axis, 0, 0)  17.3 us
    ppermute x4, starting transfers between devices, from_pair(): return lax.ppermute(x, 'x', [(i, i ^ bit) for i in range(CTX // 2)])  11.9 us
    dot_general x32, matrix products, dot(): return lax.dot_general(a, b, (dims, ((), ())), preferred_element_type=F32)  9.95 us
  transfers between devices with their start and end apart: 12, of which 10 were waited for; matrix products, arithmetic and copies ran while one was open for 5% of the time, Pallas kernels for 2%

profile of v13, /device:TPU:6, one launch (start us, length us, event | category | flops | bytes accessed | tf_op | source)
XLA Modules:
  0.0 227.9 jit_solution(9013910969838521263)
XLA Ops:
  0.6 25.1 %shard_map.93 = (bf16[128,2048]{1,0:T(8,128)(2,1)}, bf16[8,4,32,128]{3,2,1,0:T(8,128)(2,1)}) custom-call(bf16[128,2048]{1,0:T(8,128)(2,1)} %bitcast.119, bf16[128,2048]{1,0:T(8,128)(2,1)} %bitcast.120, bf16[3,32,128]{2,1,0:T(8,128)(2,1)} %w_qkv.1, bf16[32,128]{1,0:T(8,128)(2,1)} %bitcast.129), custom_call_target="tpu_custom_call" | custom-call | tf_op jit(solution)/shard_map/pallas_call | solution.py:119
  25.8 1.9 collective-permute-start
  27.7 15.1 %all-to-all-start = ((bf16[8,4,32,128]{3,2,1,0:T(8,128)(2,1)}), bf16[8,4,32,128]{3,2,1,0:T(8,128)(2,1)S(1)}, u32[]{:S(2)}, u32[]{:S(2)}) async-start(bf16[8,4,32,128]{3,2,1,0:T(8,128)(2,1)} %get-tuple-element.26), calls=%async_computation | async-start | bytes 524288 | tf_op jit(solution)/shard_map/all_to_all | solution.py:24
  42.8 1.4 constant_dynamic-slice_fusion.1
  45.5 1.3 select_select_fusion
  46.8 2.7 %collective-permute-start.1 = (bf16[128,2048]{1,0:T(8,128)(2,1)S(1)}, bf16[128,2048]{1,0:T(8,128)(2,1)S(1)}, u32[]{:S(2)}, u32[]{:S(2)}) collective-permute-start(bf16[128,2048]{1,0:T(8,128)(2,1)S(1)} %select_select_fusion), channel_id=1, source_target_pairs={{0,2},{2,0},{4,6},{6,4},{1,3},{3,1},{5,7},{7,5},{8,10},{10,8},{12,... | collective-permute-start | bytes 1572872 | tf_op jit(solution)/shard_map/ppermute | solution.py:44
  49.6 13.2 %collective-permute-done.1 = bf16[128,2048]{1,0:T(8,128)(2,1)S(1)} collective-permute-done((bf16[128,2048]{1,0:T(8,128)(2,1)S(1)}, bf16[128,2048]{1,0:T(8,128)(2,1)S(1)}, u32[]{:S(2)}, u32[]{:S(2)}) %collective-permute-start.1) | collective-permute-done | bytes 524320 | tf_op jit(solution)/shard_map/ppermute | solution.py:44
  62.9 1.9 all-to-all-done
  64.8 1.8 broadcast_in_dim.13
  66.7 4.6 %all-to-all-start.1 = ((bf16[8,8,4,32,128]{4,3,1,2,0:T(8,128)(2,1)}), bf16[8,8,4,32,128]{4,3,1,2,0:T(8,128)(2,1)S(1)}, u32[]{:S(2)}, u32[]{:S(2)}) async-start(bf16[8,8,4,32,128]{4,3,1,2,0:T(8,128)(2,1)} %broadcast_in_dim.13), calls=%async_computation.1 | async-start | bytes 4194304 | tf_op jit(solution)/shard_map/all_to_all | solution.py:24
  71.3 2.4 %collective-permute-start.2 = (bf16[128,2048]{1,0:T(8,128)(2,1)S(1)}, bf16[128,2048]{1,0:T(8,128)(2,1)S(1)}, u32[]{:S(2)}, u32[]{:S(2)}) collective-permute-start(bf16[128,2048]{1,0:T(8,128)(2,1)S(1)} %add.86), channel_id=1, source_target_pairs={{0,6},{2,4},{4,2},{6,0},{1,7},{3,5},{5,3},{7,1},{8,14},{10,12},{12... | collective-permute-start | bytes 1572872 | tf_op jit(solution)/shard_map/ppermute | solution.py:44
  73.7 14.2 %collective-permute-done.2 = bf16[128,2048]{1,0:T(8,128)(2,1)S(1)} collective-permute-done((bf16[128,2048]{1,0:T(8,128)(2,1)S(1)}, bf16[128,2048]{1,0:T(8,128)(2,1)S(1)}, u32[]{:S(2)}, u32[]{:S(2)}) %collective-permute-start.2) | collective-permute-done | bytes 524320 | tf_op jit(solution)/shard_map/ppermute | solution.py:44
  88.0 1.9 collective-permute-start.3
  89.9 0.6 compare_reduce_fusion
  90.5 1.2 collective-permute-done.3
  91.8 1.7 broadcast_select_fusion.5
  93.9 3.5 %all-to-all-done.1 = bf16[8,8,4,32,128]{4,3,1,2,0:T(8,128)(2,1)S(1)} async-done(((bf16[8,8,4,32,128]{4,3,1,2,0:T(8,128)(2,1)}), bf16[8,8,4,32,128]{4,3,1,2,0:T(8,128)(2,1)S(1)}, u32[]{:S(2)}, u32[]{:S(2)}) %all-to-all-start.1) | async-done | bytes 2097184 | tf_op jit(solution)/shard_map/all_to_all | solution.py:24
  97.4 0.6 copy.43
  100.0 12.9 %all_to_all.30 = bf16[8,16,2048]{2,1,0:T(8,128)(2,1)S(1)} all-to-all(bf16[8,16,2048]{2,1,0:T(8,128)(2,1)S(1)} %bitcast.121), channel_id=1, replica_groups=mesh['zp'=8,'zq'=2,'y'=4,'x'=4,'core'=2] {'x','core'}, dimensions={0} | all-to-all | bytes 1048576 | tf_op jit(solution)/shard_map/all_to_all | solution.py:24
  113.0 13.1 %all_gather.6 = bf16[128,2048]{1,0:T(8,128)(2,1)S(1)} all-gather(bf16[16,2048]{1,0:T(8,128)(2,1)S(1)} %fusion.26), channel_id=1, replica_groups=mesh['zp'=8,'zq'=2,'y'=4,'x'=4,'core'=2] {'x','core'}, dimensions={0}, use_global_device_ids=true | all-gather | bytes 589824 | tf_op jit(solution)/shard_map/all_gather | solution.py:53
  126.3 0.9 fusion.19
  130.5 12.9 %all_to_all.31 = bf16[8,16,2048]{2,1,0:T(8,128)(2,1)S(1)} all-to-all(bf16[8,16,2048]{2,1,0:T(8,128)(2,1)S(1)} %bitcast.122), channel_id=1, replica_groups=mesh['zp'=8,'zq'=2,'y'=4,'x'=4,'core'=2] {'x','core'}, dimensions={0} | all-to-all | bytes 1048576 | tf_op jit(solution)/shard_map/all_to_all | solution.py:24
  143.7 0.9 fusion.24
  144.7 13.1 %all_gather.7 = bf16[128,2048]{1,0:T(8,128)(2,1)S(1)} all-gather(bf16[16,2048]{1,0:T(8,128)(2,1)S(1)} %fusion.24), channel_id=1, replica_groups=mesh['zp'=8,'zq'=2,'y'=4,'x'=4,'core'=2] {'x','core'}, dimensions={0}, use_global_device_ids=true | all-gather | bytes 589824 | tf_op jit(solution)/shard_map/all_gather | solution.py:53
  158.8 0.5 convolution_convert_fusion.4
  159.3 0.5 convolution_convert_fusion.3
  159.8 0.5 convolution_convert_fusion.2
  160.3 0.5 convolution_convert_fusion.1
  160.8 1.8 copy_bitcast_fusion
  162.6 3.8 %all-to-all-start.4 = ((bf16[8,8,4,32,128]{4,3,2,1,0:T(8,128)(2,1)}), bf16[8,8,4,32,128]{4,3,2,1,0:T(8,128)(2,1)S(1)}, u32[]{:S(2)}, u32[]{:S(2)}) async-start(bf16[8,8,4,32,128]{4,3,2,1,0:T(8,128)(2,1)} %copy_bitcast_fusion), calls=%async_computation.4 | async-start | bytes 4194304 | tf_op jit(solution)/shard_map/all_to_all | solution.py:24
  166.4 1.4 convolution_convert_fusion
  169.2 2.3 collective-permute-start.4
  171.5 1.5 collective-permute-done.4
  173.3 2.8 %collective-permute-start.5 = (bf16[128,2048]{1,0:T(8,128)(2,1)S(1)}, bf16[128,2048]{1,0:T(8,128)(2,1)S(1)}, u32[]{:S(2)}, u32[]{:S(2)}) collective-permute-start(bf16[128,2048]{1,0:T(8,128)(2,1)S(1)} %add_convert_fusion.2), channel_id=1, source_target_pairs={{0,2},{2,0},{4,6},{6,4},{1,3},{3,1},{5,7},{7,5},{8,10},{10,8},{12,... | collective-permute-start | bytes 1572872 | tf_op jit(solution)/shard_map/ppermute | solution.py:44
  176.0 13.3 %collective-permute-done.5 = bf16[128,2048]{1,0:T(8,128)(2,1)S(1)} collective-permute-done((bf16[128,2048]{1,0:T(8,128)(2,1)S(1)}, bf16[128,2048]{1,0:T(8,128)(2,1)S(1)}, u32[]{:S(2)}, u32[]{:S(2)}) %collective-permute-start.5) | collective-permute-done | bytes 524320 | tf_op jit(solution)/shard_map/ppermute | solution.py:44
  189.3 0.9 add_convert_fusion.1
  190.2 4.0 %collective-permute-start.6 = (bf16[128,2048]{1,0:T(8,128)(2,1)}, bf16[128,2048]{1,0:T(8,128)(2,1)}, u32[]{:S(2)}, u32[]{:S(2)}) collective-permute-start(bf16[128,2048]{1,0:T(8,128)(2,1)} %add_convert_fusion.1), channel_id=1, source_target_pairs={{0,6},{2,4},{4,2},{6,0},{1,7},{3,5},{5,3},{7,1},{8,14},{10,12},{12... | collective-permute-start | bytes 1572872 | tf_op jit(solution)/shard_map/ppermute | solution.py:44
  194.4 1.6 shard_map.94
  196.0 9.5 %all-to-all-start.5 = ((bf16[8,4,32,128]{3,2,1,0:T(8,128)(2,1)}), bf16[8,4,32,128]{3,2,1,0:T(8,128)(2,1)S(1)}, u32[]{:S(2)}, u32[]{:S(2)}) async-start(bf16[8,4,32,128]{3,2,1,0:T(8,128)(2,1)} %shard_map.94), calls=%async_computation.5 | async-start | bytes 524288 | tf_op jit(solution)/shard_map/all_to_all | solution.py:24
  205.5 1.6 collective-permute-done.6
  207.0 1.3 add_convert_fusion.tile
  208.4 1.9 collective-permute-start.7
  210.3 1.3 broadcast_select_fusion
  211.6 0.6 collective-permute-done.7.other
  212.2 2.6 %shard_map.95 = (bf16[128,2048]{1,0:T(8,128)(2,1)}, bf16[128,2048]{1,0:T(8,128)(2,1)}) custom-call(s32[2]{0:T(128)S(1)} %pad_add_fusion.flags, bf16[128,2048]{1,0:T(8,128)(2,1)S(1)} %add_convert_fusion.tile, bf16[128,2048]{1,0:T(8,128)(2,1)S(1)} %collective-permute-done.7.other, bf16[128,2048]{1,0:T(8,128)(2,1)S(1)} %get-tuple-element.74.base_h, ...), custom_call_target="tpu_custom_call" | custom-call | tf_op jit(solution)/shard_map/pallas_call | solution.py:164
  214.8 11.8 %all-to-all-done.5 = bf16[8,4,32,128]{3,2,1,0:T(8,128)(2,1)S(1)} async-done(((bf16[8,4,32,128]{3,2,1,0:T(8,128)(2,1)}), bf16[8,4,32,128]{3,2,1,0:T(8,128)(2,1)S(1)}, u32[]{:S(2)}, u32[]{:S(2)}) %all-to-all-start.5) | async-done | bytes 262176 | tf_op jit(solution)/shard_map/all_to_all | solution.py:24
  226.6 0.6 convert_reduce_fusion.2
  227.3 0.6 convert_reduce_fusion.3
  (69 shorter events, 9.1 us)
Async XLA Ops:
  25.8 19.8 %collective-permute-start = (bf16[128,2048]{1,0:T(8,128)(2,1)}, bf16[128,2048]{1,0:T(8,128)(2,1)S(1)}, u32[]{:S(2)}, u32[]{:S(2)}) collective-permute-start(bf16[128,2048]{1,0:T(8,128)(2,1)} %get-tuple-element.27), channel_id=1, source_target_pairs={{0,1},{1,0},{2,3},{3,2},{4,5},{5,4},{6,7},{7,6},{8,9},{9,8},{10,11... | collective-permute-start | bytes 1572872 | tf_op jit(solution)/shard_map/ppermute | solution.py:40
  27.7 37.1 %all-to-all-start = ((bf16[8,4,32,128]{3,2,1,0:T(8,128)(2,1)}), bf16[8,4,32,128]{3,2,1,0:T(8,128)(2,1)S(1)}, u32[]{:S(2)}, u32[]{:S(2)}) async-start(bf16[8,4,32,128]{3,2,1,0:T(8,128)(2,1)} %get-tuple-element.26), calls=%async_computation | async-start | bytes 524288 | tf_op jit(solution)/shard_map/all_to_all | solution.py:24
  46.8 15.9 %collective-permute-start.1 = (bf16[128,2048]{1,0:T(8,128)(2,1)S(1)}, bf16[128,2048]{1,0:T(8,128)(2,1)S(1)}, u32[]{:S(2)}, u32[]{:S(2)}) collective-permute-start(bf16[128,2048]{1,0:T(8,128)(2,1)S(1)} %select_select_fusion), channel_id=1, source_target_pairs={{0,2},{2,0},{4,6},{6,4},{1,3},{3,1},{5,7},{7,5},{8,10},{10,8},{12,... | collective-permute-start | bytes 1572872 | tf_op jit(solution)/shard_map/ppermute | solution.py:44
  66.7 23.2 %copy-start.9 = (s32[1,8]{1,0:T(1,128)S(1)}, s32[1,8]{1,0:T(1,128)}, u32[]{:S(2)}) copy-start(s32[1,8]{1,0:T(1,128)} %param.8) | copy-start | bytes 100
  66.7 30.7 %all-to-all-start.1 = ((bf16[8,8,4,32,128]{4,3,1,2,0:T(8,128)(2,1)}), bf16[8,8,4,32,128]{4,3,1,2,0:T(8,128)(2,1)S(1)}, u32[]{:S(2)}, u32[]{:S(2)}) async-start(bf16[8,8,4,32,128]{4,3,1,2,0:T(8,128)(2,1)} %broadcast_in_dim.13), calls=%async_computation.1 | async-start | bytes 4194304 | tf_op jit(solution)/shard_map/all_to_all | solution.py:24
  71.3 22.4 %copy-start = (f32[2048]{0:T(1024)S(1)}, f32[2048]{0:T(1024)}, u32[]{:S(2)}) copy-start(f32[2048]{0:T(1024)} %param.11) | copy-start | bytes 24580
  71.3 16.5 %collective-permute-start.2 = (bf16[128,2048]{1,0:T(8,128)(2,1)S(1)}, bf16[128,2048]{1,0:T(8,128)(2,1)S(1)}, u32[]{:S(2)}, u32[]{:S(2)}) collective-permute-start(bf16[128,2048]{1,0:T(8,128)(2,1)S(1)} %add.86), channel_id=1, source_target_pairs={{0,6},{2,4},{4,2},{6,0},{1,7},{3,5},{5,3},{7,1},{8,14},{10,12},{12... | collective-permute-start | bytes 1572872 | tf_op jit(solution)/shard_map/ppermute | solution.py:44
  88.0 3.8 %collective-permute-start.3 = (bf16[128,2048]{1,0:T(8,128)(2,1)S(1)}, bf16[128,2048]{1,0:T(8,128)(2,1)S(1)}, u32[]{:S(2)}, u32[]{:S(2)}) collective-permute-start(bf16[128,2048]{1,0:T(8,128)(2,1)S(1)} %add.87), channel_id=1, source_target_pairs={{0,1},{1,0},{2,3},{3,2},{4,5},{5,4},{6,7},{7,6},{8,9},{9,8},{10,11... | collective-permute-start | bytes 1572872 | tf_op jit(solution)/shard_map/ppermute | solution.py:40
  98.3 31.6 %copy-start.4 = (bf16[1,8,8,32,128]{4,3,2,1,0:T(8,128)(2,1)}, bf16[1,8,8,32,128]{4,3,2,1,0:T(8,128)(2,1)S(1)}, u32[]{:S(2)}) copy-start(bf16[1,8,8,32,128]{4,3,2,1,0:T(8,128)(2,1)S(1)} %get-tuple-element.54) | copy-start | bytes 1572868
  98.3 31.9 %copy-start.2 = (bf16[1,8,8,32,128]{4,3,2,1,0:T(8,128)(2,1)}, bf16[1,8,8,32,128]{4,3,2,1,0:T(8,128)(2,1)S(1)}, u32[]{:S(2)}) copy-start(bf16[1,8,8,32,128]{4,3,2,1,0:T(8,128)(2,1)S(1)} %get-tuple-element.53) | copy-start | bytes 1572868
  98.3 59.4 %copy-start.1 = (bf16[1,8,8,32,128]{4,3,2,1,0:T(8,128)(2,1)}, bf16[1,8,8,32,128]{4,3,2,1,0:T(8,128)(2,1)S(1)}, u32[]{:S(2)}) copy-start(bf16[1,8,8,32,128]{4,3,2,1,0:T(8,128)(2,1)S(1)} %get-tuple-element.52) | copy-start | bytes 1572868
  126.1 17.6 %copy-start.6 = (bf16[128,2048]{1,0:T(8,128)(2,1)}, bf16[128,2048]{1,0:T(8,128)(2,1)S(1)}, u32[]{:S(2)}) copy-start(bf16[128,2048]{1,0:T(8,128)(2,1)S(1)} %all_gather.6) | copy-start | bytes 1572868
  126.3 1.8 copy-start.8
  157.8 2.5 %copy-start.7 = (bf16[128,2048]{1,0:T(8,128)(2,1)}, bf16[128,2048]{1,0:T(8,128)(2,1)S(1)}, u32[]{:S(2)}) copy-start(bf16[128,2048]{1,0:T(8,128)(2,1)S(1)} %all_gather.7) | copy-start | bytes 1572868
  162.6 31.8 %all-to-all-start.4 = ((bf16[8,8,4,32,128]{4,3,2,1,0:T(8,128)(2,1)}), bf16[8,8,4,32,128]{4,3,2,1,0:T(8,128)(2,1)S(1)}, u32[]{:S(2)}, u32[]{:S(2)}) async-start(bf16[8,8,4,32,128]{4,3,2,1,0:T(8,128)(2,1)} %copy_bitcast_fusion), calls=%async_computation.4 | async-start | bytes 4194304 | tf_op jit(solution)/shard_map/all_to_all | solution.py:24
  166.4 1.7 copy-start.5
  167.8 1.0 copy-start.3
  169.2 3.8 %collective-permute-start.4 = (bf16[128,2048]{1,0:T(8,128)(2,1)S(1)}, bf16[128,2048]{1,0:T(8,128)(2,1)S(1)}, u32[]{:S(2)}, u32[]{:S(2)}) collective-permute-start(bf16[128,2048]{1,0:T(8,128)(2,1)S(1)} %get-tuple-element.71), channel_id=1, source_target_pairs={{0,1},{1,0},{2,3},{3,2},{4,5},{5,4},{6,7},{7,6},{8,9},{9,8},{10,11... | collective-permute-start | bytes 1572872 | tf_op jit(solution)/shard_map/ppermute | solution.py:40
  173.3 16.1 %collective-permute-start.5 = (bf16[128,2048]{1,0:T(8,128)(2,1)S(1)}, bf16[128,2048]{1,0:T(8,128)(2,1)S(1)}, u32[]{:S(2)}, u32[]{:S(2)}) collective-permute-start(bf16[128,2048]{1,0:T(8,128)(2,1)S(1)} %add_convert_fusion.2), channel_id=1, source_target_pairs={{0,2},{2,0},{4,6},{6,4},{1,3},{3,1},{5,7},{7,5},{8,10},{10,8},{12,... | collective-permute-start | bytes 1572872 | tf_op jit(solution)/shard_map/ppermute | solution.py:44
  190.2 16.8 %collective-permute-start.6 = (bf16[128,2048]{1,0:T(8,128)(2,1)}, bf16[128,2048]{1,0:T(8,128)(2,1)}, u32[]{:S(2)}, u32[]{:S(2)}) collective-permute-start(bf16[128,2048]{1,0:T(8,128)(2,1)} %add_convert_fusion.1), channel_id=1, source_target_pairs={{0,6},{2,4},{4,2},{6,0},{1,7},{3,5},{5,3},{7,1},{8,14},{10,12},{12... | collective-permute-start | bytes 1572872 | tf_op jit(solution)/shard_map/ppermute | solution.py:44
  196.0 30.6 %all-to-all-start.5 = ((bf16[8,4,32,128]{3,2,1,0:T(8,128)(2,1)}), bf16[8,4,32,128]{3,2,1,0:T(8,128)(2,1)S(1)}, u32[]{:S(2)}, u32[]{:S(2)}) async-start(bf16[8,4,32,128]{3,2,1,0:T(8,128)(2,1)} %shard_map.94), calls=%async_computation.5 | async-start | bytes 524288 | tf_op jit(solution)/shard_map/all_to_all | solution.py:24
  208.4 3.8 %collective-permute-start.7 = (bf16[128,2048]{1,0:T(8,128)(2,1)S(1)}, bf16[128,2048]{1,0:T(8,128)(2,1)S(1)}, u32[]{:S(2)}, u32[]{:S(2)}) collective-permute-start(bf16[128,2048]{1,0:T(8,128)(2,1)S(1)} %add_convert_fusion.tile), channel_id=1, source_target_pairs={{0,1},{1,0},{2,3},{3,2},{4,5},{5,4},{6,7},{7,6},{8,9},{9,8},{10,11... | collective-permute-start | bytes 1572872 | tf_op jit(solution)/shard_map/ppermute | solution.py:40

commit v14 on v13

--- a/solution.py
+++ b/solution.py
@@ -95,22 +95,31 @@
     return inv * u - x32 * inv**3 * jnp.mean(x32 * u, -1, keepdims=True)
 
 
-def first_kernel(h, g, w_qkv, w_out, sent, shards, sems, tile_sems):
-    parts = []
-    for i in range(NP):
-        parts.append(pltpu.make_async_copy(w_qkv, shards.at[i, pl.ds(0, 3)], sems.at[i, 0]))
-        parts.append(pltpu.make_async_copy(w_out, shards.at[i, 3], sems.at[i, 1]))
-    for part in parts:
-        part.start()
+def first_kernel(h, g, w_qkv, w_out, sent, shards, tile_in, qkv_in, out_in, sems, out_sems):
+    weights = [
+        pltpu.make_async_copy(w_qkv, qkv_in, sems.at[0]),
+        pltpu.make_async_copy(w_out, out_in, sems.at[1]),
+    ]
+    for copy in weights:
+        copy.start()
     core = lax.axis_index("core")
     for i, tile in enumerate((g, h)):
 
         @pl.when(core == i)
         def _(i=i, tile=tile):
-            copy = pltpu.make_async_copy(tile, sent, tile_sems.at[i])
+            copy = pltpu.make_async_copy(tile, tile_in, sems.at[2 + i])
             copy.start()
             copy.wait()
 
+    parts = [pltpu.make_async_copy(tile_in, sent, sems.at[4])]
+    parts[0].start()
+    for copy in weights:
+        copy.wait()
+    for i in range(NP):
+        for k, part in enumerate((qkv_in, out_in)):
+            place = shards.at[i, pl.ds(0, 3)] if k == 0 else shards.at[i, 3]
+            parts.append(pltpu.make_async_copy(part, place, out_sems.at[i, k]))
+            parts[-1].start()
     for part in parts:
         part.wait()
 
@@ -124,7 +133,13 @@
             jax.ShapeDtypeStruct((TILE, D), BF),
             jax.ShapeDtypeStruct((NP, 4, 32, HD), BF),
         ],
-        scratch_shapes=[pltpu.SemaphoreType.DMA((NP, 2)), pltpu.SemaphoreType.DMA((2,))],
+        scratch_shapes=[
+            pltpu.VMEM((TILE, D), BF),
+            pltpu.VMEM((3, 32, HD), BF),
+            pltpu.VMEM((32, HD), BF),
+            pltpu.SemaphoreType.DMA((5,)),
+            pltpu.SemaphoreType.DMA((NP, 2)),
+        ],
         compiler_params=pltpu.CompilerParams(vmem_limit_bytes=60 * 2**20),
     )(h, g, w_qkv, w_out)
 
@@ -139,9 +154,6 @@
 def sum_terms(terms):
     return pl.pallas_call(
         sum_kernel,
-        grid=(NP // 2,),
-        in_specs=[pl.BlockSpec((NN, 2, 4, 32, HD), lambda i: (0, i, 0, 0, 0))],
-        out_specs=pl.BlockSpec((2, 4, 32, HD), lambda i: (i, 0, 0, 0)),
         out_shape=jax.ShapeDtypeStruct((NP, 4, 32, HD), BF),
         compiler_params=pltpu.CompilerParams(vmem_limit_bytes=16 * 2**20),
     )(terms)

time: 229 us -> 206 us (0.90)
  Pallas kernels: 29.3 us -> 5.71 us
    pallas_call x1, Pallas kernels: 25.1 us -> 2.12 us  [first_step(): pl.pallas_call(first_kernel, in_specs=[pl.BlockSpec(memory_space=pl.ANY)]...]
  transfers between devices with their start and end apart: 12 -> 12, of which waited for: 10 -> 10; matrix products, arithmetic and copies ran while one was open for 5% -> 6% of each run, Pallas kernels for 2% -> 2%
where the time goes in v14:
time: 206 us; the launch traced here: 204 us
  waiting for transfers between devices  62.8 us (30%)
  starting transfers between devices  52.8 us (26%)
  blocking collectives  52.1 us (25%)
  other arithmetic  13.8 us (7%)
  matrix products  9.96 us (5%)
  Pallas kernels  5.71 us (3%)
  local copies, waits for them, and re-layouts  4.74 us (2%)
  between operations  2.45 us (1%)
    ppermute x4, waiting for transfers between devices, from_pair(): return lax.ppermute(x, 'x', [(i, i ^ bit) for i in range(CTX // 2)])  42.8 us
    all_to_all x4, starting transfers between devices, swap(): return lax.all_to_all(x, axis, 0, 0)  32.9 us
    all_gather x2, blocking collectives, all_rows(): return lax.all_gather(chunk, CONTEXT, tiled=True)  26.2 us
    all_to_all x2, blocking collectives, swap(): return lax.all_to_all(x, axis, 0, 0)  25.8 us
    all_to_all x4, waiting for transfers between devices, swap(): return lax.all_to_all(x, axis, 0, 0)  16.6 us
    ppermute x4, starting transfers between devices, from_pair(): return lax.ppermute(x, 'x', [(i, i ^ bit) for i in range(CTX // 2)])  11.9 us
    dot_general x32, matrix products, dot(): return lax.dot_general(a, b, (dims, ((), ())), preferred_element_type=F32)  9.96 us
    ppermute x4, starting transfers between devices, from_core(): return lax.ppermute(x, 'core', [(0, 1), (1, 0)])  8.02 us
  transfers between devices with their start and end apart: 12, of which 10 were waited for; matrix products, arithmetic and copies ran while one was open for 6% of the time, Pallas kernels for 2%

profile of v14, /device:TPU:6, one launch (start us, length us, event | category | flops | bytes accessed | tf_op | source)
XLA Modules:
  0.0 204.3 jit_solution(17495586578478510960)
XLA Ops:
  0.6 2.1 %shard_map.93 = (bf16[128,2048]{1,0:T(8,128)(2,1)}, bf16[8,4,32,128]{3,2,1,0:T(8,128)(2,1)}) custom-call(bf16[128,2048]{1,0:T(8,128)(2,1)} %bitcast.119, bf16[128,2048]{1,0:T(8,128)(2,1)} %bitcast.120, bf16[3,32,128]{2,1,0:T(8,128)(2,1)} %w_qkv.1, bf16[32,128]{1,0:T(8,128)(2,1)} %bitcast.129), custom_call_target="tpu_custom_call" | custom-call | tf_op jit(solution)/shard_map/pallas_call | solution.py:128
  2.8 1.9 collective-permute-start
  4.7 15.1 %all-to-all-start = ((bf16[8,4,32,128]{3,2,1,0:T(8,128)(2,1)}), bf16[8,4,32,128]{3,2,1,0:T(8,128)(2,1)S(1)}, u32[]{:S(2)}, u32[]{:S(2)}) async-start(bf16[8,4,32,128]{3,2,1,0:T(8,128)(2,1)} %get-tuple-element.26), calls=%async_computation | async-start | bytes 524288 | tf_op jit(solution)/shard_map/all_to_all | solution.py:24
  19.8 1.4 constant_dynamic-slice_fusion.1
  22.5 1.3 select_select_fusion
  23.8 2.7 %collective-permute-start.1 = (bf16[128,2048]{1,0:T(8,128)(2,1)S(1)}, bf16[128,2048]{1,0:T(8,128)(2,1)S(1)}, u32[]{:S(2)}, u32[]{:S(2)}) collective-permute-start(bf16[128,2048]{1,0:T(8,128)(2,1)S(1)} %select_select_fusion), channel_id=1, source_target_pairs={{0,2},{2,0},{4,6},{6,4},{1,3},{3,1},{5,7},{7,5},{8,10},{10,8},{12,... | collective-permute-start | bytes 1572872 | tf_op jit(solution)/shard_map/ppermute | solution.py:44
  26.6 13.2 %collective-permute-done.1 = bf16[128,2048]{1,0:T(8,128)(2,1)S(1)} collective-permute-done((bf16[128,2048]{1,0:T(8,128)(2,1)S(1)}, bf16[128,2048]{1,0:T(8,128)(2,1)S(1)}, u32[]{:S(2)}, u32[]{:S(2)}) %collective-permute-start.1) | collective-permute-done | bytes 524320 | tf_op jit(solution)/shard_map/ppermute | solution.py:44
  39.9 1.9 all-to-all-done
  41.8 1.8 broadcast_in_dim.13
  43.7 4.6 %all-to-all-start.1 = ((bf16[8,8,4,32,128]{4,3,1,2,0:T(8,128)(2,1)}), bf16[8,8,4,32,128]{4,3,1,2,0:T(8,128)(2,1)S(1)}, u32[]{:S(2)}, u32[]{:S(2)}) async-start(bf16[8,8,4,32,128]{4,3,1,2,0:T(8,128)(2,1)} %broadcast_in_dim.13), calls=%async_computation.1 | async-start | bytes 4194304 | tf_op jit(solution)/shard_map/all_to_all | solution.py:24
  48.3 2.4 %collective-permute-start.2 = (bf16[128,2048]{1,0:T(8,128)(2,1)S(1)}, bf16[128,2048]{1,0:T(8,128)(2,1)S(1)}, u32[]{:S(2)}, u32[]{:S(2)}) collective-permute-start(bf16[128,2048]{1,0:T(8,128)(2,1)S(1)} %add.86), channel_id=1, source_target_pairs={{0,6},{2,4},{4,2},{6,0},{1,7},{3,5},{5,3},{7,1},{8,14},{10,12},{12... | collective-permute-start | bytes 1572872 | tf_op jit(solution)/shard_map/ppermute | solution.py:44
  50.7 14.2 %collective-permute-done.2 = bf16[128,2048]{1,0:T(8,128)(2,1)S(1)} collective-permute-done((bf16[128,2048]{1,0:T(8,128)(2,1)S(1)}, bf16[128,2048]{1,0:T(8,128)(2,1)S(1)}, u32[]{:S(2)}, u32[]{:S(2)}) %collective-permute-start.2) | collective-permute-done | bytes 524320 | tf_op jit(solution)/shard_map/ppermute | solution.py:44
  65.0 1.9 collective-permute-start.3
  66.9 0.6 compare_reduce_fusion
  67.5 1.2 collective-permute-done.3
  68.8 1.7 broadcast_select_fusion.5
  70.9 3.5 %all-to-all-done.1 = bf16[8,8,4,32,128]{4,3,1,2,0:T(8,128)(2,1)S(1)} async-done(((bf16[8,8,4,32,128]{4,3,1,2,0:T(8,128)(2,1)}), bf16[8,8,4,32,128]{4,3,1,2,0:T(8,128)(2,1)S(1)}, u32[]{:S(2)}, u32[]{:S(2)}) %all-to-all-start.1) | async-done | bytes 2097184 | tf_op jit(solution)/shard_map/all_to_all | solution.py:24
  74.4 0.6 copy.43
  77.0 12.9 %all_to_all.30 = bf16[8,16,2048]{2,1,0:T(8,128)(2,1)S(1)} all-to-all(bf16[8,16,2048]{2,1,0:T(8,128)(2,1)S(1)} %bitcast.121), channel_id=1, replica_groups=mesh['zp'=8,'zq'=2,'y'=4,'x'=4,'core'=2] {'x','core'}, dimensions={0} | all-to-all | bytes 1048576 | tf_op jit(solution)/shard_map/all_to_all | solution.py:24
  90.0 13.1 %all_gather.6 = bf16[128,2048]{1,0:T(8,128)(2,1)S(1)} all-gather(bf16[16,2048]{1,0:T(8,128)(2,1)S(1)} %fusion.26), channel_id=1, replica_groups=mesh['zp'=8,'zq'=2,'y'=4,'x'=4,'core'=2] {'x','core'}, dimensions={0}, use_global_device_ids=true | all-gather | bytes 589824 | tf_op jit(solution)/shard_map/all_gather | solution.py:53
  103.3 0.9 fusion.19
  107.5 12.9 %all_to_all.31 = bf16[8,16,2048]{2,1,0:T(8,128)(2,1)S(1)} all-to-all(bf16[8,16,2048]{2,1,0:T(8,128)(2,1)S(1)} %bitcast.122), channel_id=1, replica_groups=mesh['zp'=8,'zq'=2,'y'=4,'x'=4,'core'=2] {'x','core'}, dimensions={0} | all-to-all | bytes 1048576 | tf_op jit(solution)/shard_map/all_to_all | solution.py:24
  120.7 0.9 fusion.24
  121.7 13.1 %all_gather.7 = bf16[128,2048]{1,0:T(8,128)(2,1)S(1)} all-gather(bf16[16,2048]{1,0:T(8,128)(2,1)S(1)} %fusion.24), channel_id=1, replica_groups=mesh['zp'=8,'zq'=2,'y'=4,'x'=4,'core'=2] {'x','core'}, dimensions={0}, use_global_device_ids=true | all-gather | bytes 589824 | tf_op jit(solution)/shard_map/all_gather | solution.py:53
  135.8 0.5 convolution_convert_fusion.4
  136.3 0.5 convolution_convert_fusion.3
  136.8 0.5 convolution_convert_fusion.2
  137.3 0.5 convolution_convert_fusion.1
  137.8 1.8 copy_bitcast_fusion
  139.6 3.8 %all-to-all-start.4 = ((bf16[8,8,4,32,128]{4,3,2,1,0:T(8,128)(2,1)}), bf16[8,8,4,32,128]{4,3,2,1,0:T(8,128)(2,1)S(1)}, u32[]{:S(2)}, u32[]{:S(2)}) async-start(bf16[8,8,4,32,128]{4,3,2,1,0:T(8,128)(2,1)} %copy_bitcast_fusion), calls=%async_computation.4 | async-start | bytes 4194304 | tf_op jit(solution)/shard_map/all_to_all | solution.py:24
  143.4 1.4 convolution_convert_fusion
  146.2 2.3 %collective-permute-start.4 = (bf16[128,2048]{1,0:T(8,128)(2,1)S(1)}, bf16[128,2048]{1,0:T(8,128)(2,1)S(1)}, u32[]{:S(2)}, u32[]{:S(2)}) collective-permute-start(bf16[128,2048]{1,0:T(8,128)(2,1)S(1)} %get-tuple-element.71), channel_id=1, source_target_pairs={{0,1},{1,0},{2,3},{3,2},{4,5},{5,4},{6,7},{7,6},{8,9},{9,8},{10,11... | collective-permute-start | bytes 1572872 | tf_op jit(solution)/shard_map/ppermute | solution.py:40
  148.5 1.5 collective-permute-done.4
  150.3 2.8 %collective-permute-start.5 = (bf16[128,2048]{1,0:T(8,128)(2,1)S(1)}, bf16[128,2048]{1,0:T(8,128)(2,1)S(1)}, u32[]{:S(2)}, u32[]{:S(2)}) collective-permute-start(bf16[128,2048]{1,0:T(8,128)(2,1)S(1)} %add_convert_fusion.2), channel_id=1, source_target_pairs={{0,2},{2,0},{4,6},{6,4},{1,3},{3,1},{5,7},{7,5},{8,10},{10,8},{12,... | collective-permute-start | bytes 1572872 | tf_op jit(solution)/shard_map/ppermute | solution.py:44
  153.0 13.3 %collective-permute-done.5 = bf16[128,2048]{1,0:T(8,128)(2,1)S(1)} collective-permute-done((bf16[128,2048]{1,0:T(8,128)(2,1)S(1)}, bf16[128,2048]{1,0:T(8,128)(2,1)S(1)}, u32[]{:S(2)}, u32[]{:S(2)}) %collective-permute-start.5) | collective-permute-done | bytes 524320 | tf_op jit(solution)/shard_map/ppermute | solution.py:44
  166.3 0.9 add_convert_fusion.1
  167.3 4.0 %collective-permute-start.6 = (bf16[128,2048]{1,0:T(8,128)(2,1)}, bf16[128,2048]{1,0:T(8,128)(2,1)}, u32[]{:S(2)}, u32[]{:S(2)}) collective-permute-start(bf16[128,2048]{1,0:T(8,128)(2,1)} %add_convert_fusion.1), channel_id=1, source_target_pairs={{0,6},{2,4},{4,2},{6,0},{1,7},{3,5},{5,3},{7,1},{8,14},{10,12},{12... | collective-permute-start | bytes 1572872 | tf_op jit(solution)/shard_map/ppermute | solution.py:44
  171.4 1.0 shard_map.94
  172.4 9.5 %all-to-all-start.5 = ((bf16[8,4,32,128]{3,2,1,0:T(8,128)(2,1)}), bf16[8,4,32,128]{3,2,1,0:T(8,128)(2,1)S(1)}, u32[]{:S(2)}, u32[]{:S(2)}) async-start(bf16[8,4,32,128]{3,2,1,0:T(8,128)(2,1)} %shard_map.94), calls=%async_computation.5 | async-start | bytes 524288 | tf_op jit(solution)/shard_map/all_to_all | solution.py:24
  181.8 2.2 %collective-permute-done.6 = bf16[128,2048]{1,0:T(8,128)(2,1)} collective-permute-done((bf16[128,2048]{1,0:T(8,128)(2,1)}, bf16[128,2048]{1,0:T(8,128)(2,1)}, u32[]{:S(2)}, u32[]{:S(2)}) %collective-permute-start.6) | collective-permute-done | bytes 524320 | tf_op jit(solution)/shard_map/ppermute | solution.py:44
  184.0 1.3 add_convert_fusion.tile
  185.4 1.9 collective-permute-start.7
  187.3 1.3 broadcast_select_fusion
  188.6 0.6 collective-permute-done.7.other
  189.2 2.6 %shard_map.95 = (bf16[128,2048]{1,0:T(8,128)(2,1)}, bf16[128,2048]{1,0:T(8,128)(2,1)}) custom-call(s32[2]{0:T(128)S(1)} %pad_add_fusion.flags, bf16[128,2048]{1,0:T(8,128)(2,1)S(1)} %add_convert_fusion.tile, bf16[128,2048]{1,0:T(8,128)(2,1)S(1)} %collective-permute-done.7.other, bf16[128,2048]{1,0:T(8,128)(2,1)S(1)} %get-tuple-element.74.base_h, ...), custom_call_target="tpu_custom_call" | custom-call | tf_op jit(solution)/shard_map/pallas_call | solution.py:176
  191.8 11.2 %all-to-all-done.5 = bf16[8,4,32,128]{3,2,1,0:T(8,128)(2,1)S(1)} async-done(((bf16[8,4,32,128]{3,2,1,0:T(8,128)(2,1)}), bf16[8,4,32,128]{3,2,1,0:T(8,128)(2,1)S(1)}, u32[]{:S(2)}, u32[]{:S(2)}) %all-to-all-start.5) | async-done | bytes 262176 | tf_op jit(solution)/shard_map/all_to_all | solution.py:24
  203.0 0.6 convert_reduce_fusion.2
  203.7 0.6 convert_reduce_fusion.3
  (69 shorter events, 9.1 us)
Async XLA Ops:
  2.8 19.8 %collective-permute-start = (bf16[128,2048]{1,0:T(8,128)(2,1)}, bf16[128,2048]{1,0:T(8,128)(2,1)S(1)}, u32[]{:S(2)}, u32[]{:S(2)}) collective-permute-start(bf16[128,2048]{1,0:T(8,128)(2,1)} %get-tuple-element.27), channel_id=1, source_target_pairs={{0,1},{1,0},{2,3},{3,2},{4,5},{5,4},{6,7},{7,6},{8,9},{9,8},{10,11... | collective-permute-start | bytes 1572872 | tf_op jit(solution)/shard_map/ppermute | solution.py:40
  4.7 37.1 %all-to-all-start = ((bf16[8,4,32,128]{3,2,1,0:T(8,128)(2,1)}), bf16[8,4,32,128]{3,2,1,0:T(8,128)(2,1)S(1)}, u32[]{:S(2)}, u32[]{:S(2)}) async-start(bf16[8,4,32,128]{3,2,1,0:T(8,128)(2,1)} %get-tuple-element.26), calls=%async_computation | async-start | bytes 524288 | tf_op jit(solution)/shard_map/all_to_all | solution.py:24
  23.8 15.9 %collective-permute-start.1 = (bf16[128,2048]{1,0:T(8,128)(2,1)S(1)}, bf16[128,2048]{1,0:T(8,128)(2,1)S(1)}, u32[]{:S(2)}, u32[]{:S(2)}) collective-permute-start(bf16[128,2048]{1,0:T(8,128)(2,1)S(1)} %select_select_fusion), channel_id=1, source_target_pairs={{0,2},{2,0},{4,6},{6,4},{1,3},{3,1},{5,7},{7,5},{8,10},{10,8},{12,... | collective-permute-start | bytes 1572872 | tf_op jit(solution)/shard_map/ppermute | solution.py:44
  43.7 23.2 %copy-start.9 = (s32[1,8]{1,0:T(1,128)S(1)}, s32[1,8]{1,0:T(1,128)}, u32[]{:S(2)}) copy-start(s32[1,8]{1,0:T(1,128)} %param.8) | copy-start | bytes 100
  43.7 30.7 %all-to-all-start.1 = ((bf16[8,8,4,32,128]{4,3,1,2,0:T(8,128)(2,1)}), bf16[8,8,4,32,128]{4,3,1,2,0:T(8,128)(2,1)S(1)}, u32[]{:S(2)}, u32[]{:S(2)}) async-start(bf16[8,8,4,32,128]{4,3,1,2,0:T(8,128)(2,1)} %broadcast_in_dim.13), calls=%async_computation.1 | async-start | bytes 4194304 | tf_op jit(solution)/shard_map/all_to_all | solution.py:24
  48.3 22.4 %copy-start = (f32[2048]{0:T(1024)S(1)}, f32[2048]{0:T(1024)}, u32[]{:S(2)}) copy-start(f32[2048]{0:T(1024)} %param.11) | copy-start | bytes 24580
  48.3 16.5 %collective-permute-start.2 = (bf16[128,2048]{1,0:T(8,128)(2,1)S(1)}, bf16[128,2048]{1,0:T(8,128)(2,1)S(1)}, u32[]{:S(2)}, u32[]{:S(2)}) collective-permute-start(bf16[128,2048]{1,0:T(8,128)(2,1)S(1)} %add.86), channel_id=1, source_target_pairs={{0,6},{2,4},{4,2},{6,0},{1,7},{3,5},{5,3},{7,1},{8,14},{10,12},{12... | collective-permute-start | bytes 1572872 | tf_op jit(solution)/shard_map/ppermute | solution.py:44
  65.0 3.8 %collective-permute-start.3 = (bf16[128,2048]{1,0:T(8,128)(2,1)S(1)}, bf16[128,2048]{1,0:T(8,128)(2,1)S(1)}, u32[]{:S(2)}, u32[]{:S(2)}) collective-permute-start(bf16[128,2048]{1,0:T(8,128)(2,1)S(1)} %add.87), channel_id=1, source_target_pairs={{0,1},{1,0},{2,3},{3,2},{4,5},{5,4},{6,7},{7,6},{8,9},{9,8},{10,11... | collective-permute-start | bytes 1572872 | tf_op jit(solution)/shard_map/ppermute | solution.py:40
  75.3 31.6 %copy-start.4 = (bf16[1,8,8,32,128]{4,3,2,1,0:T(8,128)(2,1)}, bf16[1,8,8,32,128]{4,3,2,1,0:T(8,128)(2,1)S(1)}, u32[]{:S(2)}) copy-start(bf16[1,8,8,32,128]{4,3,2,1,0:T(8,128)(2,1)S(1)} %get-tuple-element.54) | copy-start | bytes 1572868
  75.3 31.9 %copy-start.2 = (bf16[1,8,8,32,128]{4,3,2,1,0:T(8,128)(2,1)}, bf16[1,8,8,32,128]{4,3,2,1,0:T(8,128)(2,1)S(1)}, u32[]{:S(2)}) copy-start(bf16[1,8,8,32,128]{4,3,2,1,0:T(8,128)(2,1)S(1)} %get-tuple-element.53) | copy-start | bytes 1572868
  75.3 59.4 %copy-start.1 = (bf16[1,8,8,32,128]{4,3,2,1,0:T(8,128)(2,1)}, bf16[1,8,8,32,128]{4,3,2,1,0:T(8,128)(2,1)S(1)}, u32[]{:S(2)}) copy-start(bf16[1,8,8,32,128]{4,3,2,1,0:T(8,128)(2,1)S(1)} %get-tuple-element.52) | copy-start | bytes 1572868
  103.1 17.6 %copy-start.6 = (bf16[128,2048]{1,0:T(8,128)(2,1)}, bf16[128,2048]{1,0:T(8,128)(2,1)S(1)}, u32[]{:S(2)}) copy-start(bf16[128,2048]{1,0:T(8,128)(2,1)S(1)} %all_gather.6) | copy-start | bytes 1572868
  103.3 1.8 copy-start.8
  134.8 2.5 %copy-start.7 = (bf16[128,2048]{1,0:T(8,128)(2,1)}, bf16[128,2048]{1,0:T(8,128)(2,1)S(1)}, u32[]{:S(2)}) copy-start(bf16[128,2048]{1,0:T(8,128)(2,1)S(1)} %all_gather.7) | copy-start | bytes 1572868
  139.6 31.8 %all-to-all-start.4 = ((bf16[8,8,4,32,128]{4,3,2,1,0:T(8,128)(2,1)}), bf16[8,8,4,32,128]{4,3,2,1,0:T(8,128)(2,1)S(1)}, u32[]{:S(2)}, u32[]{:S(2)}) async-start(bf16[8,8,4,32,128]{4,3,2,1,0:T(8,128)(2,1)} %copy_bitcast_fusion), calls=%async_computation.4 | async-start | bytes 4194304 | tf_op jit(solution)/shard_map/all_to_all | solution.py:24
  143.4 1.7 copy-start.5
  144.9 1.0 copy-start.3
  146.2 3.8 %collective-permute-start.4 = (bf16[128,2048]{1,0:T(8,128)(2,1)S(1)}, bf16[128,2048]{1,0:T(8,128)(2,1)S(1)}, u32[]{:S(2)}, u32[]{:S(2)}) collective-permute-start(bf16[128,2048]{1,0:T(8,128)(2,1)S(1)} %get-tuple-element.71), channel_id=1, source_target_pairs={{0,1},{1,0},{2,3},{3,2},{4,5},{5,4},{6,7},{7,6},{8,9},{9,8},{10,11... | collective-permute-start | bytes 1572872 | tf_op jit(solution)/shard_map/ppermute | solution.py:40
  150.3 16.1 %collective-permute-start.5 = (bf16[128,2048]{1,0:T(8,128)(2,1)S(1)}, bf16[128,2048]{1,0:T(8,128)(2,1)S(1)}, u32[]{:S(2)}, u32[]{:S(2)}) collective-permute-start(bf16[128,2048]{1,0:T(8,128)(2,1)S(1)} %add_convert_fusion.2), channel_id=1, source_target_pairs={{0,2},{2,0},{4,6},{6,4},{1,3},{3,1},{5,7},{7,5},{8,10},{10,8},{12,... | collective-permute-start | bytes 1572872 | tf_op jit(solution)/shard_map/ppermute | solution.py:44
  167.3 16.8 %collective-permute-start.6 = (bf16[128,2048]{1,0:T(8,128)(2,1)}, bf16[128,2048]{1,0:T(8,128)(2,1)}, u32[]{:S(2)}, u32[]{:S(2)}) collective-permute-start(bf16[128,2048]{1,0:T(8,128)(2,1)} %add_convert_fusion.1), channel_id=1, source_target_pairs={{0,6},{2,4},{4,2},{6,0},{1,7},{3,5},{5,3},{7,1},{8,14},{10,12},{12... | collective-permute-start | bytes 1572872 | tf_op jit(solution)/shard_map/ppermute | solution.py:44
  172.4 30.6 %all-to-all-start.5 = ((bf16[8,4,32,128]{3,2,1,0:T(8,128)(2,1)}), bf16[8,4,32,128]{3,2,1,0:T(8,128)(2,1)S(1)}, u32[]{:S(2)}, u32[]{:S(2)}) async-start(bf16[8,4,32,128]{3,2,1,0:T(8,128)(2,1)} %shard_map.94), calls=%async_computation.5 | async-start | bytes 524288 | tf_op jit(solution)/shard_map/all_to_all | solution.py:24
  185.4 3.8 %collective-permute-start.7 = (bf16[128,2048]{1,0:T(8,128)(2,1)S(1)}, bf16[128,2048]{1,0:T(8,128)(2,1)S(1)}, u32[]{:S(2)}, u32[]{:S(2)}) collective-permute-start(bf16[128,2048]{1,0:T(8,128)(2,1)S(1)} %add_convert_fusion.tile), channel_id=1, source_target_pairs={{0,1},{1,0},{2,3},{3,2},{4,5},{5,4},{6,7},{7,6},{8,9},{9,8},{10,11... | collective-permute-start | bytes 1572872 | tf_op jit(solution)/shard_map/ppermute | solution.py:40

commit v15 on v14

--- a/solution.py
+++ b/solution.py
@@ -144,6 +144,27 @@
     )(h, g, w_qkv, w_out)
 
 
+def copies_kernel(near, out, block, sems):
+    for t in range(4):
+        block[t] = near[:, t]
+    parts = [pltpu.make_async_copy(block, out.at[i], sems.at[i]) for i in range(NN)]
+    for part in parts:
+        part.start()
+    for part in parts:
+        part.wait()
+
+
+def copies(near):
+    return pl.pallas_call(
+        copies_kernel,
+        in_specs=[pl.BlockSpec(memory_space=pltpu.VMEM)],
+        out_specs=pl.BlockSpec(memory_space=pl.ANY),
+        out_shape=jax.ShapeDtypeStruct((NN, 4, NP, 32, HD), BF),
+        scratch_shapes=[pltpu.VMEM((4, NP, 32, HD), BF), pltpu.SemaphoreType.DMA((NN,))],
+        compiler_params=pltpu.CompilerParams(vmem_limit_bytes=16 * 2**20),
+    )(near)
+
+
 def sum_kernel(terms, out):
     total = terms[0].astype(F32)
     for i in range(1, NN):
@@ -205,7 +226,7 @@
 
     near = swap(shards, "zp")
     near, tile = lax.optimization_barrier((near, tile))
-    w = spread(near, NEAR, NN).transpose(2, 1, 0, 3, 4).reshape(4, D, HD)
+    w = swap(copies(near).transpose(0, 2, 1, 3, 4), NEAR).transpose(2, 1, 0, 3, 4).reshape(4, D, HD)
     tile = tile + from_pair(tile, 3)
     other = from_core(tile)
     h1, g3 = jnp.where(core == 0, tile, other), jnp.where(core == 0, other, tile)

time: 206 us -> 205 us (level)
  local copies, waits for them, and re-layouts: 4.74 us -> 2.48 us
where the time goes in v15:
time: 205 us; the launch traced here: 203 us
  waiting for transfers between devices  62.6 us (31%)
  starting transfers between devices  52.6 us (26%)
  blocking collectives  52.1 us (25%)
  other arithmetic  13.9 us (7%)
  matrix products  9.9 us (5%)
  Pallas kernels  7.15 us (3%)
  local copies, waits for them, and re-layouts  2.48 us (1%)
  between operations  2.47 us (1%)
    ppermute x4, waiting for transfers between devices, from_pair(): return lax.ppermute(x, 'x', [(i, i ^ bit) for i in range(CTX // 2)])  42.8 us
    all_to_all x4, starting transfers between devices, swap(): return lax.all_to_all(x, axis, 0, 0)  32.7 us
    all_gather x2, blocking collectives, all_rows(): return lax.all_gather(chunk, CONTEXT, tiled=True)  26.2 us
    all_to_all x2, blocking collectives, swap(): return lax.all_to_all(x, axis, 0, 0)  25.8 us
    all_to_all x4, waiting for transfers between devices, swap(): return lax.all_to_all(x, axis, 0, 0)  16.5 us
    ppermute x4, starting transfers between devices, from_pair(): return lax.ppermute(x, 'x', [(i, i ^ bit) for i in range(CTX // 2)])  11.9 us
    dot_general x32, matrix products, dot(): return lax.dot_general(a, b, (dims, ((), ())), preferred_element_type=F32)  9.9 us
    ppermute x4, starting transfers between devices, from_core(): return lax.ppermute(x, 'core', [(0, 1), (1, 0)])  8 us
  transfers between devices with their start and end apart: 12, of which 10 were waited for; matrix products, arithmetic and copies ran while one was open for 6% of the time, Pallas kernels for 2%

profile of v15, /device:TPU:6, one launch (start us, length us, event | category | flops | bytes accessed | tf_op | source)
XLA Modules:
  0.0 203.1 jit_solution(4751601020741539052)
XLA Ops:
  0.6 2.1 %shard_map.93 = (bf16[128,2048]{1,0:T(8,128)(2,1)}, bf16[8,4,32,128]{3,2,1,0:T(8,128)(2,1)}) custom-call(bf16[128,2048]{1,0:T(8,128)(2,1)} %bitcast.118, bf16[128,2048]{1,0:T(8,128)(2,1)} %bitcast.119, bf16[3,32,128]{2,1,0:T(8,128)(2,1)} %w_qkv.1, bf16[32,128]{1,0:T(8,128)(2,1)} %bitcast.128), custom_call_target="tpu_custom_call" | custom-call | tf_op jit(solution)/shard_map/pallas_call | solution.py:128
  2.8 1.9 collective-permute-start
  4.7 15.1 %all-to-all-start = ((bf16[8,4,32,128]{3,2,1,0:T(8,128)(2,1)}), bf16[8,4,32,128]{3,2,1,0:T(8,128)(2,1)S(1)}, u32[]{:S(2)}, u32[]{:S(2)}) async-start(bf16[8,4,32,128]{3,2,1,0:T(8,128)(2,1)} %get-tuple-element.26), calls=%async_computation | async-start | bytes 524288 | tf_op jit(solution)/shard_map/all_to_all | solution.py:24
  19.8 1.4 constant_dynamic-slice_fusion.1
  22.5 1.3 select_select_fusion
  23.9 2.7 %collective-permute-start.1 = (bf16[128,2048]{1,0:T(8,128)(2,1)S(1)}, bf16[128,2048]{1,0:T(8,128)(2,1)S(1)}, u32[]{:S(2)}, u32[]{:S(2)}) collective-permute-start(bf16[128,2048]{1,0:T(8,128)(2,1)S(1)} %select_select_fusion), channel_id=1, source_target_pairs={{0,2},{2,0},{4,6},{6,4},{1,3},{3,1},{5,7},{7,5},{8,10},{10,8},{12,... | collective-permute-start | bytes 1572872 | tf_op jit(solution)/shard_map/ppermute | solution.py:44
  26.6 13.2 %collective-permute-done.1 = bf16[128,2048]{1,0:T(8,128)(2,1)S(1)} collective-permute-done((bf16[128,2048]{1,0:T(8,128)(2,1)S(1)}, bf16[128,2048]{1,0:T(8,128)(2,1)S(1)}, u32[]{:S(2)}, u32[]{:S(2)}) %collective-permute-start.1) | collective-permute-done | bytes 524320 | tf_op jit(solution)/shard_map/ppermute | solution.py:44
  40.0 1.9 all-to-all-done.near
  41.8 1.4 shard_map.94
  43.3 4.5 %all-to-all-start.1 = ((bf16[8,8,4,32,128]{4,3,1,2,0:T(8,128)(2,1)}), bf16[8,8,4,32,128]{4,3,1,2,0:T(8,128)(2,1)S(1)}, u32[]{:S(2)}, u32[]{:S(2)}) async-start(bf16[8,8,4,32,128]{4,3,1,2,0:T(8,128)(2,1)} %bitcast.7), calls=%async_computation.1 | async-start | bytes 4194304 | tf_op jit(solution)/shard_map/all_to_all | solution.py:24
  47.8 2.4 %collective-permute-start.2 = (bf16[128,2048]{1,0:T(8,128)(2,1)S(1)}, bf16[128,2048]{1,0:T(8,128)(2,1)S(1)}, u32[]{:S(2)}, u32[]{:S(2)}) collective-permute-start(bf16[128,2048]{1,0:T(8,128)(2,1)S(1)} %add.86), channel_id=1, source_target_pairs={{0,6},{2,4},{4,2},{6,0},{1,7},{3,5},{5,3},{7,1},{8,14},{10,12},{12... | collective-permute-start | bytes 1572872 | tf_op jit(solution)/shard_map/ppermute | solution.py:44
  50.2 14.2 %collective-permute-done.2 = bf16[128,2048]{1,0:T(8,128)(2,1)S(1)} collective-permute-done((bf16[128,2048]{1,0:T(8,128)(2,1)S(1)}, bf16[128,2048]{1,0:T(8,128)(2,1)S(1)}, u32[]{:S(2)}, u32[]{:S(2)}) %collective-permute-start.2) | collective-permute-done | bytes 524320 | tf_op jit(solution)/shard_map/ppermute | solution.py:44
  64.5 1.9 collective-permute-start.3
  66.4 0.6 compare_reduce_fusion
  67.0 1.2 collective-permute-done.3
  68.3 1.7 broadcast_select_fusion.5
  70.4 3.5 %all-to-all-done.1 = bf16[8,8,4,32,128]{4,3,1,2,0:T(8,128)(2,1)S(1)} async-done(((bf16[8,8,4,32,128]{4,3,1,2,0:T(8,128)(2,1)}), bf16[8,8,4,32,128]{4,3,1,2,0:T(8,128)(2,1)S(1)}, u32[]{:S(2)}, u32[]{:S(2)}) %all-to-all-start.1) | async-done | bytes 2097184 | tf_op jit(solution)/shard_map/all_to_all | solution.py:24
  76.1 12.9 %all_to_all.30 = bf16[8,16,2048]{2,1,0:T(8,128)(2,1)S(1)} all-to-all(bf16[8,16,2048]{2,1,0:T(8,128)(2,1)S(1)} %bitcast.120), channel_id=1, replica_groups=mesh['zp'=8,'zq'=2,'y'=4,'x'=4,'core'=2] {'x','core'}, dimensions={0} | all-to-all | bytes 1048576 | tf_op jit(solution)/shard_map/all_to_all | solution.py:24
  89.1 13.1 %all_gather.6 = bf16[128,2048]{1,0:T(8,128)(2,1)S(1)} all-gather(bf16[16,2048]{1,0:T(8,128)(2,1)S(1)} %fusion.26), channel_id=1, replica_groups=mesh['zp'=8,'zq'=2,'y'=4,'x'=4,'core'=2] {'x','core'}, dimensions={0}, use_global_device_ids=true | all-gather | bytes 589824 | tf_op jit(solution)/shard_map/all_gather | solution.py:53
  102.4 0.9 fusion.19
  106.6 12.9 %all_to_all.31 = bf16[8,16,2048]{2,1,0:T(8,128)(2,1)S(1)} all-to-all(bf16[8,16,2048]{2,1,0:T(8,128)(2,1)S(1)} %bitcast.121), channel_id=1, replica_groups=mesh['zp'=8,'zq'=2,'y'=4,'x'=4,'core'=2] {'x','core'}, dimensions={0} | all-to-all | bytes 1048576 | tf_op jit(solution)/shard_map/all_to_all | solution.py:24
  119.8 0.9 fusion.24
  120.7 13.1 %all_gather.7 = bf16[128,2048]{1,0:T(8,128)(2,1)S(1)} all-gather(bf16[16,2048]{1,0:T(8,128)(2,1)S(1)} %fusion.24), channel_id=1, replica_groups=mesh['zp'=8,'zq'=2,'y'=4,'x'=4,'core'=2] {'x','core'}, dimensions={0}, use_global_device_ids=true | all-gather | bytes 589824 | tf_op jit(solution)/shard_map/all_gather | solution.py:53
  134.8 0.5 convolution_convert_fusion.4
  135.3 0.5 convolution_convert_fusion.3
  135.8 0.5 convolution_convert_fusion.2
  136.3 0.5 convolution_convert_fusion.1
  136.8 1.9 copy_bitcast_fusion
  138.7 3.6 %all-to-all-start.4 = ((bf16[8,8,4,32,128]{4,3,2,1,0:T(8,128)(2,1)}), bf16[8,8,4,32,128]{4,3,2,1,0:T(8,128)(2,1)S(1)}, u32[]{:S(2)}, u32[]{:S(2)}) async-start(bf16[8,8,4,32,128]{4,3,2,1,0:T(8,128)(2,1)} %copy_bitcast_fusion), calls=%async_computation.4 | async-start | bytes 4194304 | tf_op jit(solution)/shard_map/all_to_all | solution.py:24
  142.4 1.4 convolution_convert_fusion
  144.4 0.4 copy-done.5
  145.1 2.2 %collective-permute-start.4 = (bf16[128,2048]{1,0:T(8,128)(2,1)S(1)}, bf16[128,2048]{1,0:T(8,128)(2,1)S(1)}, u32[]{:S(2)}, u32[]{:S(2)}) collective-permute-start(bf16[128,2048]{1,0:T(8,128)(2,1)S(1)} %get-tuple-element.71), channel_id=1, source_target_pairs={{0,1},{1,0},{2,3},{3,2},{4,5},{5,4},{6,7},{7,6},{8,9},{9,8},{10,11... | collective-permute-start | bytes 1572872 | tf_op jit(solution)/shard_map/ppermute | solution.py:40
  147.4 1.6 collective-permute-done.4
  149.2 2.8 %collective-permute-start.5 = (bf16[128,2048]{1,0:T(8,128)(2,1)S(1)}, bf16[128,2048]{1,0:T(8,128)(2,1)S(1)}, u32[]{:S(2)}, u32[]{:S(2)}) collective-permute-start(bf16[128,2048]{1,0:T(8,128)(2,1)S(1)} %add_convert_fusion.2), channel_id=1, source_target_pairs={{0,2},{2,0},{4,6},{6,4},{1,3},{3,1},{5,7},{7,5},{8,10},{10,8},{12,... | collective-permute-start | bytes 1572872 | tf_op jit(solution)/shard_map/ppermute | solution.py:44
  152.0 13.3 %collective-permute-done.5 = bf16[128,2048]{1,0:T(8,128)(2,1)S(1)} collective-permute-done((bf16[128,2048]{1,0:T(8,128)(2,1)S(1)}, bf16[128,2048]{1,0:T(8,128)(2,1)S(1)}, u32[]{:S(2)}, u32[]{:S(2)}) %collective-permute-start.5) | collective-permute-done | bytes 524320 | tf_op jit(solution)/shard_map/ppermute | solution.py:44
  165.2 0.9 add_convert_fusion.1
  166.2 4.0 %collective-permute-start.6 = (bf16[128,2048]{1,0:T(8,128)(2,1)}, bf16[128,2048]{1,0:T(8,128)(2,1)}, u32[]{:S(2)}, u32[]{:S(2)}) collective-permute-start(bf16[128,2048]{1,0:T(8,128)(2,1)} %add_convert_fusion.1), channel_id=1, source_target_pairs={{0,6},{2,4},{4,2},{6,0},{1,7},{3,5},{5,3},{7,1},{8,14},{10,12},{12... | collective-permute-start | bytes 1572872 | tf_op jit(solution)/shard_map/ppermute | solution.py:44
  170.3 1.0 shard_map.95
  171.3 9.5 %all-to-all-start.5 = ((bf16[8,4,32,128]{3,2,1,0:T(8,128)(2,1)}), bf16[8,4,32,128]{3,2,1,0:T(8,128)(2,1)S(1)}, u32[]{:S(2)}, u32[]{:S(2)}) async-start(bf16[8,4,32,128]{3,2,1,0:T(8,128)(2,1)} %shard_map.95), calls=%async_computation.5 | async-start | bytes 524288 | tf_op jit(solution)/shard_map/all_to_all | solution.py:24
  180.8 2.1 %collective-permute-done.6 = bf16[128,2048]{1,0:T(8,128)(2,1)} collective-permute-done((bf16[128,2048]{1,0:T(8,128)(2,1)}, bf16[128,2048]{1,0:T(8,128)(2,1)}, u32[]{:S(2)}, u32[]{:S(2)}) %collective-permute-start.6) | collective-permute-done | bytes 524320 | tf_op jit(solution)/shard_map/ppermute | solution.py:44
  182.9 1.3 add_convert_fusion.tile
  184.3 1.9 collective-permute-start.7
  186.2 1.3 broadcast_select_fusion
  187.5 0.6 collective-permute-done.7.other
  188.1 2.6 %shard_map.96 = (bf16[128,2048]{1,0:T(8,128)(2,1)}, bf16[128,2048]{1,0:T(8,128)(2,1)}) custom-call(s32[2]{0:T(128)S(1)} %pad_add_fusion.flags, bf16[128,2048]{1,0:T(8,128)(2,1)S(1)} %add_convert_fusion.tile, bf16[128,2048]{1,0:T(8,128)(2,1)S(1)} %collective-permute-done.7.other, bf16[128,2048]{1,0:T(8,128)(2,1)S(1)} %get-tuple-element.74.base_h, ...), custom_call_target="tpu_custom_call" | custom-call | tf_op jit(solution)/shard_map/pallas_call | solution.py:197
  190.7 11.1 %all-to-all-done.5 = bf16[8,4,32,128]{3,2,1,0:T(8,128)(2,1)S(1)} async-done(((bf16[8,4,32,128]{3,2,1,0:T(8,128)(2,1)}), bf16[8,4,32,128]{3,2,1,0:T(8,128)(2,1)S(1)}, u32[]{:S(2)}, u32[]{:S(2)}) %all-to-all-start.5) | async-done | bytes 262176 | tf_op jit(solution)/shard_map/all_to_all | solution.py:24
  201.8 0.6 convert_reduce_fusion.2
  202.5 0.6 convert_reduce_fusion.3
  (71 shorter events, 8.8 us)
Async XLA Ops:
  2.8 19.8 %collective-permute-start = (bf16[128,2048]{1,0:T(8,128)(2,1)}, bf16[128,2048]{1,0:T(8,128)(2,1)S(1)}, u32[]{:S(2)}, u32[]{:S(2)}) collective-permute-start(bf16[128,2048]{1,0:T(8,128)(2,1)} %get-tuple-element.27), channel_id=1, source_target_pairs={{0,1},{1,0},{2,3},{3,2},{4,5},{5,4},{6,7},{7,6},{8,9},{9,8},{10,11... | collective-permute-start | bytes 1572872 | tf_op jit(solution)/shard_map/ppermute | solution.py:40
  4.7 37.1 %all-to-all-start = ((bf16[8,4,32,128]{3,2,1,0:T(8,128)(2,1)}), bf16[8,4,32,128]{3,2,1,0:T(8,128)(2,1)S(1)}, u32[]{:S(2)}, u32[]{:S(2)}) async-start(bf16[8,4,32,128]{3,2,1,0:T(8,128)(2,1)} %get-tuple-element.26), calls=%async_computation | async-start | bytes 524288 | tf_op jit(solution)/shard_map/all_to_all | solution.py:24
  23.9 15.9 %collective-permute-start.1 = (bf16[128,2048]{1,0:T(8,128)(2,1)S(1)}, bf16[128,2048]{1,0:T(8,128)(2,1)S(1)}, u32[]{:S(2)}, u32[]{:S(2)}) collective-permute-start(bf16[128,2048]{1,0:T(8,128)(2,1)S(1)} %select_select_fusion), channel_id=1, source_target_pairs={{0,2},{2,0},{4,6},{6,4},{1,3},{3,1},{5,7},{7,5},{8,10},{10,8},{12,... | collective-permute-start | bytes 1572872 | tf_op jit(solution)/shard_map/ppermute | solution.py:44
  43.3 23.1 %copy-start.9 = (s32[1,8]{1,0:T(1,128)S(1)}, s32[1,8]{1,0:T(1,128)}, u32[]{:S(2)}) copy-start(s32[1,8]{1,0:T(1,128)} %param.8) | copy-start | bytes 100
  43.3 30.6 %all-to-all-start.1 = ((bf16[8,8,4,32,128]{4,3,1,2,0:T(8,128)(2,1)}), bf16[8,8,4,32,128]{4,3,1,2,0:T(8,128)(2,1)S(1)}, u32[]{:S(2)}, u32[]{:S(2)}) async-start(bf16[8,8,4,32,128]{4,3,1,2,0:T(8,128)(2,1)} %bitcast.7), calls=%async_computation.1 | async-start | bytes 4194304 | tf_op jit(solution)/shard_map/all_to_all | solution.py:24
  47.8 22.4 %copy-start = (f32[2048]{0:T(1024)S(1)}, f32[2048]{0:T(1024)}, u32[]{:S(2)}) copy-start(f32[2048]{0:T(1024)} %param.11) | copy-start | bytes 24580
  47.8 16.5 %collective-permute-start.2 = (bf16[128,2048]{1,0:T(8,128)(2,1)S(1)}, bf16[128,2048]{1,0:T(8,128)(2,1)S(1)}, u32[]{:S(2)}, u32[]{:S(2)}) collective-permute-start(bf16[128,2048]{1,0:T(8,128)(2,1)S(1)} %add.86), channel_id=1, source_target_pairs={{0,6},{2,4},{4,2},{6,0},{1,7},{3,5},{5,3},{7,1},{8,14},{10,12},{12... | collective-permute-start | bytes 1572872 | tf_op jit(solution)/shard_map/ppermute | solution.py:44
  64.5 3.8 %collective-permute-start.3 = (bf16[128,2048]{1,0:T(8,128)(2,1)S(1)}, bf16[128,2048]{1,0:T(8,128)(2,1)S(1)}, u32[]{:S(2)}, u32[]{:S(2)}) collective-permute-start(bf16[128,2048]{1,0:T(8,128)(2,1)S(1)} %add.87), channel_id=1, source_target_pairs={{0,1},{1,0},{2,3},{3,2},{4,5},{5,4},{6,7},{7,6},{8,9},{9,8},{10,11... | collective-permute-start | bytes 1572872 | tf_op jit(solution)/shard_map/ppermute | solution.py:40
  74.3 31.7 %copy-start.2 = (bf16[1,8,8,32,128]{4,3,2,1,0:T(8,128)(2,1)}, bf16[1,8,8,32,128]{4,3,2,1,0:T(8,128)(2,1)S(1)}, u32[]{:S(2)}) copy-start(bf16[1,8,8,32,128]{4,3,2,1,0:T(8,128)(2,1)S(1)} %copy.16) | copy-start | bytes 1572868
  75.0 31.3 %copy-start.4 = (bf16[1,8,8,32,128]{4,3,2,1,0:T(8,128)(2,1)}, bf16[1,8,8,32,128]{4,3,2,1,0:T(8,128)(2,1)S(1)}, u32[]{:S(2)}) copy-start(bf16[1,8,8,32,128]{4,3,2,1,0:T(8,128)(2,1)S(1)} %copy.17) | copy-start | bytes 1572868
  75.3 58.5 %copy-start.1 = (bf16[1,8,8,32,128]{4,3,2,1,0:T(8,128)(2,1)}, bf16[1,8,8,32,128]{4,3,2,1,0:T(8,128)(2,1)S(1)}, u32[]{:S(2)}) copy-start(bf16[1,8,8,32,128]{4,3,2,1,0:T(8,128)(2,1)S(1)} %copy.18) | copy-start | bytes 1572868
  102.2 17.6 %copy-start.6 = (bf16[128,2048]{1,0:T(8,128)(2,1)}, bf16[128,2048]{1,0:T(8,128)(2,1)S(1)}, u32[]{:S(2)}) copy-start(bf16[128,2048]{1,0:T(8,128)(2,1)S(1)} %all_gather.6) | copy-start | bytes 1572868
  102.4 1.8 copy-start.8
  133.8 2.5 %copy-start.7 = (bf16[128,2048]{1,0:T(8,128)(2,1)}, bf16[128,2048]{1,0:T(8,128)(2,1)S(1)}, u32[]{:S(2)}) copy-start(bf16[128,2048]{1,0:T(8,128)(2,1)S(1)} %all_gather.7) | copy-start | bytes 1572868
  138.7 31.6 %all-to-all-start.4 = ((bf16[8,8,4,32,128]{4,3,2,1,0:T(8,128)(2,1)}), bf16[8,8,4,32,128]{4,3,2,1,0:T(8,128)(2,1)S(1)}, u32[]{:S(2)}, u32[]{:S(2)}) async-start(bf16[8,8,4,32,128]{4,3,2,1,0:T(8,128)(2,1)} %copy_bitcast_fusion), calls=%async_computation.4 | async-start | bytes 4194304 | tf_op jit(solution)/shard_map/all_to_all | solution.py:24
  142.4 1.7 copy-start.3
  143.8 1.0 copy-start.5
  145.1 3.8 %collective-permute-start.4 = (bf16[128,2048]{1,0:T(8,128)(2,1)S(1)}, bf16[128,2048]{1,0:T(8,128)(2,1)S(1)}, u32[]{:S(2)}, u32[]{:S(2)}) collective-permute-start(bf16[128,2048]{1,0:T(8,128)(2,1)S(1)} %get-tuple-element.71), channel_id=1, source_target_pairs={{0,1},{1,0},{2,3},{3,2},{4,5},{5,4},{6,7},{7,6},{8,9},{9,8},{10,11... | collective-permute-start | bytes 1572872 | tf_op jit(solution)/shard_map/ppermute | solution.py:40
  149.2 16.1 %collective-permute-start.5 = (bf16[128,2048]{1,0:T(8,128)(2,1)S(1)}, bf16[128,2048]{1,0:T(8,128)(2,1)S(1)}, u32[]{:S(2)}, u32[]{:S(2)}) collective-permute-start(bf16[128,2048]{1,0:T(8,128)(2,1)S(1)} %add_convert_fusion.2), channel_id=1, source_target_pairs={{0,2},{2,0},{4,6},{6,4},{1,3},{3,1},{5,7},{7,5},{8,10},{10,8},{12,... | collective-permute-start | bytes 1572872 | tf_op jit(solution)/shard_map/ppermute | solution.py:44
  166.2 16.8 %collective-permute-start.6 = (bf16[128,2048]{1,0:T(8,128)(2,1)}, bf16[128,2048]{1,0:T(8,128)(2,1)}, u32[]{:S(2)}, u32[]{:S(2)}) collective-permute-start(bf16[128,2048]{1,0:T(8,128)(2,1)} %add_convert_fusion.1), channel_id=1, source_target_pairs={{0,6},{2,4},{4,2},{6,0},{1,7},{3,5},{5,3},{7,1},{8,14},{10,12},{12... | collective-permute-start | bytes 1572872 | tf_op jit(solution)/shard_map/ppermute | solution.py:44
  171.3 30.5 %all-to-all-start.5 = ((bf16[8,4,32,128]{3,2,1,0:T(8,128)(2,1)}), bf16[8,4,32,128]{3,2,1,0:T(8,128)(2,1)S(1)}, u32[]{:S(2)}, u32[]{:S(2)}) async-start(bf16[8,4,32,128]{3,2,1,0:T(8,128)(2,1)} %shard_map.95), calls=%async_computation.5 | async-start | bytes 524288 | tf_op jit(solution)/shard_map/all_to_all | solution.py:24
  184.3 3.8 %collective-permute-start.7 = (bf16[128,2048]{1,0:T(8,128)(2,1)S(1)}, bf16[128,2048]{1,0:T(8,128)(2,1)S(1)}, u32[]{:S(2)}, u32[]{:S(2)}) collective-permute-start(bf16[128,2048]{1,0:T(8,128)(2,1)S(1)} %add_convert_fusion.tile), channel_id=1, source_target_pairs={{0,1},{1,0},{2,3},{3,2},{4,5},{5,4},{6,7},{7,6},{8,9},{9,8},{10,11... | collective-permute-start | bytes 1572872 | tf_op jit(solution)/shard_map/ppermute | solution.py:40

commit v16 on v15

--- a/solution.py
+++ b/solution.py
@@ -2,7 +2,6 @@
 import jax.numpy as jnp
 from jax import lax
 from jax.experimental import pallas as pl
-from jax.experimental.layout import Layout, with_layout_constraint
 from jax.experimental.pallas import tpu as pltpu
 from jax.sharding import Mesh, PartitionSpec as P
 
@@ -165,6 +164,20 @@
     )(near)
 
 
+def order_kernel(q, k, v, o, out):
+    for t, part in enumerate((q, k, v, o)):
+        for n in range(NN):
+            out[n, :, t] = part[:, n]
+
+
+def in_order(q, k, v, o):
+    return pl.pallas_call(
+        order_kernel,
+        out_shape=jax.ShapeDtypeStruct((NN, NP, 4, 32, HD), BF),
+        compiler_params=pltpu.CompilerParams(vmem_limit_bytes=16 * 2**20),
+    )(q, k, v, o)
+
+
 def sum_kernel(terms, out):
     total = terms[0].astype(F32)
     for i in range(1, NN):
@@ -261,8 +274,7 @@
 
     terms = [product(rows3, d3, rows2, d2) for d3, d2 in zip(dqkv3, dqkv2)]
     terms.append(product(dy3, keep3[-1], g2, attn2))
-    terms = jnp.stack(terms, 2).transpose(1, 0, 2, 3, 4)
-    terms = with_layout_constraint(terms, Layout((0, 1, 2, 3, 4)))
+    terms = in_order(*terms)
     terms, dqkv2, old_h, old_g = lax.optimization_barrier((terms, dqkv2, h2, g2))
     terms = swap(terms, NEAR)
     base_h = jnp.where(mine, old_h, hidden_in[0])

time: 205 us -> 205 us (level)
  no operation moved by 1% of the time
where the time goes in v16:
time: 205 us; the launch traced here: 203 us
  waiting for transfers between devices  62.6 us (31%)
  starting transfers between devices  52.6 us (26%)
  blocking collectives  52.1 us (25%)
  other arithmetic  12 us (6%)
  matrix products  9.9 us (5%)
  Pallas kernels  7.31 us (4%)
  local copies, waits for them, and re-layouts  3.82 us (2%)
  between operations  2.49 us (1%)
    ppermute x4, waiting for transfers between devices, from_pair(): return lax.ppermute(x, 'x', [(i, i ^ bit) for i in range(CTX // 2)])  42.7 us
    all_to_all x4, starting transfers between devices, swap(): return lax.all_to_all(x, axis, 0, 0)  32.7 us
    all_gather x2, blocking collectives, all_rows(): return lax.all_gather(chunk, CONTEXT, tiled=True)  26.2 us
    all_to_all x2, blocking collectives, swap(): return lax.all_to_all(x, axis, 0, 0)  25.8 us
    all_to_all x4, waiting for transfers between devices, swap(): return lax.all_to_all(x, axis, 0, 0)  16.6 us
    ppermute x4, starting transfers between devices, from_pair(): return lax.ppermute(x, 'x', [(i, i ^ bit) for i in range(CTX // 2)])  11.9 us
    dot_general x32, matrix products, dot(): return lax.dot_general(a, b, (dims, ((), ())), preferred_element_type=F32)  9.9 us
    ppermute x4, starting transfers between devices, from_core(): return lax.ppermute(x, 'core', [(0, 1), (1, 0)])  8 us
  transfers between devices with their start and end apart: 12, of which 10 were waited for; matrix products, arithmetic and copies ran while one was open for 6% of the time, Pallas kernels for 2%

profile of v16, /device:TPU:6, one launch (start us, length us, event | category | flops | bytes accessed | tf_op | source)
XLA Modules:
  0.0 202.8 jit_solution(12674553727061192146)
XLA Ops:
  0.6 2.1 %shard_map.93 = (bf16[128,2048]{1,0:T(8,128)(2,1)}, bf16[8,4,32,128]{3,2,1,0:T(8,128)(2,1)}) custom-call(bf16[128,2048]{1,0:T(8,128)(2,1)} %bitcast.120, bf16[128,2048]{1,0:T(8,128)(2,1)} %bitcast.121, bf16[3,32,128]{2,1,0:T(8,128)(2,1)} %w_qkv.1, bf16[32,128]{1,0:T(8,128)(2,1)} %bitcast.126), custom_call_target="tpu_custom_call" | custom-call | tf_op jit(solution)/shard_map/pallas_call | solution.py:127
  2.8 1.9 collective-permute-start
  4.7 15.1 %all-to-all-start = ((bf16[8,4,32,128]{3,2,1,0:T(8,128)(2,1)}), bf16[8,4,32,128]{3,2,1,0:T(8,128)(2,1)S(1)}, u32[]{:S(2)}, u32[]{:S(2)}) async-start(bf16[8,4,32,128]{3,2,1,0:T(8,128)(2,1)} %get-tuple-element.26), calls=%async_computation | async-start | bytes 524288 | tf_op jit(solution)/shard_map/all_to_all | solution.py:23
  19.8 1.4 constant_dynamic-slice_fusion.1
  22.5 1.3 select_select_fusion
  23.9 2.7 %collective-permute-start.1 = (bf16[128,2048]{1,0:T(8,128)(2,1)S(1)}, bf16[128,2048]{1,0:T(8,128)(2,1)S(1)}, u32[]{:S(2)}, u32[]{:S(2)}) collective-permute-start(bf16[128,2048]{1,0:T(8,128)(2,1)S(1)} %select_select_fusion), channel_id=1, source_target_pairs={{0,2},{2,0},{4,6},{6,4},{1,3},{3,1},{5,7},{7,5},{8,10},{10,8},{12,... | collective-permute-start | bytes 1572872 | tf_op jit(solution)/shard_map/ppermute | solution.py:43
  26.6 13.2 %collective-permute-done.1 = bf16[128,2048]{1,0:T(8,128)(2,1)S(1)} collective-permute-done((bf16[128,2048]{1,0:T(8,128)(2,1)S(1)}, bf16[128,2048]{1,0:T(8,128)(2,1)S(1)}, u32[]{:S(2)}, u32[]{:S(2)}) %collective-permute-start.1) | collective-permute-done | bytes 524320 | tf_op jit(solution)/shard_map/ppermute | solution.py:43
  40.0 1.9 all-to-all-done.near
  41.8 1.4 shard_map.94
  43.3 4.5 %all-to-all-start.1 = ((bf16[8,8,4,32,128]{4,3,1,2,0:T(8,128)(2,1)}), bf16[8,8,4,32,128]{4,3,1,2,0:T(8,128)(2,1)S(1)}, u32[]{:S(2)}, u32[]{:S(2)}) async-start(bf16[8,8,4,32,128]{4,3,1,2,0:T(8,128)(2,1)} %bitcast.7), calls=%async_computation.1 | async-start | bytes 4194304 | tf_op jit(solution)/shard_map/all_to_all | solution.py:23
  47.8 2.4 %collective-permute-start.2 = (bf16[128,2048]{1,0:T(8,128)(2,1)S(1)}, bf16[128,2048]{1,0:T(8,128)(2,1)S(1)}, u32[]{:S(2)}, u32[]{:S(2)}) collective-permute-start(bf16[128,2048]{1,0:T(8,128)(2,1)S(1)} %add.86), channel_id=1, source_target_pairs={{0,6},{2,4},{4,2},{6,0},{1,7},{3,5},{5,3},{7,1},{8,14},{10,12},{12... | collective-permute-start | bytes 1572872 | tf_op jit(solution)/shard_map/ppermute | solution.py:43
  50.2 14.2 %collective-permute-done.2 = bf16[128,2048]{1,0:T(8,128)(2,1)S(1)} collective-permute-done((bf16[128,2048]{1,0:T(8,128)(2,1)S(1)}, bf16[128,2048]{1,0:T(8,128)(2,1)S(1)}, u32[]{:S(2)}, u32[]{:S(2)}) %collective-permute-start.2) | collective-permute-done | bytes 524320 | tf_op jit(solution)/shard_map/ppermute | solution.py:43
  64.5 1.9 collective-permute-start.3
  66.4 0.6 compare_reduce_fusion
  67.0 1.2 collective-permute-done.3
  68.3 1.7 broadcast_select_fusion.5
  70.4 3.5 %all-to-all-done.1 = bf16[8,8,4,32,128]{4,3,1,2,0:T(8,128)(2,1)S(1)} async-done(((bf16[8,8,4,32,128]{4,3,1,2,0:T(8,128)(2,1)}), bf16[8,8,4,32,128]{4,3,1,2,0:T(8,128)(2,1)S(1)}, u32[]{:S(2)}, u32[]{:S(2)}) %all-to-all-start.1) | async-done | bytes 2097184 | tf_op jit(solution)/shard_map/all_to_all | solution.py:23
  76.1 12.9 %all_to_all.30 = bf16[8,16,2048]{2,1,0:T(8,128)(2,1)S(1)} all-to-all(bf16[8,16,2048]{2,1,0:T(8,128)(2,1)S(1)} %bitcast.122), channel_id=1, replica_groups=mesh['zp'=8,'zq'=2,'y'=4,'x'=4,'core'=2] {'x','core'}, dimensions={0} | all-to-all | bytes 1048576 | tf_op jit(solution)/shard_map/all_to_all | solution.py:23
  89.1 13.1 %all_gather.6 = bf16[128,2048]{1,0:T(8,128)(2,1)S(1)} all-gather(bf16[16,2048]{1,0:T(8,128)(2,1)S(1)} %fusion.26), channel_id=1, replica_groups=mesh['zp'=8,'zq'=2,'y'=4,'x'=4,'core'=2] {'x','core'}, dimensions={0}, use_global_device_ids=true | all-gather | bytes 589824 | tf_op jit(solution)/shard_map/all_gather | solution.py:52
  102.4 0.9 fusion.19
  106.6 12.9 %all_to_all.31 = bf16[8,16,2048]{2,1,0:T(8,128)(2,1)S(1)} all-to-all(bf16[8,16,2048]{2,1,0:T(8,128)(2,1)S(1)} %bitcast.123), channel_id=1, replica_groups=mesh['zp'=8,'zq'=2,'y'=4,'x'=4,'core'=2] {'x','core'}, dimensions={0} | all-to-all | bytes 1048576 | tf_op jit(solution)/shard_map/all_to_all | solution.py:23
  119.8 0.9 fusion.24
  120.7 13.1 %all_gather.7 = bf16[128,2048]{1,0:T(8,128)(2,1)S(1)} all-gather(bf16[16,2048]{1,0:T(8,128)(2,1)S(1)} %fusion.24), channel_id=1, replica_groups=mesh['zp'=8,'zq'=2,'y'=4,'x'=4,'core'=2] {'x','core'}, dimensions={0}, use_global_device_ids=true | all-gather | bytes 589824 | tf_op jit(solution)/shard_map/all_gather | solution.py:52
  134.8 0.5 convolution_convert_fusion.1
  135.3 0.5 convolution_convert_fusion.2
  135.8 0.5 convolution_convert_fusion.3
  136.3 0.5 convolution_convert_fusion.4
  137.0 1.3 copy-done
  138.4 3.6 %all-to-all-start.4 = ((bf16[8,8,4,32,128]{4,3,2,1,0:T(8,128)(2,1)}), bf16[8,8,4,32,128]{4,3,2,1,0:T(8,128)(2,1)S(1)}, u32[]{:S(2)}, u32[]{:S(2)}) async-start(bf16[8,8,4,32,128]{4,3,2,1,0:T(8,128)(2,1)} %copy-done), calls=%async_computation.4 | async-start | bytes 4194304 | tf_op jit(solution)/shard_map/all_to_all | solution.py:23
  142.0 1.4 convolution_convert_fusion
  144.0 0.4 copy-done.6
  144.7 2.2 %collective-permute-start.4 = (bf16[128,2048]{1,0:T(8,128)(2,1)S(1)}, bf16[128,2048]{1,0:T(8,128)(2,1)S(1)}, u32[]{:S(2)}, u32[]{:S(2)}) collective-permute-start(bf16[128,2048]{1,0:T(8,128)(2,1)S(1)} %get-tuple-element.71), channel_id=1, source_target_pairs={{0,1},{1,0},{2,3},{3,2},{4,5},{5,4},{6,7},{7,6},{8,9},{9,8},{10,11... | collective-permute-start | bytes 1572872 | tf_op jit(solution)/shard_map/ppermute | solution.py:39
  147.0 1.6 collective-permute-done.4
  148.8 2.8 %collective-permute-start.5 = (bf16[128,2048]{1,0:T(8,128)(2,1)S(1)}, bf16[128,2048]{1,0:T(8,128)(2,1)S(1)}, u32[]{:S(2)}, u32[]{:S(2)}) collective-permute-start(bf16[128,2048]{1,0:T(8,128)(2,1)S(1)} %add_convert_fusion.2), channel_id=1, source_target_pairs={{0,2},{2,0},{4,6},{6,4},{1,3},{3,1},{5,7},{7,5},{8,10},{10,8},{12,... | collective-permute-start | bytes 1572872 | tf_op jit(solution)/shard_map/ppermute | solution.py:43
  151.6 13.3 %collective-permute-done.5 = bf16[128,2048]{1,0:T(8,128)(2,1)S(1)} collective-permute-done((bf16[128,2048]{1,0:T(8,128)(2,1)S(1)}, bf16[128,2048]{1,0:T(8,128)(2,1)S(1)}, u32[]{:S(2)}, u32[]{:S(2)}) %collective-permute-start.5) | collective-permute-done | bytes 524320 | tf_op jit(solution)/shard_map/ppermute | solution.py:43
  164.9 0.9 add_convert_fusion.1
  165.8 4.0 %collective-permute-start.6 = (bf16[128,2048]{1,0:T(8,128)(2,1)}, bf16[128,2048]{1,0:T(8,128)(2,1)}, u32[]{:S(2)}, u32[]{:S(2)}) collective-permute-start(bf16[128,2048]{1,0:T(8,128)(2,1)} %add_convert_fusion.1), channel_id=1, source_target_pairs={{0,6},{2,4},{4,2},{6,0},{1,7},{3,5},{5,3},{7,1},{8,14},{10,12},{12... | collective-permute-start | bytes 1572872 | tf_op jit(solution)/shard_map/ppermute | solution.py:43
  170.0 1.0 shard_map.96
  170.9 9.5 %all-to-all-start.5 = ((bf16[8,4,32,128]{3,2,1,0:T(8,128)(2,1)}), bf16[8,4,32,128]{3,2,1,0:T(8,128)(2,1)S(1)}, u32[]{:S(2)}, u32[]{:S(2)}) async-start(bf16[8,4,32,128]{3,2,1,0:T(8,128)(2,1)} %shard_map.96), calls=%async_computation.5 | async-start | bytes 524288 | tf_op jit(solution)/shard_map/all_to_all | solution.py:23
  180.4 2.1 %collective-permute-done.6 = bf16[128,2048]{1,0:T(8,128)(2,1)} collective-permute-done((bf16[128,2048]{1,0:T(8,128)(2,1)}, bf16[128,2048]{1,0:T(8,128)(2,1)}, u32[]{:S(2)}, u32[]{:S(2)}) %collective-permute-start.6) | collective-permute-done | bytes 524320 | tf_op jit(solution)/shard_map/ppermute | solution.py:43
  182.6 1.3 add_convert_fusion.tile
  183.9 1.9 collective-permute-start.7
  185.8 1.3 broadcast_select_fusion
  187.1 0.6 collective-permute-done.7.other
  187.7 2.6 %shard_map.97 = (bf16[128,2048]{1,0:T(8,128)(2,1)}, bf16[128,2048]{1,0:T(8,128)(2,1)}) custom-call(s32[2]{0:T(128)S(1)} %pad_add_fusion.flags, bf16[128,2048]{1,0:T(8,128)(2,1)S(1)} %add_convert_fusion.tile, bf16[128,2048]{1,0:T(8,128)(2,1)S(1)} %collective-permute-done.7.other, bf16[128,2048]{1,0:T(8,128)(2,1)S(1)} %get-tuple-element.74.base_h, ...), custom_call_target="tpu_custom_call" | custom-call | tf_op jit(solution)/shard_map/pallas_call | solution.py:210
  190.3 11.2 %all-to-all-done.5 = bf16[8,4,32,128]{3,2,1,0:T(8,128)(2,1)S(1)} async-done(((bf16[8,4,32,128]{3,2,1,0:T(8,128)(2,1)}), bf16[8,4,32,128]{3,2,1,0:T(8,128)(2,1)S(1)}, u32[]{:S(2)}, u32[]{:S(2)}) %all-to-all-start.5) | async-done | bytes 262176 | tf_op jit(solution)/shard_map/all_to_all | solution.py:23
  201.5 0.6 convert_reduce_fusion.2
  202.2 0.6 convert_reduce_fusion.3
  (73 shorter events, 8.9 us)
Async XLA Ops:
  2.8 19.8 %collective-permute-start = (bf16[128,2048]{1,0:T(8,128)(2,1)}, bf16[128,2048]{1,0:T(8,128)(2,1)S(1)}, u32[]{:S(2)}, u32[]{:S(2)}) collective-permute-start(bf16[128,2048]{1,0:T(8,128)(2,1)} %get-tuple-element.27), channel_id=1, source_target_pairs={{0,1},{1,0},{2,3},{3,2},{4,5},{5,4},{6,7},{7,6},{8,9},{9,8},{10,11... | collective-permute-start | bytes 1572872 | tf_op jit(solution)/shard_map/ppermute | solution.py:39
  4.7 37.1 %all-to-all-start = ((bf16[8,4,32,128]{3,2,1,0:T(8,128)(2,1)}), bf16[8,4,32,128]{3,2,1,0:T(8,128)(2,1)S(1)}, u32[]{:S(2)}, u32[]{:S(2)}) async-start(bf16[8,4,32,128]{3,2,1,0:T(8,128)(2,1)} %get-tuple-element.26), calls=%async_computation | async-start | bytes 524288 | tf_op jit(solution)/shard_map/all_to_all | solution.py:23
  23.9 15.9 %collective-permute-start.1 = (bf16[128,2048]{1,0:T(8,128)(2,1)S(1)}, bf16[128,2048]{1,0:T(8,128)(2,1)S(1)}, u32[]{:S(2)}, u32[]{:S(2)}) collective-permute-start(bf16[128,2048]{1,0:T(8,128)(2,1)S(1)} %select_select_fusion), channel_id=1, source_target_pairs={{0,2},{2,0},{4,6},{6,4},{1,3},{3,1},{5,7},{7,5},{8,10},{10,8},{12,... | collective-permute-start | bytes 1572872 | tf_op jit(solution)/shard_map/ppermute | solution.py:43
  43.3 23.1 %copy-start.10 = (s32[1,8]{1,0:T(1,128)S(1)}, s32[1,8]{1,0:T(1,128)}, u32[]{:S(2)}) copy-start(s32[1,8]{1,0:T(1,128)} %param.8) | copy-start | bytes 100
  43.3 30.6 %all-to-all-start.1 = ((bf16[8,8,4,32,128]{4,3,1,2,0:T(8,128)(2,1)}), bf16[8,8,4,32,128]{4,3,1,2,0:T(8,128)(2,1)S(1)}, u32[]{:S(2)}, u32[]{:S(2)}) async-start(bf16[8,8,4,32,128]{4,3,1,2,0:T(8,128)(2,1)} %bitcast.7), calls=%async_computation.1 | async-start | bytes 4194304 | tf_op jit(solution)/shard_map/all_to_all | solution.py:23
  47.8 22.4 %copy-start.1 = (f32[2048]{0:T(1024)S(1)}, f32[2048]{0:T(1024)}, u32[]{:S(2)}) copy-start(f32[2048]{0:T(1024)} %param.11) | copy-start | bytes 24580
  47.8 16.5 %collective-permute-start.2 = (bf16[128,2048]{1,0:T(8,128)(2,1)S(1)}, bf16[128,2048]{1,0:T(8,128)(2,1)S(1)}, u32[]{:S(2)}, u32[]{:S(2)}) collective-permute-start(bf16[128,2048]{1,0:T(8,128)(2,1)S(1)} %add.86), channel_id=1, source_target_pairs={{0,6},{2,4},{4,2},{6,0},{1,7},{3,5},{5,3},{7,1},{8,14},{10,12},{12... | collective-permute-start | bytes 1572872 | tf_op jit(solution)/shard_map/ppermute | solution.py:43
  64.5 3.8 %collective-permute-start.3 = (bf16[128,2048]{1,0:T(8,128)(2,1)S(1)}, bf16[128,2048]{1,0:T(8,128)(2,1)S(1)}, u32[]{:S(2)}, u32[]{:S(2)}) collective-permute-start(bf16[128,2048]{1,0:T(8,128)(2,1)S(1)} %add.87), channel_id=1, source_target_pairs={{0,1},{1,0},{2,3},{3,2},{4,5},{5,4},{6,7},{7,6},{8,9},{9,8},{10,11... | collective-permute-start | bytes 1572872 | tf_op jit(solution)/shard_map/ppermute | solution.py:39
  74.3 31.7 %copy-start.3 = (bf16[1,8,8,32,128]{4,3,2,1,0:T(8,128)(2,1)}, bf16[1,8,8,32,128]{4,3,2,1,0:T(8,128)(2,1)S(1)}, u32[]{:S(2)}) copy-start(bf16[1,8,8,32,128]{4,3,2,1,0:T(8,128)(2,1)S(1)} %copy.16) | copy-start | bytes 1572868
  75.0 31.3 %copy-start.5 = (bf16[1,8,8,32,128]{4,3,2,1,0:T(8,128)(2,1)}, bf16[1,8,8,32,128]{4,3,2,1,0:T(8,128)(2,1)S(1)}, u32[]{:S(2)}) copy-start(bf16[1,8,8,32,128]{4,3,2,1,0:T(8,128)(2,1)S(1)} %copy.17) | copy-start | bytes 1572868
  75.3 58.5 %copy-start.2 = (bf16[1,8,8,32,128]{4,3,2,1,0:T(8,128)(2,1)}, bf16[1,8,8,32,128]{4,3,2,1,0:T(8,128)(2,1)S(1)}, u32[]{:S(2)}) copy-start(bf16[1,8,8,32,128]{4,3,2,1,0:T(8,128)(2,1)S(1)} %copy.18) | copy-start | bytes 1572868
  102.2 17.6 %copy-start.7 = (bf16[128,2048]{1,0:T(8,128)(2,1)}, bf16[128,2048]{1,0:T(8,128)(2,1)S(1)}, u32[]{:S(2)}) copy-start(bf16[128,2048]{1,0:T(8,128)(2,1)S(1)} %all_gather.6) | copy-start | bytes 1572868
  102.4 1.8 copy-start.9
  133.8 1.0 copy-start.8
  137.0 1.4 copy-start
  138.4 31.6 %all-to-all-start.4 = ((bf16[8,8,4,32,128]{4,3,2,1,0:T(8,128)(2,1)}), bf16[8,8,4,32,128]{4,3,2,1,0:T(8,128)(2,1)S(1)}, u32[]{:S(2)}, u32[]{:S(2)}) async-start(bf16[8,8,4,32,128]{4,3,2,1,0:T(8,128)(2,1)} %copy-done), calls=%async_computation.4 | async-start | bytes 4194304 | tf_op jit(solution)/shard_map/all_to_all | solution.py:23
  142.0 1.7 copy-start.4
  143.4 1.0 copy-start.6
  144.7 3.8 %collective-permute-start.4 = (bf16[128,2048]{1,0:T(8,128)(2,1)S(1)}, bf16[128,2048]{1,0:T(8,128)(2,1)S(1)}, u32[]{:S(2)}, u32[]{:S(2)}) collective-permute-start(bf16[128,2048]{1,0:T(8,128)(2,1)S(1)} %get-tuple-element.71), channel_id=1, source_target_pairs={{0,1},{1,0},{2,3},{3,2},{4,5},{5,4},{6,7},{7,6},{8,9},{9,8},{10,11... | collective-permute-start | bytes 1572872 | tf_op jit(solution)/shard_map/ppermute | solution.py:39
  148.8 16.1 %collective-permute-start.5 = (bf16[128,2048]{1,0:T(8,128)(2,1)S(1)}, bf16[128,2048]{1,0:T(8,128)(2,1)S(1)}, u32[]{:S(2)}, u32[]{:S(2)}) collective-permute-start(bf16[128,2048]{1,0:T(8,128)(2,1)S(1)} %add_convert_fusion.2), channel_id=1, source_target_pairs={{0,2},{2,0},{4,6},{6,4},{1,3},{3,1},{5,7},{7,5},{8,10},{10,8},{12,... | collective-permute-start | bytes 1572872 | tf_op jit(solution)/shard_map/ppermute | solution.py:43
  165.8 16.8 %collective-permute-start.6 = (bf16[128,2048]{1,0:T(8,128)(2,1)}, bf16[128,2048]{1,0:T(8,128)(2,1)}, u32[]{:S(2)}, u32[]{:S(2)}) collective-permute-start(bf16[128,2048]{1,0:T(8,128)(2,1)} %add_convert_fusion.1), channel_id=1, source_target_pairs={{0,6},{2,4},{4,2},{6,0},{1,7},{3,5},{5,3},{7,1},{8,14},{10,12},{12... | collective-permute-start | bytes 1572872 | tf_op jit(solution)/shard_map/ppermute | solution.py:43
  170.9 30.6 %all-to-all-start.5 = ((bf16[8,4,32,128]{3,2,1,0:T(8,128)(2,1)}), bf16[8,4,32,128]{3,2,1,0:T(8,128)(2,1)S(1)}, u32[]{:S(2)}, u32[]{:S(2)}) async-start(bf16[8,4,32,128]{3,2,1,0:T(8,128)(2,1)} %shard_map.96), calls=%async_computation.5 | async-start | bytes 524288 | tf_op jit(solution)/shard_map/all_to_all | solution.py:23
  183.9 3.8 %collective-permute-start.7 = (bf16[128,2048]{1,0:T(8,128)(2,1)S(1)}, bf16[128,2048]{1,0:T(8,128)(2,1)S(1)}, u32[]{:S(2)}, u32[]{:S(2)}) collective-permute-start(bf16[128,2048]{1,0:T(8,128)(2,1)S(1)} %add_convert_fusion.tile), channel_id=1, source_target_pairs={{0,1},{1,0},{2,3},{3,2},{4,5},{5,4},{6,7},{7,6},{8,9},{9,8},{10,11... | collective-permute-start | bytes 1572872 | tf_op jit(solution)/shard_map/ppermute | solution.py:39
